TPU v7x, 32 devices: a whole 2x2x4 slice. The times are simulated.
32 devices in a mesh: dp: 8 (over z, x), tensor: 4 (over y, core).
Axes of the slice: x: 2, y: 2, z: 4, core: 2. Of those that a mesh axis runs over, the one named last changes fastest.
Arguments:
- hidden_in: bfloat16 [2, 8, 256, 1152], P(None, 'dp'), may hold values from -6 to 6
- grad_out: bfloat16 [2, 8, 256, 1152], P(None, 'dp'), may hold values from -0.0059814453 to 0.0059814453
- features: bfloat16 [2, 8, 256, 768], P(None, 'dp'), may hold values from -6 to 6
- seg_ids: int32 [2, 8, 256], P(None, 'dp'), may hold values from 0 to 3, never falling along the last dimension, each value on 1 to 128 neighbouring positions
- valid_mask: int32 [2, 8, 256], P(None, 'dp'), may hold values 0 or 1
- time_ids: int32 [2, 8, 4], P(None, 'dp'), may hold values from 0 to 999
- class_ids: int32 [2, 8, 4], P(None, 'dp'), may hold values from 0 to 1000
- class_table: bfloat16 [1152, 1001], P('dp'), may hold values from -6 to 6
- ada_w: bfloat16 [6912, 1152], P('dp'), may hold values from -0.1875 to 0.1875
- ada_b: bfloat16 [6912], P('dp'), may hold values from -3 to 3
- qkv_w: bfloat16 [3, 1152, 1152], P(None, None, 'tensor'), may hold values from -0.1875 to 0.1875
- qv_bias: bfloat16 [2, 1152], P(None, 'tensor'), may hold values from -3 to 3
- out_w: bfloat16 [1152, 1152], P('tensor'), may hold values from -0.75 to 0.75
- out_b: bfloat16 [1152], replicated, may hold values from -3 to 3
- fc1_w: bfloat16 [1152, 4608], P(None, 'tensor'), may hold values from -0.1875 to 0.1875
- fc1_b: bfloat16 [4608], P('tensor'), may hold values from -3 to 3
- fc2_w: bfloat16 [4608, 1152], P('tensor'), may hold values from -0.09375 to 0.09375
- fc2_b: bfloat16 [1152], replicated, may hold values from -3 to 3
- repa_w1: bfloat16 [1152, 2048], P('dp'), may hold values from -0.1875 to 0.1875
- repa_b1: bfloat16 [2048], P('dp'), may hold values from -3 to 3
- repa_w2: bfloat16 [2048, 2048], P('dp'), may hold values from -0.125 to 0.125
- repa_b2: bfloat16 [2048], P('dp'), may hold values from -3 to 3
- repa_w3: bfloat16 [2048, 768], P('dp'), may hold values from -0.125 to 0.125
- repa_b3: bfloat16 [768], P('dp'), may hold values from -3 to 3
Outputs:
- block_out: bfloat16 [2, 8, 256, 1152], P(None, 'dp')
- grad_in: float32 [2, 8, 256, 1152], P(None, 'dp')
- grad_class_table: float32 [1152, 1001], P('dp')
- grad_ada_w: float32 [6912, 1152], P('dp')
- grad_ada_b: float32 [6912], P('dp')
- grad_qkv_w: float32 [3, 1152, 1152], P(None, 'dp', 'tensor')
- grad_qv_bias: float32 [2, 1152], P(None, 'tensor')
- grad_out_w: float32 [1152, 1152], P('tensor', 'dp')
- grad_out_b: float32 [1152], replicated
- grad_fc1_w: float32 [1152, 4608], P('dp', 'tensor')
- grad_fc1_b: float32 [4608], P('tensor')
- grad_fc2_w: float32 [4608, 1152], P('tensor', 'dp')
- grad_fc2_b: float32 [1152], replicated
- grad_repa_w1: float32 [1152, 2048], P('dp')
- grad_repa_b1: float32 [2048], P('dp')
- grad_repa_w2: float32 [2048, 2048], P('dp')
- grad_repa_b2: float32 [2048], P('dp')
- grad_repa_w3: float32 [2048, 768], P('dp')
- grad_repa_b3: float32 [768], P('dp')
Inputs may be any that keep to these rules, and one draw needn't show every extreme that they name: `seg_ids`: within each row the ids never fall, every image 0 to 3 appears, and no image has more than half of 256 tokens.
All inputs are finite; a program needn't handle non-finite values. No bound on the sum of `valid_mask` on one device may be relied on, other than what follows from the above.
Results may differ from a plain program's by a relative error of at most 0.02615.
Values may be sent and summed in bfloat16 or wider, within the bound.
No kernel may reach another device: no remote copies, remote signals or barrier semaphores. Data moves between devices by JAX's collectives and lax.ppermute only.
A program may use at most 320 MiB of HBM per device.

v0:
```python
import math

import jax
import jax.numpy as jnp
from jax import lax
from jax.sharding import PartitionSpec as P

HEAD_DIM = 72


HIGH = lax.Precision.HIGHEST
norm_eps = 1e-06
cos_eps = 1e-06
repa_weight = 0.5


def sinusoid(times, model_width):
    half_width = model_width // 2
    freqs = jnp.exp(-math.log(10000.0) * jnp.arange(half_width, dtype=jnp.float32) / half_width)
    angles = times.astype(jnp.float32)[:, None] * freqs[None, :]
    return jnp.concatenate([jnp.cos(angles), jnp.sin(angles)], axis=-1)


def layer_norm(field):
    centered = field - jnp.mean(field, axis=-1, keepdims=True)
    return centered * lax.rsqrt(jnp.mean(centered * centered, axis=-1, keepdims=True) + norm_eps)


def modulate(field, shift, scaling):
    return layer_norm(field) * (1.0 + scaling) + shift


def silu_slope(field):
    sigma = jax.nn.sigmoid(field)
    return sigma * (1.0 + field * (1.0 - sigma))


def open_pairs(row_seg, row_valid):
    seq_len = row_seg.shape[0]
    query_pos = lax.broadcasted_iota(jnp.int32, (seq_len, seq_len), 0)
    key_pos = lax.broadcasted_iota(jnp.int32, (seq_len, seq_len), 1)
    return (row_seg[:, None] == row_seg[None, :]) & (
        (row_valid[None, :] == 1) | (query_pos == key_pos)
    )


def masked_scores(queries, key_rows, row_seg, row_valid):
    score_scale = queries.shape[-1] ** (-0.5)
    scores = (
        jnp.einsum("qhd,khd->hqk", queries, key_rows, preferred_element_type=jnp.float32)
        * score_scale
    )
    return jnp.where(open_pairs(row_seg, row_valid)[None], scores, -1e30)


def attend_row(pieces):
    queries, key_rows, value_rows, row_seg, row_valid = pieces
    scores = masked_scores(queries, key_rows, row_seg, row_valid)
    row_top = jnp.max(scores, axis=-1, keepdims=True)
    exponent = jnp.exp(scores - row_top)
    row_total = jnp.sum(exponent, axis=-1, keepdims=True)
    probs = (exponent / row_total).astype(jnp.bfloat16)
    mixed = jnp.einsum("hqk,khd->qhd", probs, value_rows, preferred_element_type=jnp.float32)
    log_total = row_top[..., 0] + jnp.log(row_total[..., 0])
    return (mixed.reshape(mixed.shape[0], -1).astype(jnp.bfloat16), log_total)


def attend_back_row(pieces):
    queries, key_rows, value_rows, grad_mixed, log_total, row_seg, row_valid = pieces
    score_scale = queries.shape[-1] ** (-0.5)
    scores = masked_scores(queries, key_rows, row_seg, row_valid)
    probs = jnp.exp(scores - log_total[..., None])
    grad_probs = jnp.einsum(
        "qhd,khd->hqk", grad_mixed, value_rows, preferred_element_type=jnp.float32
    )
    row_delta = jnp.sum(probs * grad_probs, axis=-1, keepdims=True)
    grad_scores = (probs * (grad_probs - row_delta)).astype(jnp.bfloat16)
    grad_q = (
        jnp.einsum("hqk,khd->qhd", grad_scores, key_rows, preferred_element_type=jnp.float32)
        * score_scale
    ).astype(jnp.bfloat16)
    grad_k = (
        jnp.einsum("hqk,qhd->khd", grad_scores, queries, preferred_element_type=jnp.float32)
        * score_scale
    ).astype(jnp.bfloat16)
    grad_v = jnp.einsum(
        "hqk,qhd->khd", probs.astype(jnp.bfloat16), grad_mixed, preferred_element_type=jnp.float32
    ).astype(jnp.bfloat16)
    seq_len = queries.shape[0]
    return (grad_q.reshape(seq_len, -1), grad_k.reshape(seq_len, -1), grad_v.reshape(seq_len, -1))


def settle(pieces):
    (
        g_table,
        g_fc1_w,
        g_w1,
        g_b1,
        g_w2,
        g_b2,
        g_w3,
        g_b3,
        g_ada_w,
        g_ada_b,
        g_qkv_w,
        g_out_w,
        g_fc2_w,
        g_qv_bias,
        g_out_b,
        g_fc1_b,
        g_fc2_b,
    ) = pieces
    row_part = (
        lax.psum_scatter(
            g_table.astype(jnp.bfloat16), "dp", scatter_dimension=0, tiled=True
        ).astype(jnp.float32),
        lax.psum_scatter(
            g_fc1_w.astype(jnp.bfloat16), "dp", scatter_dimension=0, tiled=True
        ).astype(jnp.float32),
        lax.psum_scatter(g_w1.astype(jnp.bfloat16), "dp", scatter_dimension=0, tiled=True).astype(
            jnp.float32
        ),
        lax.psum_scatter(g_b1.astype(jnp.bfloat16), "dp", scatter_dimension=0, tiled=True).astype(
            jnp.float32
        ),
        lax.psum_scatter(g_w2.astype(jnp.bfloat16), "dp", scatter_dimension=0, tiled=True).astype(
            jnp.float32
        ),
        lax.psum_scatter(g_b2.astype(jnp.bfloat16), "dp", scatter_dimension=0, tiled=True).astype(
            jnp.float32
        ),
        lax.psum_scatter(g_w3.astype(jnp.bfloat16), "dp", scatter_dimension=0, tiled=True).astype(
            jnp.float32
        ),
        lax.psum_scatter(g_b3.astype(jnp.bfloat16), "dp", scatter_dimension=0, tiled=True).astype(
            jnp.float32
        ),
        lax.psum_scatter(
            g_ada_w.astype(jnp.bfloat16), "dp", scatter_dimension=0, tiled=True
        ).astype(jnp.float32),
        lax.psum_scatter(
            g_ada_b.astype(jnp.bfloat16), "dp", scatter_dimension=0, tiled=True
        ).astype(jnp.float32),
    )
    col_part = (
        lax.psum_scatter(
            g_qkv_w.astype(jnp.bfloat16), "dp", scatter_dimension=1, tiled=True
        ).astype(jnp.float32),
        lax.psum_scatter(
            g_out_w.astype(jnp.bfloat16), "dp", scatter_dimension=1, tiled=True
        ).astype(jnp.float32),
        lax.psum_scatter(
            g_fc2_w.astype(jnp.bfloat16), "dp", scatter_dimension=1, tiled=True
        ).astype(jnp.float32),
    )
    bias_part = lax.psum((g_qv_bias, g_out_b, g_fc1_b, g_fc2_b), "dp")
    return tuple(row_part) + tuple(col_part) + tuple(bias_part)


def add_tuples(first, second):
    if first is None:
        return tuple(second)
    return tuple((left + right for left, right in zip(first, second)))


def body(
    hidden_in,
    grad_out,
    features,
    seg_ids,
    valid_mask,
    time_ids,
    class_ids,
    class_table,
    ada_w,
    ada_b,
    qkv_w,
    qv_bias,
    out_w,
    out_b,
    fc1_w,
    fc1_b,
    fc2_w,
    fc2_b,
    repa_w1,
    repa_b1,
    repa_w2,
    repa_b2,
    repa_w3,
    repa_b3,
):
    micro_count, rows_dev, seq_len, model_width = hidden_in.shape
    image_slots = time_ids.shape[-1]
    tokens = rows_dev * seq_len
    images = rows_dev * image_slots
    heads_local = qkv_w.shape[2] // HEAD_DIM
    shape4 = (rows_dev, seq_len, heads_local, HEAD_DIM)
    outs_list = []
    grads_list = []
    settled = None
    pending = None
    for micro_index in range(micro_count):
        table_full, ada_full, ada_bias_full, w_one, b_one, w_two, b_two, w_three, b_three = (
            lax.all_gather(class_table, "dp", axis=0, tiled=True),
            lax.all_gather(ada_w, "dp", axis=0, tiled=True),
            lax.all_gather(ada_b, "dp", axis=0, tiled=True),
            lax.all_gather(repa_w1, "dp", axis=0, tiled=True),
            lax.all_gather(repa_b1, "dp", axis=0, tiled=True),
            lax.all_gather(repa_w2, "dp", axis=0, tiled=True),
            lax.all_gather(repa_b2, "dp", axis=0, tiled=True),
            lax.all_gather(repa_w3, "dp", axis=0, tiled=True),
            lax.all_gather(repa_b3, "dp", axis=0, tiled=True),
        )
        class_hot = class_ids[micro_index].reshape(images)[:, None] == lax.broadcasted_iota(
            jnp.int32, (images, table_full.shape[1]), 1
        )
        condition = sinusoid(time_ids[micro_index].reshape(images), model_width) + jnp.einsum(
            "ic,dc->id",
            class_hot.astype(jnp.bfloat16),
            table_full,
            preferred_element_type=jnp.float32,
        )
        cond_act = jax.nn.silu(condition).astype(jnp.bfloat16)
        modulation = jnp.einsum(
            "id,od->io", cond_act, ada_full, preferred_element_type=jnp.float32
        ) + ada_bias_full.astype(jnp.float32)
        image_of = (
            lax.broadcasted_iota(jnp.int32, (rows_dev, seq_len), 0) * image_slots
            + seg_ids[micro_index]
        ).reshape(tokens)
        image_hot = (
            image_of[:, None] == lax.broadcasted_iota(jnp.int32, (tokens, images), 1)
        ).astype(jnp.float32)
        token_mod = jnp.dot(
            image_hot, modulation, precision=HIGH, preferred_element_type=jnp.float32
        )
        shift1, scale1, gate1, shift2, scale2, gate2 = jnp.split(token_mod, 6, axis=-1)
        x_now = hidden_in[micro_index].reshape(tokens, model_width).astype(jnp.float32)
        m_one_full, ln_one_back = jax.vjp(modulate, x_now, shift1, scale1)
        m_one = m_one_full.astype(jnp.bfloat16)
        queries = (
            jnp.dot(m_one, qkv_w[0], preferred_element_type=jnp.float32)
            + qv_bias[0].astype(jnp.float32)
        ).astype(jnp.bfloat16)
        key_rows = jnp.dot(m_one, qkv_w[1], preferred_element_type=jnp.float32).astype(jnp.bfloat16)
        value_rows = (
            jnp.dot(m_one, qkv_w[2], preferred_element_type=jnp.float32)
            + qv_bias[1].astype(jnp.float32)
        ).astype(jnp.bfloat16)
        q_four = queries.reshape(shape4)
        k_four = key_rows.reshape(shape4)
        v_four = value_rows.reshape(shape4)
        mixed, log_total = lax.map(
            attend_row, (q_four, k_four, v_four, seg_ids[micro_index], valid_mask[micro_index])
        )
        mixed = mixed.reshape(tokens, -1)
        attn_out = lax.psum(
            jnp.dot(mixed, out_w, preferred_element_type=jnp.float32), "tensor"
        ) + out_b.astype(jnp.float32)
        h_one = x_now + gate1 * attn_out
        m_two_full, ln_two_back = jax.vjp(modulate, h_one, shift2, scale2)
        m_two = m_two_full.astype(jnp.bfloat16)
        hidden_pre = jnp.dot(m_two, fc1_w, preferred_element_type=jnp.float32) + fc1_b.astype(
            jnp.float32
        )
        hidden_full, gelu_back = jax.vjp(
            lambda field: jax.nn.gelu(field, approximate=True), hidden_pre
        )
        hidden_act = hidden_full.astype(jnp.bfloat16)
        mlp_out = lax.psum(
            jnp.dot(hidden_act, fc2_w, preferred_element_type=jnp.float32), "tensor"
        ) + fc2_b.astype(jnp.float32)
        h_out = h_one + gate2 * mlp_out
        h_low = h_out.astype(jnp.bfloat16)
        outs_list.append(h_low.reshape(rows_dev, seq_len, model_width))
        a_one = jnp.dot(h_low, w_one, preferred_element_type=jnp.float32) + b_one.astype(
            jnp.float32
        )
        s_one = jax.nn.silu(a_one).astype(jnp.bfloat16)
        a_two = jnp.dot(s_one, w_two, preferred_element_type=jnp.float32) + b_two.astype(
            jnp.float32
        )
        s_two = jax.nn.silu(a_two).astype(jnp.bfloat16)
        z_proj = jnp.dot(s_two, w_three, preferred_element_type=jnp.float32) + b_three.astype(
            jnp.float32
        )
        feats = features[micro_index].reshape(tokens, -1).astype(jnp.float32)
        inv_z = lax.rsqrt(jnp.sum(z_proj * z_proj, axis=-1) + cos_eps)
        inv_f = lax.rsqrt(jnp.sum(feats * feats, axis=-1) + cos_eps)
        z_dot_f = jnp.sum(z_proj * feats, axis=-1)
        keep = valid_mask[micro_index].reshape(tokens).astype(jnp.float32)
        coeff = -repa_weight * keep * inv_z * inv_f
        grad_z = (coeff[:, None] * (feats - (z_dot_f * inv_z * inv_z)[:, None] * z_proj)).astype(
            jnp.bfloat16
        )
        g_w3 = jnp.einsum("ta,tb->ab", s_two, grad_z, preferred_element_type=jnp.float32)
        g_b3 = jnp.sum(grad_z.astype(jnp.float32), axis=0)
        grad_a_two = (
            jnp.einsum("tb,ab->ta", grad_z, w_three, preferred_element_type=jnp.float32)
            * silu_slope(a_two)
        ).astype(jnp.bfloat16)
        g_w2 = jnp.einsum("ta,tb->ab", s_one, grad_a_two, preferred_element_type=jnp.float32)
        g_b2 = jnp.sum(grad_a_two.astype(jnp.float32), axis=0)
        grad_a_one = (
            jnp.einsum("tb,ab->ta", grad_a_two, w_two, preferred_element_type=jnp.float32)
            * silu_slope(a_one)
        ).astype(jnp.bfloat16)
        g_w1 = jnp.einsum("ta,tb->ab", h_low, grad_a_one, preferred_element_type=jnp.float32)
        g_b1 = jnp.sum(grad_a_one.astype(jnp.float32), axis=0)
        grad_h = grad_out[micro_index].reshape(tokens, model_width).astype(
            jnp.float32
        ) + jnp.einsum("tb,ab->ta", grad_a_one, w_one, preferred_element_type=jnp.float32)
        grad_mlp = (gate2 * grad_h).astype(jnp.bfloat16)
        grad_gate2 = grad_h * mlp_out
        g_fc2_b = jnp.sum(grad_mlp.astype(jnp.float32), axis=0)
        g_fc2_w = jnp.einsum("tf,td->fd", hidden_act, grad_mlp, preferred_element_type=jnp.float32)
        grad_act = jnp.einsum("td,fd->tf", grad_mlp, fc2_w, preferred_element_type=jnp.float32)
        grad_pre = gelu_back(grad_act)[0].astype(jnp.bfloat16)
        g_fc1_b = jnp.sum(grad_pre.astype(jnp.float32), axis=0)
        g_fc1_w = jnp.einsum("td,tf->df", m_two, grad_pre, preferred_element_type=jnp.float32)
        grad_m_two = lax.psum(
            jnp.einsum("tf,df->td", grad_pre, fc1_w, preferred_element_type=jnp.float32), "tensor"
        )
        grad_h_ln, grad_shift2, grad_scale2 = ln_two_back(grad_m_two)
        grad_h_one = grad_h + grad_h_ln
        grad_attn = (gate1 * grad_h_one).astype(jnp.bfloat16)
        grad_gate1 = grad_h_one * attn_out
        g_out_b = jnp.sum(grad_attn.astype(jnp.float32), axis=0)
        g_out_w = jnp.einsum("ta,td->ad", mixed, grad_attn, preferred_element_type=jnp.float32)
        grad_mixed = jnp.einsum(
            "td,ad->ta", grad_attn, out_w, preferred_element_type=jnp.float32
        ).astype(jnp.bfloat16)
        grad_q, grad_k, grad_v = lax.map(
            attend_back_row,
            (
                q_four,
                k_four,
                v_four,
                grad_mixed.reshape(shape4),
                log_total,
                seg_ids[micro_index],
                valid_mask[micro_index],
            ),
        )
        grad_q = grad_q.reshape(tokens, -1)
        grad_k = grad_k.reshape(tokens, -1)
        grad_v = grad_v.reshape(tokens, -1)
        g_qv_bias = jnp.stack(
            [
                jnp.sum(grad_q.astype(jnp.float32), axis=0),
                jnp.sum(grad_v.astype(jnp.float32), axis=0),
            ]
        )
        g_qkv_w = jnp.stack(
            [
                jnp.einsum("td,ta->da", m_one, grad_q, preferred_element_type=jnp.float32),
                jnp.einsum("td,ta->da", m_one, grad_k, preferred_element_type=jnp.float32),
                jnp.einsum("td,ta->da", m_one, grad_v, preferred_element_type=jnp.float32),
            ]
        )
        grad_m_part = (
            jnp.einsum("ta,da->td", grad_q, qkv_w[0], preferred_element_type=jnp.float32)
            + jnp.einsum("ta,da->td", grad_k, qkv_w[1], preferred_element_type=jnp.float32)
            + jnp.einsum("ta,da->td", grad_v, qkv_w[2], preferred_element_type=jnp.float32)
        )
        grad_m_one = lax.psum(grad_m_part.astype(jnp.bfloat16), "tensor").astype(jnp.float32)
        grad_x_ln, grad_shift1, grad_scale1 = ln_one_back(grad_m_one)
        grads_list.append((grad_h_one + grad_x_ln).reshape(rows_dev, seq_len, model_width))
        token_grads = jnp.concatenate(
            [grad_shift1, grad_scale1, grad_gate1, grad_shift2, grad_scale2, grad_gate2], axis=-1
        )
        grad_mod = jnp.einsum(
            "ti,to->io", image_hot, token_grads, precision=HIGH, preferred_element_type=jnp.float32
        ).astype(jnp.bfloat16)
        g_ada_w = jnp.einsum("io,id->od", grad_mod, cond_act, preferred_element_type=jnp.float32)
        g_ada_b = jnp.sum(grad_mod.astype(jnp.float32), axis=0)
        grad_cond_act = jnp.einsum(
            "io,od->id", grad_mod, ada_full, preferred_element_type=jnp.float32
        )
        grad_cond = grad_cond_act * silu_slope(condition)
        g_table = jnp.einsum(
            "id,ic->dc",
            grad_cond,
            class_hot.astype(jnp.float32),
            precision=HIGH,
            preferred_element_type=jnp.float32,
        )
        local = (
            g_table,
            g_fc1_w,
            g_w1,
            g_b1,
            g_w2,
            g_b2,
            g_w3,
            g_b3,
            g_ada_w,
            g_ada_b,
            g_qkv_w,
            g_out_w,
            g_fc2_w,
            g_qv_bias,
            g_out_b,
            g_fc1_b,
            g_fc2_b,
        )
        pending = add_tuples(pending, local)
    settled = settle(pending)
    (
        s_table,
        s_fc1_w,
        s_w1,
        s_b1,
        s_w2,
        s_b2,
        s_w3,
        s_b3,
        s_ada_w,
        s_ada_b,
        s_qkv_w,
        s_out_w,
        s_fc2_w,
        s_qv_bias,
        s_out_b,
        s_fc1_b,
        s_fc2_b,
    ) = settled
    return (
        jnp.stack(outs_list),
        jnp.stack(grads_list),
        s_table,
        s_ada_w,
        s_ada_b,
        s_qkv_w,
        s_qv_bias,
        s_out_w,
        s_out_b,
        s_fc1_w,
        s_fc1_b,
        s_fc2_w,
        s_fc2_b,
        s_w1,
        s_b1,
        s_w2,
        s_b2,
        s_w3,
        s_b3,
    )


def solution(mesh):
    placed = (
        P(None, "dp", None, None),
        P(None, "dp", None, None),
        P(None, "dp", None, None),
        P(None, "dp", None),
        P(None, "dp", None),
        P(None, "dp", None),
        P(None, "dp", None),
        P("dp", None),
        P("dp", None),
        P("dp"),
        P(None, None, "tensor"),
        P(None, "tensor"),
        P("tensor", None),
        P(),
        P(None, "tensor"),
        P("tensor"),
        P("tensor", None),
        P(),
        P("dp", None),
        P("dp"),
        P("dp", None),
        P("dp"),
        P("dp", None),
        P("dp"),
    )
    return jax.shard_map(
        body,
        mesh=mesh,
        in_specs=placed,
        out_specs=(
            P(None, "dp", None, None),
            P(None, "dp", None, None),
            P("dp", None),
            P("dp", None),
            P("dp"),
            P(None, "dp", "tensor"),
            P(None, "tensor"),
            P("tensor", "dp"),
            P(),
            P("dp", "tensor"),
            P("tensor"),
            P("tensor", "dp"),
            P(),
            P("dp", None),
            P("dp"),
            P("dp", None),
            P("dp"),
            P("dp", None),
            P("dp"),
        ),
        check_vma=False,
    )
```

profile of v0, /device:TPU:0, one launch (start us, length us, event | category | flops | bytes accessed | tf_op | source)
XLA Modules:
  0.0 1834.5 jit_solution(11670072136833022996)
XLA Ops:
  11.2 39.3 %all-reduce.11 = (bf16[768]{0:T(1024)(128)(2,1)S(1)}, bf16[6912]{0:T(1024)(128)(2,1)S(1)}) all-reduce(bf16[768]{0:T(1024)(128)(2,1)S(1)} %dynamic-update-slice.1, bf16[6912]{0:T(1024)(128)(2,1)S(1)} %dynamic-update-slice), channel_id=1, replica_groups=mesh['dp'=8,'tensor'=4] {'dp'}, use_global_device_ids=true, to_apply=%add.1 | all-reduce | flops 7680 | bytes 30720
  53.5 11.8 all-gather.8.cloned.1.call-done
  68.5 214.8 %all-gather.10.cloned.1.call-done = bf16[6912,1152]{1,0:T(8,128)(2,1)} async-done(((bf16[864,1152]{1,0:T(8,128)(2,1)}), bf16[6912,1152]{1,0:T(8,128)(2,1)}) %all-gather.10.cloned.1.call-update) | async-done | bytes 15925264 | tf_op jit(solution)/shard_map/all_gather | solution.py:205
  283.3 9.7 convolution_add_fusion.3
  293.1 5.2 fusion.110
  298.3 9.7 convolution_add_fusion.4
  308.0 3.0 fusion.111
  311.1 4.1 fusion.29
  325.5 53.5 %all-reduce.22.cloned.1.call-done = (f32[256,1152]{1,0:T(8,128)}, f32[256,1152]{1,0:T(8,128)}) async-done(((f32[256,1152]{1,0:T(8,128)}, f32[256,1152]{1,0:T(8,128)}), (f32[256,1152]{1,0:T(8,128)}, f32[256,1152]{1,0:T(8,128)})) %all-reduce.22.cloned.1.call-update) | async-done | bytes 2359312 | tf_op jit(solution)/shard_map/psum | solution.py:257
  379.0 3.2 fusion.141
  396.0 20.5 %all-gather.1 = bf16[8,1,256]{2,1,0:T(2,128)(2,1)S(1)} all-gather(bf16[1,1,256]{2,1,0:T(2,128)(2,1)S(1)} %reshape.463), channel_id=1, replica_groups=mesh['dp'=8,'tensor'=4] {'dp'}, dimensions={0}, use_global_device_ids=true | all-gather | bytes 4608 | tf_op jit(solution)/shard_map/all_gather | solution.py:210
  416.5 16.7 all-gather
  433.3 16.7 all-reduce.20.cloned.1.call-done
  450.0 4.4 add_convert_fusion.4
  454.4 77.6 %all-gather.12.cloned.1.call-done = bf16[1152,2048]{1,0:T(8,128)(2,1)} async-done(((bf16[144,2048]{1,0:T(8,128)(2,1)}), bf16[1152,2048]{1,0:T(8,128)(2,1)}) %all-gather.12.cloned.1.call-update) | async-done | bytes 4718608 | tf_op jit(solution)/shard_map/all_gather | solution.py:207
  532.0 5.5 convolution_add_fusion.18
  540.4 116.7 %all-gather.14.cloned.1.call-done = bf16[2048,2048]{1,0:T(8,128)(2,1)} async-done(((bf16[256,2048]{1,0:T(8,128)(2,1)}), bf16[2048,2048]{1,0:T(8,128)(2,1)}) %all-gather.14.cloned.1.call-update) | async-done | bytes 8388624 | tf_op jit(solution)/shard_map/all_gather | solution.py:209
  657.1 7.9 convolution_add_fusion.15
  665.0 3.8 convolution_add_fusion.17
  668.8 49.2 %all-gather.16.cloned.1.call-done = bf16[2048,768]{1,0:T(8,128)(2,1)} async-done(((bf16[256,768]{1,0:T(8,128)(2,1)}), bf16[2048,768]{1,0:T(8,128)(2,1)}) %all-gather.16.cloned.1.call-update) | async-done | bytes 3145744 | tf_op jit(solution)/shard_map/all_gather | solution.py:211
  718.0 3.9 convolution_add_fusion.21
  727.0 3.6 convert_reduce_fusion.3
  730.7 5.0 convert_reduce_fusion.7
  740.2 3.4 convert_reduce_fusion.2
  743.6 4.3 convert_reduce_fusion.6
  754.6 54.1 %all-reduce.18.cloned.1.call-done = (f32[256,1152]{1,0:T(8,128)}, f32[256,1152]{1,0:T(8,128)}) async-done(((f32[256,1152]{1,0:T(8,128)}, f32[256,1152]{1,0:T(8,128)}), (f32[256,1152]{1,0:T(8,128)}, f32[256,1152]{1,0:T(8,128)})) %all-reduce.18.cloned.1.call-update) | async-done | bytes 2359312 | tf_op jit(solution)/shard_map/psum | solution.py:321
  842.5 7.2 copy.69
  849.7 7.5 reshape.471
  870.2 3.2 fusion.130
  873.4 3.1 add_convert_fusion.2
  876.9 3.1 fusion.33
  895.4 5.7 convert_reduce_fusion.19
  910.4 3.8 fusion.4
  917.0 3.6 fusion
  920.7 10.3 fusion.129
  931.0 11.6 add_convert_fusion.1
  942.9 12.7 fusion.125
  955.6 18.5 %add_convert_fusion = bf16[6912,1152]{1,0:T(8,128)(2,1)} fusion(f32[6912,1152]{1,0:T(8,128)} %fusion.125, bf16[4,6912]{1,0:T(4,128)(2,1)S(1)} %get-tuple-element.292, f32[4,1152]{1,0:T(4,128)S(1)} %copy-done.98), kind=kOutput, calls=%fused_computation | convolution fusion | flops 79649280 | bytes 47849472 | tf_op jit(solution)/shard_map/io,id->od/dot_general | solution.py:375
  977.9 37.8 %all-reduce.6 = (f32[2,288]{1,0:T(2,128)}, f32[1152]{0:T(1024)}, f32[1152]{0:T(1024)}, f32[1152]{0:T(1024)}) all-reduce(f32[2,288]{1,0:T(2,128)S(1)} %maximum_add_fusion.1, f32[1152]{0:T(1024)S(1)} %add.544, f32[1152]{0:T(1024)S(1)} %add.546, f32[1152]{0:T(1024)S(1)} %add.548), channel_id=1, replica_groups=mesh['dp'=8,'tensor'=4] {'dp'}, use_global_device_ids=true, to_apply=%region_46.47 | all-reduce | flops 4032 | bytes 32256 | tf_op jit(solution)/shard_map/psum | solution.py:156
  1015.7 33.7 %all-reduce.10 = (bf16[6912]{0:T(1024)(128)(2,1)S(1)}, bf16[2048]{0:T(1024)(128)(2,1)S(1)}, bf16[2048]{0:T(1024)(128)(2,1)S(1)}, bf16[768]{0:T(1024)(128)(2,1)S(1)}) all-reduce(bf16[6912]{0:T(1024)(128)(2,1)S(1)} %add_convert_fusion.5, bf16[2048]{0:T(1024)(128)(2,1)S(1)} %add_convert_fusion.7, ...), channel_id=4, replica_groups=mesh['dp'=8,'tensor'=4] {'dp'}, use_global_device_ids=true, to_apply=%region_40.41.clone | all-reduce | flops 11776 | bytes 47104
  1059.4 18.0 reduce-scatter.20.cloned.1.call-done
  1079.2 72.4 %reduce-scatter.18.cloned.1.call-done = bf16[144,1152]{1,0:T(8,128)(2,1)} async-done(((bf16[1152,1152]{1,0:T(8,128)(2,1)}), bf16[144,1152]{1,0:T(8,128)(2,1)}) %reduce-scatter.18.cloned.1.call-update) | async-done | bytes 331792 | tf_op jit(solution)/shard_map/reduce_scatter | solution.py:117
  1153.4 75.6 %reduce-scatter.26.cloned.1.call-done = bf16[256,768]{1,0:T(8,128)(2,1)} async-done(((bf16[2048,768]{1,0:T(8,128)(2,1)}), bf16[256,768]{1,0:T(8,128)(2,1)}) %reduce-scatter.26.cloned.1.call-update) | async-done | bytes 393232 | tf_op jit(solution)/shard_map/reduce_scatter | solution.py:132
  1230.9 69.6 %reduce-scatter.12.cloned.1.call-done = bf16[144,1001]{1,0:T(8,128)(2,1)} async-done(((bf16[1152,1001]{1,0:T(8,128)(2,1)}), bf16[144,1001]{1,0:T(8,128)(2,1)}) %reduce-scatter.12.cloned.1.call-update) | async-done | bytes 288304 | tf_op jit(solution)/shard_map/reduce_scatter | solution.py:114
  1302.4 96.2 %reduce-scatter.22.cloned.1.call-done = bf16[144,2048]{1,0:T(8,128)(2,1)} async-done(((bf16[1152,2048]{1,0:T(8,128)(2,1)}), bf16[144,2048]{1,0:T(8,128)(2,1)}) %reduce-scatter.22.cloned.1.call-update) | async-done | bytes 589840 | tf_op jit(solution)/shard_map/reduce_scatter | solution.py:120
  1400.8 150.1 %reduce-scatter.24.cloned.1.call-done = bf16[256,2048]{1,0:T(8,128)(2,1)} async-done(((bf16[2048,2048]{1,0:T(8,128)(2,1)}), bf16[256,2048]{1,0:T(8,128)(2,1)}) %reduce-scatter.24.cloned.1.call-update) | async-done | bytes 1048592 | tf_op jit(solution)/shard_map/reduce_scatter | solution.py:126
  1553.6 269.7 %reduce-scatter.14.cloned.1.call-done = bf16[864,1152]{1,0:T(8,128)(2,1)} async-done(((bf16[6912,1152]{1,0:T(8,128)(2,1)}), bf16[864,1152]{1,0:T(8,128)(2,1)}) %reduce-scatter.14.cloned.1.call-update) | async-done | bytes 1990672 | tf_op jit(solution)/shard_map/reduce_scatter | solution.py:138
  1823.3 3.9 convert_element_type.546
  (515 shorter events, 149.6 us)
Async XLA Ops:
  7.2 382.6 %copy-start = (bf16[1152,1152]{1,0:T(8,128)(2,1)S(1)}, bf16[1152,1152]{1,0:T(8,128)(2,1)}, u32[]{:S(2)}) copy-start(bf16[1152,1152]{1,0:T(8,128)(2,1)} %param.40) | copy-start | bytes 7962628
  7.2 43.3 %copy-start.124 = (s32[2,1,256]{2,1,0:T(1,128)S(1)}, s32[2,1,256]{2,1,0:T(1,128)}, u32[]{:S(2)}) copy-start(s32[2,1,256]{2,1,0:T(1,128)} %param.28) | copy-start | bytes 6148
  7.3 43.4 %copy-start.125 = (bf16[2,288]{1,0:T(2,128)(2,1)S(1)}, bf16[2,288]{1,0:T(2,128)(2,1)}, u32[]{:S(2)}) copy-start(bf16[2,288]{1,0:T(2,128)(2,1)} %param.35) | copy-start | bytes 3460
  7.3 58.0 %all-gather.8.cloned.1.call-start = ((), (), s32[]{:S(2)}) async-start(), calls=%async_computation.9 | async-start | bytes 2654208 | tf_op jit(solution)/shard_map/all_gather | solution.py:204
  8.0 275.3 %all-gather.10.cloned.1.call-start = ((), (), s32[]{:S(2)}) async-start(), calls=%async_computation.10 | async-start | bytes 17915904 | tf_op jit(solution)/shard_map/all_gather | solution.py:205
  8.7 370.2 %all-reduce.22.cloned.1.call-start = ((), (), s32[]{:S(2)}) async-start(), calls=%async_computation.25 | async-start | bytes 4718592 | tf_op jit(solution)/shard_map/psum | solution.py:257
  52.7 15.1 copy-start.112
  52.7 15.0 copy-start.126
  52.8 15.1 copy-start.128
  52.8 240.3 %copy-start.105 = (s32[1,1,256]{2,1,0:T(1,128)}, s32[1,1,256]{2,1,0:T(1,128)S(1)}, u32[]{:S(2)}) copy-start(s32[1,1,256]{2,1,0:T(1,128)S(1)} %get-tuple-element.266) | copy-start | bytes 3076
  52.8 255.2 %copy-start.107 = (s32[1,1,256]{2,1,0:T(1,128)}, s32[1,1,256]{2,1,0:T(1,128)S(1)}, u32[]{:S(2)}) copy-start(s32[1,1,256]{2,1,0:T(1,128)S(1)} %get-tuple-element.267) | copy-start | bytes 3076
  67.8 215.6 %copy-start.97 = (f32[4,1152]{1,0:T(4,128)}, f32[4,1152]{1,0:T(4,128)S(1)}, u32[]{:S(2)}) copy-start(f32[4,1152]{1,0:T(4,128)S(1)} %convolution_add_fusion.19) | copy-start | bytes 55300
  68.5 229.8 %copy-start.99 = (f32[4,1152]{1,0:T(4,128)}, f32[4,1152]{1,0:T(4,128)S(1)}, u32[]{:S(2)}) copy-start(f32[4,1152]{1,0:T(4,128)S(1)} %convolution_add_fusion.20) | copy-start | bytes 55300
  324.8 125.2 %all-reduce.20.cloned.1.call-start = ((), (), s32[]{:S(2)}) async-start(), calls=%async_computation.24 | async-start | bytes 4718592 | tf_op jit(solution)/shard_map/psum | solution.py:270
  394.0 39.3 %copy-start.132 = (bf16[1152]{0:T(1024)(128)(2,1)S(1)}, bf16[1152]{0:T(1024)(128)(2,1)}, u32[]{:S(2)}) copy-start(bf16[1152]{0:T(1024)(128)(2,1)} %param.41) | copy-start | bytes 6916
  394.0 138.0 %all-gather.12.cloned.1.call-start = ((), (), s32[]{:S(2)}) async-start(), calls=%async_computation.11 | async-start | bytes 5308416 | tf_op jit(solution)/shard_map/all_gather | solution.py:207
  394.6 262.5 %all-gather.14.cloned.1.call-start = ((), (), s32[]{:S(2)}) async-start(), calls=%async_computation.12 | async-start | bytes 9437184 | tf_op jit(solution)/shard_map/all_gather | solution.py:209
  395.2 322.8 %all-gather.16.cloned.1.call-start = ((), (), s32[]{:S(2)}) async-start(), calls=%async_computation.13 | async-start | bytes 3538944 | tf_op jit(solution)/shard_map/all_gather | solution.py:211
  395.9 412.9 %all-reduce.18.cloned.1.call-start = ((), (), s32[]{:S(2)}) async-start(), calls=%async_computation.23 | async-start | bytes 4718592 | tf_op jit(solution)/shard_map/psum | solution.py:321
  657.1 7.9 copy-start.61
  657.1 7.9 copy-start.138
  724.8 12.8 copy-start.93
  724.8 5.8 slice-start.6
  737.6 14.4 copy-start.79
  754.1 54.7 %copy-start.6 = (f32[256,1152]{1,0:T(8,128)S(1)}, f32[256,1152]{1,0:T(8,128)}, u32[]{:S(2)}) copy-start(f32[256,1152]{1,0:T(8,128)} %copy-done.5) | copy-start | bytes 3538948
  754.1 122.7 %all-reduce.24.cloned.1.call-start = ((), (), s32[]{:S(2)}) async-start(), calls=%async_computation.26 | async-start | bytes 2359296 | tf_op jit(solution)/shard_map/psum | solution.py:366
  812.7 6.6 slice-start.4
  819.2 8.6 copy-start.67
  825.3 5.9 copy-start.65
  832.6 222.2 %reduce-scatter.16.cloned.1.call-start = ((), (), s32[]{:S(2)}) async-start(), calls=%async_computation.16 | async-start | bytes 995328 | tf_op jit(solution)/shard_map/reduce_scatter | solution.py:149
  835.9 220.5 %reduce-scatter.28.cloned.1.call-start = ((), (), s32[]{:S(2)}) async-start(), calls=%async_computation.22 | async-start | bytes 2322432
  857.2 220.2 %reduce-scatter.20.cloned.1.call-start = ((), (), s32[]{:S(2)}) async-start(), calls=%async_computation.18 | async-start | bytes 2985984 | tf_op jit(solution)/shard_map/reduce_scatter | solution.py:152
  863.5 288.1 %reduce-scatter.18.cloned.1.call-start = ((), (), s32[]{:S(2)}) async-start(), calls=%async_computation.17 | async-start | bytes 2985984 | tf_op jit(solution)/shard_map/reduce_scatter | solution.py:117
  869.2 359.8 %reduce-scatter.26.cloned.1.call-start = ((), (), s32[]{:S(2)}) async-start(), calls=%async_computation.21 | async-start | bytes 3538944 | tf_op jit(solution)/shard_map/reduce_scatter | solution.py:132
  876.6 424.0 %reduce-scatter.12.cloned.1.call-start = ((), (), s32[]{:S(2)}) async-start(), calls=%async_computation.14 | async-start | bytes 2654208 | tf_op jit(solution)/shard_map/reduce_scatter | solution.py:114
  880.0 5.8 copy-start.40
  880.1 5.8 copy-start.41
  880.1 5.8 copy-start.42
  885.9 15.2 slice-start
  885.9 15.2 slice-start.1
  891.3 9.7 slice-start.2
  894.0 7.1 slice-start.3
  914.2 484.4 %reduce-scatter.22.cloned.1.call-start = ((), (), s32[]{:S(2)}) async-start(), calls=%async_computation.19 | async-start | bytes 5308416 | tf_op jit(solution)/shard_map/reduce_scatter | solution.py:120
  920.6 10.4 copy-start.76
  920.6 630.2 %reduce-scatter.24.cloned.1.call-start = ((), (), s32[]{:S(2)}) async-start(), calls=%async_computation.20 | async-start | bytes 9437184 | tf_op jit(solution)/shard_map/reduce_scatter | solution.py:126
  920.7 10.3 copy-start.60
  942.6 880.7 %reduce-scatter.14.cloned.1.call-start = ((), (), s32[]{:S(2)}) async-start(), calls=%async_computation.15 | async-start | bytes 17915904 | tf_op jit(solution)/shard_map/reduce_scatter | solution.py:138
  976.4 75.6 %copy-start.43 = (f32[1,1,256,1152]{3,2,1,0:T(8,128)S(1)}, f32[1,1,256,1152]{3,2,1,0:T(8,128)}, u32[]{:S(2)}) copy-start(f32[1,1,256,1152]{3,2,1,0:T(8,128)} %get-tuple-element.240) | copy-start | bytes 3538948
  (129 other events, 304.1 us)
Sparse Core Ops, SparseCore 0:
  10.3 54.9 all-gather.7
  67.4 215.8 all-gather.9
  324.9 54.0 all-reduce.21
  394.1 55.9 all-reduce.19
  452.0 79.9 all-gather.11
  534.0 123.0 all-gather.13
  659.3 58.6 all-gather.15
  754.3 54.4 all-reduce.17
  832.7 37.5 all-reduce.23
  873.6 61.3 reduce-scatter.15
  938.6 65.8 reduce-scatter.27
  1007.9 69.3 reduce-scatter.19
  1081.4 70.0 reduce-scatter.17
  1155.6 73.3 reduce-scatter.25
  1232.3 68.1 reduce-scatter.11
  1304.0 94.4 reduce-scatter.21
  1402.0 148.7 reduce-scatter.23
  1555.1 268.1 reduce-scatter.13
where the time goes:
time: 1840 us; the launch traced here: 1830 us
  waiting for transfers between devices  1350 us (73%)
  matrix products  205 us (11%)
  blocking collectives  148 us (8%)
  other arithmetic  66.5 us (4%)
  local copies, waits for them, and re-layouts  44.1 us (2%)
  between operations  20 us (1%)
    reduce_scatter x1, waiting for transfers between devices, settle(): lax.psum_scatter(g_ada_w.astype(jnp.bfloat16), 'dp', scatter_dimension=0,...  270 us
    all_gather x1, waiting for transfers between devices, body(): lax.all_gather(ada_w, 'dp', axis=0, tiled=True)  215 us
    reduce_scatter x1, waiting for transfers between devices, settle(): lax.psum_scatter(g_w2.astype(jnp.bfloat16), 'dp', scatter_dimension=0, ti...  150 us
    all_gather x1, waiting for transfers between devices, body(): lax.all_gather(repa_w2, 'dp', axis=0, tiled=True)  117 us
    reduce_scatter x1, waiting for transfers between devices, settle(): lax.psum_scatter(g_w1.astype(jnp.bfloat16), 'dp', scatter_dimension=0, ti...  96.2 us
    all_gather x1, waiting for transfers between devices, body(): lax.all_gather(repa_w1, 'dp', axis=0, tiled=True)  77.6 us
    reduce_scatter x1, waiting for transfers between devices, settle(): lax.psum_scatter(g_w3.astype(jnp.bfloat16), 'dp', scatter_dimension=0, ti...  75.6 us
    unnamed x2, blocking collectives  73.1 us
  transfers between devices with their start and end apart: 18, of which 15 were waited for; matrix products, arithmetic and copies ran while one was open for 10% of the time, Pallas kernels for 0%

commit v1 on v0

v1 whole, which is shorter than its diff:
```python
import functools
import math

import jax
import jax.numpy as jnp
from jax import lax
from jax.experimental import pallas as pl
from jax.experimental.pallas import tpu as pltpu
from jax.sharding import PartitionSpec as P

HEAD_DIM = 72
norm_eps = 1e-06
cos_eps = 1e-06
repa_weight = 0.5
F32 = jnp.float32
BF16 = jnp.bfloat16
VMEM = pl.BlockSpec(memory_space=pltpu.VMEM)
SMEM = pl.BlockSpec(memory_space=pltpu.SMEM)
ANY = pl.BlockSpec(memory_space=pl.ANY)
VMEM_LIMIT = 58 * 1024 * 1024


def shape_of(shape, dtype):
    return jax.ShapeDtypeStruct(tuple(shape), dtype)


def call(kernel, outs, ins, in_specs=None, out_specs=None, scratch=(), flops=0, limit=VMEM_LIMIT, name=None):
    moved = sum(math.prod(a.shape) * a.dtype.itemsize for a in list(ins) + list(outs))
    return pl.pallas_call(
        kernel,
        out_shape=tuple(outs),
        in_specs=in_specs or [VMEM] * len(ins),
        out_specs=tuple(out_specs or [VMEM] * len(outs)),
        scratch_shapes=list(scratch),
        compiler_params=pltpu.CompilerParams(vmem_limit_bytes=limit),
        cost_estimate=pl.CostEstimate(flops=flops, bytes_accessed=moved, transcendentals=0),
        name=name,
    )(*ins)


def dot(a, b):
    return jnp.dot(a, b, preferred_element_type=F32)


def dot_nt(a, b):
    return lax.dot_general(a, b, (((1,), (1,)), ((), ())), preferred_element_type=F32)


def dot_tn(a, b):
    return lax.dot_general(a, b, (((0,), (0,)), ((), ())), preferred_element_type=F32)


def sigmoid(v):
    return 1.0 / (1.0 + jnp.exp(-v))


def silu_slope(v):
    s = sigmoid(v)
    return s * (1.0 + v * (1.0 - s))


def pick(seg, table):
    out = jnp.broadcast_to(table[0:1, :], (seg.shape[0], table.shape[1]))
    for s in range(1, table.shape[0]):
        out = jnp.where(seg == s, table[s : s + 1, :], out)
    return out


def by_image(seg, values, slots):
    rows = [jnp.sum(jnp.where(seg == s, values, 0.0), axis=0, keepdims=True) for s in range(slots)]
    return jnp.concatenate(rows, axis=0)


def norm_parts(v):
    centered = v - jnp.mean(v, axis=-1, keepdims=True)
    inv = lax.rsqrt(jnp.mean(centered * centered, axis=-1, keepdims=True) + norm_eps)
    return centered * inv, inv


def norm_back(g, xhat, inv):
    return inv * (g - jnp.mean(g, axis=-1, keepdims=True) - xhat * jnp.mean(g * xhat, axis=-1, keepdims=True))


def attend(q, k, v, open_mask, scale):
    s = dot_nt(q, k) * scale
    s = jnp.where(open_mask, s, -1e30)
    e = jnp.exp(s - jnp.max(s, axis=-1, keepdims=True))
    return e * (1.0 / jnp.sum(e, axis=-1, keepdims=True))


def open_of(segc, segr, valr):
    n = segc.shape[0]
    same = lax.broadcasted_iota(jnp.int32, (n, n), 0) == lax.broadcasted_iota(jnp.int32, (n, n), 1)
    return (segc == segr) & ((valr == 1) | same)


def fwd_kernel(heads, order, hid, mods, segc, segr, valr, w, b, m_ref, q_ref, k_ref, v_ref, mix_ref):
    half, width = hid.shape[1], hid.shape[2]
    seq = 2 * half
    scale = HEAD_DIM ** (-0.5)
    for micro in range(2):
        x = jnp.concatenate([hid[order[2 * micro]], hid[order[2 * micro + 1]]], axis=0).astype(F32)
        rows = slice(micro * seq, (micro + 1) * seq)
        seg = segc[rows, :]
        xhat, _ = norm_parts(x)
        shift = pick(seg, mods[micro][:, 0:width])
        scaling = pick(seg, mods[micro][:, width : 2 * width])
        m = (xhat * (1.0 + scaling) + shift).astype(BF16)
        m_ref[rows, :] = m
        q = (dot(m, w[0]) + b[0:1, :]).astype(BF16)
        k = dot(m, w[1]).astype(BF16)
        v = (dot(m, w[2]) + b[1:2, :]).astype(BF16)
        q_ref[rows, :] = q
        k_ref[rows, :] = k
        v_ref[rows, :] = v
        mask = open_of(seg, segr[micro : micro + 1, :], valr[micro : micro + 1, :])
        mixed = []
        for h in range(heads):
            cols = slice(h * HEAD_DIM, (h + 1) * HEAD_DIM)
            p = attend(q[:, cols], k[:, cols], v[:, cols], mask, scale)
            mixed.append(dot(p.astype(BF16), v[:, cols]).astype(BF16))
        mix_ref[rows, :] = jnp.concatenate(mixed, axis=1)


def bwd_kernel(heads, g0, g1, g2, g3, out_w, q_ref, k_ref, v_ref, segc, segr, valr, w, gqkv_ref, part_q, part_y, send_q, send_y, bias_ref, gfull_ref):
    half = g0.shape[0]
    seq = 2 * half
    scale = HEAD_DIM ** (-0.5)
    wide = heads * HEAD_DIM
    sums = []
    for micro in range(2):
        rows = slice(micro * seq, (micro + 1) * seq)
        g = jnp.concatenate([g0[...], g1[...]] if micro == 0 else [g2[...], g3[...]], axis=0)
        gfull_ref[rows, :] = g
        gm = dot_nt(g, out_w[...]).astype(BF16)
        q, k, v = q_ref[rows, :], k_ref[rows, :], v_ref[rows, :]
        mask = open_of(segc[rows, :], segr[micro : micro + 1, :], valr[micro : micro + 1, :])
        gq, gk, gv = [], [], []
        for h in range(heads):
            cols = slice(h * HEAD_DIM, (h + 1) * HEAD_DIM)
            qh, kh, vh, gh = q[:, cols], k[:, cols], v[:, cols], gm[:, cols]
            p = attend(qh, kh, vh, mask, scale)
            gp = dot_nt(gh, vh)
            gs = (p * (gp - jnp.sum(p * gp, axis=-1, keepdims=True))).astype(BF16)
            gq.append((dot(gs, kh) * scale).astype(BF16))
            gk.append((dot_tn(gs, qh) * scale).astype(BF16))
            gv.append(dot_tn(p.astype(BF16), gh).astype(BF16))
        gq, gk, gv = (jnp.concatenate(a, axis=1) for a in (gq, gk, gv))
        gqkv_ref[rows, 0:wide] = gq
        gqkv_ref[rows, wide : 2 * wide] = gk
        gqkv_ref[rows, 2 * wide : 3 * wide] = gv
        sums.append(
            jnp.concatenate(
                [jnp.sum(gq.astype(F32), axis=0, keepdims=True), jnp.sum(gv.astype(F32), axis=0, keepdims=True)],
                axis=0,
            )
        )
        part = dot_nt(gq, w[0]) + dot_nt(gk, w[1]) + dot_nt(gv, w[2])
        if micro == 0:
            part_q[...] = part[:half]
            part_y[...] = part[half:]
        else:
            send_q[...] = part[:half].astype(BF16)
            send_y[...] = part[half:].astype(BF16)
    bias_ref[...] = sums[0] + sums[1]


def mid_kernel(order, hid, mods, segc, m0, m1, m2, m3, w0, w1, w2, w3, out_b, attn_q, h_q, m_two):
    half, width = hid.shape[1], hid.shape[2]
    seq = 2 * half
    x = jnp.concatenate([hid[order[0]], hid[order[1]]], axis=0).astype(F32)
    seg = segc[0:seq, :]
    m2, m3 = (jnp.concatenate([m[half:, :], m[:half, :]], axis=0) for m in (m2, m3))
    attn = dot(m0[...], w0[...]) + dot(m1[...], w1[...]) + dot(m2, w2[...]) + dot(m3, w3[...])
    attn = attn + out_b[...]
    h = x + pick(seg, mods[:, 2 * width : 3 * width]) * attn
    attn_q[...] = attn[:half]
    h_q[...] = h[:half]
    xhat, _ = norm_parts(h)
    m_two[...] = (
        xhat * (1.0 + pick(seg, mods[:, 4 * width : 5 * width])) + pick(seg, mods[:, 3 * width : 4 * width])
    ).astype(BF16)


SPLITS = ((0, 512), (512, 1152))
K0 = math.sqrt(2.0 / math.pi)


def mlp_kernel(m_own, m_par, fc1, b1, fc2, m_full, pre_ref, act_ref, part_q, part_y, send_q, send_y):
    seq = m_own.shape[0]
    half = seq // 2
    for micro, m_ref in enumerate((m_own, m_par)):
        rows = slice(micro * seq, (micro + 1) * seq)
        m = m_ref[...]
        m_full[rows, :] = m
        for lo, hi in SPLITS:
            pre = dot(m, fc1[:, lo:hi]) + b1[:, lo:hi]
            pre_ref[rows, lo:hi] = pre
            t = jnp.tanh(K0 * (pre + 0.044715 * (pre * pre * pre)))
            act_ref[rows, lo:hi] = (0.5 * pre * (1.0 + t)).astype(BF16)
        act = act_ref[rows, :]
        for lo, hi in SPLITS:
            part = dot(act, fc2[:, lo:hi])
            if micro == 0:
                part_q[:, lo:hi] = part[:half]
                part_y[:, lo:hi] = part[half:]
            else:
                send_q[:, lo:hi] = part[:half].astype(BF16)
                send_y[:, lo:hi] = part[half:].astype(BF16)


def mlp_back_kernel(g0, g1, g2, g3, pre_ref, fc1, fc2, g_full, gpre_ref, part_q, part_y, send_q, send_y, bias):
    half = g0.shape[0]
    seq = 2 * half
    for micro in range(2):
        rows = slice(micro * seq, (micro + 1) * seq)
        g = jnp.concatenate([g0[...], g1[...]] if micro == 0 else [g2[...], g3[...]], axis=0)
        g_full[rows, :] = g
        for lo, hi in SPLITS:
            ga = dot_nt(g, fc2[lo:hi, :])
            v = pre_ref[rows, lo:hi]
            t = jnp.tanh(K0 * (v + 0.044715 * (v * v * v)))
            slope = 0.5 * (1.0 + t) + 0.5 * v * (1.0 - t * t) * (K0 * (1.0 + 3.0 * 0.044715 * (v * v)))
            gp = (ga * slope).astype(BF16)
            gpre_ref[rows, lo:hi] = gp
            total = jnp.sum(gp.astype(F32), axis=0, keepdims=True)
            bias[:, lo:hi] = total if micro == 0 else bias[:, lo:hi] + total
        gp = gpre_ref[rows, :]
        for lo, hi in SPLITS:
            part = dot_nt(gp, fc1[lo:hi, :])
            if micro == 0:
                part_q[:, lo:hi] = part[:half]
                part_y[:, lo:hi] = part[half:]
            else:
                send_q[:, lo:hi] = part[:half].astype(BF16)
                send_y[:, lo:hi] = part[half:].astype(BF16)


def proj_kernel(plan, n_pieces, meta, *refs):
    (part, rq, ry, h_one, mods, seg_ref, fc2_b, grad_out, feat_ref, keep_ref, b1, b2, b3) = refs[:13]
    pieces = refs[13 : 13 + n_pieces]
    (h_low, grad_h, g_mlp, gate_sum, s1, s2, gz_ref, ga2_ref, ga1_ref, gb1, gb2, gb3, gbf) = refs[13 + n_pieces : 26 + n_pieces]
    w1, w2, w3, a1, a2, sems = refs[26 + n_pieces :]
    weights = (w1, w2, w3)
    width = h_low.shape[1]
    slots = mods.shape[0]
    for piece, (which, place) in zip(pieces, plan):
        for source, target in place(piece, weights[which], meta):
            pltpu.make_async_copy(source, target, sems.at[which]).start()
    seg = seg_ref[...]
    gate = pick(seg, mods[:, 5 * width : 6 * width])
    mlp = part[...] + rq[...].astype(F32) + ry[...].astype(F32) + fc2_b[...]
    h = h_one[...] + gate * mlp
    hl = h.astype(BF16)
    h_low[...] = hl
    hidden = w1.shape[1]
    step = 512
    pltpu.make_async_copy(w1, w1, sems.at[0]).wait()
    for lo in range(0, hidden, step):
        a = dot(hl, w1[:, lo : lo + step]) + b1[:, lo : lo + step]
        a1[:, lo : lo + step] = a
        s1[:, lo : lo + step] = (a * sigmoid(a)).astype(BF16)
    pltpu.make_async_copy(w2, w2, sems.at[1]).wait()
    s = s1[...]
    for lo in range(0, hidden, step):
        a = dot(s, w2[:, lo : lo + step]) + b2[:, lo : lo + step]
        a2[:, lo : lo + step] = a
        s2[:, lo : lo + step] = (a * sigmoid(a)).astype(BF16)
    pltpu.make_async_copy(w3, w3, sems.at[2]).wait()
    z = dot(s2[...], w3[...]) + b3[...]
    feat = feat_ref[...].astype(F32)
    inv_z = lax.rsqrt(jnp.sum(z * z, axis=-1, keepdims=True) + cos_eps)
    inv_f = lax.rsqrt(jnp.sum(feat * feat, axis=-1, keepdims=True) + cos_eps)
    zf = jnp.sum(z * feat, axis=-1, keepdims=True)
    coeff = -repa_weight * keep_ref[...] * inv_z * inv_f
    gz = (coeff * (feat - (zf * inv_z * inv_z) * z)).astype(BF16)
    gz_ref[...] = gz
    gb3[...] = jnp.sum(gz.astype(F32), axis=0, keepdims=True)
    for lo in range(0, hidden, step):
        g = (dot_nt(gz, w3[lo : lo + step, :]) * silu_slope(a2[:, lo : lo + step])).astype(BF16)
        ga2_ref[:, lo : lo + step] = g
        gb2[:, lo : lo + step] = jnp.sum(g.astype(F32), axis=0, keepdims=True)
    ga2 = ga2_ref[...]
    for lo in range(0, hidden, step):
        g = (dot_nt(ga2, w2[lo : lo + step, :]) * silu_slope(a1[:, lo : lo + step])).astype(BF16)
        ga1_ref[:, lo : lo + step] = g
        gb1[:, lo : lo + step] = jnp.sum(g.astype(F32), axis=0, keepdims=True)
    gh = grad_out[...].astype(F32) + dot_nt(ga1_ref[...], w1[...])
    grad_h[...] = gh
    gm = (gate * gh).astype(BF16)
    g_mlp[...] = gm
    gbf[...] = jnp.sum(gm.astype(F32), axis=0, keepdims=True)
    gate_sum[...] = by_image(seg, gh * mlp, slots)


def second_back_kernel(part, rq, ry, grad_h, h_one, attn, mods, seg_ref, g_one, g_attn, gate_sum, shift_sum, scale_sum, bias):
    width = h_one.shape[1]
    slots = mods.shape[0]
    seg = seg_ref[...]
    g = part[...] + rq[...].astype(F32) + ry[...].astype(F32)
    xhat, inv = norm_parts(h_one[...])
    total = grad_h[...] + norm_back(g * (1.0 + pick(seg, mods[:, 4 * width : 5 * width])), xhat, inv)
    g_one[...] = total
    ga = (pick(seg, mods[:, 2 * width : 3 * width]) * total).astype(BF16)
    g_attn[...] = ga
    bias[...] = jnp.sum(ga.astype(F32), axis=0, keepdims=True)
    gate_sum[...] = by_image(seg, total * attn[...], slots)
    shift_sum[...] = by_image(seg, g, slots)
    scale_sum[...] = by_image(seg, g * xhat, slots)


def first_back_kernel(order, part, rq, ry, g_one, hid, mods, seg_ref, g_in, shift_sum, scale_sum):
    width = g_one.shape[1]
    slots = mods.shape[0]
    seg = seg_ref[...]
    g = part[...] + rq[...].astype(F32) + ry[...].astype(F32)
    xhat, inv = norm_parts(hid[order[0]].astype(F32))
    total = g_one[...] + norm_back(g * (1.0 + pick(seg, mods[:, width : 2 * width])), xhat, inv)
    g_in[...] = total.astype(BF16)
    shift_sum[...] = by_image(seg, g, slots)
    scale_sum[...] = by_image(seg, g * xhat, slots)


def wgrad_kernel(place, n_outs, step, meta, a_ref, b_ref, *refs):
    outs, (g, sem) = refs[:n_outs], refs[n_outs:]
    rows = g.shape[0]
    for lo in range(0, rows, step):
        hi = min(lo + step, rows)
        g[lo:hi, :] = dot_tn(a_ref[:, lo:hi], b_ref[...]).astype(BF16)
    place(g, outs, sem, meta)
    pltpu.make_async_copy(g, g, sem).wait()


def body(mesh, hidden_in, grad_out, features, seg_ids, valid_mask, time_ids, class_ids, class_table, ada_w, ada_b, qkv_w, qv_bias, out_w, out_b, fc1_w, fc1_b, fc2_w, fc2_b, repa_w1, repa_b1, repa_w2, repa_b2, repa_w3, repa_b3):
    n_dp = mesh.shape["dp"]
    inner = 4 if n_dp % 16 == 0 else 2
    outer = n_dp // inner
    micro_count, rows_dev, seq, width = hidden_in.shape
    slots = time_ids.shape[-1]
    images = micro_count * rows_dev * slots
    half = seq // 2
    wide = qkv_w.shape[2]
    heads = wide // HEAD_DIM
    ff = fc1_w.shape[1]
    hidden = repa_w1.shape[1]
    repr_width = repa_w3.shape[1]

    d = lax.axis_index("dp")
    t = lax.axis_index("tensor")
    o, i = d // inner, d % inner
    y, c = t // 2, t % 2
    meta = jnp.stack([o, i, y, c]).astype(jnp.int32)

    def from_inner(x, r):
        return lax.ppermute(x, "dp", [(k * inner + (j + r) % inner, k * inner + j) for k in range(outer) for j in range(inner)])

    def from_outer(x, r):
        return lax.ppermute(x, "dp", [(((k + r) % outer) * inner + j, k * inner + j) for k in range(outer) for j in range(inner)])

    def swap_y(x):
        return lax.ppermute(x, "tensor", [(0, 2), (2, 0), (1, 3), (3, 1)])

    def swap_core(x):
        return lax.ppermute(x, "tensor", [(0, 1), (1, 0), (2, 3), (3, 2)])

    def to_natural(stack, me, n, axis=0):
        twice = jnp.concatenate([stack, stack], axis=axis)
        return lax.dynamic_slice_in_dim(twice, n - me, n, axis=axis)

    def to_relative(stack, me, n, axis=0):
        twice = jnp.concatenate([stack, stack], axis=axis)
        return lax.dynamic_slice_in_dim(twice, me, n, axis=axis)

    def gather_dp(x):
        xs = jnp.stack([x] + [from_inner(x, r) for r in range(1, inner)])
        xs = jnp.stack([xs] + [from_outer(xs, r) for r in range(1, outer)])
        xs = to_natural(to_natural(xs, i, inner, 1), o, outer, 0)
        return xs.reshape((n_dp,) + x.shape)

    def exchange_dp(x):
        x = x.reshape((outer, inner) + x.shape[1:])
        rel = to_relative(x, i, inner, 1)
        ys = jnp.stack([rel[:, 0]] + [from_inner(rel[:, inner - r], r) for r in range(1, inner)])
        rel = to_relative(ys, o, outer, 1)
        zs = jnp.stack([rel[:, 0]] + [from_outer(rel[:, outer - r], r) for r in range(1, outer)])
        zs = to_natural(to_natural(zs, i, inner, 1), o, outer, 0)
        return zs.reshape((n_dp,) + zs.shape[2:])

    def bulk_gather(piece):
        zs = jnp.stack([piece] + [from_outer(piece, r) for r in range(1, outer)])
        xs = [zs] + [from_inner(zs, r) for r in range(1, inner)]
        ys = [swap_y(a) for a in xs]
        found = {}
        for yr, group in ((0, xs), (1, ys)):
            for r, a in enumerate(group):
                found[(yr, 0, r)] = a
                found[(yr, 1, r)] = swap_core(a)
        return found

    def cols_of(w):
        n = w.shape[1] // 4
        return lax.dynamic_slice_in_dim(w, t * n, n, axis=1)

    def rows_of(w):
        n = w.shape[0] // 4
        return lax.dynamic_slice_in_dim(w, t * n, n, axis=0)

    w1_found = bulk_gather(cols_of(repa_w1))
    w3_found = bulk_gather(rows_of(repa_w3))
    w2_found = bulk_gather(cols_of(repa_w2))
    out_y = swap_y(out_w)
    out_c = swap_core(out_w)
    out_yc = swap_core(out_y)
    b_all = gather_dp(jnp.concatenate([repa_b1, repa_b2, repa_b3]))
    n1, n2 = repa_b1.shape[0], repa_b2.shape[0]
    b_one = b_all[:, :n1].reshape(1, -1).astype(F32)
    b_two = b_all[:, n1 : n1 + n2].reshape(1, -1).astype(F32)
    b_three = b_all[:, n1 + n2 :].reshape(1, -1).astype(F32)

    ids = gather_dp(jnp.concatenate([class_ids.reshape(images), time_ids.reshape(images)]))
    all_class = ids[:, :images].reshape(1, n_dp * images)
    all_time = ids[:, images:].reshape(1, n_dp * images)
    feats = class_table.shape[0]
    class_hot = lax.broadcasted_iota(jnp.int32, (class_table.shape[1], n_dp * images), 0) == all_class
    place = d * feats + lax.broadcasted_iota(jnp.int32, (feats, 1), 0)
    half_width = width // 2
    freqs = jnp.exp(-math.log(10000.0) * (place % half_width).astype(F32) / half_width)
    angles = all_time.astype(F32) * freqs
    condition = jnp.where(place < half_width, jnp.cos(angles), jnp.sin(angles)) + dot(class_table, class_hot.astype(BF16))
    cond_act = gather_dp(jax.nn.silu(condition).astype(BF16)).reshape(width, n_dp * images)
    mod_part = lax.dot_general(cond_act, ada_w, (((0,), (1,)), ((), ())), preferred_element_type=F32) + ada_b.astype(F32)
    mod_parts = exchange_dp(mod_part.reshape(n_dp, images, -1))
    modulation = mod_parts.transpose(1, 0, 2).reshape(micro_count, slots, -1)
    mods_own = lax.dynamic_index_in_dim(modulation, c, 0, keepdims=False)
    mods_par = lax.dynamic_index_in_dim(modulation, 1 - c, 0, keepdims=False)

    order = jnp.stack([2 * c + y, 2 * c + 1 - y, 2 * (1 - c) + y, 2 * (1 - c) + 1 - y]).astype(jnp.int32)
    hid = hidden_in.reshape(4, half, width)

    def ordered(a):
        a = a.reshape(4, half)
        return jnp.concatenate([lax.dynamic_index_in_dim(a, order[n], 0, keepdims=False) for n in range(4)])

    seg_line = ordered(seg_ids)
    val_line = ordered(valid_mask)
    seg_rows = seg_line.reshape(2, seq)
    val_rows = val_line.reshape(2, seq)
    seg_cols = seg_line.reshape(2 * seq, 1)
    seg_q = seg_cols[:half]
    keep_q = val_line[:half].reshape(half, 1).astype(F32)
    go_q = lax.dynamic_index_in_dim(grad_out.reshape(4, half, width), order[0], 0, keepdims=False)
    feat_q = lax.dynamic_index_in_dim(features.reshape(4, half, repr_width), order[0], 0, keepdims=False)

    tokens = 2 * seq
    T = tokens

    def fwd(order_, hid_, a, b, *rest):
        return functools.partial(fwd_kernel, heads)(order_, hid_, (a, b), *rest)

    m_one, q, k, v, mixed = call(
        fwd,
        [shape_of((T, width), BF16)] + [shape_of((T, wide), BF16)] * 4,
        [order, hid, mods_own, mods_par, seg_cols, seg_rows, val_rows, qkv_w, qv_bias.astype(F32)],
        in_specs=[SMEM] + [VMEM] * 8,
        flops=2 * T * width * wide * 3 + 4 * T * seq * wide,
        name="attention",
    )

    mix_own, mix_send = mixed[:seq], mixed[seq:]
    mix_y = swap_y(mix_own)
    mix_c = swap_core(mix_send)
    mix_yc = swap_y(mix_c)
    attn_q, h_q, m_two = call(
        mid_kernel,
        [shape_of((half, width), F32), shape_of((half, width), F32), shape_of((seq, width), BF16)],
        [order, hid, mods_own, seg_cols, mix_own, mix_c, mix_y, mix_yc, out_w, out_c, out_y, out_yc, out_b.astype(F32).reshape(1, width)],
        in_specs=[SMEM] + [VMEM] * 12,
        flops=2 * seq * width * width,
        name="middle",
    )
    m_par = swap_core(m_two)

    quarter = [shape_of((half, width), F32), shape_of((half, width), F32), shape_of((half, width), BF16), shape_of((half, width), BF16)]

    def settle_quarter(part_y, send_q, send_y):
        ry = swap_core(send_y)
        rq = swap_core(send_q)
        passed = swap_y((part_y + ry.astype(F32)).astype(BF16))
        return rq, passed

    def spread_quarter(g):
        gy = swap_y(g)
        return g, gy, swap_core(g), swap_core(gy)

    m_full, pre, act, part_q, part_y, send_q, send_y = call(
        mlp_kernel,
        [shape_of((T, width), BF16), shape_of((T, ff), F32), shape_of((T, ff), BF16)] + quarter,
        [m_two, m_par, fc1_w, fc1_b.astype(F32).reshape(1, ff), fc2_w],
        flops=4 * T * width * ff,
        name="mlp",
    )
    rq, ry = settle_quarter(part_y, send_q, send_y)

    def k_of(w):
        return w.shape[0]

    def position(meta_, r, n, zr):
        zo = lax.rem(meta_[0] + zr, outer)
        zi = lax.rem(meta_[1] + r, inner)
        return zo * inner + zi

    def quarter_of(meta_, yr, cr):
        ty = meta_[2] if yr == 0 else 1 - meta_[2]
        tc = meta_[3] if cr == 0 else 1 - meta_[3]
        return ty * 2 + tc

    def col_place(key, depth):
        yr, cr, r = key

        def places(piece, target, meta_):
            n = piece.shape[2]
            col = pl.ds(pl.multiple_of(quarter_of(meta_, yr, cr) * n, 128), n)
            return [
                (piece.at[zr], target.at[pl.ds(pl.multiple_of(position(meta_, r, n, zr) * depth, 16), depth), col])
                for zr in range(outer)
            ]

        return places

    def row_place(key, depth):
        yr, cr, r = key

        def places(piece, target, meta_):
            n = piece.shape[1]
            return [
                (
                    piece.at[zr],
                    target.at[pl.ds(pl.multiple_of(position(meta_, r, n, zr) * depth + quarter_of(meta_, yr, cr) * n, 16), n), :],
                )
                for zr in range(outer)
            ]

        return places

    def whole(piece, target, meta_):
        return [(piece, target)]

    def pair(stack, me, axis):
        first, second = stack
        same = me == 0
        return jnp.concatenate([jnp.where(same, first, second), jnp.where(same, second, first)], axis=axis)

    plan, pieces = [], []
    for which, (found, w, by_cols) in enumerate(((w1_found, repa_w1, True), (w2_found, repa_w2, True), (w3_found, repa_w3, False))):
        depth = k_of(w)
        aligned = depth % 16 == 0 if by_cols else (depth // 4) % 16 == 0
        if aligned:
            for key, a in found.items():
                plan.append((which, (col_place if by_cols else row_place)(key, depth)))
                pieces.append(a)
        else:
            natural = {}
            for yr in range(2):
                for cr in range(2):
                    a = jnp.stack([found[(yr, cr, r)] for r in range(inner)], axis=1)
                    natural[(yr, cr)] = to_natural(to_natural(a, i, inner, 1), o, outer, 0).reshape((n_dp,) + a.shape[2:])
            axis = 2 if by_cols else 1
            cat = pair([pair([natural[(yr, 0)], natural[(yr, 1)]], c, axis) for yr in range(2)], y, axis)
            plan.append((which, whole))
            pieces.append(cat.reshape(n_dp * depth, w.shape[1]))

    small_ins = [part_q, rq, ry, h_q, mods_own, seg_q, fc2_b.astype(F32).reshape(1, width), go_q, feat_q, keep_q, b_one, b_two, b_three]
    h_low, grad_h, g_mlp, gate_two, s_one, s_two, gz, ga_two, ga_one, g_b1, g_b2, g_b3, g_fc2_b = call(
        functools.partial(proj_kernel, plan, len(pieces)),
        [
            shape_of((half, width), BF16),
            shape_of((half, width), F32),
            shape_of((half, width), BF16),
            shape_of((slots, width), F32),
            shape_of((half, hidden), BF16),
            shape_of((half, hidden), BF16),
            shape_of((half, repr_width), BF16),
            shape_of((half, hidden), BF16),
            shape_of((half, hidden), BF16),
            shape_of((1, hidden), F32),
            shape_of((1, hidden), F32),
            shape_of((1, repr_width), F32),
            shape_of((1, width), F32),
        ],
        [meta] + small_ins + pieces,
        in_specs=[SMEM] + [VMEM] * len(small_ins) + [ANY] * len(pieces),
        scratch=[
            pltpu.VMEM((width, hidden), BF16),
            pltpu.VMEM((hidden, hidden), BF16),
            pltpu.VMEM((hidden, repr_width), BF16),
            pltpu.VMEM((half, hidden), F32),
            pltpu.VMEM((half, hidden), F32),
            pltpu.SemaphoreType.DMA((3,)),
        ],
        flops=4 * half * (width * hidden + hidden * hidden + hidden * repr_width),
        name="projector",
    )
    g_mlp_all = spread_quarter(g_mlp)

    def wgrad_dp(a, b, step, name):
        rows, cols = a.shape[1], b.shape[1]
        depth = rows // n_dp
        flops = 2 * a.shape[0] * rows * cols
        scratch = [pltpu.VMEM((rows, cols), BF16), pltpu.SemaphoreType.DMA]
        if depth % 16 == 0:

            def place(g, outs, sem, meta_):
                for r in range(inner):
                    for zr in range(outer):
                        at = position(meta_, r, 0, zr)
                        pltpu.make_async_copy(g.at[pl.ds(pl.multiple_of(at * depth, 16), depth), :], outs[r].at[zr], sem).start()

            return call(
                functools.partial(wgrad_kernel, place, inner, step),
                [shape_of((outer, depth, cols), BF16)] * inner,
                [meta, a, b],
                in_specs=[SMEM, VMEM, VMEM],
                out_specs=[ANY] * inner,
                scratch=scratch,
                flops=flops,
                name=name,
            )

        def place(g, outs, sem, meta_):
            pltpu.make_async_copy(g, outs[0], sem).start()

        (nat,) = call(
            functools.partial(wgrad_kernel, place, 1, step),
            [shape_of((rows, cols), BF16)],
            [meta, a, b],
            in_specs=[SMEM, VMEM, VMEM],
            out_specs=[ANY],
            scratch=scratch,
            flops=flops,
            name=name,
        )
        nat = nat.reshape(outer, inner, depth, cols)
        rel = to_relative(to_relative(nat, i, inner, 1), o, outer, 0)
        return [rel[:, r] for r in range(inner)]

    def reduce_dp(parts):
        v = parts[0].astype(F32)
        for r in range(1, inner):
            v = v + from_inner(parts[inner - r], r).astype(F32)
        out = v[0]
        for r in range(1, outer):
            out = out + from_outer(v[outer - r].astype(BF16), r).astype(F32)
        return out

    def wgrad_all(a, b, by_cols, step, name):
        rows, cols = a.shape[1], b.shape[1]
        depth = rows // n_dp
        rb, cb = (depth, cols // 4) if by_cols else (depth // 4, cols)
        flops = 2 * a.shape[0] * rows * cols
        scratch = [pltpu.VMEM((rows, cols), BF16), pltpu.SemaphoreType.DMA]
        n_outs = 4
        if rb % 16 == 0:

            def place(g, outs, sem, meta_):
                for cr in range(2):
                    for yr in range(2):
                        for r in range(inner):
                            for zr in range(outer):
                                at = position(meta_, r, 0, zr)
                                part = quarter_of(meta_, yr, cr)
                                if by_cols:
                                    source = g.at[pl.ds(pl.multiple_of(at * depth, 16), rb), pl.ds(pl.multiple_of(part * cb, 128), cb)]
                                else:
                                    source = g.at[pl.ds(pl.multiple_of(at * depth + part * rb, 16), rb), :]
                                pltpu.make_async_copy(source, outs[2 * cr + yr].at[r, zr], sem).start()

            keep_q_, keep_y_, send_q_, send_y_ = call(
                functools.partial(wgrad_kernel, place, n_outs, step),
                [shape_of((inner, outer, rb, cb), BF16)] * n_outs,
                [meta, a, b],
                in_specs=[SMEM, VMEM, VMEM],
                out_specs=[ANY] * n_outs,
                scratch=scratch,
                flops=flops,
                name=name,
            )
            return keep_q_, keep_y_, send_q_, send_y_

        def place(g, outs, sem, meta_):
            pltpu.make_async_copy(g, outs[0], sem).start()

        (nat,) = call(
            functools.partial(wgrad_kernel, place, 1, step),
            [shape_of((rows, cols), BF16)],
            [meta, a, b],
            in_specs=[SMEM, VMEM, VMEM],
            out_specs=[ANY],
            scratch=scratch,
            flops=flops,
            name=name,
        )
        if by_cols:
            nat = nat.reshape(outer, inner, rb, 2, 2, cb).transpose(4, 3, 1, 0, 2, 5)
        else:
            nat = nat.reshape(outer, inner, 2, 2, rb, cb).transpose(3, 2, 1, 0, 4, 5)
        rel = to_relative(to_relative(to_relative(to_relative(nat, c, 2, 0), y, 2, 1), i, inner, 2), o, outer, 3)
        return rel[0, 0], rel[0, 1], rel[1, 0], rel[1, 1]

    def reduce_all(parts):
        keep_q_, keep_y_, send_q_, send_y_ = parts
        ry_ = swap_core(send_y_)
        rq_ = swap_core(send_q_)
        passed = swap_y((keep_y_.astype(F32) + ry_.astype(F32)).astype(BF16))
        total = keep_q_.astype(F32) + rq_.astype(F32) + passed.astype(F32)
        rest = [total[0]] + [total[r].astype(BF16) for r in range(1, inner)]
        return reduce_dp(rest)

    def spread_tensor(block, by_cols):
        block = block.astype(BF16)
        axis = 1 if by_cols else 0
        other = swap_y(block)
        c0, c1 = swap_core(block), swap_core(other)
        own = pair([block, c0], c, axis)
        peer = pair([other, c1], c, axis)
        return pair([own, peer], y, axis).astype(F32)

    g_w3 = spread_tensor(reduce_all(wgrad_all(s_two, gz, False, 512, "grad_w3")), False)
    g_w2 = spread_tensor(reduce_all(wgrad_all(s_one, ga_two, True, 256, "grad_w2")), True)
    g_w1 = spread_tensor(reduce_all(wgrad_all(h_low, ga_one, True, 384, "grad_w1")), True)

    g_mlp_full, gpre, part_q, part_y, send_q, send_y, g_fc1_b = call(
        mlp_back_kernel,
        [shape_of((T, width), BF16), shape_of((T, ff), BF16)] + quarter + [shape_of((1, ff), F32)],
        list(g_mlp_all) + [pre, fc1_w, fc2_w],
        flops=4 * T * width * ff,
        name="mlp_back",
    )
    rq, ry = settle_quarter(part_y, send_q, send_y)
    g_one, g_attn, gate_one, shift_two, scale_two, g_out_b = call(
        second_back_kernel,
        [shape_of((half, width), F32), shape_of((half, width), BF16)] + [shape_of((slots, width), F32)] * 3 + [shape_of((1, width), F32)],
        [part_q, rq, ry, grad_h, h_q, attn_q, mods_own, seg_q],
        name="second_back",
    )
    g_attn_all = spread_quarter(g_attn)
    g_fc2_t = reduce_dp(wgrad_dp(g_mlp_full, act, 384, "grad_fc2"))
    g_fc1 = reduce_dp(wgrad_dp(m_full, gpre, 384, "grad_fc1"))

    gqkv, part_q, part_y, send_q, send_y, g_qv_b, g_attn_full = call(
        functools.partial(bwd_kernel, heads),
        [shape_of((T, 3 * wide), BF16)] + quarter + [shape_of((2, wide), F32), shape_of((T, width), BF16)],
        list(g_attn_all) + [out_w, q, k, v, seg_cols, seg_rows, val_rows, qkv_w],
        flops=8 * T * width * wide + 10 * T * seq * wide,
        name="attention_back",
    )
    rq, ry = settle_quarter(part_y, send_q, send_y)
    g_in, shift_one, scale_one = call(
        first_back_kernel,
        [shape_of((half, width), BF16)] + [shape_of((slots, width), F32)] * 2,
        [order, part_q, rq, ry, g_one, hid, mods_own, seg_q],
        in_specs=[SMEM] + [VMEM] * 7,
        name="first_back",
    )
    g_qkv = reduce_dp(wgrad_dp(m_one, gqkv, 384, "grad_qkv"))
    g_out_t = reduce_dp(wgrad_dp(g_attn_full, mixed, 384, "grad_out"))

    g_mod = jnp.concatenate([shift_one, scale_one, gate_one, shift_two, scale_two, gate_two], axis=-1)
    g_mod = (g_mod + swap_y(g_mod)).astype(BF16)
    g_mod = exchange_dp(g_mod.reshape(slots, n_dp, -1).transpose(1, 0, 2))
    g_mod = pair([g_mod, swap_core(g_mod)], c, 1).reshape(n_dp * images, -1)
    g_ada_w = lax.dot_general(g_mod, cond_act, (((0,), (1,)), ((), ())), preferred_element_type=F32)
    g_ada_b = jnp.sum(g_mod.astype(F32), axis=0)
    g_cond = lax.dot_general(ada_w, g_mod, (((0,), (1,)), ((), ())), preferred_element_type=F32)
    g_cond = g_cond.reshape(outer, inner, feats, n_dp * images)
    rel = to_relative(to_relative(g_cond, i, inner, 1), o, outer, 0)
    v_now = rel[:, 0]
    for r in range(1, inner):
        v_now = v_now + from_inner(rel[:, inner - r], r)
    g_cond = v_now[0]
    for r in range(1, outer):
        g_cond = g_cond + from_outer(v_now[outer - r], r)
    g_cond = g_cond * silu_slope(condition)
    g_table = lax.dot_general(
        g_cond, class_hot.astype(F32), (((1,), (1,)), ((), ())), precision=lax.Precision.HIGHEST, preferred_element_type=F32
    )

    def total_dp(x):
        step = 1
        while step < n_dp:
            x = x + lax.ppermute(x, "dp", [(k_, k_ ^ step) for k_ in range(n_dp)])
            step *= 2
        return x

    early = jnp.concatenate([g_b1, g_b2, g_b3, g_fc2_b], axis=1)
    early = early + swap_core(early)
    early = early + swap_y(early)
    early = total_dp(early)
    late_own = g_out_b + swap_core(g_out_b)
    late_own = late_own + swap_y(late_own)
    late = total_dp(jnp.concatenate([g_fc1_b, late_own, g_qv_b.reshape(1, 2 * wide)], axis=1))

    def my_part(x, n):
        return lax.dynamic_slice_in_dim(x.reshape(-1), d * n, n)

    s_b1 = my_part(early[:, :hidden], n1)
    s_b2 = my_part(early[:, hidden : 2 * hidden], n2)
    s_b3 = my_part(early[:, 2 * hidden : 2 * hidden + repr_width], repa_b3.shape[0])
    s_fc2_b = early[0, 2 * hidden + repr_width :]
    s_fc1_b = late[0, :ff]
    s_out_b = late[0, ff : ff + width]
    s_qv_b = late[0, ff + width :].reshape(2, wide)

    def spread_tokens(block):
        other = swap_y(block)
        c0, c1 = swap_core(block), swap_core(other)
        own = pair([block, other], y, 0)
        peer = pair([c0, c1], y, 0)
        return pair([own, peer], c, 0).reshape(micro_count, rows_dev, seq, width)

    block_out = spread_tokens(h_low)
    grad_in = spread_tokens(g_in).astype(F32)
    depth = width // n_dp
    return (
        block_out,
        grad_in,
        g_table,
        g_ada_w,
        g_ada_b,
        jnp.stack([g_qkv[:, :wide], g_qkv[:, wide : 2 * wide], g_qkv[:, 2 * wide :]]),
        s_qv_b,
        g_out_t.T,
        s_out_b,
        g_fc1,
        s_fc1_b,
        g_fc2_t.T,
        s_fc2_b,
        g_w1,
        s_b1,
        g_w2,
        s_b2,
        g_w3,
        s_b3,
    )


def solution(mesh):
    dp, tensor = "dp", "tensor"
    rows4, rows3 = P(None, dp, None, None), P(None, dp, None)
    ins = (rows4, rows4, rows4, rows3, rows3, rows3, rows3, P(dp, None), P(dp, None), P(dp), P(None, None, tensor), P(None, tensor), P(tensor, None), P(), P(None, tensor), P(tensor), P(tensor, None), P(), P(dp, None), P(dp), P(dp, None), P(dp), P(dp, None), P(dp))
    outs = (rows4, rows4, P(dp, None), P(dp, None), P(dp), P(None, dp, tensor), P(None, tensor), P(tensor, dp), P(), P(dp, tensor), P(tensor), P(tensor, dp), P(), P(dp, None), P(dp), P(dp, None), P(dp), P(dp, None), P(dp))
    return jax.shard_map(functools.partial(body, mesh), mesh=mesh, in_specs=ins, out_specs=outs, check_vma=False)
```

time: 1840 us -> 686 us (0.37)
  waiting for transfers between devices: 1350 us -> 334 us
  matrix products: 205 us -> 7.17 us
  blocking collectives: 148 us -> 0 us
  starting transfers between devices: 1.81 us -> 140 us
  Pallas kernels: 0 us -> 101 us
  other arithmetic: 66.5 us -> 48 us
    reduce_scatter x8 -> x0, waiting for transfers between devices: 751 us -> none  [the longest x1 270 us: settle(): lax.psum_scatter(g_ada_w.astype(jnp.bfloat16), 'dp', scatter_dimension=0,...]
    all_gather x5 -> x0, waiting for transfers between devices: 470 us -> none  [the longest x1 215 us: body(): lax.all_gather(ada_w, 'dp', axis=0, tiled=True)]
    ppermute x0 -> x140, waiting for transfers between devices: none -> 334 us  [the longest x25 138 us: swap_y(): return lax.ppermute(x, 'tensor', [(0, 2), (2, 0), (1, 3), (3, 1)])]
    dot_general x80 -> x5, matrix products: 205 us -> 7.17 us  [the longest x1 2.66 us: body(): lax.dot_general(g_mod, cond_act, (((0,), (1,)), ((), ())), preferred_elem...]
    ppermute x0 -> x140, starting transfers between devices: none -> 140 us  [the longest x48 76 us: from_outer(): lax.ppermute(x, 'dp', [((k + r) % outer * inner + j, k * inner + j) for k...]
    psum x4 -> x0, waiting for transfers between devices: 124 us -> none  [the longest x1 54.1 us: body(): lax.psum(jnp.einsum('tf,df->td', grad_pre, fc1_w, preferred_element_type=...]
    pallas_call x0 -> x15, Pallas kernels: none -> 101 us  [call(): pl.pallas_call(kernel, out_shape=tuple(outs), in_specs=in_specs or [VMEM]...]
    unnamed x2 -> x0, blocking collectives: 73.1 us -> none
  transfers between devices with their start and end apart: 18 -> 140, of which waited for: 15 -> 52; matrix products, arithmetic and copies ran while one was open for 10% -> 13% of each run, Pallas kernels for 0% -> 13%
where the time goes in v1:
time: 686 us; the launch traced here: 676 us
  waiting for transfers between devices  334 us (49%)
  starting transfers between devices  140 us (20%)
  Pallas kernels  101 us (15%)
  other arithmetic  48 us (7%)
  local copies, waits for them, and re-layouts  43.5 us (6%)
  matrix products  7.17 us (1%)
    ppermute x25, waiting for transfers between devices, swap_y(): return lax.ppermute(x, 'tensor', [(0, 2), (2, 0), (1, 3), (3, 1)])  138 us
    ppermute x48, waiting for transfers between devices, from_outer(): lax.ppermute(x, 'dp', [((k + r) % outer * inner + j, k * inner + j) for k...  115 us
    pallas_call x15, Pallas kernels, call(): pl.pallas_call(kernel, out_shape=tuple(outs), in_specs=in_specs or [VMEM]...  101 us
    ppermute x48, starting transfers between devices, from_outer(): lax.ppermute(x, 'dp', [((k + r) % outer * inner + j, k * inner + j) for k...  76 us
    ppermute x6, waiting for transfers between devices, total_dp(): x = x + lax.ppermute(x, 'dp', [(k_, k_ ^ step) for k_ in range(n_dp)])  38.3 us
    ppermute x16, waiting for transfers between devices, from_inner(): lax.ppermute(x, 'dp', [(k * inner + (j + r) % inner, k * inner + j) for k...  37.4 us
    ppermute x25, starting transfers between devices, swap_y(): return lax.ppermute(x, 'tensor', [(0, 2), (2, 0), (1, 3), (3, 1)])  32.7 us
    ppermute x16, starting transfers between devices, from_inner(): lax.ppermute(x, 'dp', [(k * inner + (j + r) % inner, k * inner + j) for k...  17 us
  transfers between devices with their start and end apart: 140, of which 52 were waited for; matrix products, arithmetic and copies ran while one was open for 13% of the time, Pallas kernels for 13%

profile of v1, /device:TPU:0, one launch (start us, length us, event | category | flops | bytes accessed | tf_op | source)
XLA Modules:
  0.0 676.1 jit_solution(14944497343469638665)
XLA Ops:
  1.8 5.0 collective-permute-start.46
  26.0 3.3 collective-permute-done.4
  42.2 4.2 copy.84.rest_3_.w
  51.3 3.5 collective-permute-start.26
  61.3 10.1 %attention.1 = (bf16[512,1152]{1,0:T(8,128)(2,1)}, bf16[512,288]{1,0:T(8,128)(2,1)}, bf16[512,288]{1,0:T(8,128)(2,1)}, bf16[512,288]{1,0:T(8,128)(2,1)}, bf16[512,288]{1,0:T(8,128)(2,1)}) custom-call(s32[4]{0:T(128)} %pad_add_fusion.4.order_.order, bf16[4,128,1152]{2,1,0:T(8,128)(2,1)} %bitcast.333, f32[4,6912]{1,0:T(4,128)} %get-tuple-element.296.a.mods.refs_4_, ...), custom_call_target="tpu_custom_call" | custom-call | flops 1170210816 | bytes 5759248 | tf_op jit(solution)/shard_map/attention/pallas_call | solution.py:29
  80.1 19.2 %collective-permute-done.27 = bf16[144,512]{1,0:T(8,128)(2,1)S(1)} collective-permute-done((bf16[144,512]{1,0:T(8,128)(2,1)S(1)}, bf16[144,512]{1,0:T(8,128)(2,1)S(1)}, u32[]{:S(2)}, u32[]{:S(2)}) %collective-permute-start.27) | collective-permute-done | bytes 147488 | tf_op jit(solution)/shard_map/ppermute | solution.py:358
  105.8 16.5 %collective-permute-done.13.m2 = bf16[256,288]{1,0:T(8,128)(2,1)S(1)} collective-permute-done((bf16[256,288]{1,0:T(8,128)(2,1)S(1)}, bf16[256,288]{1,0:T(8,128)(2,1)S(1)}, u32[]{:S(2)}, u32[]{:S(2)}) %collective-permute-start.13) | collective-permute-done | bytes 147488 | tf_op jit(solution)/shard_map/ppermute | solution.py:361
  126.8 3.5 collective-permute-done.52.refs_33_
  133.7 3.2 collective-permute-done.14.m3
  143.0 10.3 %collective-permute-done.32.refs_17_ = bf16[4,144,512]{2,1,0:T(8,128)(2,1)} collective-permute-done((bf16[4,144,512]{2,1,0:T(8,128)(2,1)S(1)}, bf16[4,144,512]{2,1,0:T(8,128)(2,1)}, u32[]{:S(2)}, u32[]{:S(2)}) %collective-permute-start.32) | collective-permute-done | bytes 589856 | tf_op jit(solution)/shard_map/ppermute | solution.py:361
  156.6 5.8 middle.1
  171.8 8.3 %mlp.1 = (bf16[512,1152]{1,0:T(8,128)(2,1)}, f32[512,1152]{1,0:T(8,128)}, bf16[512,1152]{1,0:T(8,128)(2,1)}, f32[128,1152]{1,0:T(8,128)}, f32[128,1152]{1,0:T(8,...) custom-call(bf16[256,1152]{1,0:T(8,128)(2,1)} %get-tuple-element.91.m_own, ...), custom_call_target="tpu_custom_call" | custom-call | flops 2717908992 | bytes 12980736 | tf_op jit(solution)/shard_map/mlp/pallas_call | solution.py:29
  180.2 4.0 collective-permute-done.42.refs_25_
  185.4 31.7 %collective-permute-done.34.refs_19_ = bf16[4,144,512]{2,1,0:T(8,128)(2,1)} collective-permute-done((bf16[4,144,512]{2,1,0:T(8,128)(2,1)}, bf16[4,144,512]{2,1,0:T(8,128)(2,1)}, u32[]{:S(2)}, u32[]{:S(2)}) %collective-permute-start.34) | collective-permute-done | bytes 589856 | tf_op jit(solution)/shard_map/ppermute | solution.py:361
  226.3 5.9 collective-permute-done.21.refs_2_
  232.3 15.7 %projector.1 = (bf16[128,1152]{1,0:T(8,128)(2,1)}, f32[128,1152]{1,0:T(8,128)}, bf16[128,1152]{1,0:T(8,128)(2,1)}, f32[4,1152]{1,0:T(4,128)}, bf16[128,2048]{1,0...) custom-call(s32[4]{0:T(128)} %pad_add_fusion.3.meta, ...), custom_call_target="tpu_custom_call" | custom-call | flops 4160749568 | bytes 22165520 | tf_op jit(solution)/shard_map/projector/pallas_call | solution.py:29
  257.5 6.9 %grad_w2.1 = (bf16[2,4,256,512]{3,2,1,0:T(8,128)(2,1)}, bf16[2,4,256,512]{3,2,1,0:T(8,128)(2,1)}, bf16[2,4,256,512]{3,2,1,0:T(8,128)(2,1)}, bf16[2,4,256,512]{3,2,1,0:T(8,128)(2,1)}) custom-call(s32[4]{0:T(128)} %pad_add_fusion.3.meta, bf16[128,2048]{1,0:T(8,128)(2,1)} %get-tuple-element.149.a_ref, bf16[128,2048]{1,0:T(8,128)(2,1)} %get-tuple-element.150.b_ref), custom_call_target="tpu_custom_call" | custom-call | flops 1073741824 | bytes 9437200 | tf_op jit(solution)/shard_map/grad_w2/pallas_call | solution.py:29
  264.5 4.8 grad_w1.1
  270.9 3.7 grad_w3.1
  279.9 9.2 %mlp_back.1 = (bf16[512,1152]{1,0:T(8,128)(2,1)}, bf16[512,1152]{1,0:T(8,128)(2,1)}, f32[128,1152]{1,0:T(8,128)}, f32[128,1152]{1,0:T(8,128)}, bf16[128,1152]{1,...) custom-call(bf16[128,1152]{1,0:T(8,128)(2,1)} %get-tuple-element.98.g0, bf16[128,1152]{1,0:T(8,128)(2,1)} %copy-done.61, ...), custom_call_target="tpu_custom_call" | custom-call | flops 2717908992 | bytes 12980736 | tf_op jit(solution)/shard_map/mlp_back/pallas_call | solution.py:29
  293.5 4.9 grad_fc2.1
  299.5 17.1 %collective-permute-done.64.ry = bf16[128,1152]{1,0:T(8,128)(2,1)} collective-permute-done((bf16[128,1152]{1,0:T(8,128)(2,1)}, bf16[128,1152]{1,0:T(8,128)(2,1)}, u32[]{:S(2)}, u32[]{:S(2)}) %collective-permute-start.64) | collective-permute-done | bytes 294944 | tf_op jit(solution)/shard_map/ppermute | solution.py:361
  316.5 4.2 second_back.1
  320.8 5.1 grad_fc1.1
  329.5 6.2 collective-permute-done.89
  341.8 11.7 %attention_back.1 = (bf16[512,864]{1,0:T(8,128)(2,1)}, f32[128,1152]{1,0:T(8,128)}, f32[128,1152]{1,0:T(8,128)}, bf16[128,1152]{1,0:T(8,128)(2,1)}, bf16[128,115...) custom-call(bf16[128,1152]{1,0:T(8,128)(2,1)} %get-tuple-element.106.g0, bf16[128,1152]{1,0:T(8,128)(2,1)} %copy-done.64, ...), custom_call_target="tpu_custom_call" | custom-call | flops 1736441856 | bytes 8560896 | tf_op jit(solution)/shard_map/attention_back/pallas_call | solution.py:29
  358.3 38.3 %collective-permute-done.90 = f32[1,2880]{1,0:T(1,128)S(1)} collective-permute-done((f32[1,2880]{1,0:T(1,128)S(1)}, f32[1,2880]{1,0:T(1,128)S(1)}, u32[]{:S(2)}, u32[]{:S(2)}) %collective-permute-start.90) | collective-permute-done | bytes 11552 | tf_op jit(solution)/shard_map/ppermute | solution.py:790
  398.1 4.4 grad_qkv.1
  422.1 4.4 collective-permute-done.135
  435.3 3.5 add_convert_fusion
  438.8 13.6 %collective-permute-done.94 = bf16[144,288]{1,0:T(8,128)(2,1)S(1)} collective-permute-done((bf16[144,288]{1,0:T(8,128)(2,1)S(1)}, bf16[144,288]{1,0:T(8,128)(2,1)S(1)}, u32[]{:S(2)}, u32[]{:S(2)}) %collective-permute-start.94) | collective-permute-done | bytes 82976 | tf_op jit(solution)/shard_map/ppermute | solution.py:358
  452.4 11.4 %collective-permute-start.96 = (bf16[144,288]{1,0:T(8,128)(2,1)S(1)}, bf16[144,288]{1,0:T(8,128)(2,1)S(1)}, u32[]{:S(2)}, u32[]{:S(2)}) collective-permute-start(bf16[144,288]{1,0:T(8,128)(2,1)S(1)} %get-tuple-element.273), channel_id=1, source_target_pairs={{24,0},{28,4},{0,8},{4,12},{8,16},{12,20},{16,24},{20,28},{25,1},{... | collective-permute-start | bytes 248840 | tf_op jit(solution)/shard_map/ppermute | solution.py:358
  479.1 4.8 collective-permute-done.98
  485.7 12.3 %collective-permute-done.99 = bf16[144,1152]{1,0:T(8,128)(2,1)S(1)} collective-permute-done((bf16[144,1152]{1,0:T(8,128)(2,1)S(1)}, bf16[144,1152]{1,0:T(8,128)(2,1)S(1)}, u32[]{:S(2)}, u32[]{:S(2)}) %collective-permute-start.99) | collective-permute-done | bytes 331808 | tf_op jit(solution)/shard_map/ppermute | solution.py:358
  499.1 8.6 %collective-permute-done.70.ry = bf16[128,1152]{1,0:T(8,128)(2,1)S(1)} collective-permute-done((bf16[128,1152]{1,0:T(8,128)(2,1)S(1)}, bf16[128,1152]{1,0:T(8,128)(2,1)S(1)}, u32[]{:S(2)}, u32[]{:S(2)}) %collective-permute-start.70) | collective-permute-done | bytes 294944 | tf_op jit(solution)/shard_map/ppermute | solution.py:361
  508.3 3.7 first_back.1
  534.8 3.5 convert_add_fusion.3
  541.8 19.2 %collective-permute-done.80 = f32[4,144,64]{1,2,0:T(8,128)S(1)} collective-permute-done((f32[4,144,64]{1,2,0:T(8,128)S(1)}, f32[4,144,64]{1,2,0:T(8,128)S(1)}, u32[]{:S(2)}, u32[]{:S(2)}) %collective-permute-start.80) | collective-permute-done | bytes 147488 | tf_op jit(solution)/shard_map/ppermute | solution.py:355
  566.4 18.4 %collective-permute-done.71 = bf16[128,1152]{1,0:T(8,128)(2,1)S(1)} collective-permute-done((bf16[128,1152]{1,0:T(8,128)(2,1)S(1)}, bf16[128,1152]{1,0:T(8,128)(2,1)S(1)}, u32[]{:S(2)}, u32[]{:S(2)}) %collective-permute-start.71) | collective-permute-done | bytes 294944 | tf_op jit(solution)/shard_map/ppermute | solution.py:361
  587.3 3.4 collective-permute-done.82
  595.6 6.4 collective-permute-done.113
  605.6 3.7 collective-permute-start.114
  616.1 6.0 collective-permute-start.115
  622.1 9.1 %collective-permute-done.86 = bf16[144,864]{1,0:T(8,128)(2,1)S(1)} collective-permute-done((bf16[144,864]{1,0:T(8,128)(2,1)S(1)}, bf16[144,864]{1,0:T(8,128)(2,1)S(1)}, u32[]{:S(2)}, u32[]{:S(2)}) %collective-permute-start.86) | collective-permute-done | bytes 248864 | tf_op jit(solution)/shard_map/ppermute | solution.py:358
  631.6 3.7 collective-permute-done.115
  644.7 5.7 collective-permute-done.124
  650.4 14.0 %collective-permute-done.125 = bf16[256,512]{1,0:T(8,128)(2,1)S(1)} collective-permute-done((bf16[256,512]{1,0:T(8,128)(2,1)S(1)}, bf16[256,512]{1,0:T(8,128)(2,1)S(1)}, u32[]{:S(2)}, u32[]{:S(2)}) %collective-permute-start.125) | collective-permute-done | bytes 262176 | tf_op jit(solution)/shard_map/ppermute | solution.py:358
  665.2 7.4 %collective-permute-done.128 = bf16[256,512]{1,0:T(8,128)(2,1)S(1)} collective-permute-done((bf16[256,512]{1,0:T(8,128)(2,1)S(1)}, bf16[256,512]{1,0:T(8,128)(2,1)S(1)}, u32[]{:S(2)}, u32[]{:S(2)}) %collective-permute-start.128) | collective-permute-done | bytes 262176 | tf_op jit(solution)/shard_map/ppermute | solution.py:361
  (566 shorter events, 244.1 us)
Async XLA Ops:
  1.8 72.7 %collective-permute-start.46 = (bf16[64,768]{1,0:T(8,128)(2,1)S(1)}, bf16[64,768]{1,0:T(8,128)(2,1)S(1)}, u32[]{:S(2)}, u32[]{:S(2)}) collective-permute-start(bf16[64,768]{1,0:T(8,128)(2,1)S(1)} %constant_dynamic-slice_fusion.16), channel_id=1, source_target_pairs={{8,0},{12,4},{16,8},{20,12},{24,16},{28,20},{0,24},{4,28},{9,1},{1... | collective-permute-start | bytes 294920 | tf_op jit(solution)/shard_map/ppermute | solution.py:358
  6.8 67.6 %collective-permute-start.47 = (bf16[64,768]{1,0:T(8,128)(2,1)S(1)}, bf16[64,768]{1,0:T(8,128)(2,1)S(1)}, u32[]{:S(2)}, u32[]{:S(2)}) collective-permute-start(bf16[64,768]{1,0:T(8,128)(2,1)S(1)} %constant_dynamic-slice_fusion.16), channel_id=1, source_target_pairs={{16,0},{20,4},{24,8},{28,12},{0,16},{4,20},{8,24},{12,28},{17,1},{... | collective-permute-start | bytes 294920 | tf_op jit(solution)/shard_map/ppermute | solution.py:358
  51.3 26.1 %collective-permute-start.26 = (bf16[144,512]{1,0:T(8,128)(2,1)S(1)}, bf16[144,512]{1,0:T(8,128)(2,1)S(1)}, u32[]{:S(2)}, u32[]{:S(2)}) collective-permute-start(bf16[144,512]{1,0:T(8,128)(2,1)S(1)} %constant_dynamic-slice_fusion.18), channel_id=1, source_target_pairs={{8,0},{12,4},{16,8},{20,12},{24,16},{28,20},{0,24},{4,28},{9,1},{1... | collective-permute-start | bytes 442376 | tf_op jit(solution)/shard_map/ppermute | solution.py:358
  71.4 30.5 %collective-permute-start.36 = (bf16[256,512]{1,0:T(8,128)(2,1)S(1)}, bf16[256,512]{1,0:T(8,128)(2,1)S(1)}, u32[]{:S(2)}, u32[]{:S(2)}) collective-permute-start(bf16[256,512]{1,0:T(8,128)(2,1)S(1)} %constant_dynamic-slice_fusion.17), channel_id=1, source_target_pairs={{8,0},{12,4},{16,8},{20,12},{24,16},{28,20},{0,24},{4,28},{9,1},{1... | collective-permute-start | bytes 786440 | tf_op jit(solution)/shard_map/ppermute | solution.py:358
  74.4 27.6 %collective-permute-start.37 = (bf16[256,512]{1,0:T(8,128)(2,1)S(1)}, bf16[256,512]{1,0:T(8,128)(2,1)S(1)}, u32[]{:S(2)}, u32[]{:S(2)}) collective-permute-start(bf16[256,512]{1,0:T(8,128)(2,1)S(1)} %constant_dynamic-slice_fusion.17), channel_id=1, source_target_pairs={{16,0},{20,4},{24,8},{28,12},{0,16},{4,20},{8,24},{12,28},{17,1},{... | collective-permute-start | bytes 786440 | tf_op jit(solution)/shard_map/ppermute | solution.py:358
  74.5 28.2 %collective-permute-start.38 = (bf16[256,512]{1,0:T(8,128)(2,1)S(1)}, bf16[256,512]{1,0:T(8,128)(2,1)S(1)}, u32[]{:S(2)}, u32[]{:S(2)}) collective-permute-start(bf16[256,512]{1,0:T(8,128)(2,1)S(1)} %constant_dynamic-slice_fusion.17), channel_id=1, source_target_pairs={{24,0},{28,4},{0,8},{4,12},{8,16},{12,20},{16,24},{20,28},{25,1},{... | collective-permute-start | bytes 786440 | tf_op jit(solution)/shard_map/ppermute | solution.py:358
  75.1 24.2 %collective-permute-start.27 = (bf16[144,512]{1,0:T(8,128)(2,1)S(1)}, bf16[144,512]{1,0:T(8,128)(2,1)S(1)}, u32[]{:S(2)}, u32[]{:S(2)}) collective-permute-start(bf16[144,512]{1,0:T(8,128)(2,1)S(1)} %constant_dynamic-slice_fusion.18), channel_id=1, source_target_pairs={{16,0},{20,4},{24,8},{28,12},{0,16},{4,20},{8,24},{12,28},{17,1},{... | collective-permute-start | bytes 442376 | tf_op jit(solution)/shard_map/ppermute | solution.py:358
  100.3 33.4 %collective-permute-start.16 = (bf16[288,1152]{1,0:T(8,128)(2,1)S(1)}, bf16[288,1152]{1,0:T(8,128)(2,1)S(1)}, u32[]{:S(2)}, u32[]{:S(2)}) collective-permute-start(bf16[288,1152]{1,0:T(8,128)(2,1)S(1)} %copy-done.20), channel_id=1, source_target_pairs={{0,2},{2,0},{1,3},{3,1},{4,6},{6,4},{5,7},{7,5},{8,10},{10,8},{9,1... | collective-permute-start | bytes 1990664 | tf_op jit(solution)/shard_map/ppermute | solution.py:361
  101.8 36.6 %collective-permute-start.15 = (bf16[288,1152]{1,0:T(8,128)(2,1)S(1)}, bf16[288,1152]{1,0:T(8,128)(2,1)S(1)}, u32[]{:S(2)}, u32[]{:S(2)}) collective-permute-start(bf16[288,1152]{1,0:T(8,128)(2,1)S(1)} %copy-done.20), channel_id=1, source_target_pairs={{0,1},{1,0},{2,3},{3,2},{4,5},{5,4},{6,7},{7,6},{8,9},{9,8},{10,11... | collective-permute-start | bytes 1990664 | tf_op jit(solution)/shard_map/ppermute | solution.py:364
  104.3 26.1 %collective-permute-start.52 = (bf16[4,64,768]{2,1,0:T(8,128)(2,1)S(1)}, bf16[4,64,768]{2,1,0:T(8,128)(2,1)}, u32[]{:S(2)}, u32[]{:S(2)}) collective-permute-start(bf16[4,64,768]{2,1,0:T(8,128)(2,1)S(1)} %pad_maximum_fusion.11.refs_29_), channel_id=1, source_target_pairs={{0,2},{2,0},{1,3},{3,1},{4,6},{6,4},{5,7},{7,5},{8,10},{10,8},{9,1... | collective-permute-start | bytes 1179656 | tf_op jit(solution)/shard_map/ppermute | solution.py:361
  132.1 31.4 %collective-permute-start.40 = (bf16[4,256,512]{2,1,0:T(8,128)(2,1)S(1)}, bf16[4,256,512]{2,1,0:T(8,128)(2,1)}, u32[]{:S(2)}, u32[]{:S(2)}) collective-permute-start(bf16[4,256,512]{2,1,0:T(8,128)(2,1)S(1)} %pad_maximum_fusion.2.refs_21_), channel_id=1, source_target_pairs={{4,0},{0,4},{12,8},{8,12},{20,16},{16,20},{28,24},{24,28},{5,1},{1... | collective-permute-start | bytes 3145736 | tf_op jit(solution)/shard_map/ppermute | solution.py:355
  153.3 30.9 %collective-permute-start.42 = (bf16[4,256,512]{2,1,0:T(8,128)(2,1)S(1)}, bf16[4,256,512]{2,1,0:T(8,128)(2,1)}, u32[]{:S(2)}, u32[]{:S(2)}) collective-permute-start(bf16[4,256,512]{2,1,0:T(8,128)(2,1)S(1)} %pad_maximum_fusion.2.refs_21_), channel_id=1, source_target_pairs={{0,2},{2,0},{1,3},{3,1},{4,6},{6,4},{5,7},{7,5},{8,10},{10,8},{9,1... | collective-permute-start | bytes 3145736 | tf_op jit(solution)/shard_map/ppermute | solution.py:361
  163.6 54.1 %collective-permute-start.44 = (bf16[4,256,512]{2,1,0:T(8,128)(2,1)}, bf16[4,256,512]{2,1,0:T(8,128)(2,1)}, u32[]{:S(2)}, u32[]{:S(2)}) collective-permute-start(bf16[4,256,512]{2,1,0:T(8,128)(2,1)} %collective-permute-done.40.refs_23_), channel_id=1, source_target_pairs={{0,2},{2,0},{1,3},{3,1},{4,6},{6,4},{5,7},{7,5},{8,10},{10,8},{9,1... | collective-permute-start | bytes 3145736 | tf_op jit(solution)/shard_map/ppermute | solution.py:361
  171.1 46.0 %collective-permute-start.34 = (bf16[4,144,512]{2,1,0:T(8,128)(2,1)}, bf16[4,144,512]{2,1,0:T(8,128)(2,1)}, u32[]{:S(2)}, u32[]{:S(2)}) collective-permute-start(bf16[4,144,512]{2,1,0:T(8,128)(2,1)} %copy-done.24), channel_id=1, source_target_pairs={{0,2},{2,0},{1,3},{3,1},{4,6},{6,4},{5,7},{7,5},{8,10},{10,8},{9,1... | collective-permute-start | bytes 1769480 | tf_op jit(solution)/shard_map/ppermute | solution.py:361
  171.6 45.5 %collective-permute-start.31 = (bf16[4,144,512]{2,1,0:T(8,128)(2,1)}, bf16[4,144,512]{2,1,0:T(8,128)(2,1)}, u32[]{:S(2)}, u32[]{:S(2)}) collective-permute-start(bf16[4,144,512]{2,1,0:T(8,128)(2,1)} %copy-done.24), channel_id=1, source_target_pairs={{0,1},{1,0},{2,3},{3,2},{4,5},{5,4},{6,7},{7,6},{8,9},{9,8},{10,11... | collective-permute-start | bytes 1769480 | tf_op jit(solution)/shard_map/ppermute | solution.py:364
  184.2 33.4 %collective-permute-start.20 = (bf16[128,1152]{1,0:T(8,128)(2,1)}, bf16[128,1152]{1,0:T(8,128)(2,1)S(1)}, u32[]{:S(2)}, u32[]{:S(2)}) collective-permute-start(bf16[128,1152]{1,0:T(8,128)(2,1)} %get-tuple-element.95), channel_id=1, source_target_pairs={{0,1},{1,0},{2,3},{3,2},{4,5},{5,4},{6,7},{7,6},{8,9},{9,8},{10,11... | collective-permute-start | bytes 884744 | tf_op jit(solution)/shard_map/ppermute | solution.py:364
  184.9 35.2 %collective-permute-start.33 = (bf16[4,144,512]{2,1,0:T(8,128)(2,1)}, bf16[4,144,512]{2,1,0:T(8,128)(2,1)}, u32[]{:S(2)}, u32[]{:S(2)}) collective-permute-start(bf16[4,144,512]{2,1,0:T(8,128)(2,1)} %collective-permute-done.32.refs_17_), channel_id=1, source_target_pairs={{0,1},{1,0},{2,3},{3,2},{4,5},{5,4},{6,7},{7,6},{8,9},{9,8},{10,11... | collective-permute-start | bytes 1769480 | tf_op jit(solution)/shard_map/ppermute | solution.py:364
  253.6 23.5 %collective-permute-start.59 = (bf16[128,1152]{1,0:T(8,128)(2,1)}, bf16[128,1152]{1,0:T(8,128)(2,1)S(1)}, u32[]{:S(2)}, u32[]{:S(2)}) collective-permute-start(bf16[128,1152]{1,0:T(8,128)(2,1)} %get-tuple-element.98.g0), channel_id=1, source_target_pairs={{0,2},{2,0},{1,3},{3,1},{4,6},{6,4},{5,7},{7,5},{8,10},{10,8},{9,1... | collective-permute-start | bytes 884744 | tf_op jit(solution)/shard_map/ppermute | solution.py:361
  254.1 23.7 %collective-permute-start.60 = (bf16[128,1152]{1,0:T(8,128)(2,1)}, bf16[128,1152]{1,0:T(8,128)(2,1)S(1)}, u32[]{:S(2)}, u32[]{:S(2)}) collective-permute-start(bf16[128,1152]{1,0:T(8,128)(2,1)} %get-tuple-element.98.g0), channel_id=1, source_target_pairs={{0,1},{1,0},{2,3},{3,2},{4,5},{5,4},{6,7},{7,6},{8,9},{9,8},{10,11... | collective-permute-start | bytes 884744 | tf_op jit(solution)/shard_map/ppermute | solution.py:364
  254.1 23.5 %collective-permute-start.56 = (bf16[128,1152]{1,0:T(8,128)(2,1)}, bf16[128,1152]{1,0:T(8,128)(2,1)S(1)}, u32[]{:S(2)}, u32[]{:S(2)}) collective-permute-start(bf16[128,1152]{1,0:T(8,128)(2,1)} %get-tuple-element.97.a_ref), channel_id=1, source_target_pairs={{0,2},{2,0},{1,3},{3,1},{4,6},{6,4},{5,7},{7,5},{8,10},{10,8},{9,1... | collective-permute-start | bytes 884744 | tf_op jit(solution)/shard_map/ppermute | solution.py:361
  255.6 33.5 %collective-permute-start.57 = (bf16[128,1152]{1,0:T(8,128)(2,1)}, bf16[128,1152]{1,0:T(8,128)(2,1)S(1)}, u32[]{:S(2)}, u32[]{:S(2)}) collective-permute-start(bf16[128,1152]{1,0:T(8,128)(2,1)} %get-tuple-element.97.a_ref), channel_id=1, source_target_pairs={{0,1},{1,0},{2,3},{3,2},{4,5},{5,4},{6,7},{7,6},{8,9},{9,8},{10,11... | collective-permute-start | bytes 884744 | tf_op jit(solution)/shard_map/ppermute | solution.py:364
  277.8 58.4 %collective-permute-start.130 = (bf16[2,4,64,768]{3,2,1,0:T(8,128)(2,1)}, bf16[2,4,64,768]{3,2,1,0:T(8,128)(2,1)}, u32[]{:S(2)}, u32[]{:S(2)}) collective-permute-start(bf16[2,4,64,768]{3,2,1,0:T(8,128)(2,1)} %get-tuple-element.158), channel_id=1, source_target_pairs={{0,1},{1,0},{2,3},{3,2},{4,5},{5,4},{6,7},{7,6},{8,9},{9,8},{10,11... | collective-permute-start | bytes 2359304 | tf_op jit(solution)/shard_map/ppermute | solution.py:364
  279.5 48.2 %collective-permute-start.111 = (bf16[2,4,144,512]{3,2,1,0:T(8,128)(2,1)}, bf16[2,4,144,512]{3,2,1,0:T(8,128)(2,1)S(1)}, u32[]{:S(2)}, u32[]{:S(2)}) collective-permute-start(bf16[2,4,144,512]{3,2,1,0:T(8,128)(2,1)} %get-tuple-element.148), channel_id=1, source_target_pairs={{0,1},{1,0},{2,3},{3,2},{4,5},{5,4},{6,7},{7,6},{8,9},{9,8},{10,11... | collective-permute-start | bytes 3538952 | tf_op jit(solution)/shard_map/ppermute | solution.py:364
  290.5 47.4 %collective-permute-start.132 = (bf16[2,4,64,768]{3,2,1,0:T(8,128)(2,1)S(1)}, bf16[2,4,64,768]{3,2,1,0:T(8,128)(2,1)S(1)}, u32[]{:S(2)}, u32[]{:S(2)}) collective-permute-start(bf16[2,4,64,768]{3,2,1,0:T(8,128)(2,1)S(1)} %add_convert_fusion.2), channel_id=1, source_target_pairs={{0,2},{2,0},{1,3},{3,1},{4,6},{6,4},{5,7},{7,5},{8,10},{10,8},{9,1... | collective-permute-start | bytes 2359304 | tf_op jit(solution)/shard_map/ppermute | solution.py:361
  293.0 23.5 %collective-permute-start.64 = (bf16[128,1152]{1,0:T(8,128)(2,1)}, bf16[128,1152]{1,0:T(8,128)(2,1)}, u32[]{:S(2)}, u32[]{:S(2)}) collective-permute-start(bf16[128,1152]{1,0:T(8,128)(2,1)} %add_convert_fusion.4), channel_id=1, source_target_pairs={{0,2},{2,0},{1,3},{3,1},{4,6},{6,4},{5,7},{7,5},{8,10},{10,8},{9,1... | collective-permute-start | bytes 884744 | tf_op jit(solution)/shard_map/ppermute | solution.py:361
  299.5 133.1 %collective-permute-start.121 = (bf16[2,4,256,512]{3,2,1,0:T(8,128)(2,1)}, bf16[2,4,256,512]{3,2,1,0:T(8,128)(2,1)}, u32[]{:S(2)}, u32[]{:S(2)}) collective-permute-start(bf16[2,4,256,512]{3,2,1,0:T(8,128)(2,1)} %get-tuple-element.154), channel_id=1, source_target_pairs={{0,1},{1,0},{2,3},{3,2},{4,5},{5,4},{6,7},{7,6},{8,9},{9,8},{10,11... | collective-permute-start | bytes 6291464 | tf_op jit(solution)/shard_map/ppermute | solution.py:364
  335.7 73.5 %collective-permute-start.101 = (bf16[4,144,1152]{2,1,0:T(8,128)(2,1)}, bf16[4,144,1152]{2,1,0:T(8,128)(2,1)}, u32[]{:S(2)}, u32[]{:S(2)}) collective-permute-start(bf16[4,144,1152]{2,1,0:T(8,128)(2,1)} %get-tuple-element.139), channel_id=1, source_target_pairs={{4,0},{0,4},{12,8},{8,12},{20,16},{16,20},{28,24},{24,28},{5,1},{1... | collective-permute-start | bytes 3981320 | tf_op jit(solution)/shard_map/ppermute | solution.py:355
  336.2 74.8 %collective-permute-start.97 = (bf16[4,144,1152]{2,1,0:T(8,128)(2,1)}, bf16[4,144,1152]{2,1,0:T(8,128)(2,1)}, u32[]{:S(2)}, u32[]{:S(2)}) collective-permute-start(bf16[4,144,1152]{2,1,0:T(8,128)(2,1)} %get-tuple-element.135), channel_id=1, source_target_pairs={{4,0},{0,4},{12,8},{8,12},{20,16},{16,20},{28,24},{24,28},{5,1},{1... | collective-permute-start | bytes 3981320 | tf_op jit(solution)/shard_map/ppermute | solution.py:355
  354.3 42.3 %collective-permute-start.90 = (f32[1,2880]{1,0:T(1,128)S(1)}, f32[1,2880]{1,0:T(1,128)S(1)}, u32[]{:S(2)}, u32[]{:S(2)}) collective-permute-start(f32[1,2880]{1,0:T(1,128)S(1)} %pad_maximum_fusion.20), channel_id=1, source_target_pairs={{0,4},{4,0},{8,12},{12,8},{16,20},{20,16},{24,28},{28,24},{1,5},{5... | collective-permute-start | bytes 34568 | tf_op jit(solution)/shard_map/ppermute | solution.py:790
  356.7 56.1 %collective-permute-start.133 = (bf16[4,64,768]{2,1,0:T(8,128)(2,1)}, bf16[4,64,768]{2,1,0:T(8,128)(2,1)}, u32[]{:S(2)}, u32[]{:S(2)}) collective-permute-start(bf16[4,64,768]{2,1,0:T(8,128)(2,1)} %fusion.24), channel_id=1, source_target_pairs={{4,0},{0,4},{12,8},{8,12},{20,16},{16,20},{28,24},{24,28},{5,1},{1... | collective-permute-start | bytes 1179656 | tf_op jit(solution)/shard_map/ppermute | solution.py:355
  426.5 43.2 %collective-permute-start.102 = (bf16[144,1152]{1,0:T(8,128)(2,1)S(1)}, bf16[144,1152]{1,0:T(8,128)(2,1)S(1)}, u32[]{:S(2)}, u32[]{:S(2)}) collective-permute-start(bf16[144,1152]{1,0:T(8,128)(2,1)S(1)} %get-tuple-element.232), channel_id=1, source_target_pairs={{8,0},{12,4},{16,8},{20,12},{24,16},{28,20},{0,24},{4,28},{9,1},{1... | collective-permute-start | bytes 995336 | tf_op jit(solution)/shard_map/ppermute | solution.py:358
  427.5 43.8 %collective-permute-start.103 = (bf16[144,1152]{1,0:T(8,128)(2,1)S(1)}, bf16[144,1152]{1,0:T(8,128)(2,1)S(1)}, u32[]{:S(2)}, u32[]{:S(2)}) collective-permute-start(bf16[144,1152]{1,0:T(8,128)(2,1)S(1)} %get-tuple-element.234), channel_id=1, source_target_pairs={{16,0},{20,4},{24,8},{28,12},{0,16},{4,20},{8,24},{12,28},{17,1},{... | collective-permute-start | bytes 995336 | tf_op jit(solution)/shard_map/ppermute | solution.py:358
  428.7 42.7 %collective-permute-start.104 = (bf16[144,1152]{1,0:T(8,128)(2,1)S(1)}, bf16[144,1152]{1,0:T(8,128)(2,1)S(1)}, u32[]{:S(2)}, u32[]{:S(2)}) collective-permute-start(bf16[144,1152]{1,0:T(8,128)(2,1)S(1)} %get-tuple-element.233), channel_id=1, source_target_pairs={{24,0},{28,4},{0,8},{4,12},{8,16},{12,20},{16,24},{20,28},{25,1},{... | collective-permute-start | bytes 995336 | tf_op jit(solution)/shard_map/ppermute | solution.py:358
  438.8 25.9 %collective-permute-start.95 = (bf16[144,288]{1,0:T(8,128)(2,1)S(1)}, bf16[144,288]{1,0:T(8,128)(2,1)S(1)}, u32[]{:S(2)}, u32[]{:S(2)}) collective-permute-start(bf16[144,288]{1,0:T(8,128)(2,1)S(1)} %get-tuple-element.274), channel_id=1, source_target_pairs={{16,0},{20,4},{24,8},{28,12},{0,16},{4,20},{8,24},{12,28},{17,1},{... | collective-permute-start | bytes 248840 | tf_op jit(solution)/shard_map/ppermute | solution.py:358
  464.6 70.0 %collective-permute-start.110 = (bf16[2,4,144,512]{3,2,1,0:T(8,128)(2,1)}, bf16[2,4,144,512]{3,2,1,0:T(8,128)(2,1)}, u32[]{:S(2)}, u32[]{:S(2)}) collective-permute-start(bf16[2,4,144,512]{3,2,1,0:T(8,128)(2,1)} %get-tuple-element.146), channel_id=1, source_target_pairs={{0,1},{1,0},{2,3},{3,2},{4,5},{5,4},{6,7},{7,6},{8,9},{9,8},{10,11... | collective-permute-start | bytes 3538952 | tf_op jit(solution)/shard_map/ppermute | solution.py:364
  471.3 26.7 %collective-permute-start.99 = (bf16[144,1152]{1,0:T(8,128)(2,1)S(1)}, bf16[144,1152]{1,0:T(8,128)(2,1)S(1)}, u32[]{:S(2)}, u32[]{:S(2)}) collective-permute-start(bf16[144,1152]{1,0:T(8,128)(2,1)S(1)} %get-tuple-element.237), channel_id=1, source_target_pairs={{16,0},{20,4},{24,8},{28,12},{0,16},{4,20},{8,24},{12,28},{17,1},{... | collective-permute-start | bytes 995336 | tf_op jit(solution)/shard_map/ppermute | solution.py:358
  476.3 58.5 %collective-permute-start.112 = (bf16[2,4,144,512]{3,2,1,0:T(8,128)(2,1)S(1)}, bf16[2,4,144,512]{3,2,1,0:T(8,128)(2,1)}, u32[]{:S(2)}, u32[]{:S(2)}) collective-permute-start(bf16[2,4,144,512]{3,2,1,0:T(8,128)(2,1)S(1)} %copy-done.12), channel_id=1, source_target_pairs={{0,2},{2,0},{1,3},{3,1},{4,6},{6,4},{5,7},{7,5},{8,10},{10,8},{9,1... | collective-permute-start | bytes 3538952 | tf_op jit(solution)/shard_map/ppermute | solution.py:361
  484.0 23.7 %collective-permute-start.70 = (bf16[128,1152]{1,0:T(8,128)(2,1)S(1)}, bf16[128,1152]{1,0:T(8,128)(2,1)S(1)}, u32[]{:S(2)}, u32[]{:S(2)}) collective-permute-start(bf16[128,1152]{1,0:T(8,128)(2,1)S(1)} %add_convert_fusion.3), channel_id=1, source_target_pairs={{0,2},{2,0},{1,3},{3,1},{4,6},{6,4},{5,7},{7,5},{8,10},{10,8},{9,1... | collective-permute-start | bytes 884744 | tf_op jit(solution)/shard_map/ppermute | solution.py:361
  530.0 75.5 %collective-permute-start.120 = (bf16[2,4,256,512]{3,2,1,0:T(8,128)(2,1)}, bf16[2,4,256,512]{3,2,1,0:T(8,128)(2,1)}, u32[]{:S(2)}, u32[]{:S(2)}) collective-permute-start(bf16[2,4,256,512]{3,2,1,0:T(8,128)(2,1)} %get-tuple-element.152), channel_id=1, source_target_pairs={{0,1},{1,0},{2,3},{3,2},{4,5},{5,4},{6,7},{7,6},{8,9},{9,8},{10,11... | collective-permute-start | bytes 6291464 | tf_op jit(solution)/shard_map/ppermute | solution.py:364
  531.0 62.6 %collective-permute-start.84 = (bf16[4,144,864]{2,1,0:T(8,128)(2,1)}, bf16[4,144,864]{2,1,0:T(8,128)(2,1)}, u32[]{:S(2)}, u32[]{:S(2)}) collective-permute-start(bf16[4,144,864]{2,1,0:T(8,128)(2,1)} %get-tuple-element.125), channel_id=1, source_target_pairs={{4,0},{0,4},{12,8},{8,12},{20,16},{16,20},{28,24},{24,28},{5,1},{1... | collective-permute-start | bytes 2985992 | tf_op jit(solution)/shard_map/ppermute | solution.py:355
  532.6 76.6 %collective-permute-start.122 = (bf16[2,4,256,512]{3,2,1,0:T(8,128)(2,1)}, bf16[2,4,256,512]{3,2,1,0:T(8,128)(2,1)}, u32[]{:S(2)}, u32[]{:S(2)}) collective-permute-start(bf16[2,4,256,512]{3,2,1,0:T(8,128)(2,1)} %add_convert_fusion), channel_id=1, source_target_pairs={{0,2},{2,0},{1,3},{3,1},{4,6},{6,4},{5,7},{7,5},{8,10},{10,8},{9,1... | collective-permute-start | bytes 6291464 | tf_op jit(solution)/shard_map/ppermute | solution.py:361
  541.5 43.3 %collective-permute-start.71 = (bf16[128,1152]{1,0:T(8,128)(2,1)S(1)}, bf16[128,1152]{1,0:T(8,128)(2,1)S(1)}, u32[]{:S(2)}, u32[]{:S(2)}) collective-permute-start(bf16[128,1152]{1,0:T(8,128)(2,1)S(1)} %copy-done.34), channel_id=1, source_target_pairs={{0,2},{2,0},{1,3},{3,1},{4,6},{6,4},{5,7},{7,5},{8,10},{10,8},{9,1... | collective-permute-start | bytes 884744 | tf_op jit(solution)/shard_map/ppermute | solution.py:361
  561.1 24.4 %collective-permute-start.81 = (f32[144,64]{0,1:T(8,128)S(1)}, f32[144,64]{0,1:T(8,128)S(1)}, u32[]{:S(2)}, u32[]{:S(2)}) collective-permute-start(f32[144,64]{0,1:T(8,128)S(1)} %get-tuple-element.286), channel_id=1, source_target_pairs={{8,0},{12,4},{16,8},{20,12},{24,16},{28,20},{0,24},{4,28},{9,1},{1... | collective-permute-start | bytes 110600 | tf_op jit(solution)/shard_map/ppermute | solution.py:358
  604.8 26.4 %collective-permute-start.86 = (bf16[144,864]{1,0:T(8,128)(2,1)S(1)}, bf16[144,864]{1,0:T(8,128)(2,1)S(1)}, u32[]{:S(2)}, u32[]{:S(2)}) collective-permute-start(bf16[144,864]{1,0:T(8,128)(2,1)S(1)} %get-tuple-element.249), channel_id=1, source_target_pairs={{16,0},{20,4},{24,8},{28,12},{0,16},{4,20},{8,24},{12,28},{17,1},{... | collective-permute-start | bytes 746504 | tf_op jit(solution)/shard_map/ppermute | solution.py:358
  605.3 26.0 %collective-permute-start.87 = (bf16[144,864]{1,0:T(8,128)(2,1)S(1)}, bf16[144,864]{1,0:T(8,128)(2,1)S(1)}, u32[]{:S(2)}, u32[]{:S(2)}) collective-permute-start(bf16[144,864]{1,0:T(8,128)(2,1)S(1)} %get-tuple-element.248), channel_id=1, source_target_pairs={{24,0},{28,4},{0,8},{4,12},{8,16},{12,20},{16,24},{20,28},{25,1},{... | collective-permute-start | bytes 746504 | tf_op jit(solution)/shard_map/ppermute | solution.py:358
  605.6 26.0 %collective-permute-start.114 = (bf16[144,512]{1,0:T(8,128)(2,1)S(1)}, bf16[144,512]{1,0:T(8,128)(2,1)S(1)}, u32[]{:S(2)}, u32[]{:S(2)}) collective-permute-start(bf16[144,512]{1,0:T(8,128)(2,1)S(1)} %get-tuple-element.254), channel_id=1, source_target_pairs={{8,0},{12,4},{16,8},{20,12},{24,16},{28,20},{0,24},{4,28},{9,1},{1... | collective-permute-start | bytes 442376 | tf_op jit(solution)/shard_map/ppermute | solution.py:358
  612.4 27.8 %collective-permute-start.123 = (bf16[4,256,512]{2,1,0:T(8,128)(2,1)S(1)}, bf16[4,256,512]{2,1,0:T(8,128)(2,1)S(1)}, u32[]{:S(2)}, u32[]{:S(2)}) collective-permute-start(bf16[4,256,512]{2,1,0:T(8,128)(2,1)S(1)} %fusion.3), channel_id=1, source_target_pairs={{4,0},{0,4},{12,8},{8,12},{20,16},{16,20},{28,24},{24,28},{5,1},{1... | collective-permute-start | bytes 3145736 | tf_op jit(solution)/shard_map/ppermute | solution.py:355
  640.8 23.6 %collective-permute-start.125 = (bf16[256,512]{1,0:T(8,128)(2,1)S(1)}, bf16[256,512]{1,0:T(8,128)(2,1)S(1)}, u32[]{:S(2)}, u32[]{:S(2)}) collective-permute-start(bf16[256,512]{1,0:T(8,128)(2,1)S(1)} %get-tuple-element.246), channel_id=1, source_target_pairs={{16,0},{20,4},{24,8},{28,12},{0,16},{4,20},{8,24},{12,28},{17,1},{... | collective-permute-start | bytes 786440 | tf_op jit(solution)/shard_map/ppermute | solution.py:358
  (160 other events, 1978.8 us)

commit v2 on v1

--- a/solution.py
+++ b/solution.py
@@ -107,9 +107,9 @@
         scaling = pick(seg, mods[micro][:, width : 2 * width])
         m = (xhat * (1.0 + scaling) + shift).astype(BF16)
         m_ref[rows, :] = m
-        q = (dot(m, w[0]) + b[0:1, :]).astype(BF16)
-        k = dot(m, w[1]).astype(BF16)
-        v = (dot(m, w[2]) + b[1:2, :]).astype(BF16)
+        q = (dot_nt(m, w[0]) + b[0:1, :]).astype(BF16)
+        k = dot_nt(m, w[1]).astype(BF16)
+        v = (dot_nt(m, w[2]) + b[1:2, :]).astype(BF16)
         q_ref[rows, :] = q
         k_ref[rows, :] = k
         v_ref[rows, :] = v
@@ -155,7 +155,7 @@
                 axis=0,
             )
         )
-        part = dot_nt(gq, w[0]) + dot_nt(gk, w[1]) + dot_nt(gv, w[2])
+        part = dot(gq, w[0]) + dot(gk, w[1]) + dot(gv, w[2])
         if micro == 0:
             part_q[...] = part[:half]
             part_y[...] = part[half:]
@@ -236,7 +236,7 @@
                 send_y[:, lo:hi] = part[half:].astype(BF16)
 
 
-def proj_kernel(plan, n_pieces, meta, *refs):
+def proj_kernel(plan, n_pieces, *refs):
     (part, rq, ry, h_one, mods, seg_ref, fc2_b, grad_out, feat_ref, keep_ref, b1, b2, b3) = refs[:13]
     pieces = refs[13 : 13 + n_pieces]
     (h_low, grad_h, g_mlp, gate_sum, s1, s2, gz_ref, ga2_ref, ga1_ref, gb1, gb2, gb3, gbf) = refs[13 + n_pieces : 26 + n_pieces]
@@ -244,8 +244,8 @@
     weights = (w1, w2, w3)
     width = h_low.shape[1]
     slots = mods.shape[0]
-    for piece, (which, place) in zip(pieces, plan):
-        for source, target in place(piece, weights[which], meta):
+    for which, load in enumerate(plan):
+        for source, target in load(pieces, weights[which]):
             pltpu.make_async_copy(source, target, sems.at[which]).start()
     seg = seg_ref[...]
     gate = pick(seg, mods[:, 5 * width : 6 * width])
@@ -321,14 +321,20 @@
     scale_sum[...] = by_image(seg, g * xhat, slots)
 
 
-def wgrad_kernel(place, n_outs, step, meta, a_ref, b_ref, *refs):
-    outs, (g, sem) = refs[:n_outs], refs[n_outs:]
-    rows = g.shape[0]
-    for lo in range(0, rows, step):
-        hi = min(lo + step, rows)
-        g[lo:hi, :] = dot_tn(a_ref[:, lo:hi], b_ref[...]).astype(BF16)
-    place(g, outs, sem, meta)
-    pltpu.make_async_copy(g, g, sem).wait()
+def wgrad_kernel(place, jobs, n_outs, *refs):
+    meta = refs[0]
+    n_ins = 1 + max(max(a, b) for a, b, _ in jobs)
+    ins, outs, (*results, sem) = refs[1 : 1 + n_ins], refs[1 + n_ins : 1 + n_ins + n_outs], refs[1 + n_ins + n_outs :]
+    for n, (a, b, step) in enumerate(jobs):
+        g = results[n]
+        rows = g.shape[0]
+        for lo in range(0, rows, step):
+            hi = min(lo + step, rows)
+            g[lo:hi, :] = dot_tn(ins[a][:, lo:hi], ins[b][...]).astype(BF16)
+        for source, target in place(n, g, outs, meta):
+            pltpu.make_async_copy(source, target, sem.at[n]).start()
+    for n, g in enumerate(results):
+        pltpu.make_async_copy(g, g, sem.at[n]).wait()
 
 
 def body(mesh, hidden_in, grad_out, features, seg_ids, valid_mask, time_ids, class_ids, class_table, ada_w, ada_b, qkv_w, qv_bias, out_w, out_b, fc1_w, fc1_b, fc2_w, fc2_b, repa_w1, repa_b1, repa_w2, repa_b2, repa_w3, repa_b3):
@@ -340,6 +346,7 @@
     images = micro_count * rows_dev * slots
     half = seq // 2
     wide = qkv_w.shape[2]
+    qkv_t = qkv_w.transpose(0, 2, 1)
     heads = wide // HEAD_DIM
     ff = fc1_w.shape[1]
     hidden = repa_w1.shape[1]
@@ -386,17 +393,6 @@
         zs = to_natural(to_natural(zs, i, inner, 1), o, outer, 0)
         return zs.reshape((n_dp,) + zs.shape[2:])
 
-    def bulk_gather(piece):
-        zs = jnp.stack([piece] + [from_outer(piece, r) for r in range(1, outer)])
-        xs = [zs] + [from_inner(zs, r) for r in range(1, inner)]
-        ys = [swap_y(a) for a in xs]
-        found = {}
-        for yr, group in ((0, xs), (1, ys)):
-            for r, a in enumerate(group):
-                found[(yr, 0, r)] = a
-                found[(yr, 1, r)] = swap_core(a)
-        return found
-
     def cols_of(w):
         n = w.shape[1] // 4
         return lax.dynamic_slice_in_dim(w, t * n, n, axis=1)
@@ -405,17 +401,30 @@
         n = w.shape[0] // 4
         return lax.dynamic_slice_in_dim(w, t * n, n, axis=0)
 
-    w1_found = bulk_gather(cols_of(repa_w1))
-    w3_found = bulk_gather(rows_of(repa_w3))
-    w2_found = bulk_gather(cols_of(repa_w2))
+    k1, k2, k3 = repa_w1.shape[0], repa_w2.shape[0], repa_w3.shape[0]
+    block = hidden // 4
+    r3 = k3 // 4
+    folds = repr_width * r3 // block
+    third = rows_of(repa_w3)
+
+    def fold(w):
+        left, right = w[:, :block], w[:, block:]
+        n = right.shape[0] // 2
+        return jnp.concatenate([left, jnp.concatenate([right[:n], right[n:]], axis=1)], axis=0)
+
+    def unfold(w):
+        n = w.shape[-2] * 2 // 3
+        left, low = w[..., :n, :], w[..., n:, :]
+        m = block // 2
+        return jnp.concatenate([left, jnp.concatenate([low[..., :m], low[..., m:]], axis=-2)], axis=-1)
+
+    packed = jnp.concatenate([cols_of(repa_w2), fold(third), cols_of(repa_w1)], axis=0)
+    gathered = lax.all_gather(packed, ("dp", "tensor"), axis=0)
+    off3, off1 = k2, k2 + folds
     out_y = swap_y(out_w)
     out_c = swap_core(out_w)
     out_yc = swap_core(out_y)
-    b_all = gather_dp(jnp.concatenate([repa_b1, repa_b2, repa_b3]))
-    n1, n2 = repa_b1.shape[0], repa_b2.shape[0]
-    b_one = b_all[:, :n1].reshape(1, -1).astype(F32)
-    b_two = b_all[:, n1 : n1 + n2].reshape(1, -1).astype(F32)
-    b_three = b_all[:, n1 + n2 :].reshape(1, -1).astype(F32)
+    n1, n2, n3 = repa_b1.shape[0], repa_b2.shape[0], repa_b3.shape[0]
 
     ids = gather_dp(jnp.concatenate([class_ids.reshape(images), time_ids.reshape(images)]))
     all_class = ids[:, :images].reshape(1, n_dp * images)
@@ -427,7 +436,16 @@
     freqs = jnp.exp(-math.log(10000.0) * (place % half_width).astype(F32) / half_width)
     angles = all_time.astype(F32) * freqs
     condition = jnp.where(place < half_width, jnp.cos(angles), jnp.sin(angles)) + dot(class_table, class_hot.astype(BF16))
-    cond_act = gather_dp(jax.nn.silu(condition).astype(BF16)).reshape(width, n_dp * images)
+    n_images = n_dp * images
+    biases = jnp.concatenate([repa_b1, repa_b2, repa_b3])
+    lines = -(-biases.shape[0] // n_images)
+    biases = jnp.pad(biases, (0, lines * n_images - biases.shape[0])).reshape(lines, n_images)
+    found = gather_dp(jnp.concatenate([jax.nn.silu(condition).astype(BF16), biases], axis=0))
+    cond_act = found[:, :feats].reshape(width, n_images)
+    b_all = found[:, feats:].reshape(n_dp, -1)
+    b_one = b_all[:, :n1].reshape(1, -1).astype(F32)
+    b_two = b_all[:, n1 : n1 + n2].reshape(1, -1).astype(F32)
+    b_three = b_all[:, n1 + n2 : n1 + n2 + n3].reshape(1, -1).astype(F32)
     mod_part = lax.dot_general(cond_act, ada_w, (((0,), (1,)), ((), ())), preferred_element_type=F32) + ada_b.astype(F32)
     mod_parts = exchange_dp(mod_part.reshape(n_dp, images, -1))
     modulation = mod_parts.transpose(1, 0, 2).reshape(micro_count, slots, -1)
@@ -460,7 +478,7 @@
     m_one, q, k, v, mixed = call(
         fwd,
         [shape_of((T, width), BF16)] + [shape_of((T, wide), BF16)] * 4,
-        [order, hid, mods_own, mods_par, seg_cols, seg_rows, val_rows, qkv_w, qv_bias.astype(F32)],
+        [order, hid, mods_own, mods_par, seg_cols, seg_rows, val_rows, qkv_t, qv_bias.astype(F32)],
         in_specs=[SMEM] + [VMEM] * 8,
         flops=2 * T * width * wide * 3 + 4 * T * seq * wide,
         name="attention",
@@ -514,60 +532,45 @@
         tc = meta_[3] if cr == 0 else 1 - meta_[3]
         return ty * 2 + tc
 
-    def col_place(key, depth):
-        yr, cr, r = key
-
-        def places(piece, target, meta_):
-            n = piece.shape[2]
-            col = pl.ds(pl.multiple_of(quarter_of(meta_, yr, cr) * n, 128), n)
-            return [
-                (piece.at[zr], target.at[pl.ds(pl.multiple_of(position(meta_, r, n, zr) * depth, 16), depth), col])
-                for zr in range(outer)
-            ]
-
-        return places
-
-    def row_place(key, depth):
-        yr, cr, r = key
-
-        def places(piece, target, meta_):
-            n = piece.shape[1]
-            return [
-                (
-                    piece.at[zr],
-                    target.at[pl.ds(pl.multiple_of(position(meta_, r, n, zr) * depth + quarter_of(meta_, yr, cr) * n, 16), n), :],
-                )
-                for zr in range(outer)
-            ]
-
-        return places
-
-    def whole(piece, target, meta_):
-        return [(piece, target)]
-
     def pair(stack, me, axis):
         first, second = stack
         same = me == 0
         return jnp.concatenate([jnp.where(same, first, second), jnp.where(same, second, first)], axis=axis)
 
-    plan, pieces = [], []
-    for which, (found, w, by_cols) in enumerate(((w1_found, repa_w1, True), (w2_found, repa_w2, True), (w3_found, repa_w3, False))):
-        depth = k_of(w)
-        aligned = depth % 16 == 0 if by_cols else (depth // 4) % 16 == 0
-        if aligned:
-            for key, a in found.items():
-                plan.append((which, (col_place if by_cols else row_place)(key, depth)))
-                pieces.append(a)
-        else:
-            natural = {}
-            for yr in range(2):
-                for cr in range(2):
-                    a = jnp.stack([found[(yr, cr, r)] for r in range(inner)], axis=1)
-                    natural[(yr, cr)] = to_natural(to_natural(a, i, inner, 1), o, outer, 0).reshape((n_dp,) + a.shape[2:])
-            axis = 2 if by_cols else 1
-            cat = pair([pair([natural[(yr, 0)], natural[(yr, 1)]], c, axis) for yr in range(2)], y, axis)
-            plan.append((which, whole))
-            pieces.append(cat.reshape(n_dp * depth, w.shape[1]))
+    aligned = k1 % 16 == 0 and k2 % 16 == 0 and r3 % 32 == 0
+    n_all = 4 * n_dp
+
+    def load_two(refs, target):
+        for s in range(n_all):
+            at, part = s // 4, s % 4
+            yield refs[0].at[s, 0:k2, :], target.at[at * k2 : (at + 1) * k2, part * block : (part + 1) * block]
+
+    def load_one(refs, target):
+        for s in range(n_all):
+            at, part = s // 4, s % 4
+            yield refs[0].at[s, off1 : off1 + k1, :], target.at[at * k1 : (at + 1) * k1, part * block : (part + 1) * block]
+
+    def load_three(refs, target):
+        n, m = r3 // 2, block // 2
+        for s in range(n_all):
+            top = (s // 4) * k3 + (s % 4) * r3
+            yield refs[0].at[s, off3 : off3 + r3, :], target.at[top : top + r3, 0:block]
+            yield refs[0].at[s, off3 + r3 : off3 + r3 + n, 0:m], target.at[top : top + n, block : block + m]
+            yield refs[0].at[s, off3 + r3 : off3 + r3 + n, m : 2 * m], target.at[top + n : top + r3, block : block + m]
+
+    def whole(n):
+        def load(refs, target):
+            yield refs[n], target
+
+        return load
+
+    if aligned:
+        pieces = [gathered]
+        plan = [load_one, load_two, load_three]
+    else:
+        by_cols = lambda a: a.reshape(n_dp, 4, -1, block).transpose(0, 2, 1, 3).reshape(-1, hidden)
+        pieces = [by_cols(gathered[:, off1:]), by_cols(gathered[:, :off3]), unfold(gathered[:, off3:off1]).reshape(hidden, repr_width)]
+        plan = [whole(0), whole(1), whole(2)]
 
     small_ins = [part_q, rq, ry, h_q, mods_own, seg_q, fc2_b.astype(F32).reshape(1, width), go_q, feat_q, keep_q, b_one, b_two, b_three]
     h_low, grad_h, g_mlp, gate_two, s_one, s_two, gz, ga_two, ga_one, g_b1, g_b2, g_b3, g_fc2_b = call(
@@ -587,8 +590,8 @@
             shape_of((1, repr_width), F32),
             shape_of((1, width), F32),
         ],
-        [meta] + small_ins + pieces,
-        in_specs=[SMEM] + [VMEM] * len(small_ins) + [ANY] * len(pieces),
+        small_ins + pieces,
+        in_specs=[VMEM] * len(small_ins) + [ANY] * len(pieces),
         scratch=[
             pltpu.VMEM((width, hidden), BF16),
             pltpu.VMEM((hidden, hidden), BF16),
@@ -602,44 +605,38 @@
     )
     g_mlp_all = spread_quarter(g_mlp)
 
-    def wgrad_dp(a, b, step, name):
-        rows, cols = a.shape[1], b.shape[1]
+    def wgrad(place, jobs, ins, outs, name):
+        shapes = [(ins[a].shape[1], ins[b].shape[1]) for a, b, _ in jobs]
+        return call(
+            functools.partial(wgrad_kernel, place, jobs, len(outs)),
+            outs,
+            [meta] + ins,
+            in_specs=[SMEM] + [VMEM] * len(ins),
+            out_specs=[ANY] * len(outs),
+            scratch=[pltpu.VMEM(s, BF16) for s in shapes] + [pltpu.SemaphoreType.DMA((len(jobs),))],
+            flops=sum(2 * ins[a].shape[0] * r * n for (a, _, _), (r, n) in zip(jobs, shapes)),
+            name=name,
+        )
+
+    def wgrad_natural(jobs, ins, name):
+        outs = [shape_of((ins[a].shape[1], ins[b].shape[1]), BF16) for a, b, _ in jobs]
+        return wgrad(lambda n, g, outs_, meta_: [(g, outs_[n])], jobs, ins, outs, name)
+
+    def wgrad_dp(jobs, ins, name):
+        rows = ins[jobs[0][0]].shape[1]
+        widths = [ins[b].shape[1] for _, b, _ in jobs]
         depth = rows // n_dp
-        flops = 2 * a.shape[0] * rows * cols
-        scratch = [pltpu.VMEM((rows, cols), BF16), pltpu.SemaphoreType.DMA]
-        if depth % 16 == 0:
-
-            def place(g, outs, sem, meta_):
+        if depth % 16 == 0 and all(w % 128 == 0 for w in widths[:-1]):
+
+            def place(n, g, outs, meta_):
+                lo = sum(widths[:n])
                 for r in range(inner):
                     for zr in range(outer):
-                        at = position(meta_, r, 0, zr)
-                        pltpu.make_async_copy(g.at[pl.ds(pl.multiple_of(at * depth, 16), depth), :], outs[r].at[zr], sem).start()
-
-            return call(
-                functools.partial(wgrad_kernel, place, inner, step),
-                [shape_of((outer, depth, cols), BF16)] * inner,
-                [meta, a, b],
-                in_specs=[SMEM, VMEM, VMEM],
-                out_specs=[ANY] * inner,
-                scratch=scratch,
-                flops=flops,
-                name=name,
-            )
-
-        def place(g, outs, sem, meta_):
-            pltpu.make_async_copy(g, outs[0], sem).start()
-
-        (nat,) = call(
-            functools.partial(wgrad_kernel, place, 1, step),
-            [shape_of((rows, cols), BF16)],
-            [meta, a, b],
-            in_specs=[SMEM, VMEM, VMEM],
-            out_specs=[ANY],
-            scratch=scratch,
-            flops=flops,
-            name=name,
-        )
-        nat = nat.reshape(outer, inner, depth, cols)
+                        at = pl.multiple_of(position(meta_, r, 0, zr) * depth, 16)
+                        yield g.at[pl.ds(at, depth), :], outs[r].at[zr, :, lo : lo + widths[n]]
+
+            return wgrad(place, jobs, ins, [shape_of((outer, depth, sum(widths)), BF16)] * inner, name)
+        nat = jnp.concatenate(wgrad_natural(jobs, ins, name), axis=1).reshape(outer, inner, depth, sum(widths))
         rel = to_relative(to_relative(nat, i, inner, 1), o, outer, 0)
         return [rel[:, r] for r in range(inner)]
 
@@ -652,81 +649,87 @@
             out = out + from_outer(v[outer - r].astype(BF16), r).astype(F32)
         return out
 
-    def wgrad_all(a, b, by_cols, step, name):
-        rows, cols = a.shape[1], b.shape[1]
-        depth = rows // n_dp
-        rb, cb = (depth, cols // 4) if by_cols else (depth // 4, cols)
-        flops = 2 * a.shape[0] * rows * cols
-        scratch = [pltpu.VMEM((rows, cols), BF16), pltpu.SemaphoreType.DMA]
-        n_outs = 4
-        if rb % 16 == 0:
-
-            def place(g, outs, sem, meta_):
+    def relative_all(nat):
+        nat = nat.transpose((3, 2, 1, 0) + tuple(range(4, nat.ndim)))
+        return to_relative(to_relative(to_relative(to_relative(nat, c, 2, 0), y, 2, 1), i, inner, 2), o, outer, 3)
+
+    def wgrad_two():
+        jobs = [(0, 1, 256)]
+        ins = [s_one, ga_two]
+        shape = (2, inner, outer, k2, block)
+        if aligned:
+
+            def place(n, g, outs, meta_):
+                for cr in range(2):
+                    for yr in range(2):
+                        part = pl.multiple_of(quarter_of(meta_, yr, cr) * block, 128)
+                        for r in range(inner):
+                            for zr in range(outer):
+                                at = pl.multiple_of(position(meta_, r, 0, zr) * k2, 16)
+                                yield g.at[pl.ds(at, k2), pl.ds(part, block)], outs[cr].at[yr, r, zr]
+
+            return wgrad(place, jobs, ins, [shape_of(shape, BF16)] * 2, "grad_w2")
+        (nat,) = wgrad_natural(jobs, ins, "grad_w2")
+        rel = relative_all(nat.reshape(outer, inner, k2, 2, 2, block).transpose(0, 1, 3, 4, 2, 5))
+        return rel[0], rel[1]
+
+    def wgrad_others():
+        jobs = [(0, 1, 512), (2, 3, 384)]
+        ins = [s_two, gz, h_low, ga_one]
+        shape = (2, inner, outer, folds + k1, block)
+        if aligned:
+            half3, half_block = r3 // 2, block // 2
+
+            def place(n, g, outs, meta_):
                 for cr in range(2):
                     for yr in range(2):
                         for r in range(inner):
                             for zr in range(outer):
+                                part = quarter_of(meta_, yr, cr)
                                 at = position(meta_, r, 0, zr)
-                                part = quarter_of(meta_, yr, cr)
-                                if by_cols:
-                                    source = g.at[pl.ds(pl.multiple_of(at * depth, 16), rb), pl.ds(pl.multiple_of(part * cb, 128), cb)]
-                                else:
-                                    source = g.at[pl.ds(pl.multiple_of(at * depth + part * rb, 16), rb), :]
-                                pltpu.make_async_copy(source, outs[2 * cr + yr].at[r, zr], sem).start()
-
-            keep_q_, keep_y_, send_q_, send_y_ = call(
-                functools.partial(wgrad_kernel, place, n_outs, step),
-                [shape_of((inner, outer, rb, cb), BF16)] * n_outs,
-                [meta, a, b],
-                in_specs=[SMEM, VMEM, VMEM],
-                out_specs=[ANY] * n_outs,
-                scratch=scratch,
-                flops=flops,
-                name=name,
-            )
-            return keep_q_, keep_y_, send_q_, send_y_
-
-        def place(g, outs, sem, meta_):
-            pltpu.make_async_copy(g, outs[0], sem).start()
-
-        (nat,) = call(
-            functools.partial(wgrad_kernel, place, 1, step),
-            [shape_of((rows, cols), BF16)],
-            [meta, a, b],
-            in_specs=[SMEM, VMEM, VMEM],
-            out_specs=[ANY],
-            scratch=scratch,
-            flops=flops,
-            name=name,
-        )
-        if by_cols:
-            nat = nat.reshape(outer, inner, rb, 2, 2, cb).transpose(4, 3, 1, 0, 2, 5)
-        else:
-            nat = nat.reshape(outer, inner, 2, 2, rb, cb).transpose(3, 2, 1, 0, 4, 5)
-        rel = to_relative(to_relative(to_relative(to_relative(nat, c, 2, 0), y, 2, 1), i, inner, 2), o, outer, 3)
-        return rel[0, 0], rel[0, 1], rel[1, 0], rel[1, 1]
+                                to = outs[cr].at[yr, r, zr]
+                                if n == 1:
+                                    col = pl.ds(pl.multiple_of(part * block, 128), block)
+                                    yield g.at[pl.ds(pl.multiple_of(at * k1, 16), k1), col], to.at[folds : folds + k1, :]
+                                    continue
+                                top = pl.multiple_of(at * k3 + part * r3, 16)
+                                yield g.at[pl.ds(top, r3), 0:block], to.at[0:r3, :]
+                                yield g.at[pl.ds(top, half3), block : block + half_block], to.at[r3 : r3 + half3, 0:half_block]
+                                low = pl.multiple_of(at * k3 + part * r3 + half3, 16)
+                                yield g.at[pl.ds(low, half3), block : block + half_block], to.at[r3 : r3 + half3, half_block:block]
+
+            return wgrad(place, jobs, ins, [shape_of(shape, BF16)] * 2, "grad_w13")
+        three, one = wgrad_natural(jobs, ins, "grad_w13")
+        left, right = three[:, :block].reshape(n_all, r3, block), three[:, block:].reshape(n_all, 2, r3 // 2, block // 2)
+        low = jnp.concatenate([right[:, 0], right[:, 1]], axis=-1)
+        three = jnp.concatenate([left, low], axis=1).reshape(outer, inner, 2, 2, folds, block)
+        one = one.reshape(outer, inner, k1, 2, 2, block).transpose(0, 1, 3, 4, 2, 5)
+        rel = relative_all(jnp.concatenate([three, one], axis=4))
+        return rel[0], rel[1]
 
     def reduce_all(parts):
-        keep_q_, keep_y_, send_q_, send_y_ = parts
-        ry_ = swap_core(send_y_)
-        rq_ = swap_core(send_q_)
-        passed = swap_y((keep_y_.astype(F32) + ry_.astype(F32)).astype(BF16))
-        total = keep_q_.astype(F32) + rq_.astype(F32) + passed.astype(F32)
-        rest = [total[0]] + [total[r].astype(BF16) for r in range(1, inner)]
-        return reduce_dp(rest)
-
-    def spread_tensor(block, by_cols):
-        block = block.astype(BF16)
-        axis = 1 if by_cols else 0
-        other = swap_y(block)
-        c0, c1 = swap_core(block), swap_core(other)
-        own = pair([block, c0], c, axis)
-        peer = pair([other, c1], c, axis)
-        return pair([own, peer], y, axis).astype(F32)
-
-    g_w3 = spread_tensor(reduce_all(wgrad_all(s_two, gz, False, 512, "grad_w3")), False)
-    g_w2 = spread_tensor(reduce_all(wgrad_all(s_one, ga_two, True, 256, "grad_w2")), True)
-    g_w1 = spread_tensor(reduce_all(wgrad_all(h_low, ga_one, True, 384, "grad_w1")), True)
+        keep, send = parts
+        got = swap_core(send)
+        passed = swap_y((keep[1].astype(F32) + got[1].astype(F32)).astype(BF16))
+        total = keep[0].astype(F32) + got[0].astype(F32) + passed.astype(F32)
+        return reduce_dp([total[0]] + [total[r].astype(BF16) for r in range(1, inner)])
+
+    def quarters(mine):
+        mine = mine.astype(BF16)
+        other = swap_y(mine)
+        c0, c1 = swap_core(mine), swap_core(other)
+        own = pair([mine[None], c0[None]], c, 0)
+        peer = pair([other[None], c1[None]], c, 0)
+        return pair([own, peer], y, 0)
+
+    def side_by_side(q):
+        return jnp.concatenate([q[n] for n in range(4)], axis=1).astype(F32)
+
+    q2 = quarters(reduce_all(wgrad_two()))
+    g_w2 = side_by_side(q2)
+    q13 = quarters(reduce_all(wgrad_others()))
+    g_w1 = side_by_side(q13[:, folds:])
+    g_w3 = unfold(q13[:, :folds]).reshape(k3, repr_width).astype(F32)
 
     g_mlp_full, gpre, part_q, part_y, send_q, send_y, g_fc1_b = call(
         mlp_back_kernel,
@@ -743,13 +746,13 @@
         name="second_back",
     )
     g_attn_all = spread_quarter(g_attn)
-    g_fc2_t = reduce_dp(wgrad_dp(g_mlp_full, act, 384, "grad_fc2"))
-    g_fc1 = reduce_dp(wgrad_dp(m_full, gpre, 384, "grad_fc1"))
+    g_fc = reduce_dp(wgrad_dp([(0, 1, 384), (2, 3, 384)], [g_mlp_full, act, m_full, gpre], "grad_fc"))
+    g_fc2_t, g_fc1 = g_fc[:, :ff], g_fc[:, ff:]
 
     gqkv, part_q, part_y, send_q, send_y, g_qv_b, g_attn_full = call(
         functools.partial(bwd_kernel, heads),
         [shape_of((T, 3 * wide), BF16)] + quarter + [shape_of((2, wide), F32), shape_of((T, width), BF16)],
-        list(g_attn_all) + [out_w, q, k, v, seg_cols, seg_rows, val_rows, qkv_w],
+        list(g_attn_all) + [out_w, q, k, v, seg_cols, seg_rows, val_rows, qkv_t],
         flops=8 * T * width * wide + 10 * T * seq * wide,
         name="attention_back",
     )
@@ -761,11 +764,16 @@
         in_specs=[SMEM] + [VMEM] * 7,
         name="first_back",
     )
-    g_qkv = reduce_dp(wgrad_dp(m_one, gqkv, 384, "grad_qkv"))
-    g_out_t = reduce_dp(wgrad_dp(g_attn_full, mixed, 384, "grad_out"))
+    g_heads = reduce_dp(wgrad_dp([(0, 1, 384)], [m_one, gqkv], "grad_qkv"))
+    g_qkv = g_heads
+    g_out_t = reduce_dp(wgrad_dp([(0, 1, 384)], [g_attn_full, mixed], "grad_out"))
 
     g_mod = jnp.concatenate([shift_one, scale_one, gate_one, shift_two, scale_two, gate_two], axis=-1)
-    g_mod = (g_mod + swap_y(g_mod)).astype(BF16)
+    early = jnp.concatenate([g_b1, g_b2, g_b3, g_fc2_b, g_out_b], axis=1)
+    early = early + swap_core(early)
+    both = jnp.concatenate([g_mod.reshape(1, -1), early], axis=1)
+    both = both + swap_y(both)
+    g_mod, early = both[:, : slots * 6 * width].reshape(slots, -1).astype(BF16), both[:, slots * 6 * width :]
     g_mod = exchange_dp(g_mod.reshape(slots, n_dp, -1).transpose(1, 0, 2))
     g_mod = pair([g_mod, swap_core(g_mod)], c, 1).reshape(n_dp * images, -1)
     g_ada_w = lax.dot_general(g_mod, cond_act, (((0,), (1,)), ((), ())), preferred_element_type=F32)
@@ -791,24 +799,16 @@
             step *= 2
         return x
 
-    early = jnp.concatenate([g_b1, g_b2, g_b3, g_fc2_b], axis=1)
-    early = early + swap_core(early)
-    early = early + swap_y(early)
-    early = total_dp(early)
-    late_own = g_out_b + swap_core(g_out_b)
-    late_own = late_own + swap_y(late_own)
-    late = total_dp(jnp.concatenate([g_fc1_b, late_own, g_qv_b.reshape(1, 2 * wide)], axis=1))
+    sums = total_dp(jnp.concatenate([early, g_fc1_b, g_qv_b.reshape(1, 2 * wide)], axis=1)).reshape(-1)
+    cuts = [hidden, hidden, repr_width, width, width, ff, 2 * wide]
+    marks = [sum(cuts[:n]) for n in range(len(cuts) + 1)]
+    s_one_b, s_two_b, s_three_b, s_fc2_b, s_out_b, s_fc1_b, s_qv_b = (sums[lo:hi] for lo, hi in zip(marks, marks[1:]))
 
     def my_part(x, n):
         return lax.dynamic_slice_in_dim(x.reshape(-1), d * n, n)
 
-    s_b1 = my_part(early[:, :hidden], n1)
-    s_b2 = my_part(early[:, hidden : 2 * hidden], n2)
-    s_b3 = my_part(early[:, 2 * hidden : 2 * hidden + repr_width], repa_b3.shape[0])
-    s_fc2_b = early[0, 2 * hidden + repr_width :]
-    s_fc1_b = late[0, :ff]
-    s_out_b = late[0, ff : ff + width]
-    s_qv_b = late[0, ff + width :].reshape(2, wide)
+    s_b1, s_b2, s_b3 = my_part(s_one_b, n1), my_part(s_two_b, n2), my_part(s_three_b, n3)
+    s_qv_b = s_qv_b.reshape(2, wide)
 
     def spread_tokens(block):
         other = swap_y(block)

time: 686 us -> 509 us (0.74)
  waiting for transfers between devices: 334 us -> 241 us
  starting transfers between devices: 140 us -> 79.7 us
  other arithmetic: 48 us -> 32.7 us
  between operations: 2.53 us -> 15.4 us
  local copies, waits for them, and re-layouts: 43.5 us -> 34.8 us
    ppermute x25 -> x15, waiting for transfers between devices: 138 us -> 84.2 us  [swap_y(): return lax.ppermute(x, 'tensor', [(0, 2), (2, 0), (1, 3), (3, 1)])]
    ppermute x6 -> x3, waiting for transfers between devices: 38.3 us -> 3.12 us  [total_dp(): x = x + lax.ppermute(x, 'dp', [(k_, k_ ^ step) for k_ in range(n_dp)])]
    ppermute x48 -> x30, waiting for transfers between devices: 115 us -> 83.5 us  [from_outer(): lax.ppermute(x, 'dp', [((k + r) % outer * inner + j, k * inner + j) for k...]
    ppermute x48 -> x30, starting transfers between devices: 76 us -> 46.7 us  [from_outer(): lax.ppermute(x, 'dp', [((k + r) % outer * inner + j, k * inner + j) for k...]
    ppermute x25 -> x15, starting transfers between devices: 32.7 us -> 13.7 us  [swap_y(): return lax.ppermute(x, 'tensor', [(0, 2), (2, 0), (1, 3), (3, 1)])]
    all_gather x0 -> x1, waiting for transfers between devices: none -> 14.4 us  [body(): gathered = lax.all_gather(packed, ('dp', 'tensor'), axis=0)]
    ppermute x16 -> x10, waiting for transfers between devices: 37.4 us -> 48.5 us  [from_inner(): lax.ppermute(x, 'dp', [(k * inner + (j + r) % inner, k * inner + j) for k...]
    pallas_call x15 -> x13, Pallas kernels: 101 us -> 95 us  [call(): pl.pallas_call(kernel, out_shape=tuple(outs), in_specs=in_specs or [VMEM]...]
  transfers between devices with their start and end apart: 140 -> 85, of which waited for: 52 -> 42; matrix products, arithmetic and copies ran while one was open for 13% -> 12% of each run, Pallas kernels for 13% -> 16%
where the time goes in v2:
time: 509 us; the launch traced here: 504 us
  waiting for transfers between devices  241 us (47%)
  Pallas kernels  95 us (19%)
  starting transfers between devices  79.7 us (16%)
  local copies, waits for them, and re-layouts  34.8 us (7%)
  other arithmetic  32.7 us (6%)
  between operations  15.4 us (3%)
  matrix products  6.22 us (1%)
    pallas_call x13, Pallas kernels, call(): pl.pallas_call(kernel, out_shape=tuple(outs), in_specs=in_specs or [VMEM]...  95 us
    ppermute x15, waiting for transfers between devices, swap_y(): return lax.ppermute(x, 'tensor', [(0, 2), (2, 0), (1, 3), (3, 1)])  84.2 us
    ppermute x30, waiting for transfers between devices, from_outer(): lax.ppermute(x, 'dp', [((k + r) % outer * inner + j, k * inner + j) for k...  83.5 us
    ppermute x10, waiting for transfers between devices, from_inner(): lax.ppermute(x, 'dp', [(k * inner + (j + r) % inner, k * inner + j) for k...  48.5 us
    ppermute x30, starting transfers between devices, from_outer(): lax.ppermute(x, 'dp', [((k + r) % outer * inner + j, k * inner + j) for k...  46.7 us
    ppermute x10, starting transfers between devices, from_inner(): lax.ppermute(x, 'dp', [(k * inner + (j + r) % inner, k * inner + j) for k...  14.6 us
    all_gather x1, waiting for transfers between devices, body(): gathered = lax.all_gather(packed, ('dp', 'tensor'), axis=0)  14.4 us
    ppermute x15, starting transfers between devices, swap_y(): return lax.ppermute(x, 'tensor', [(0, 2), (2, 0), (1, 3), (3, 1)])  13.7 us
  transfers between devices with their start and end apart: 85, of which 42 were waited for; matrix products, arithmetic and copies ran while one was open for 12% of the time, Pallas kernels for 16%

profile of v2, /device:TPU:0, one launch (start us, length us, event | category | flops | bytes accessed | tf_op | source)
XLA Modules:
  0.0 504.5 jit_solution(15345111083529751525)
XLA Ops:
  11.9 3.0 collective-permute-start.16
  26.8 3.1 collective-permute-done.3
  37.5 8.2 %collective-permute-done.6 = bf16[2,154,64]{1,2,0:T(8,128)(2,1)S(1)} collective-permute-done((bf16[2,154,64]{1,2,0:T(8,128)(2,1)S(1)}, bf16[2,154,64]{1,2,0:T(8,128)(2,1)S(1)}, u32[]{:S(2)}, u32[]{:S(2)}) %collective-permute-start.6) | collective-permute-done | bytes 39456 | tf_op jit(solution)/shard_map/ppermute | solution.py:365
  48.9 4.3 collective-permute-done.8
  54.0 3.4 collective-permute-start.9
  60.8 2.8 collective-permute-done.10
  64.8 9.8 %attention.1 = (bf16[512,1152]{1,0:T(8,128)(2,1)}, bf16[512,288]{1,0:T(8,128)(2,1)}, bf16[512,288]{1,0:T(8,128)(2,1)}, bf16[512,288]{1,0:T(8,128)(2,1)}, bf16[512,288]{1,0:T(8,128)(2,1)}) custom-call(s32[4]{0:T(128)} %pad_add_fusion.3.order_.order, bf16[4,128,1152]{2,1,0:T(8,128)(2,1)} %bitcast.326, f32[4,6912]{1,0:T(4,128)} %get-tuple-element.277.a.mods.refs_4_, ...), custom_call_target="tpu_custom_call" | custom-call | flops 1170210816 | bytes 5759248 | tf_op jit(solution)/shard_map/attention/pallas_call | solution.py:29
  78.9 5.1 %collective-permute-done.13.m2 = bf16[256,288]{1,0:T(8,128)(2,1)S(1)} collective-permute-done((bf16[256,288]{1,0:T(8,128)(2,1)S(1)}, bf16[256,288]{1,0:T(8,128)(2,1)S(1)}, u32[]{:S(2)}, u32[]{:S(2)}) %collective-permute-start.13) | collective-permute-done | bytes 147488 | tf_op jit(solution)/shard_map/ppermute | solution.py:368
  84.0 3.9 collective-permute-done.14.m3
  89.4 5.8 %middle.1 = (f32[128,1152]{1,0:T(8,128)}, f32[128,1152]{1,0:T(8,128)}, bf16[256,1152]{1,0:T(8,128)(2,1)}) custom-call(s32[4]{0:T(128)} %pad_add_fusion.3.order_.order, bf16[4,128,1152]{2,1,0:T(8,128)(2,1)} %bitcast.327, f32[4,6912]{1,0:T(4,128)} %get-tuple-element.277.a.mods.refs_4_, s32[512,1]{1,0:T(8,128)} %copy.82.rest_0_.segc, ...), custom_call_target="tpu_custom_call" | custom-call | flops 679477248 | bytes 6310416 | tf_op jit(solution)/shard_map/middle/pallas_call | solution.py:29
  100.3 8.4 %mlp.1 = (bf16[512,1152]{1,0:T(8,128)(2,1)}, f32[512,1152]{1,0:T(8,128)}, bf16[512,1152]{1,0:T(8,128)(2,1)}, f32[128,1152]{1,0:T(8,128)}, f32[128,1152]{1,0:T(8,...) custom-call(bf16[256,1152]{1,0:T(8,128)(2,1)} %get-tuple-element.81.m_own, bf16[256,1152]{1,0:T(8,128)(2,1)} %copy-done.45, ...), custom_call_target="tpu_custom_call" | custom-call | flops 2717908992 | bytes 12980736 | tf_op jit(solution)/shard_map/mlp/pallas_call | solution.py:29
  115.5 7.4 %collective-permute-done.21.refs_2_ = bf16[128,1152]{1,0:T(8,128)(2,1)S(1)} collective-permute-done((bf16[128,1152]{1,0:T(8,128)(2,1)S(1)}, bf16[128,1152]{1,0:T(8,128)(2,1)S(1)}, u32[]{:S(2)}, u32[]{:S(2)}) %collective-permute-start.21) | collective-permute-done | bytes 294944 | tf_op jit(solution)/shard_map/ppermute | solution.py:368
  123.0 14.4 %all-gather.3.cloned.1.call-done = bf16[15872,512]{1,0:T(8,128)(2,1)} async-done(((bf16[496,512]{1,0:T(8,128)(2,1)}), bf16[15872,512]{1,0:T(8,128)(2,1)}) %all-gather.3.cloned.1.call-update) | async-done | bytes 16252944 | tf_op jit(solution)/shard_map/all_gather | solution.py:422
  137.4 15.4 %projector.1 = (bf16[128,1152]{1,0:T(8,128)(2,1)}, f32[128,1152]{1,0:T(8,128)}, bf16[128,1152]{1,0:T(8,128)(2,1)}, f32[4,1152]{1,0:T(4,128)}, bf16[128,2048]{1,0...) custom-call(f32[128,1152]{1,0:T(8,128)} %get-tuple-element.82.refs_0, ...), custom_call_target="tpu_custom_call" | custom-call | flops 4160749568 | bytes 22165504 | tf_op jit(solution)/shard_map/projector/pallas_call | solution.py:29
  155.1 5.9 %grad_w13.1 = (bf16[2,2,4,240,512]{4,3,2,1,0:T(8,128)(2,1)}, bf16[2,2,4,240,512]{4,3,2,1,0:T(8,128)(2,1)}) custom-call(s32[4]{0:T(128)} %pad_add_fusion.5.refs_0_, bf16[128,2048]{1,0:T(8,128)(2,1)} %get-tuple-element.132.refs_1_, bf16[128,768]{1,0:T(8,128)(2,1)} %get-tuple-element.133.refs_2_, bf16[128,1152]{1,0:T(8,128)(2,1)} %get-tuple-element.87.refs_3_, ...), custom_call_target="tpu_custom_call" | custom-call | flops 1006632960 | bytes 9404432 | tf_op jit(solution)/shard_map/grad_w13/pallas_call | solution.py:29
  163.2 5.1 %collective-permute-done.27.g3 = bf16[128,1152]{1,0:T(8,128)(2,1)S(1)} collective-permute-done((bf16[128,1152]{1,0:T(8,128)(2,1)S(1)}, bf16[128,1152]{1,0:T(8,128)(2,1)S(1)}, u32[]{:S(2)}, u32[]{:S(2)}) %collective-permute-start.27) | collective-permute-done | bytes 294944 | tf_op jit(solution)/shard_map/ppermute | solution.py:371
  169.0 9.0 %mlp_back.1 = (bf16[512,1152]{1,0:T(8,128)(2,1)}, bf16[512,1152]{1,0:T(8,128)(2,1)}, f32[128,1152]{1,0:T(8,128)}, f32[128,1152]{1,0:T(8,128)}, bf16[128,1152]{1,...) custom-call(bf16[128,1152]{1,0:T(8,128)(2,1)} %get-tuple-element.88.g0, bf16[128,1152]{1,0:T(8,128)(2,1)} %copy-done.49, ...), custom_call_target="tpu_custom_call" | custom-call | flops 2717908992 | bytes 12980736 | tf_op jit(solution)/shard_map/mlp_back/pallas_call | solution.py:29
  178.3 7.0 %grad_w2.1 = (bf16[2,2,4,256,512]{4,3,2,1,0:T(8,128)(2,1)}, bf16[2,2,4,256,512]{4,3,2,1,0:T(8,128)(2,1)}) custom-call(s32[4]{0:T(128)} %pad_add_fusion.5.refs_0_, bf16[128,2048]{1,0:T(8,128)(2,1)} %get-tuple-element.137.refs_1_, bf16[128,2048]{1,0:T(8,128)(2,1)} %get-tuple-element.138.refs_2_), custom_call_target="tpu_custom_call" | custom-call | flops 1073741824 | bytes 9437200 | tf_op jit(solution)/shard_map/grad_w2/pallas_call | solution.py:29
  187.7 7.6 %collective-permute-done.30.ry = bf16[128,1152]{1,0:T(8,128)(2,1)S(1)} collective-permute-done((bf16[128,1152]{1,0:T(8,128)(2,1)S(1)}, bf16[128,1152]{1,0:T(8,128)(2,1)S(1)}, u32[]{:S(2)}, u32[]{:S(2)}) %collective-permute-start.30) | collective-permute-done | bytes 294944 | tf_op jit(solution)/shard_map/ppermute | solution.py:368
  196.0 4.2 second_back.1
  201.3 7.5 %collective-permute-done.31.g1 = bf16[128,1152]{1,0:T(8,128)(2,1)S(1)} collective-permute-done((bf16[128,1152]{1,0:T(8,128)(2,1)}, bf16[128,1152]{1,0:T(8,128)(2,1)S(1)}, u32[]{:S(2)}, u32[]{:S(2)}) %collective-permute-start.31) | collective-permute-done | bytes 294944 | tf_op jit(solution)/shard_map/ppermute | solution.py:368
  211.1 11.4 %attention_back.1 = (bf16[512,864]{1,0:T(8,128)(2,1)}, f32[128,1152]{1,0:T(8,128)}, f32[128,1152]{1,0:T(8,128)}, bf16[128,1152]{1,0:T(8,128)(2,1)}, bf16[128,115...) custom-call(bf16[128,1152]{1,0:T(8,128)(2,1)} %get-tuple-element.96.g0, bf16[128,1152]{1,0:T(8,128)(2,1)} %copy-done.47, ...), custom_call_target="tpu_custom_call" | custom-call | flops 1736441856 | bytes 8560896 | tf_op jit(solution)/shard_map/attention_back/pallas_call | solution.py:29
  223.1 7.2 %grad_fc.1 = (bf16[4,144,2304]{2,1,0:T(8,128)(2,1)}, bf16[4,144,2304]{2,1,0:T(8,128)(2,1)}) custom-call(s32[4]{0:T(128)} %pad_add_fusion.5.refs_0_, bf16[512,1152]{1,0:T(8,128)(2,1)} %get-tuple-element.126.refs_1_, bf16[512,1152]{1,0:T(8,128)(2,1)} %get-tuple-element.127.refs_2_, bf16[512,1152]{1,0:T(8,128)(2,1)} %get-tuple-element.128.refs_3_, ...), custom_call_target="tpu_custom_call" | custom-call | flops 2717908992 | bytes 10027024 | tf_op jit(solution)/shard_map/grad_fc/pallas_call | solution.py:29
  230.7 3.1 grad_out.1
  233.8 2.9 collective-permute-start.58
  237.8 4.3 grad_qkv.1
  242.2 5.4 %collective-permute-done.58 = bf16[4,144,288]{2,1,0:T(8,128)(2,1)} collective-permute-done((bf16[4,144,288]{2,1,0:T(8,128)(2,1)}, bf16[4,144,288]{2,1,0:T(8,128)(2,1)}, u32[]{:S(2)}, u32[]{:S(2)}) %collective-permute-start.58) | collective-permute-done | bytes 331808 | tf_op jit(solution)/shard_map/ppermute | solution.py:362
  248.8 3.7 first_back.1
  255.4 4.2 collective-permute-done.41
  266.7 2.7 collective-permute-start.43
  274.1 4.8 collective-permute-done.59
  281.0 3.1 collective-permute-done.56
  292.6 6.3 %collective-permute-done.37 = bf16[128,1152]{1,0:T(8,128)(2,1)S(1)} collective-permute-done((bf16[128,1152]{1,0:T(8,128)(2,1)S(1)}, bf16[128,1152]{1,0:T(8,128)(2,1)S(1)}, u32[]{:S(2)}, u32[]{:S(2)}) %collective-permute-start.37) | collective-permute-done | bytes 294944 | tf_op jit(solution)/shard_map/ppermute | solution.py:368
  299.7 7.1 %collective-permute-done.47 = f32[4,144,64]{1,2,0:T(8,128)S(1)} collective-permute-done((f32[4,144,64]{1,2,0:T(8,128)S(1)}, f32[4,144,64]{1,2,0:T(8,128)S(1)}, u32[]{:S(2)}, u32[]{:S(2)}) %collective-permute-start.47) | collective-permute-done | bytes 147488 | tf_op jit(solution)/shard_map/ppermute | solution.py:362
  311.2 3.6 collective-permute-done.50
  314.9 5.1 %collective-permute-done.49 = f32[144,64]{0,1:T(8,128)S(1)} collective-permute-done((f32[144,64]{0,1:T(8,128)S(1)}, f32[144,64]{0,1:T(8,128)S(1)}, u32[]{:S(2)}, u32[]{:S(2)}) %collective-permute-start.49) | collective-permute-done | bytes 36896 | tf_op jit(solution)/shard_map/ppermute | solution.py:365
  329.5 4.8 collective-permute-done.52
  335.8 7.5 %collective-permute-done.53 = bf16[144,864]{1,0:T(8,128)(2,1)S(1)} collective-permute-done((bf16[144,864]{1,0:T(8,128)(2,1)S(1)}, bf16[144,864]{1,0:T(8,128)(2,1)S(1)}, u32[]{:S(2)}, u32[]{:S(2)}) %collective-permute-start.53) | collective-permute-done | bytes 248864 | tf_op jit(solution)/shard_map/ppermute | solution.py:365
  349.5 25.9 %collective-permute-done.62 = bf16[4,144,2304]{2,1,0:T(8,128)(2,1)S(1)} collective-permute-done((bf16[4,144,2304]{2,1,0:T(8,128)(2,1)S(1)}, bf16[4,144,2304]{2,1,0:T(8,128)(2,1)S(1)}, u32[]{:S(2)}, u32[]{:S(2)}) %collective-permute-start.62) | collective-permute-done | bytes 2654240 | tf_op jit(solution)/shard_map/ppermute | solution.py:362
  376.2 3.9 collective-permute-done.67
  386.1 30.3 %collective-permute-done.76 = bf16[2,4,256,512]{3,2,1,0:T(8,128)(2,1)S(1)} collective-permute-done((bf16[2,4,256,512]{3,2,1,0:T(8,128)(2,1)S(1)}, bf16[2,4,256,512]{3,2,1,0:T(8,128)(2,1)S(1)}, u32[]{:S(2)}, u32[]{:S(2)}) %collective-permute-start.76) | collective-permute-done | bytes 2097184 | tf_op jit(solution)/shard_map/ppermute | solution.py:368
  420.7 3.6 collective-permute-start.69
  424.3 13.7 %collective-permute-start.71 = (bf16[240,512]{1,0:T(8,128)(2,1)S(1)}, bf16[240,512]{1,0:T(8,128)(2,1)S(1)}, u32[]{:S(2)}, u32[]{:S(2)}) collective-permute-start(bf16[240,512]{1,0:T(8,128)(2,1)S(1)} %get-tuple-element.229), channel_id=1, source_target_pairs={{24,0},{28,4},{0,8},{4,12},{8,16},{12,20},{16,24},{20,28},{25,1},{... | collective-permute-start | bytes 737288 | tf_op jit(solution)/shard_map/ppermute | solution.py:365
  438.1 15.0 %collective-permute-done.64 = bf16[144,2304]{1,0:T(8,128)(2,1)S(1)} collective-permute-done((bf16[144,2304]{1,0:T(8,128)(2,1)S(1)}, bf16[144,2304]{1,0:T(8,128)(2,1)S(1)}, u32[]{:S(2)}, u32[]{:S(2)}) %collective-permute-start.64) | collective-permute-done | bytes 663584 | tf_op jit(solution)/shard_map/ppermute | solution.py:365
  453.4 5.0 collective-permute-done.70
  464.9 11.5 %collective-permute-done.78 = bf16[256,512]{1,0:T(8,128)(2,1)S(1)} collective-permute-done((bf16[256,512]{1,0:T(8,128)(2,1)S(1)}, bf16[256,512]{1,0:T(8,128)(2,1)S(1)}, u32[]{:S(2)}, u32[]{:S(2)}) %collective-permute-start.78) | collective-permute-done | bytes 262176 | tf_op jit(solution)/shard_map/ppermute | solution.py:365
  476.4 8.9 %collective-permute-done.79 = bf16[256,512]{1,0:T(8,128)(2,1)S(1)} collective-permute-done((bf16[256,512]{1,0:T(8,128)(2,1)S(1)}, bf16[256,512]{1,0:T(8,128)(2,1)S(1)}, u32[]{:S(2)}, u32[]{:S(2)}) %collective-permute-start.79) | collective-permute-done | bytes 262176 | tf_op jit(solution)/shard_map/ppermute | solution.py:365
  487.4 6.0 %collective-permute-done.82 = bf16[256,512]{1,0:T(8,128)(2,1)S(1)} collective-permute-done((bf16[256,512]{1,0:T(8,128)(2,1)S(1)}, bf16[256,512]{1,0:T(8,128)(2,1)S(1)}, u32[]{:S(2)}, u32[]{:S(2)}) %collective-permute-start.82) | collective-permute-done | bytes 262176 | tf_op jit(solution)/shard_map/ppermute | solution.py:368
  (411 shorter events, 136.8 us)
Async XLA Ops:
  7.3 130.1 %all-gather.3.cloned.1.call-start = ((), (), s32[]{:S(2)}) async-start(), calls=%async_computation | async-start | bytes 16760832 | tf_op jit(solution)/shard_map/all_gather | solution.py:422
  11.9 52.1 %collective-permute-start.16 = (bf16[288,1152]{1,0:T(8,128)(2,1)}, bf16[288,1152]{1,0:T(8,128)(2,1)}, u32[]{:S(2)}, u32[]{:S(2)}) collective-permute-start(bf16[288,1152]{1,0:T(8,128)(2,1)} %out_w.1), channel_id=1, source_target_pairs={{0,2},{2,0},{1,3},{3,1},{4,6},{6,4},{5,7},{7,5},{8,10},{10,8},{9,1... | collective-permute-start | bytes 1990664 | tf_op jit(solution)/shard_map/ppermute | solution.py:368
  14.9 73.0 %collective-permute-start.15 = (bf16[288,1152]{1,0:T(8,128)(2,1)}, bf16[288,1152]{1,0:T(8,128)(2,1)}, u32[]{:S(2)}, u32[]{:S(2)}) collective-permute-start(bf16[288,1152]{1,0:T(8,128)(2,1)} %out_w.1), channel_id=1, source_target_pairs={{0,1},{1,0},{2,3},{3,2},{4,5},{5,4},{6,7},{7,6},{8,9},{9,8},{10,11... | collective-permute-start | bytes 1990664 | tf_op jit(solution)/shard_map/ppermute | solution.py:371
  35.3 10.4 %collective-permute-start.6 = (bf16[2,154,64]{1,2,0:T(8,128)(2,1)S(1)}, bf16[2,154,64]{1,2,0:T(8,128)(2,1)S(1)}, u32[]{:S(2)}, u32[]{:S(2)}) collective-permute-start(bf16[2,154,64]{1,2,0:T(8,128)(2,1)S(1)} %get-tuple-element.280), channel_id=1, source_target_pairs={{16,0},{20,4},{24,8},{28,12},{0,16},{4,20},{8,24},{12,28},{17,1},{... | collective-permute-start | bytes 118280 | tf_op jit(solution)/shard_map/ppermute | solution.py:365
  35.3 10.3 %collective-permute-start.5 = (bf16[2,154,64]{1,2,0:T(8,128)(2,1)S(1)}, bf16[2,154,64]{1,2,0:T(8,128)(2,1)S(1)}, u32[]{:S(2)}, u32[]{:S(2)}) collective-permute-start(bf16[2,154,64]{1,2,0:T(8,128)(2,1)S(1)} %get-tuple-element.280), channel_id=1, source_target_pairs={{8,0},{12,4},{16,8},{20,12},{24,16},{28,20},{0,24},{4,28},{9,1},{1... | collective-permute-start | bytes 118280 | tf_op jit(solution)/shard_map/ppermute | solution.py:365
  36.6 9.1 %collective-permute-start.7 = (bf16[2,154,64]{1,2,0:T(8,128)(2,1)S(1)}, bf16[2,154,64]{1,2,0:T(8,128)(2,1)S(1)}, u32[]{:S(2)}, u32[]{:S(2)}) collective-permute-start(bf16[2,154,64]{1,2,0:T(8,128)(2,1)S(1)} %get-tuple-element.280), channel_id=1, source_target_pairs={{24,0},{28,4},{0,8},{4,12},{8,16},{12,20},{16,24},{20,28},{25,1},{... | collective-permute-start | bytes 118280 | tf_op jit(solution)/shard_map/ppermute | solution.py:365
  53.7 9.9 %collective-permute-start.10 = (f32[2,8,864]{2,1,0:T(8,128)S(1)}, f32[2,8,864]{2,1,0:T(8,128)S(1)}, u32[]{:S(2)}, u32[]{:S(2)}) collective-permute-start(f32[2,8,864]{2,1,0:T(8,128)S(1)} %get-tuple-element.271), channel_id=1, source_target_pairs={{16,0},{20,4},{24,8},{28,12},{0,16},{4,20},{8,24},{12,28},{17,1},{... | collective-permute-start | bytes 165896 | tf_op jit(solution)/shard_map/ppermute | solution.py:365
  54.0 9.7 %collective-permute-start.9 = (f32[2,8,864]{2,1,0:T(8,128)S(1)}, f32[2,8,864]{2,1,0:T(8,128)S(1)}, u32[]{:S(2)}, u32[]{:S(2)}) collective-permute-start(f32[2,8,864]{2,1,0:T(8,128)S(1)} %get-tuple-element.272), channel_id=1, source_target_pairs={{8,0},{12,4},{16,8},{20,12},{24,16},{28,20},{0,24},{4,28},{9,1},{1... | collective-permute-start | bytes 165896 | tf_op jit(solution)/shard_map/ppermute | solution.py:365
  64.0 23.9 %collective-permute-start.17 = (bf16[288,1152]{1,0:T(8,128)(2,1)}, bf16[288,1152]{1,0:T(8,128)(2,1)S(1)}, u32[]{:S(2)}, u32[]{:S(2)}) collective-permute-start(bf16[288,1152]{1,0:T(8,128)(2,1)} %collective-permute-done.16.w2), channel_id=1, source_target_pairs={{0,1},{1,0},{2,3},{3,2},{4,5},{5,4},{6,7},{7,6},{8,9},{9,8},{10,11... | collective-permute-start | bytes 1990664 | tf_op jit(solution)/shard_map/ppermute | solution.py:371
  77.3 10.6 %collective-permute-start.14 = (bf16[256,288]{1,0:T(8,128)(2,1)S(1)}, bf16[256,288]{1,0:T(8,128)(2,1)S(1)}, u32[]{:S(2)}, u32[]{:S(2)}) collective-permute-start(bf16[256,288]{1,0:T(8,128)(2,1)S(1)} %collective-permute-done.12.m1), channel_id=1, source_target_pairs={{0,2},{2,0},{1,3},{3,1},{4,6},{6,4},{5,7},{7,5},{8,10},{10,8},{9,1... | collective-permute-start | bytes 442376 | tf_op jit(solution)/shard_map/ppermute | solution.py:368
  113.5 9.5 %collective-permute-start.21 = (bf16[128,1152]{1,0:T(8,128)(2,1)S(1)}, bf16[128,1152]{1,0:T(8,128)(2,1)S(1)}, u32[]{:S(2)}, u32[]{:S(2)}) collective-permute-start(bf16[128,1152]{1,0:T(8,128)(2,1)S(1)} %add_convert_fusion.4), channel_id=1, source_target_pairs={{0,2},{2,0},{1,3},{3,1},{4,6},{6,4},{5,7},{7,5},{8,10},{10,8},{9,1... | collective-permute-start | bytes 884744 | tf_op jit(solution)/shard_map/ppermute | solution.py:368
  152.8 10.4 %collective-permute-start.26 = (bf16[128,1152]{1,0:T(8,128)(2,1)}, bf16[128,1152]{1,0:T(8,128)(2,1)S(1)}, u32[]{:S(2)}, u32[]{:S(2)}) collective-permute-start(bf16[128,1152]{1,0:T(8,128)(2,1)} %get-tuple-element.88.g0), channel_id=1, source_target_pairs={{0,1},{1,0},{2,3},{3,2},{4,5},{5,4},{6,7},{7,6},{8,9},{9,8},{10,11... | collective-permute-start | bytes 884744 | tf_op jit(solution)/shard_map/ppermute | solution.py:371
  153.1 10.0 %collective-permute-start.25 = (bf16[128,1152]{1,0:T(8,128)(2,1)}, bf16[128,1152]{1,0:T(8,128)(2,1)S(1)}, u32[]{:S(2)}, u32[]{:S(2)}) collective-permute-start(bf16[128,1152]{1,0:T(8,128)(2,1)} %get-tuple-element.88.g0), channel_id=1, source_target_pairs={{0,2},{2,0},{1,3},{3,1},{4,6},{6,4},{5,7},{7,5},{8,10},{10,8},{9,1... | collective-permute-start | bytes 884744 | tf_op jit(solution)/shard_map/ppermute | solution.py:368
  154.1 47.1 %collective-permute-start.23 = (bf16[128,1152]{1,0:T(8,128)(2,1)}, bf16[128,1152]{1,0:T(8,128)(2,1)S(1)}, u32[]{:S(2)}, u32[]{:S(2)}) collective-permute-start(bf16[128,1152]{1,0:T(8,128)(2,1)} %get-tuple-element.87.refs_3_), channel_id=1, source_target_pairs={{0,1},{1,0},{2,3},{3,2},{4,5},{5,4},{6,7},{7,6},{8,9},{9,8},{10,11... | collective-permute-start | bytes 884744 | tf_op jit(solution)/shard_map/ppermute | solution.py:371
  154.1 31.2 %collective-permute-start.22 = (bf16[128,1152]{1,0:T(8,128)(2,1)}, bf16[128,1152]{1,0:T(8,128)(2,1)S(1)}, u32[]{:S(2)}, u32[]{:S(2)}) collective-permute-start(bf16[128,1152]{1,0:T(8,128)(2,1)} %get-tuple-element.87.refs_3_), channel_id=1, source_target_pairs={{0,2},{2,0},{1,3},{3,1},{4,6},{6,4},{5,7},{7,5},{8,10},{10,8},{9,1... | collective-permute-start | bytes 884744 | tf_op jit(solution)/shard_map/ppermute | solution.py:368
  161.0 165.1 %collective-permute-start.66 = (bf16[2,2,4,240,512]{4,3,2,1,0:T(8,128)(2,1)}, bf16[2,2,4,240,512]{4,3,2,1,0:T(8,128)(2,1)}, u32[]{:S(2)}, u32[]{:S(2)}) collective-permute-start(bf16[2,2,4,240,512]{4,3,2,1,0:T(8,128)(2,1)} %get-tuple-element.136), channel_id=1, source_target_pairs={{0,1},{1,0},{2,3},{3,2},{4,5},{5,4},{6,7},{7,6},{8,9},{9,8},{10,11... | collective-permute-start | bytes 11796488 | tf_op jit(solution)/shard_map/ppermute | solution.py:371
  185.3 15.8 %collective-permute-start.24 = (bf16[128,1152]{1,0:T(8,128)(2,1)S(1)}, bf16[128,1152]{1,0:T(8,128)(2,1)S(1)}, u32[]{:S(2)}, u32[]{:S(2)}) collective-permute-start(bf16[128,1152]{1,0:T(8,128)(2,1)S(1)} %collective-permute-done.22), channel_id=1, source_target_pairs={{0,1},{1,0},{2,3},{3,2},{4,5},{5,4},{6,7},{7,6},{8,9},{9,8},{10,11... | collective-permute-start | bytes 884744 | tf_op jit(solution)/shard_map/ppermute | solution.py:371
  186.0 9.3 %collective-permute-start.30 = (bf16[128,1152]{1,0:T(8,128)(2,1)S(1)}, bf16[128,1152]{1,0:T(8,128)(2,1)S(1)}, u32[]{:S(2)}, u32[]{:S(2)}) collective-permute-start(bf16[128,1152]{1,0:T(8,128)(2,1)S(1)} %add_convert_fusion.3), channel_id=1, source_target_pairs={{0,2},{2,0},{1,3},{3,1},{4,6},{6,4},{5,7},{7,5},{8,10},{10,8},{9,1... | collective-permute-start | bytes 884744 | tf_op jit(solution)/shard_map/ppermute | solution.py:368
  187.4 157.2 %collective-permute-start.75 = (bf16[2,2,4,256,512]{4,3,2,1,0:T(8,128)(2,1)}, bf16[2,2,4,256,512]{4,3,2,1,0:T(8,128)(2,1)}, u32[]{:S(2)}, u32[]{:S(2)}) collective-permute-start(bf16[2,2,4,256,512]{4,3,2,1,0:T(8,128)(2,1)} %get-tuple-element.140), channel_id=1, source_target_pairs={{0,1},{1,0},{2,3},{3,2},{4,5},{5,4},{6,7},{7,6},{8,9},{9,8},{10,11... | collective-permute-start | bytes 12582920 | tf_op jit(solution)/shard_map/ppermute | solution.py:371
  201.2 8.9 %collective-permute-start.32 = (bf16[128,1152]{1,0:T(8,128)(2,1)}, bf16[128,1152]{1,0:T(8,128)(2,1)S(1)}, u32[]{:S(2)}, u32[]{:S(2)}) collective-permute-start(bf16[128,1152]{1,0:T(8,128)(2,1)} %get-tuple-element.96.g0), channel_id=1, source_target_pairs={{0,1},{1,0},{2,3},{3,2},{4,5},{5,4},{6,7},{7,6},{8,9},{9,8},{10,11... | collective-permute-start | bytes 884744 | tf_op jit(solution)/shard_map/ppermute | solution.py:371
  222.5 14.2 %collective-permute-start.35 = (bf16[128,1152]{1,0:T(8,128)(2,1)}, bf16[128,1152]{1,0:T(8,128)(2,1)S(1)}, u32[]{:S(2)}, u32[]{:S(2)}) collective-permute-start(bf16[128,1152]{1,0:T(8,128)(2,1)} %get-tuple-element.103), channel_id=1, source_target_pairs={{0,1},{1,0},{2,3},{3,2},{4,5},{5,4},{6,7},{7,6},{8,9},{9,8},{10,11... | collective-permute-start | bytes 884744 | tf_op jit(solution)/shard_map/ppermute | solution.py:371
  230.3 18.4 %collective-permute-start.34 = (bf16[128,1152]{1,0:T(8,128)(2,1)}, bf16[128,1152]{1,0:T(8,128)(2,1)}, u32[]{:S(2)}, u32[]{:S(2)}) collective-permute-start(bf16[128,1152]{1,0:T(8,128)(2,1)} %get-tuple-element.101), channel_id=1, source_target_pairs={{0,1},{1,0},{2,3},{3,2},{4,5},{5,4},{6,7},{7,6},{8,9},{9,8},{10,11... | collective-permute-start | bytes 884744 | tf_op jit(solution)/shard_map/ppermute | solution.py:371
  233.8 13.7 %collective-permute-start.58 = (bf16[4,144,288]{2,1,0:T(8,128)(2,1)}, bf16[4,144,288]{2,1,0:T(8,128)(2,1)}, u32[]{:S(2)}, u32[]{:S(2)}) collective-permute-start(bf16[4,144,288]{2,1,0:T(8,128)(2,1)} %get-tuple-element.125), channel_id=1, source_target_pairs={{4,0},{0,4},{12,8},{8,12},{20,16},{16,20},{28,24},{24,28},{5,1},{1... | collective-permute-start | bytes 995336 | tf_op jit(solution)/shard_map/ppermute | solution.py:362
  237.5 11.2 %collective-permute-start.36 = (bf16[128,1152]{1,0:T(8,128)(2,1)}, bf16[128,1152]{1,0:T(8,128)(2,1)}, u32[]{:S(2)}, u32[]{:S(2)}) collective-permute-start(bf16[128,1152]{1,0:T(8,128)(2,1)} %add_convert_fusion.2), channel_id=1, source_target_pairs={{0,2},{2,0},{1,3},{3,1},{4,6},{6,4},{5,7},{7,5},{8,10},{10,8},{9,1... | collective-permute-start | bytes 884744 | tf_op jit(solution)/shard_map/ppermute | solution.py:368
  270.1 8.8 %collective-permute-start.59 = (bf16[144,288]{1,0:T(8,128)(2,1)}, bf16[144,288]{1,0:T(8,128)(2,1)S(1)}, u32[]{:S(2)}, u32[]{:S(2)}) collective-permute-start(bf16[144,288]{1,0:T(8,128)(2,1)} %get-tuple-element.260), channel_id=1, source_target_pairs={{8,0},{12,4},{16,8},{20,12},{24,16},{28,20},{0,24},{4,28},{9,1},{1... | collective-permute-start | bytes 248840 | tf_op jit(solution)/shard_map/ppermute | solution.py:365
  270.1 10.1 %collective-permute-start.61 = (bf16[144,288]{1,0:T(8,128)(2,1)}, bf16[144,288]{1,0:T(8,128)(2,1)S(1)}, u32[]{:S(2)}, u32[]{:S(2)}) collective-permute-start(bf16[144,288]{1,0:T(8,128)(2,1)} %get-tuple-element.261), channel_id=1, source_target_pairs={{24,0},{28,4},{0,8},{4,12},{8,16},{12,20},{16,24},{20,28},{25,1},{... | collective-permute-start | bytes 248840 | tf_op jit(solution)/shard_map/ppermute | solution.py:365
  278.9 29.8 %collective-permute-start.51 = (bf16[4,144,864]{2,1,0:T(8,128)(2,1)}, bf16[4,144,864]{2,1,0:T(8,128)(2,1)}, u32[]{:S(2)}, u32[]{:S(2)}) collective-permute-start(bf16[4,144,864]{2,1,0:T(8,128)(2,1)} %get-tuple-element.120), channel_id=1, source_target_pairs={{4,0},{0,4},{12,8},{8,12},{20,16},{16,20},{28,24},{24,28},{5,1},{1... | collective-permute-start | bytes 2985992 | tf_op jit(solution)/shard_map/ppermute | solution.py:362
  284.1 37.9 %collective-permute-start.38 = (bf16[128,1152]{1,0:T(8,128)(2,1)S(1)}, bf16[128,1152]{1,0:T(8,128)(2,1)S(1)}, u32[]{:S(2)}, u32[]{:S(2)}) collective-permute-start(bf16[128,1152]{1,0:T(8,128)(2,1)S(1)} %copy-done.13), channel_id=1, source_target_pairs={{0,1},{1,0},{2,3},{3,2},{4,5},{5,4},{6,7},{7,6},{8,9},{9,8},{10,11... | collective-permute-start | bytes 884744 | tf_op jit(solution)/shard_map/ppermute | solution.py:371
  289.5 9.4 %collective-permute-start.37 = (bf16[128,1152]{1,0:T(8,128)(2,1)S(1)}, bf16[128,1152]{1,0:T(8,128)(2,1)S(1)}, u32[]{:S(2)}, u32[]{:S(2)}) collective-permute-start(bf16[128,1152]{1,0:T(8,128)(2,1)S(1)} %copy-done.13), channel_id=1, source_target_pairs={{0,2},{2,0},{1,3},{3,1},{4,6},{6,4},{5,7},{7,5},{8,10},{10,8},{9,1... | collective-permute-start | bytes 884744 | tf_op jit(solution)/shard_map/ppermute | solution.py:368
  311.2 12.3 %collective-permute-start.39 = (bf16[128,1152]{1,0:T(8,128)(2,1)S(1)}, bf16[128,1152]{1,0:T(8,128)(2,1)S(1)}, u32[]{:S(2)}, u32[]{:S(2)}) collective-permute-start(bf16[128,1152]{1,0:T(8,128)(2,1)S(1)} %collective-permute-done.37), channel_id=1, source_target_pairs={{0,1},{1,0},{2,3},{3,2},{4,5},{5,4},{6,7},{7,6},{8,9},{9,8},{10,11... | collective-permute-start | bytes 884744 | tf_op jit(solution)/shard_map/ppermute | solution.py:371
  320.0 55.5 %collective-permute-start.62 = (bf16[4,144,2304]{2,1,0:T(8,128)(2,1)S(1)}, bf16[4,144,2304]{2,1,0:T(8,128)(2,1)S(1)}, u32[]{:S(2)}, u32[]{:S(2)}) collective-permute-start(bf16[4,144,2304]{2,1,0:T(8,128)(2,1)S(1)} %copy-done.44), channel_id=1, source_target_pairs={{4,0},{0,4},{12,8},{8,12},{20,16},{16,20},{28,24},{24,28},{5,1},{1... | collective-permute-start | bytes 7962632 | tf_op jit(solution)/shard_map/ppermute | solution.py:362
  322.1 12.2 %collective-permute-start.52 = (bf16[144,864]{1,0:T(8,128)(2,1)S(1)}, bf16[144,864]{1,0:T(8,128)(2,1)S(1)}, u32[]{:S(2)}, u32[]{:S(2)}) collective-permute-start(bf16[144,864]{1,0:T(8,128)(2,1)S(1)} %get-tuple-element.223), channel_id=1, source_target_pairs={{8,0},{12,4},{16,8},{20,12},{24,16},{28,20},{0,24},{4,28},{9,1},{1... | collective-permute-start | bytes 746504 | tf_op jit(solution)/shard_map/ppermute | solution.py:365
  323.6 12.3 %collective-permute-start.54 = (bf16[144,864]{1,0:T(8,128)(2,1)S(1)}, bf16[144,864]{1,0:T(8,128)(2,1)S(1)}, u32[]{:S(2)}, u32[]{:S(2)}) collective-permute-start(bf16[144,864]{1,0:T(8,128)(2,1)S(1)} %get-tuple-element.224), channel_id=1, source_target_pairs={{24,0},{28,4},{0,8},{4,12},{8,16},{12,20},{16,24},{20,28},{25,1},{... | collective-permute-start | bytes 746504 | tf_op jit(solution)/shard_map/ppermute | solution.py:365
  326.1 17.3 %collective-permute-start.53 = (bf16[144,864]{1,0:T(8,128)(2,1)S(1)}, bf16[144,864]{1,0:T(8,128)(2,1)S(1)}, u32[]{:S(2)}, u32[]{:S(2)}) collective-permute-start(bf16[144,864]{1,0:T(8,128)(2,1)S(1)} %get-tuple-element.225), channel_id=1, source_target_pairs={{16,0},{20,4},{24,8},{28,12},{0,16},{4,20},{8,24},{12,28},{17,1},{... | collective-permute-start | bytes 746504 | tf_op jit(solution)/shard_map/ppermute | solution.py:365
  334.3 45.8 %collective-permute-start.67 = (bf16[2,4,240,512]{3,2,1,0:T(8,128)(2,1)S(1)}, bf16[2,4,240,512]{3,2,1,0:T(8,128)(2,1)S(1)}, u32[]{:S(2)}, u32[]{:S(2)}) collective-permute-start(bf16[2,4,240,512]{3,2,1,0:T(8,128)(2,1)S(1)} %fusion.2), channel_id=1, source_target_pairs={{0,2},{2,0},{1,3},{3,1},{4,6},{6,4},{5,7},{7,5},{8,10},{10,8},{9,1... | collective-permute-start | bytes 5898248 | tf_op jit(solution)/shard_map/ppermute | solution.py:368
  348.2 68.2 %collective-permute-start.76 = (bf16[2,4,256,512]{3,2,1,0:T(8,128)(2,1)S(1)}, bf16[2,4,256,512]{3,2,1,0:T(8,128)(2,1)S(1)}, u32[]{:S(2)}, u32[]{:S(2)}) collective-permute-start(bf16[2,4,256,512]{3,2,1,0:T(8,128)(2,1)S(1)} %fusion), channel_id=1, source_target_pairs={{0,2},{2,0},{1,3},{3,1},{4,6},{6,4},{5,7},{7,5},{8,10},{10,8},{9,1... | collective-permute-start | bytes 6291464 | tf_op jit(solution)/shard_map/ppermute | solution.py:368
  382.5 37.8 %collective-permute-start.68 = (bf16[4,240,512]{2,1,0:T(8,128)(2,1)S(1)}, bf16[4,240,512]{2,1,0:T(8,128)(2,1)S(1)}, u32[]{:S(2)}, u32[]{:S(2)}) collective-permute-start(bf16[4,240,512]{2,1,0:T(8,128)(2,1)S(1)} %fusion.9), channel_id=1, source_target_pairs={{4,0},{0,4},{12,8},{8,12},{20,16},{16,20},{28,24},{24,28},{5,1},{1... | collective-permute-start | bytes 2949128 | tf_op jit(solution)/shard_map/ppermute | solution.py:362
  384.0 40.4 %collective-permute-start.63 = (bf16[144,2304]{1,0:T(8,128)(2,1)S(1)}, bf16[144,2304]{1,0:T(8,128)(2,1)S(1)}, u32[]{:S(2)}, u32[]{:S(2)}) collective-permute-start(bf16[144,2304]{1,0:T(8,128)(2,1)S(1)} %get-tuple-element.207), channel_id=1, source_target_pairs={{8,0},{12,4},{16,8},{20,12},{24,16},{28,20},{0,24},{4,28},{9,1},{1... | collective-permute-start | bytes 1990664 | tf_op jit(solution)/shard_map/ppermute | solution.py:365
  384.3 53.8 %collective-permute-start.65 = (bf16[144,2304]{1,0:T(8,128)(2,1)S(1)}, bf16[144,2304]{1,0:T(8,128)(2,1)S(1)}, u32[]{:S(2)}, u32[]{:S(2)}) collective-permute-start(bf16[144,2304]{1,0:T(8,128)(2,1)S(1)} %get-tuple-element.208), channel_id=1, source_target_pairs={{24,0},{28,4},{0,8},{4,12},{8,16},{12,20},{16,24},{20,28},{25,1},{... | collective-permute-start | bytes 1990664 | tf_op jit(solution)/shard_map/ppermute | solution.py:365
  386.1 67.0 %collective-permute-start.64 = (bf16[144,2304]{1,0:T(8,128)(2,1)S(1)}, bf16[144,2304]{1,0:T(8,128)(2,1)S(1)}, u32[]{:S(2)}, u32[]{:S(2)}) collective-permute-start(bf16[144,2304]{1,0:T(8,128)(2,1)S(1)} %get-tuple-element.209), channel_id=1, source_target_pairs={{16,0},{20,4},{24,8},{28,12},{0,16},{4,20},{8,24},{12,28},{17,1},{... | collective-permute-start | bytes 1990664 | tf_op jit(solution)/shard_map/ppermute | solution.py:365
  418.9 40.9 %collective-permute-start.77 = (bf16[4,256,512]{2,1,0:T(8,128)(2,1)S(1)}, bf16[4,256,512]{2,1,0:T(8,128)(2,1)S(1)}, u32[]{:S(2)}, u32[]{:S(2)}) collective-permute-start(bf16[4,256,512]{2,1,0:T(8,128)(2,1)S(1)} %fusion.8), channel_id=1, source_target_pairs={{4,0},{0,4},{12,8},{8,12},{20,16},{16,20},{28,24},{24,28},{5,1},{1... | collective-permute-start | bytes 3145736 | tf_op jit(solution)/shard_map/ppermute | solution.py:362
  420.7 32.6 %collective-permute-start.69 = (bf16[240,512]{1,0:T(8,128)(2,1)S(1)}, bf16[240,512]{1,0:T(8,128)(2,1)S(1)}, u32[]{:S(2)}, u32[]{:S(2)}) collective-permute-start(bf16[240,512]{1,0:T(8,128)(2,1)S(1)} %get-tuple-element.228), channel_id=1, source_target_pairs={{8,0},{12,4},{16,8},{20,12},{24,16},{28,20},{0,24},{4,28},{9,1},{1... | collective-permute-start | bytes 737288 | tf_op jit(solution)/shard_map/ppermute | solution.py:365
  424.3 29.0 %collective-permute-start.71 = (bf16[240,512]{1,0:T(8,128)(2,1)S(1)}, bf16[240,512]{1,0:T(8,128)(2,1)S(1)}, u32[]{:S(2)}, u32[]{:S(2)}) collective-permute-start(bf16[240,512]{1,0:T(8,128)(2,1)S(1)} %get-tuple-element.229), channel_id=1, source_target_pairs={{24,0},{28,4},{0,8},{4,12},{8,16},{12,20},{16,24},{20,28},{25,1},{... | collective-permute-start | bytes 737288 | tf_op jit(solution)/shard_map/ppermute | solution.py:365
  438.1 20.3 %collective-permute-start.70 = (bf16[240,512]{1,0:T(8,128)(2,1)S(1)}, bf16[240,512]{1,0:T(8,128)(2,1)S(1)}, u32[]{:S(2)}, u32[]{:S(2)}) collective-permute-start(bf16[240,512]{1,0:T(8,128)(2,1)S(1)} %get-tuple-element.230), channel_id=1, source_target_pairs={{16,0},{20,4},{24,8},{28,12},{0,16},{4,20},{8,24},{12,28},{17,1},{... | collective-permute-start | bytes 737288 | tf_op jit(solution)/shard_map/ppermute | solution.py:365
  460.4 16.1 %collective-permute-start.78 = (bf16[256,512]{1,0:T(8,128)(2,1)S(1)}, bf16[256,512]{1,0:T(8,128)(2,1)S(1)}, u32[]{:S(2)}, u32[]{:S(2)}) collective-permute-start(bf16[256,512]{1,0:T(8,128)(2,1)S(1)} %get-tuple-element.220), channel_id=1, source_target_pairs={{8,0},{12,4},{16,8},{20,12},{24,16},{28,20},{0,24},{4,28},{9,1},{1... | collective-permute-start | bytes 786440 | tf_op jit(solution)/shard_map/ppermute | solution.py:365
  463.1 13.3 %collective-permute-start.80 = (bf16[256,512]{1,0:T(8,128)(2,1)S(1)}, bf16[256,512]{1,0:T(8,128)(2,1)S(1)}, u32[]{:S(2)}, u32[]{:S(2)}) collective-permute-start(bf16[256,512]{1,0:T(8,128)(2,1)S(1)} %get-tuple-element.221), channel_id=1, source_target_pairs={{24,0},{28,4},{0,8},{4,12},{8,16},{12,20},{16,24},{20,28},{25,1},{... | collective-permute-start | bytes 786440 | tf_op jit(solution)/shard_map/ppermute | solution.py:365
  463.1 22.2 %collective-permute-start.79 = (bf16[256,512]{1,0:T(8,128)(2,1)S(1)}, bf16[256,512]{1,0:T(8,128)(2,1)S(1)}, u32[]{:S(2)}, u32[]{:S(2)}) collective-permute-start(bf16[256,512]{1,0:T(8,128)(2,1)S(1)} %get-tuple-element.222), channel_id=1, source_target_pairs={{16,0},{20,4},{24,8},{28,12},{0,16},{4,20},{8,24},{12,28},{17,1},{... | collective-permute-start | bytes 786440 | tf_op jit(solution)/shard_map/ppermute | solution.py:365
  464.9 21.4 %collective-permute-start.74 = (bf16[240,512]{1,0:T(8,128)(2,1)S(1)}, bf16[240,512]{1,0:T(8,128)(2,1)S(1)}, u32[]{:S(2)}, u32[]{:S(2)}) collective-permute-start(bf16[240,512]{1,0:T(8,128)(2,1)S(1)} %collective-permute-done.73), channel_id=1, source_target_pairs={{0,1},{1,0},{2,3},{3,2},{4,5},{5,4},{6,7},{7,6},{8,9},{9,8},{10,11... | collective-permute-start | bytes 737288 | tf_op jit(solution)/shard_map/ppermute | solution.py:371
  (91 other events, 771.0 us)
Sparse Core Ops, SparseCore 0:
  12.0 125.3 all-gather.2

commit v3 on v2

v3 whole, which is shorter than its diff:
```python
import functools
import math

import jax
import jax.numpy as jnp
from jax import lax
from jax.experimental import pallas as pl
from jax.experimental.pallas import tpu as pltpu
from jax.sharding import PartitionSpec as P

HEAD_DIM = 72
norm_eps = 1e-06
cos_eps = 1e-06
repa_weight = 0.5
F32 = jnp.float32
BF16 = jnp.bfloat16
VMEM = pl.BlockSpec(memory_space=pltpu.VMEM)
SMEM = pl.BlockSpec(memory_space=pltpu.SMEM)
ANY = pl.BlockSpec(memory_space=pl.ANY)
VMEM_LIMIT = 58 * 1024 * 1024


def shape_of(shape, dtype):
    return jax.ShapeDtypeStruct(tuple(shape), dtype)


def call(kernel, outs, ins, in_specs=None, out_specs=None, scratch=(), flops=0, limit=VMEM_LIMIT, name=None, after=()):
    n = len(ins)
    after = list(after)
    inner_kernel = kernel

    def kernel(*refs):
        inner_kernel(*refs[:n], *refs[n + len(after) :])

    moved = sum(math.prod(a.shape) * a.dtype.itemsize for a in list(ins) + list(outs))
    return pl.pallas_call(
        kernel,
        out_shape=tuple(outs),
        in_specs=list(in_specs or [VMEM] * n) + [ANY] * len(after),
        out_specs=tuple(out_specs or [VMEM] * len(outs)),
        scratch_shapes=list(scratch),
        compiler_params=pltpu.CompilerParams(vmem_limit_bytes=limit),
        cost_estimate=pl.CostEstimate(flops=0, bytes_accessed=0, transcendentals=0),
        name=name,
    )(*ins, *after)


def hold(arrays, after):
    n = len(arrays)
    return pl.pallas_call(
        lambda *refs: None,
        out_shape=tuple(shape_of(a.shape, a.dtype) for a in arrays),
        in_specs=[ANY] * (n + len(after)),
        out_specs=(ANY,) * n,
        input_output_aliases={k: k for k in range(n)},
        compiler_params=pltpu.CompilerParams(vmem_limit_bytes=1024 * 1024),
        name="hold",
    )(*arrays, *after)


def dot(a, b):
    return jnp.dot(a, b, preferred_element_type=F32)


def dot_nt(a, b):
    return lax.dot_general(a, b, (((1,), (1,)), ((), ())), preferred_element_type=F32)


def dot_tn(a, b):
    return lax.dot_general(a, b, (((0,), (0,)), ((), ())), preferred_element_type=F32)


def sigmoid(v):
    return 1.0 / (1.0 + jnp.exp(-v))


def silu_slope(v):
    s = sigmoid(v)
    return s * (1.0 + v * (1.0 - s))


def pick(seg, table):
    out = jnp.broadcast_to(table[0:1, :], (seg.shape[0], table.shape[1]))
    for s in range(1, table.shape[0]):
        out = jnp.where(seg == s, table[s : s + 1, :], out)
    return out


def by_image(seg, values, slots):
    rows = [jnp.sum(jnp.where(seg == s, values, 0.0), axis=0, keepdims=True) for s in range(slots)]
    return jnp.concatenate(rows, axis=0)


def norm_parts(v):
    centered = v - jnp.mean(v, axis=-1, keepdims=True)
    inv = lax.rsqrt(jnp.mean(centered * centered, axis=-1, keepdims=True) + norm_eps)
    return centered * inv, inv


def norm_back(g, xhat, inv):
    return inv * (g - jnp.mean(g, axis=-1, keepdims=True) - xhat * jnp.mean(g * xhat, axis=-1, keepdims=True))


def attend(q, k, v, open_mask, scale):
    s = dot_nt(q, k) * scale
    s = jnp.where(open_mask, s, -1e30)
    e = jnp.exp(s - jnp.max(s, axis=-1, keepdims=True))
    return e * (1.0 / jnp.sum(e, axis=-1, keepdims=True))


def open_of(segc, segr, valr):
    n = segc.shape[0]
    same = lax.broadcasted_iota(jnp.int32, (n, n), 0) == lax.broadcasted_iota(jnp.int32, (n, n), 1)
    return (segc == segr) & ((valr == 1) | same)


def fwd_kernel(heads, order, hid, mods, segc, segr, valr, w, b, m_ref, q_ref, k_ref, v_ref, mix_ref):
    half, width = hid.shape[1], hid.shape[2]
    seq = 2 * half
    scale = HEAD_DIM ** (-0.5)
    for micro in range(2):
        x = jnp.concatenate([hid[order[2 * micro]], hid[order[2 * micro + 1]]], axis=0).astype(F32)
        rows = slice(micro * seq, (micro + 1) * seq)
        seg = segc[rows, :]
        xhat, _ = norm_parts(x)
        shift = pick(seg, mods[micro][:, 0:width])
        scaling = pick(seg, mods[micro][:, width : 2 * width])
        m = (xhat * (1.0 + scaling) + shift).astype(BF16)
        m_ref[rows, :] = m
        q = (dot_nt(m, w[0]) + b[0:1, :]).astype(BF16)
        k = dot_nt(m, w[1]).astype(BF16)
        v = (dot_nt(m, w[2]) + b[1:2, :]).astype(BF16)
        q_ref[rows, :] = q
        k_ref[rows, :] = k
        v_ref[rows, :] = v
        mask = open_of(seg, segr[micro : micro + 1, :], valr[micro : micro + 1, :])
        mixed = []
        for h in range(heads):
            cols = slice(h * HEAD_DIM, (h + 1) * HEAD_DIM)
            p = attend(q[:, cols], k[:, cols], v[:, cols], mask, scale)
            mixed.append(dot(p.astype(BF16), v[:, cols]).astype(BF16))
        mix_ref[rows, :] = jnp.concatenate(mixed, axis=1)


def bwd_kernel(heads, g0, g1, g2, g3, out_w, q_ref, k_ref, v_ref, segc, segr, valr, w, gqkv_ref, part_q, part_y, send, bias_ref, gfull_ref):
    half = g0.shape[0]
    seq = 2 * half
    scale = HEAD_DIM ** (-0.5)
    wide = heads * HEAD_DIM
    sums = []
    for micro in range(2):
        rows = slice(micro * seq, (micro + 1) * seq)
        g = jnp.concatenate([g0[...], g1[...]] if micro == 0 else [g2[...], g3[...]], axis=0)
        gfull_ref[rows, :] = g
        gm = dot_nt(g, out_w[...]).astype(BF16)
        q, k, v = q_ref[rows, :], k_ref[rows, :], v_ref[rows, :]
        mask = open_of(segc[rows, :], segr[micro : micro + 1, :], valr[micro : micro + 1, :])
        gq, gk, gv = [], [], []
        for h in range(heads):
            cols = slice(h * HEAD_DIM, (h + 1) * HEAD_DIM)
            qh, kh, vh, gh = q[:, cols], k[:, cols], v[:, cols], gm[:, cols]
            p = attend(qh, kh, vh, mask, scale)
            gp = dot_nt(gh, vh)
            gs = (p * (gp - jnp.sum(p * gp, axis=-1, keepdims=True))).astype(BF16)
            gq.append((dot(gs, kh) * scale).astype(BF16))
            gk.append((dot_tn(gs, qh) * scale).astype(BF16))
            gv.append(dot_tn(p.astype(BF16), gh).astype(BF16))
        gq, gk, gv = (jnp.concatenate(a, axis=1) for a in (gq, gk, gv))
        gqkv_ref[rows, 0:wide] = gq
        gqkv_ref[rows, wide : 2 * wide] = gk
        gqkv_ref[rows, 2 * wide : 3 * wide] = gv
        spare = gqkv_ref.shape[1] - 3 * wide
        if spare:
            gqkv_ref[rows, 3 * wide :] = jnp.zeros((seq, spare), BF16)
        sums.append(
            jnp.concatenate(
                [jnp.sum(gq.astype(F32), axis=0, keepdims=True), jnp.sum(gv.astype(F32), axis=0, keepdims=True)],
                axis=0,
            )
        )
        part = dot(gq, w[0]) + dot(gk, w[1]) + dot(gv, w[2])
        if micro == 0:
            part_q[...] = part[:half]
            part_y[...] = part[half:]
        else:
            send[...] = part.astype(BF16)
    bias_ref[...] = sums[0] + sums[1]


def mid_kernel(order, hid, mods, segc, m0, m1, m2, m3, w0, w1, w2, w3, out_b, attn_q, h_q, m_two):
    half, width = hid.shape[1], hid.shape[2]
    seq = 2 * half
    x = jnp.concatenate([hid[order[0]], hid[order[1]]], axis=0).astype(F32)
    seg = segc[0:seq, :]
    m2, m3 = (jnp.concatenate([m[half:, :], m[:half, :]], axis=0) for m in (m2, m3))
    attn = dot(m0[...], w0[...]) + dot(m1[...], w1[...]) + dot(m2, w2[...]) + dot(m3, w3[...])
    attn = attn + out_b[...]
    h = x + pick(seg, mods[:, 2 * width : 3 * width]) * attn
    attn_q[...] = attn[:half]
    h_q[...] = h[:half]
    xhat, _ = norm_parts(h)
    m_two[...] = (
        xhat * (1.0 + pick(seg, mods[:, 4 * width : 5 * width])) + pick(seg, mods[:, 3 * width : 4 * width])
    ).astype(BF16)


SPLITS = ((0, 512), (512, 1152))
K0 = math.sqrt(2.0 / math.pi)


def mlp_kernel(m_own, m_par, fc1, b1, fc2, m_full, pre_ref, act_ref, part_q, part_y, send):
    seq = m_own.shape[0]
    half = seq // 2
    for micro, m_ref in enumerate((m_own, m_par)):
        rows = slice(micro * seq, (micro + 1) * seq)
        m = m_ref[...]
        m_full[rows, :] = m
        for lo, hi in SPLITS:
            pre = dot(m, fc1[:, lo:hi]) + b1[:, lo:hi]
            pre_ref[rows, lo:hi] = pre
            t = jnp.tanh(K0 * (pre + 0.044715 * (pre * pre * pre)))
            act_ref[rows, lo:hi] = (0.5 * pre * (1.0 + t)).astype(BF16)
        act = act_ref[rows, :]
        for lo, hi in SPLITS:
            part = dot(act, fc2[:, lo:hi])
            if micro == 0:
                part_q[:, lo:hi] = part[:half]
                part_y[:, lo:hi] = part[half:]
            else:
                send[:, lo:hi] = part.astype(BF16)


def mlp_back_kernel(g0, g1, g2, g3, pre_ref, fc1, fc2, g_full, gpre_ref, part_q, part_y, send, bias):
    half = g0.shape[0]
    seq = 2 * half
    for micro in range(2):
        rows = slice(micro * seq, (micro + 1) * seq)
        g = jnp.concatenate([g0[...], g1[...]] if micro == 0 else [g2[...], g3[...]], axis=0)
        g_full[rows, :] = g
        for lo, hi in SPLITS:
            ga = dot_nt(g, fc2[lo:hi, :])
            v = pre_ref[rows, lo:hi]
            t = jnp.tanh(K0 * (v + 0.044715 * (v * v * v)))
            slope = 0.5 * (1.0 + t) + 0.5 * v * (1.0 - t * t) * (K0 * (1.0 + 3.0 * 0.044715 * (v * v)))
            gp = (ga * slope).astype(BF16)
            gpre_ref[rows, lo:hi] = gp
            total = jnp.sum(gp.astype(F32), axis=0, keepdims=True)
            bias[:, lo:hi] = total if micro == 0 else bias[:, lo:hi] + total
        gp = gpre_ref[rows, :]
        for lo, hi in SPLITS:
            part = dot_nt(gp, fc1[lo:hi, :])
            if micro == 0:
                part_q[:, lo:hi] = part[:half]
                part_y[:, lo:hi] = part[half:]
            else:
                send[:, lo:hi] = part.astype(BF16)


def proj_kernel(plan, n_pieces, quarter_of, meta, *refs):
    (part, got, ry, h_one, mods, seg_ref, fc2_b, grad_out, feat_ref, keep_ref, b1, b2, b3) = refs[:13]
    pieces = refs[13 : 13 + n_pieces]
    (ins_ref, keep_out, send_out, grad_h, g_mlp, gate_sum, gb1, gb2, gb3, gbf) = refs[13 + n_pieces : 23 + n_pieces]
    w1, w2, w3, a1, a2, ga1_ref, ga2_ref, gz_ref, sems = refs[23 + n_pieces :]
    weights = (w1, w2, w3)
    half, width = h_one.shape
    slots = mods.shape[0]
    hidden = w1.shape[1]
    for which, load in enumerate(plan):
        for source, target in load(pieces, weights[which]):
            pltpu.make_async_copy(source, target, sems.at[which]).start()
    seg = seg_ref[...]
    gate = pick(seg, mods[:, 5 * width : 6 * width])
    mlp = part[...] + got[0:half, :].astype(F32) + ry[...].astype(F32) + fc2_b[...]
    h = h_one[...] + gate * mlp
    hl = h.astype(BF16)
    ins_ref[:, 2 * hidden :] = hl
    step = 512
    pltpu.make_async_copy(w1, w1, sems.at[0]).wait()
    for lo in range(0, hidden, step):
        a = dot(hl, w1[:, lo : lo + step]) + b1[:, lo : lo + step]
        a1[:, lo : lo + step] = a
        ins_ref[:, lo : lo + step] = (a * sigmoid(a)).astype(BF16)
    pltpu.make_async_copy(w2, w2, sems.at[1]).wait()
    s = ins_ref[:, 0:hidden]
    for lo in range(0, hidden, step):
        a = dot(s, w2[:, lo : lo + step]) + b2[:, lo : lo + step]
        a2[:, lo : lo + step] = a
        ins_ref[:, hidden + lo : hidden + lo + step] = (a * sigmoid(a)).astype(BF16)
    pltpu.make_async_copy(w3, w3, sems.at[2]).wait()
    z = dot(ins_ref[:, hidden : 2 * hidden], w3[...]) + b3[...]
    feat = feat_ref[...].astype(F32)
    inv_z = lax.rsqrt(jnp.sum(z * z, axis=-1, keepdims=True) + cos_eps)
    inv_f = lax.rsqrt(jnp.sum(feat * feat, axis=-1, keepdims=True) + cos_eps)
    zf = jnp.sum(z * feat, axis=-1, keepdims=True)
    coeff = -repa_weight * keep_ref[...] * inv_z * inv_f
    gz = (coeff * (feat - (zf * inv_z * inv_z) * z)).astype(BF16)
    gz_ref[...] = gz
    gb3[...] = jnp.sum(gz.astype(F32), axis=0, keepdims=True)
    for lo in range(0, hidden, step):
        g = (dot_nt(gz, w3[lo : lo + step, :]) * silu_slope(a2[:, lo : lo + step])).astype(BF16)
        ga2_ref[:, lo : lo + step] = g
        gb2[:, lo : lo + step] = jnp.sum(g.astype(F32), axis=0, keepdims=True)
    ga2 = ga2_ref[...]
    for lo in range(0, hidden, step):
        g = (dot_nt(ga2, w2[lo : lo + step, :]) * silu_slope(a1[:, lo : lo + step])).astype(BF16)
        ga1_ref[:, lo : lo + step] = g
        gb1[:, lo : lo + step] = jnp.sum(g.astype(F32), axis=0, keepdims=True)
    gh = grad_out[...].astype(F32) + dot_nt(ga1_ref[...], w1[...])
    grad_h[...] = gh
    gm = (gate * gh).astype(BF16)
    g_mlp[...] = gm
    gbf[...] = jnp.sum(gm.astype(F32), axis=0, keepdims=True)
    gate_sum[...] = by_image(seg, gh * mlp, slots)
    n, m = hidden // 4, gz.shape[1] // 4
    wide = 2 * n + m
    for out, cr in ((keep_out, 0), (send_out, 1)):
        for yr in range(2):
            q = quarter_of(meta, yr, cr)
            columns, low = pl.ds(pl.multiple_of(q * n, 128), n), pl.ds(pl.multiple_of(q * m, 128), m)
            out[:, yr * wide : yr * wide + n] = ga2_ref[:, columns]
            out[:, yr * wide + n : yr * wide + 2 * n] = ga1_ref[:, columns]
            out[:, yr * wide + 2 * n : (yr + 1) * wide] = gz_ref[:, low]


def proj_grad_kernel(hidden, place, n_outs, meta, f0, f1, f2, f3, keep, got, other, *refs):
    outs = refs[:n_outs]
    a, b, r2, r3, r1, in_sem, out_sem = refs[n_outs:]
    half = f0.shape[0]
    wide = b.shape[1]
    n = r2.shape[1]
    for at, piece in enumerate((f0, f1, f2, f3)):
        pltpu.make_async_copy(piece, a.at[at * half : (at + 1) * half, :], in_sem.at[0]).start()
    for at, piece in enumerate((keep.at[:, 0:wide], other.at[0], got.at[:, 0:wide], other.at[1])):
        pltpu.make_async_copy(piece, b.at[at * half : (at + 1) * half, :], in_sem.at[1]).start()
    pltpu.make_async_copy(b, b, in_sem.at[1]).wait()
    pltpu.make_async_copy(a, a, in_sem.at[0]).wait()
    for job, (first, cols, g, step) in enumerate(
        ((0, slice(0, n), r2, 512), (hidden, slice(2 * n, wide), r3, 512), (2 * hidden, slice(n, 2 * n), r1, 384))
    ):
        for lo in range(0, g.shape[0], step):
            g[lo : lo + step, :] = dot_tn(a[:, first + lo : first + lo + step], b[:, cols]).astype(BF16)
        for source, target in place(job, g, outs, meta):
            pltpu.make_async_copy(source, target, out_sem.at[job]).start()
    for job, g in enumerate((r2, r3, r1)):
        pltpu.make_async_copy(g, g, out_sem.at[job]).wait()


def second_back_kernel(part, rq, ry, grad_h, h_one, attn, mods, seg_ref, g_one, g_attn, gate_sum, shift_sum, scale_sum, bias):
    width = h_one.shape[1]
    slots = mods.shape[0]
    seg = seg_ref[...]
    g = part[...] + rq[0 : part.shape[0], :].astype(F32) + ry[...].astype(F32)
    xhat, inv = norm_parts(h_one[...])
    total = grad_h[...] + norm_back(g * (1.0 + pick(seg, mods[:, 4 * width : 5 * width])), xhat, inv)
    g_one[...] = total
    ga = (pick(seg, mods[:, 2 * width : 3 * width]) * total).astype(BF16)
    g_attn[...] = ga
    bias[...] = jnp.sum(ga.astype(F32), axis=0, keepdims=True)
    gate_sum[...] = by_image(seg, total * attn[...], slots)
    shift_sum[...] = by_image(seg, g, slots)
    scale_sum[...] = by_image(seg, g * xhat, slots)


def first_back_kernel(order, part, rq, ry, g_one, hid, mods, seg_ref, g_in, shift_sum, scale_sum):
    width = g_one.shape[1]
    slots = mods.shape[0]
    seg = seg_ref[...]
    g = part[...] + rq[0 : part.shape[0], :].astype(F32) + ry[...].astype(F32)
    xhat, inv = norm_parts(hid[order[0]].astype(F32))
    total = g_one[...] + norm_back(g * (1.0 + pick(seg, mods[:, width : 2 * width])), xhat, inv)
    g_in[...] = total.astype(BF16)
    shift_sum[...] = by_image(seg, g, slots)
    scale_sum[...] = by_image(seg, g * xhat, slots)


def wgrad_kernel(place, jobs, n_outs, *refs):
    meta = refs[0]
    n_ins = 1 + max(max(a, b) for a, b, _ in jobs)
    ins, outs, (*results, sem) = refs[1 : 1 + n_ins], refs[1 + n_ins : 1 + n_ins + n_outs], refs[1 + n_ins + n_outs :]
    for n, (a, b, step) in enumerate(jobs):
        g = results[n]
        rows = g.shape[0]
        for lo in range(0, rows, step):
            hi = min(lo + step, rows)
            g[lo:hi, :] = dot_tn(ins[a][:, lo:hi], ins[b][...]).astype(BF16)
        for source, target in place(n, g, outs, meta):
            pltpu.make_async_copy(source, target, sem.at[n]).start()
    for n, g in enumerate(results):
        pltpu.make_async_copy(g, g, sem.at[n]).wait()


def body(mesh, hidden_in, grad_out, features, seg_ids, valid_mask, time_ids, class_ids, class_table, ada_w, ada_b, qkv_w, qv_bias, out_w, out_b, fc1_w, fc1_b, fc2_w, fc2_b, repa_w1, repa_b1, repa_w2, repa_b2, repa_w3, repa_b3):
    n_dp = mesh.shape["dp"]
    top = n_dp // 2
    micro_count, rows_dev, seq, width = hidden_in.shape
    slots = time_ids.shape[-1]
    images = micro_count * rows_dev * slots
    half = seq // 2
    wide = qkv_w.shape[2]
    qkv_t = qkv_w.transpose(0, 2, 1)
    heads = wide // HEAD_DIM
    ff = fc1_w.shape[1]
    hidden = repa_w1.shape[1]
    repr_width = repa_w3.shape[1]

    d = lax.axis_index("dp")
    t = lax.axis_index("tensor")
    y, c = t // 2, t % 2
    meta = jnp.stack([d, d, y, c]).astype(jnp.int32)

    def flip_dp(x, mask):
        return lax.ppermute(x, "dp", [(k, k ^ mask) for k in range(n_dp)])

    def swap_y(x):
        return lax.ppermute(x, "tensor", [(0, 2), (2, 0), (1, 3), (3, 1)])

    def swap_core(x):
        return lax.ppermute(x, "tensor", [(0, 1), (1, 0), (2, 3), (3, 2)])

    def exchange_dp(x):
        return lax.all_to_all(x, "dp", 0, 0, tiled=True)

    def gather_dp(x):
        return exchange_dp(jnp.broadcast_to(x[None], (n_dp,) + x.shape))

    def cols_of(w):
        n = w.shape[1] // 4
        return lax.dynamic_slice_in_dim(w, t * n, n, axis=1)

    k1, k2, k3 = repa_w1.shape[0], repa_w2.shape[0], repa_w3.shape[0]
    block = hidden // 4
    third = repr_width // 4
    room = block // 2
    short = k3 // 2

    def cols_padded(w, axis_n):
        w = w.reshape(w.shape[:-1] + (4, axis_n // 4))
        return jnp.pad(w, [(0, 0)] * (w.ndim - 1) + [(0, room - axis_n // 4)]).reshape(w.shape[:-2] + (4 * room,))

    w3_mine = jnp.pad(cols_of(repa_w3), ((0, 0), (0, room - third)))
    w3_fold = jnp.concatenate([w3_mine[:short], w3_mine[short:]], axis=1)
    packed = jnp.concatenate([cols_of(repa_w2), w3_fold, cols_of(repa_w1)], axis=0)
    gathered = lax.all_gather(packed, ("dp", "tensor"), axis=0)
    off3, off1 = k2, k2 + short
    out_y = swap_y(out_w)
    out_c = swap_core(out_w)
    out_yc = swap_core(out_y)
    n1, n2, n3 = repa_b1.shape[0], repa_b2.shape[0], repa_b3.shape[0]

    ids = gather_dp(jnp.concatenate([class_ids.reshape(images), time_ids.reshape(images)]))
    all_class = ids[:, :images].reshape(1, n_dp * images)
    all_time = ids[:, images:].reshape(1, n_dp * images)
    feats = class_table.shape[0]
    class_hot = lax.broadcasted_iota(jnp.int32, (class_table.shape[1], n_dp * images), 0) == all_class
    place = d * feats + lax.broadcasted_iota(jnp.int32, (feats, 1), 0)
    half_width = width // 2
    freqs = jnp.exp(-math.log(10000.0) * (place % half_width).astype(F32) / half_width)
    angles = all_time.astype(F32) * freqs
    condition = jnp.where(place < half_width, jnp.cos(angles), jnp.sin(angles)) + dot(class_table, class_hot.astype(BF16))
    n_images = n_dp * images
    biases = jnp.concatenate([repa_b1, repa_b2, repa_b3])
    lines = -(-biases.shape[0] // n_images)
    biases = jnp.pad(biases, (0, lines * n_images - biases.shape[0])).reshape(lines, n_images)
    found = gather_dp(jnp.concatenate([jax.nn.silu(condition).astype(BF16), biases], axis=0))
    cond_act = found[:, :feats].reshape(width, n_images)
    b_all = found[:, feats:].reshape(n_dp, -1)
    b_one = b_all[:, :n1].reshape(1, -1).astype(F32)
    b_two = b_all[:, n1 : n1 + n2].reshape(1, -1).astype(F32)
    b_three = cols_padded(b_all[:, n1 + n2 : n1 + n2 + n3].reshape(1, -1).astype(F32), repr_width)
    mod_part = lax.dot_general(cond_act, ada_w, (((0,), (1,)), ((), ())), preferred_element_type=F32) + ada_b.astype(F32)
    mod_parts = exchange_dp(mod_part.reshape(n_dp, images, -1))
    modulation = mod_parts.transpose(1, 0, 2).reshape(micro_count, slots, -1)
    mods_own = lax.dynamic_index_in_dim(modulation, c, 0, keepdims=False)
    mods_par = lax.dynamic_index_in_dim(modulation, 1 - c, 0, keepdims=False)

    order = jnp.stack([2 * c + y, 2 * c + 1 - y, 2 * (1 - c) + y, 2 * (1 - c) + 1 - y]).astype(jnp.int32)
    hid = hidden_in.reshape(4, half, width)

    def ordered(a):
        a = a.reshape(4, half)
        return jnp.concatenate([lax.dynamic_index_in_dim(a, order[n], 0, keepdims=False) for n in range(4)])

    seg_line = ordered(seg_ids)
    val_line = ordered(valid_mask)
    seg_rows = seg_line.reshape(2, seq)
    val_rows = val_line.reshape(2, seq)
    seg_cols = seg_line.reshape(2 * seq, 1)
    seg_q = seg_cols[:half]
    keep_q = val_line[:half].reshape(half, 1).astype(F32)
    go_q = lax.dynamic_index_in_dim(grad_out.reshape(4, half, width), order[0], 0, keepdims=False)
    feat_q = cols_padded(lax.dynamic_index_in_dim(features.reshape(4, half, repr_width), order[0], 0, keepdims=False), repr_width)

    tokens = 2 * seq
    T = tokens

    def fwd(order_, hid_, a, b, *rest):
        return functools.partial(fwd_kernel, heads)(order_, hid_, (a, b), *rest)

    m_one, q, k, v, mixed = call(
        fwd,
        [shape_of((T, width), BF16)] + [shape_of((T, wide), BF16)] * 4,
        [order, hid, mods_own, mods_par, seg_cols, seg_rows, val_rows, qkv_t, qv_bias.astype(F32)],
        in_specs=[SMEM] + [VMEM] * 8,
        flops=2 * T * width * wide * 3 + 4 * T * seq * wide,
        name="attention",
    )

    mix_own, mix_send = mixed[:seq], mixed[seq:]
    mix_y = swap_y(mix_own)
    mix_c = swap_core(mix_send)
    mix_yc = swap_y(mix_c)
    attn_q, h_q, m_two = call(
        mid_kernel,
        [shape_of((half, width), F32), shape_of((half, width), F32), shape_of((seq, width), BF16)],
        [order, hid, mods_own, seg_cols, mix_own, mix_c, mix_y, mix_yc, out_w, out_c, out_y, out_yc, out_b.astype(F32).reshape(1, width)],
        in_specs=[SMEM] + [VMEM] * 12,
        flops=2 * seq * width * width,
        name="middle",
    )
    m_par = swap_core(m_two)

    quarter = [shape_of((half, width), F32), shape_of((half, width), F32), shape_of((seq, width), BF16)]

    def settle_quarter(part_y, send):
        got = swap_core(send)
        passed = swap_y((part_y + got[half:].astype(F32)).astype(BF16))
        return got, passed

    def spread_quarter(g):
        gy = swap_y(g)
        return g, gy, swap_core(g), swap_core(gy)

    m_full, pre, act, part_q, part_y, send = call(
        mlp_kernel,
        [shape_of((T, width), BF16), shape_of((T, ff), F32), shape_of((T, ff), BF16)] + quarter,
        [m_two, m_par, fc1_w, fc1_b.astype(F32).reshape(1, ff), fc2_w],
        flops=4 * T * width * ff,
        name="mlp",
    )
    rq, ry = settle_quarter(part_y, send)

    def k_of(w):
        return w.shape[0]

    def position(meta_, rel):
        return lax.bitwise_xor(meta_[0], jnp.int32(rel))

    def relative(nat):
        for bit in range(n_dp.bit_length() - 1):
            cut = nat.reshape((top >> bit, 2, 1 << bit) + nat.shape[1:])
            nat = jnp.where((d >> bit) & 1 == 0, cut, cut[:, ::-1]).reshape(nat.shape)
        return nat

    def quarter_of(meta_, yr, cr):
        ty = meta_[2] if yr == 0 else 1 - meta_[2]
        tc = meta_[3] if cr == 0 else 1 - meta_[3]
        return ty * 2 + tc

    def pair(stack, me, axis):
        first, second = stack
        same = me == 0
        return jnp.concatenate([jnp.where(same, first, second), jnp.where(same, second, first)], axis=axis)

    aligned = k1 % 16 == 0 and k2 % 16 == 0 and k3 % 32 == 0
    n_all = 4 * n_dp

    def load_two(refs, target):
        for s in range(n_all):
            at, part = s // 4, s % 4
            yield refs[0].at[s, 0:k2, :], target.at[at * k2 : (at + 1) * k2, part * block : (part + 1) * block]

    def load_one(refs, target):
        for s in range(n_all):
            at, part = s // 4, s % 4
            yield refs[0].at[s, off1 : off1 + k1, :], target.at[at * k1 : (at + 1) * k1, part * block : (part + 1) * block]

    def load_three(refs, target):
        for s in range(n_all):
            at, part = s // 4, s % 4
            for n in range(2):
                rows = slice(at * k3 + n * short, at * k3 + (n + 1) * short)
                yield refs[0].at[s, off3:off1, n * room : (n + 1) * room], target.at[rows, part * room : (part + 1) * room]

    def whole(n):
        def load(refs, target):
            yield refs[n], target

        return load

    if aligned:
        pieces = [gathered]
        plan = [load_one, load_two, load_three]
    else:
        by_cols = lambda a: a.reshape(n_dp, 4, -1, block).transpose(0, 2, 1, 3).reshape(-1, hidden)
        fold = gathered[:, off3:off1].reshape(n_dp, 4, short, 2, room).transpose(0, 3, 2, 1, 4).reshape(hidden, 4 * room)
        pieces = [by_cols(gathered[:, off1:]), by_cols(gathered[:, :off3]), fold]
        plan = [whole(0), whole(1), whole(2)]

    small_ins = [part_q, rq, ry, h_q, mods_own, seg_q, fc2_b.astype(F32).reshape(1, width), go_q, feat_q, keep_q, b_one, b_two, b_three]
    q_wide = 2 * block + room
    f_own, q_keep, q_send, grad_h, g_mlp, gate_two, g_b1, g_b2, g_b3, g_fc2_b = call(
        functools.partial(proj_kernel, plan, len(pieces), quarter_of),
        [
            shape_of((half, 2 * hidden + width), BF16),
            shape_of((half, 2 * q_wide), BF16),
            shape_of((half, 2 * q_wide), BF16),
            shape_of((half, width), F32),
            shape_of((half, width), BF16),
            shape_of((slots, width), F32),
            shape_of((1, hidden), F32),
            shape_of((1, hidden), F32),
            shape_of((1, 4 * room), F32),
            shape_of((1, width), F32),
        ],
        [meta] + small_ins + pieces,
        in_specs=[SMEM] + [VMEM] * len(small_ins) + [ANY] * len(pieces),
        scratch=[
            pltpu.VMEM((width, hidden), BF16),
            pltpu.VMEM((hidden, hidden), BF16),
            pltpu.VMEM((hidden, 4 * room), BF16),
            pltpu.VMEM((half, hidden), F32),
            pltpu.VMEM((half, hidden), F32),
            pltpu.VMEM((half, hidden), BF16),
            pltpu.VMEM((half, hidden), BF16),
            pltpu.VMEM((half, 4 * room), BF16),
            pltpu.SemaphoreType.DMA((3,)),
        ],
        flops=4 * half * (width * hidden + hidden * hidden + hidden * repr_width),
        name="projector",
    )
    g_mlp_y, g_mlp_c = swap_y(g_mlp), swap_core(g_mlp)
    g_mlp_yc = swap_core(g_mlp_y)
    (f_sent,) = hold([f_own], [g_mlp_y])
    f_y = swap_y(f_sent)
    q_got = swap_core(q_send)
    f_c = swap_core(f_own)
    f_yc = swap_core(f_y)
    q_other = swap_y(jnp.stack([q_keep[:, q_wide:], q_got[:, q_wide:]]))
    low_own, low_y, low_c, low_yc = (a[:, 2 * hidden :] for a in (f_own, f_y, f_c, f_yc))

    def wgrad(place, jobs, ins, outs, name, after=()):
        shapes = [(ins[a].shape[1], ins[b].shape[1]) for a, b, _ in jobs]
        return call(
            functools.partial(wgrad_kernel, place, jobs, len(outs)),
            outs,
            [meta] + ins,
            in_specs=[SMEM] + [VMEM] * len(ins),
            out_specs=[ANY] * len(outs),
            scratch=[pltpu.VMEM(s, BF16) for s in shapes] + [pltpu.SemaphoreType.DMA((len(jobs),))],
            flops=sum(2 * ins[a].shape[0] * r * n for (a, _, _), (r, n) in zip(jobs, shapes)),
            name=name,
            after=after,
        )

    def wgrad_natural(jobs, ins, name, after=()):
        outs = [shape_of((ins[a].shape[1], ins[b].shape[1]), BF16) for a, b, _ in jobs]
        return wgrad(lambda n, g, outs_, meta_: [(g, outs_[n])], jobs, ins, outs, name, after)

    ascending = [1 << n for n in range(n_dp.bit_length() - 1)]
    x_first, x_last = ascending, ascending[1:] + [1]

    def index_of(rel, masks):
        bits = [1 if rel & mask else 0 for mask in masks]
        entry = 0
        for bit in bits[1:]:
            entry = 2 * entry + bit
        return bits[0], entry

    def in_order(rel, masks):
        bits = len(masks)
        cut = rel.reshape((2,) * bits + rel.shape[1:])
        dims = [bits - mask.bit_length() for mask in masks]
        cut = cut.transpose(dims + list(range(bits, cut.ndim))).reshape(rel.shape)
        return cut[:top], cut[top:]

    def wgrad_dp(groups, ins, name, after=()):
        jobs = [job for group, _ in groups for job in group]
        owner = [(n, sum(ins[b].shape[1] for _, b, _ in group[:at])) for n, (group, _) in enumerate(groups) for at in range(len(group))]
        depths = [ins[group[0][0]].shape[1] // n_dp for group, _ in groups]
        widths = [sum(ins[b].shape[1] for _, b, _ in group) for group, _ in groups]
        if all(depth % 16 == 0 for depth in depths) and all(at % 128 == 0 for _, at in owner):

            def place(n, g, outs, meta_):
                group, lo = owner[n]
                depth = depths[group]
                for rel in range(n_dp):
                    at = pl.multiple_of(position(meta_, rel) * depth, 16)
                    side, entry = index_of(rel, groups[group][1])
                    yield g.at[pl.ds(at, depth), :], outs[2 * group + side].at[entry, :, lo : lo + g.shape[1]]

            outs = wgrad(place, jobs, ins, [shape_of((top, depth, w), BF16) for depth, w in zip(depths, widths) for _ in range(2)], name, after)
            return [(outs[2 * n], outs[2 * n + 1]) for n in range(len(groups))]
        nat = list(wgrad_natural(jobs, ins, name, after))
        found = []
        for n, (group, masks) in enumerate(groups):
            one = jnp.concatenate([nat.pop(0) for _ in group], axis=1).reshape(n_dp, depths[n], widths[n])
            found.append(in_order(relative(one), masks))
        return found

    def halves(v):
        return v.reshape((2, v.shape[0] // 2) + v.shape[1:])

    def halve(v, mask):
        return v[0].astype(F32) + flip_dp(v[1].astype(BF16), mask).astype(F32)

    def halve_all(v, masks):
        for mask in masks:
            v = halve(halves(v), mask)
        return v[0]

    f1 = k1 * block // (block + room)

    def proj_grads(after=()):
        ins = [meta, f_own, f_y, f_c, f_yc, q_keep, q_got, q_other]
        whole_rows = aligned and f1 % 32 == 0

        def place(job, g, outs, meta_):
            if not whole_rows:
                yield g, outs[job]
                return
            for rel in range(n_dp):
                side, entry = index_of(rel, x_first)
                to = outs[side].at[entry]
                at = position(meta_, rel)
                if job < 2:
                    columns = slice(0, block) if job == 0 else slice(block, block + room)
                    yield g.at[pl.ds(pl.multiple_of(at * k2, 16), k2), :], to.at[0:k2, columns]
                    continue
                low = f1 // 2
                yield g.at[pl.ds(pl.multiple_of(at * k1, 16), f1), :], to.at[k2 : k2 + f1, 0:block]
                for n in range(2):
                    yield (
                        g.at[pl.ds(pl.multiple_of(at * k1 + f1, 16), low), n * room : (n + 1) * room],
                        to.at[k2 + n * low : k2 + (n + 1) * low, block : block + room],
                    )

        grads = [(hidden, block), (hidden, room), (width, block)]
        shapes = [shape_of((top, k2 + f1, block + room), BF16)] * 2 if whole_rows else [shape_of(g, BF16) for g in grads]
        found = call(
            functools.partial(proj_grad_kernel, hidden, place, len(shapes)),
            shapes,
            ins,
            in_specs=[SMEM] + [ANY] * 7,
            out_specs=[ANY] * len(shapes),
            scratch=[
                pltpu.VMEM((T, 2 * hidden + width), BF16),
                pltpu.VMEM((T, q_wide), BF16),
                *[pltpu.VMEM(g, BF16) for g in grads],
                pltpu.SemaphoreType.DMA((2,)),
                pltpu.SemaphoreType.DMA((3,)),
            ],
            name="grad_projector",
            after=after,
        )
        if whole_rows:
            return found
        two, three, one = found
        one = one.reshape(n_dp, k1, block)
        low = one[:, f1:]
        folded = jnp.concatenate([one[:, :f1], jnp.concatenate([low[..., :room], low[..., room:]], axis=1)], axis=2)
        above = jnp.concatenate([two, three], axis=1).reshape(n_dp, k2, block + room)
        return in_order(relative(jnp.concatenate([above, folded], axis=1)), x_first)

    def unfolded(q):
        low = q[:, :, block:]
        return jnp.concatenate([q[:, :, :block], jnp.concatenate([low[:, : f1 // 2], low[:, f1 // 2 :]], axis=2)], axis=1)

    def quarters(mine):
        mine = mine.astype(BF16)
        other = swap_y(mine)
        c0, c1 = swap_core(mine), swap_core(other)
        own = pair([mine[None], c0[None]], c, 0)
        peer = pair([other[None], c1[None]], c, 0)
        return pair([own, peer], y, 0)

    def side_by_side(q):
        return jnp.concatenate([q[n] for n in range(4)], axis=1).astype(F32)

    g_mlp_full, gpre, part_q, part_y, send, g_fc1_b = call(
        mlp_back_kernel,
        [shape_of((T, width), BF16), shape_of((T, ff), BF16)] + quarter + [shape_of((1, ff), F32)],
        [g_mlp, g_mlp_y, g_mlp_c, g_mlp_yc, pre, fc1_w, fc2_w],
        flops=4 * T * width * ff,
        name="mlp_back",
        after=[f_c, q_got],
    )
    rq, ry = settle_quarter(part_y, send)
    fc2_parts, fc1_parts = wgrad_dp(
        [([(0, 1, 384)], x_last), ([(2, 3, 384)], x_first)], [g_mlp_full, act, m_full, gpre], "grad_fc"
    )
    fc2_got = flip_dp(fc2_parts[1], x_last[0])
    fc1_got = flip_dp(fc1_parts[1], 1)
    pg_first, pg_second = proj_grads(after=[fc1_parts[1]])
    pg_got = flip_dp(pg_second, 1)
    g_one, g_attn, gate_one, shift_two, scale_two, g_out_b = call(
        second_back_kernel,
        [shape_of((half, width), F32), shape_of((half, width), BF16)] + [shape_of((slots, width), F32)] * 3 + [shape_of((1, width), F32)],
        [part_q, rq, ry, grad_h, h_q, attn_q, mods_own, seg_q],
        name="second_back",
        after=[pg_second],
    )
    g_attn_all = spread_quarter(g_attn)
    fc2_got, fc1_got = hold([fc2_got, fc1_got], [g_attn])
    fc2_v = halves(fc2_parts[0].astype(F32) + fc2_got.astype(F32))
    fc2_next = flip_dp(fc2_v[1].astype(BF16), x_last[1])
    fc1_v = halves(fc1_parts[0].astype(F32) + fc1_got.astype(F32))
    fc1_next = flip_dp(fc1_v[1].astype(BF16), 2)

    gqkv, part_q, part_y, send, g_qv_b, g_attn_full = call(
        functools.partial(bwd_kernel, heads),
        [shape_of((T, -(-3 * wide // 128) * 128), BF16)] + quarter + [shape_of((2, wide), F32), shape_of((T, width), BF16)],
        list(g_attn_all) + [out_w, q, k, v, seg_cols, seg_rows, val_rows, qkv_t],
        flops=8 * T * width * wide + 10 * T * seq * wide,
        name="attention_back",
    )
    rq, ry = settle_quarter(part_y, send)
    ((heads_first, heads_second),) = wgrad_dp(
        [([(0, 1, 384), (2, 3, 384)], x_first)], [m_one, gqkv, g_attn_full, mixed], "grad_heads", after=[]
    )
    g_in, shift_one, scale_one = call(
        first_back_kernel,
        [shape_of((half, width), BF16)] + [shape_of((slots, width), F32)] * 2,
        [order, part_q, rq, ry, g_one, hid, mods_own, seg_q],
        in_specs=[SMEM] + [VMEM] * 7,
        name="first_back",
        after=[heads_second],
    )
    heads_got = flip_dp(heads_second, 1)

    fc2_next, fc1_next, pg_got = hold([fc2_next, fc1_next, pg_got], [g_in])
    pg_v = halves(pg_first.astype(F32) + pg_got.astype(F32))
    pg_sent = pg_v[1].astype(BF16)
    pg_got = flip_dp(pg_sent, 2)
    fc2_v = fc2_v[0] + fc2_next.astype(F32)
    fc1_v = halves(fc1_v[0] + fc1_next.astype(F32))
    fc2_v = halves(fc2_v)
    fc2_last = flip_dp(fc2_v[1].astype(BF16), x_last[2])
    fc1_last = flip_dp(fc1_v[1].astype(BF16), x_first[2])

    g_mod = jnp.concatenate([shift_one, scale_one, gate_one, shift_two, scale_two, gate_two], axis=-1)
    g_b3 = g_b3.reshape(4, room)[:, :third].reshape(1, repr_width)
    early = jnp.concatenate([g_b1, g_b2, g_b3, g_fc2_b, g_out_b], axis=1)
    early = early + swap_core(early)
    line = jnp.concatenate([g_mod.reshape(1, -1), early], axis=1)
    (line,) = hold([line], [pg_sent])
    line = line + swap_y(line)
    g_mod, early = line[:, : slots * 6 * width].reshape(slots, -1).astype(BF16), line[:, slots * 6 * width :]
    g_mod = exchange_dp(g_mod.reshape(slots, n_dp, -1).transpose(1, 0, 2))
    heads_got, g_in = hold([heads_got, g_in], [g_mod])
    heads_v = halves(heads_first.astype(F32) + heads_got.astype(F32))
    heads_sent = heads_v[1].astype(BF16)
    heads_got = flip_dp(heads_sent, 2)
    pg_v = halves(pg_v[0] + pg_got.astype(F32))
    pg_sent = pg_v[1].astype(BF16)
    pg_got = flip_dp(pg_sent, 4)
    fc2_last, fc1_last = hold([fc2_last, fc1_last], [g_mod])
    (g_mod,) = hold([g_mod], [heads_sent, pg_sent])
    g_mod = pair([g_mod, swap_core(g_mod)], c, 1).reshape(n_dp * images, -1)
    g_ada_w = lax.dot_general(g_mod, cond_act, (((0,), (1,)), ((), ())), preferred_element_type=F32)
    g_ada_b = jnp.sum(g_mod.astype(F32), axis=0)
    g_cond = lax.dot_general(ada_w, g_mod, (((0,), (1,)), ((), ())), preferred_element_type=F32)
    own = jnp.concatenate([early, g_fc1_b, g_qv_b.reshape(1, 2 * wide)], axis=1)
    sent = jnp.concatenate([g_cond.reshape(n_dp, feats * n_images), jnp.broadcast_to(own, (n_dp, own.shape[1]))], axis=1)
    sums = exchange_dp(sent)
    heads_v = halves(heads_v[0] + heads_got.astype(F32))
    heads_sent = heads_v[1].astype(BF16)
    heads_got = flip_dp(heads_sent, 4)
    mine = halve_all(pg_v[0] + pg_got.astype(F32), x_first[3:]).astype(BF16)
    found = quarters(mine)
    (sums,) = hold([sums], [heads_sent, mine])
    sums = jnp.sum(sums, axis=0)
    g_fc2_t = halve_all(fc2_v[0] + fc2_last.astype(F32), x_last[3:])
    g_fc1 = halve_all(fc1_v[0] + fc1_last.astype(F32), x_first[3:])
    g_heads = halve_all(heads_v[0] + heads_got.astype(F32), x_first[3:])
    g_qkv, g_out_t = g_heads[:, : 3 * wide], g_heads[:, gqkv.shape[1] :]
    g_w2 = side_by_side(found[:, :k2, :block])
    g_w3 = side_by_side(found[:, :k2, block : block + third])
    g_w1 = side_by_side(unfolded(found[:, k2:]))
    g_cond, sums = sums[: feats * n_images].reshape(feats, n_images), sums[feats * n_images :]
    g_cond = g_cond * silu_slope(condition)
    g_table = lax.dot_general(
        g_cond, class_hot.astype(F32), (((1,), (1,)), ((), ())), precision=lax.Precision.HIGHEST, preferred_element_type=F32
    )

    cuts = [hidden, hidden, repr_width, width, width, ff, 2 * wide]
    marks = [sum(cuts[:n]) for n in range(len(cuts) + 1)]
    s_one_b, s_two_b, s_three_b, s_fc2_b, s_out_b, s_fc1_b, s_qv_b = (sums[lo:hi] for lo, hi in zip(marks, marks[1:]))

    def my_part(x, n):
        return lax.dynamic_slice_in_dim(x.reshape(-1), d * n, n)

    s_b1, s_b2, s_b3 = my_part(s_one_b, n1), my_part(s_two_b, n2), my_part(s_three_b, n3)
    s_qv_b = s_qv_b.reshape(2, wide)

    def spread_tokens(block, other, c0, c1):
        own = pair([block, other], y, 0)
        peer = pair([c0, c1], y, 0)
        return pair([own, peer], c, 0).reshape(micro_count, rows_dev, seq, width)

    block_out = spread_tokens(low_own, low_y, low_c, low_yc)
    grad_in = spread_tokens(*spread_quarter(g_in)).astype(F32)
    depth = width // n_dp
    return (
        block_out,
        grad_in,
        g_table,
        g_ada_w,
        g_ada_b,
        jnp.stack([g_qkv[:, :wide], g_qkv[:, wide : 2 * wide], g_qkv[:, 2 * wide :]]),
        s_qv_b,
        g_out_t.T,
        s_out_b,
        g_fc1,
        s_fc1_b,
        g_fc2_t.T,
        s_fc2_b,
        g_w1,
        s_b1,
        g_w2,
        s_b2,
        g_w3,
        s_b3,
    )


def solution(mesh):
    dp, tensor = "dp", "tensor"
    rows4, rows3 = P(None, dp, None, None), P(None, dp, None)
    ins = (rows4, rows4, rows4, rows3, rows3, rows3, rows3, P(dp, None), P(dp, None), P(dp), P(None, None, tensor), P(None, tensor), P(tensor, None), P(), P(None, tensor), P(tensor), P(tensor, None), P(), P(dp, None), P(dp), P(dp, None), P(dp), P(dp, None), P(dp))
    outs = (rows4, rows4, P(dp, None), P(dp, None), P(dp), P(None, dp, tensor), P(None, tensor), P(tensor, dp), P(), P(dp, tensor), P(tensor), P(tensor, dp), P(), P(dp, None), P(dp), P(dp, None), P(dp), P(dp, None), P(dp))
    return jax.shard_map(functools.partial(body, mesh), mesh=mesh, in_specs=ins, out_specs=outs, check_vma=False)
```

time: 509 us -> 430 us (0.84)
  waiting for transfers between devices: 241 us -> 163 us
  starting transfers between devices: 79.7 us -> 53.1 us
  local copies, waits for them, and re-layouts: 34.8 us -> 60 us
  Pallas kernels: 95 us -> 87.3 us
  other arithmetic: 32.7 us -> 38.4 us
    ppermute x43 -> x12, waiting for transfers between devices: 135 us -> 51.6 us  [flip_dp(): return lax.ppermute(x, 'dp', [(k, k ^ mask) for k in range(n_dp)])]
    ppermute x43 -> x12, starting transfers between devices: 61.9 us -> 14.1 us  [flip_dp(): return lax.ppermute(x, 'dp', [(k, k ^ mask) for k in range(n_dp)])]
    all_to_all x0 -> x5, waiting for transfers between devices: none -> 37.9 us  [exchange_dp(): return lax.all_to_all(x, 'dp', 0, 0, tiled=True)]
    ppermute x15 -> x13, waiting for transfers between devices: 84.2 us -> 54 us  [swap_y(): return lax.ppermute(x, 'tensor', [(0, 2), (2, 0), (1, 3), (3, 1)])]
    all_to_all x0 -> x5, starting transfers between devices: none -> 23.2 us  [exchange_dp(): return lax.all_to_all(x, 'dp', 0, 0, tiled=True)]
    unnamed x121 -> x162, local copies, waits for them, and re-layouts: 11.1 us -> 22.5 us
    pallas_call x13 -> x19, Pallas kernels: 95 us -> 87.3 us  [the longest x11 87.3 us: call(): pl.pallas_call(kernel, out_shape=tuple(outs), in_specs=list(in_specs or [...]
    ppermute x15 -> x13, starting transfers between devices: 13.7 us -> 13.7 us  [swap_y(): return lax.ppermute(x, 'tensor', [(0, 2), (2, 0), (1, 3), (3, 1)])]
  transfers between devices with their start and end apart: 85 -> 51, of which waited for: 42 -> 27; matrix products, arithmetic and copies ran while one was open for 12% -> 19% of each run, Pallas kernels for 16% -> 17%
where the time goes in v3:
time: 430 us; the launch traced here: 426 us
  waiting for transfers between devices  163 us (38%)
  Pallas kernels  87.3 us (20%)
  local copies, waits for them, and re-layouts  60 us (14%)
  starting transfers between devices  53.1 us (12%)
  other arithmetic  38.4 us (9%)
  between operations  15.4 us (4%)
  matrix products  8.55 us (2%)
    pallas_call x11, Pallas kernels, call(): pl.pallas_call(kernel, out_shape=tuple(outs), in_specs=list(in_specs or [...  87.3 us
    ppermute x13, waiting for transfers between devices, swap_y(): return lax.ppermute(x, 'tensor', [(0, 2), (2, 0), (1, 3), (3, 1)])  54 us
    ppermute x12, waiting for transfers between devices, flip_dp(): return lax.ppermute(x, 'dp', [(k, k ^ mask) for k in range(n_dp)])  51.6 us
    all_to_all x5, waiting for transfers between devices, exchange_dp(): return lax.all_to_all(x, 'dp', 0, 0, tiled=True)  37.9 us
    all_to_all x5, starting transfers between devices, exchange_dp(): return lax.all_to_all(x, 'dp', 0, 0, tiled=True)  23.2 us
    unnamed x162, local copies, waits for them, and re-layouts  22.5 us
    ppermute x12, starting transfers between devices, flip_dp(): return lax.ppermute(x, 'dp', [(k, k ^ mask) for k in range(n_dp)])  14.1 us
    all_gather x1, waiting for transfers between devices, body(): gathered = lax.all_gather(packed, ('dp', 'tensor'), axis=0)  13.9 us
  transfers between devices with their start and end apart: 51, of which 27 were waited for; matrix products, arithmetic and copies ran while one was open for 19% of the time, Pallas kernels for 17%

profile of v3, /device:TPU:0, one launch (start us, length us, event | category | flops | bytes accessed | tf_op | source)
XLA Modules:
  0.0 425.6 jit_solution(7794295553448569204)
XLA Ops:
  14.1 7.3 %all-to-all-start = ((s32[8,1,16]{2,1,0:T(1,128)}), s32[8,1,16]{2,1,0:T(1,128)S(1)}, u32[]{:S(2)}, u32[]{:S(2)}) async-start(s32[8,1,16]{2,1,0:T(1,128)} %broadcast_in_dim.17), calls=%async_computation | async-start | bytes 8192 | tf_op jit(solution)/shard_map/all_to_all | solution.py:421
  21.6 6.1 %all-to-all-done = s32[8,1,16]{2,1,0:T(1,128)S(1)} async-done(((s32[8,1,16]{2,1,0:T(1,128)}), s32[8,1,16]{2,1,0:T(1,128)S(1)}, u32[]{:S(2)}, u32[]{:S(2)}) %all-to-all-start) | async-done | bytes 544 | tf_op jit(solution)/shard_map/all_to_all | solution.py:421
  29.8 3.4 all-to-all-start.1
  34.8 9.7 %all-to-all-done.1 = bf16[8,154,64]{1,2,0:T(8,128)(2,1)S(1)} async-done(((bf16[8,154,64]{1,2,0:T(8,128)(2,1)}), bf16[8,154,64]{1,2,0:T(8,128)(2,1)S(1)}, u32[]{:S(2)}, u32[]{:S(2)}) %all-to-all-start.1) | async-done | bytes 157728 | tf_op jit(solution)/shard_map/all_to_all | solution.py:421
  46.4 3.9 all-to-all-start.2
  53.7 11.4 %all-to-all-done.2 = f32[8,8,864]{2,1,0:T(8,128)S(1)} async-done(((f32[8,8,864]{2,1,0:T(8,128)}), f32[8,8,864]{2,1,0:T(8,128)S(1)}, u32[]{:S(2)}, u32[]{:S(2)}) %all-to-all-start.2) | async-done | bytes 221216 | tf_op jit(solution)/shard_map/all_to_all | solution.py:421
  66.0 9.8 %attention.1 = (bf16[512,1152]{1,0:T(8,128)(2,1)}, bf16[512,288]{1,0:T(8,128)(2,1)}, bf16[512,288]{1,0:T(8,128)(2,1)}, bf16[512,288]{1,0:T(8,128)(2,1)}, bf16[512,288]{1,0:T(8,128)(2,1)}) custom-call(s32[4]{0:T(128)} %pad_add_fusion.3.refs_0_, bf16[4,128,1152]{2,1,0:T(8,128)(2,1)} %bitcast.160, f32[4,6912]{1,0:T(4,128)} %get-tuple-element.275.refs_2_.refs_5_.refs_6_, ...), custom_call_target="tpu_custom_call" | custom-call | tf_op jit(solution)/shard_map/attention/pallas_call | solution.py:36
  80.5 4.2 collective-permute-done.1.refs_6_
  84.8 6.4 %collective-permute-done.2.refs_7_ = bf16[256,288]{1,0:T(8,128)(2,1)S(1)} collective-permute-done((bf16[256,288]{1,0:T(8,128)(2,1)S(1)}, bf16[256,288]{1,0:T(8,128)(2,1)S(1)}, u32[]{:S(2)}, u32[]{:S(2)}) %collective-permute-start.2) | collective-permute-done | bytes 147488 | tf_op jit(solution)/shard_map/ppermute | solution.py:415
  91.8 5.8 %middle.1 = (f32[128,1152]{1,0:T(8,128)}, f32[128,1152]{1,0:T(8,128)}, bf16[256,1152]{1,0:T(8,128)(2,1)}) custom-call(s32[4]{0:T(128)} %pad_add_fusion.3.refs_0_, bf16[4,128,1152]{2,1,0:T(8,128)(2,1)} %bitcast.161, f32[4,6912]{1,0:T(4,128)} %get-tuple-element.275.refs_2_.refs_5_.refs_6_, s32[512,1]{1,0:T(8,128)} %copy.120.refs_4_.refs_3_.refs_8_, ...), custom_call_target="tpu_custom_call" | custom-call | tf_op jit(solution)/shard_map/middle/pallas_call | solution.py:36
  100.6 7.9 %mlp.1 = (bf16[512,1152]{1,0:T(8,128)(2,1)}, f32[512,1152]{1,0:T(8,128)}, bf16[512,1152]{1,0:T(8,128)(2,1)}, f32[128,1152]{1,0:T(8,128)}, f32[128,1152]{1,0:T(8,128)}, /*index=5*/bf16[256,1152]{1,0:T(8,128)(2,1)}) custom-call(bf16[256,1152]{1,0:T(8,128)(2,1)} %get-tuple-element.82.refs_0_, bf16[256,1152]{1,0:T(8,128)(2,1)} %copy-done.33, ...), custom_call_target="tpu_custom_call" | custom-call | tf_op jit(solution)/shard_map/mlp/pallas_call | solution.py:36
  113.5 1.7 dynamic-slice_bitcast_fusion.refs_8_
  117.2 2.5 collective-permute-start.8
  121.6 5.6 %collective-permute-done.8.refs_3_ = bf16[128,1152]{1,0:T(8,128)(2,1)S(1)} collective-permute-done((bf16[128,1152]{1,0:T(8,128)(2,1)S(1)}, bf16[128,1152]{1,0:T(8,128)(2,1)S(1)}, u32[]{:S(2)}, u32[]{:S(2)}) %collective-permute-start.8) | collective-permute-done | bytes 294944 | tf_op jit(solution)/shard_map/ppermute | solution.py:415
  127.2 13.9 %all-gather.3.cloned.1.call-done = bf16[16896,512]{1,0:T(8,128)(2,1)} async-done(((bf16[528,512]{1,0:T(8,128)(2,1)}), bf16[16896,512]{1,0:T(8,128)(2,1)}) %all-gather.3.cloned.1.call-update) | async-done | bytes 17301520 | tf_op jit(solution)/shard_map/all_gather | solution.py:443
  141.2 15.7 %projector.1 = (bf16[128,5248]{1,0:T(8,128)(2,1)}, bf16[128,2560]{1,0:T(8,128)(2,1)}, bf16[128,2560]{1,0:T(8,128)(2,1)}, f32[128,1152]{1,0:T(8,128)}, bf16[128,1...) custom-call(s32[4]{0:T(128)} %pad_add_fusion.2.refs_0_, ...), custom_call_target="tpu_custom_call" | custom-call | tf_op jit(solution)/shard_map/projector/pallas_call | solution.py:36
  158.7 7.7 %collective-permute-done.9.refs_1_ = bf16[128,1152]{1,0:T(8,128)(2,1)S(1)} collective-permute-done((bf16[128,1152]{1,0:T(8,128)(2,1)}, bf16[128,1152]{1,0:T(8,128)(2,1)S(1)}, u32[]{:S(2)}, u32[]{:S(2)}) %collective-permute-start.9) | collective-permute-done | bytes 294944 | tf_op jit(solution)/shard_map/ppermute | solution.py:415
  167.9 1.7 slice_bitcast_fusion.1
  171.0 1.7 collective-permute-done.14.refs_3_
  173.5 9.0 %mlp_back.1 = (bf16[512,1152]{1,0:T(8,128)(2,1)}, bf16[512,1152]{1,0:T(8,128)(2,1)}, f32[128,1152]{1,0:T(8,128)}, f32[128,1152]{1,0:T(8,128)}, bf16[256,1152]{1,0:T(8,128)(2,1)}, /*index=5*/f32[1,1152]{1,0:T(1,128)}) custom-call(bf16[128,1152]{1,0:T(8,128)(2,1)} %get-tuple-element.88.refs_0_, bf16[128,1152]{1,0:T(8,128)(2,1)} %copy-done.6, ...), custom_call_target="tpu_custom_call" | custom-call | tf_op jit(solution)/shard_map/mlp_back/pallas_call | solution.py:36
  182.6 7.1 %grad_fc.1 = (bf16[4,144,1152]{2,1,0:T(8,128)(2,1)}, bf16[4,144,1152]{2,1,0:T(8,128)(2,1)}, bf16[4,144,1152]{2,1,0:T(8,128)(2,1)}, bf16[4,144,1152]{2,1,0:T(8,128)(2,1)}) custom-call(s32[4]{0:T(128)} %pad_add_fusion.2.refs_0_, bf16[512,1152]{1,0:T(8,128)(2,1)} %get-tuple-element.98.refs_1_, bf16[512,1152]{1,0:T(8,128)(2,1)} %get-tuple-element.99.refs_2_, ...), custom_call_target="tpu_custom_call" | custom-call | tf_op jit(solution)/shard_map/grad_fc/pallas_call | solution.py:36
  192.3 5.7 %collective-permute-done.10.refs_2_ = bf16[128,5248]{1,0:T(8,128)(2,1)} collective-permute-done((bf16[128,5248]{1,0:T(8,128)(2,1)S(1)}, bf16[128,5248]{1,0:T(8,128)(2,1)}, u32[]{:S(2)}, u32[]{:S(2)}) %collective-permute-start.10) | collective-permute-done | bytes 1343520 | tf_op jit(solution)/shard_map/ppermute | solution.py:415
  200.8 1.7 add_convert_fusion.1
  204.0 2.0 broadcast_select_fusion.13
  205.9 11.9 %collective-permute-done.18.refs_7_ = bf16[2,128,1280]{2,1,0:T(8,128)(2,1)} collective-permute-done((bf16[2,128,1280]{2,1,0:T(8,128)(2,1)S(1)}, bf16[2,128,1280]{2,1,0:T(8,128)(2,1)}, u32[]{:S(2)}, u32[]{:S(2)}) %collective-permute-start.18) | collective-permute-done | bytes 655392 | tf_op jit(solution)/shard_map/ppermute | solution.py:415
  218.9 7.0 %grad_projector.1 = (bf16[4,352,768]{2,1,0:T(8,128)(2,1)}, bf16[4,352,768]{2,1,0:T(8,128)(2,1)}) custom-call(s32[4]{0:T(128)} %pad_add_fusion.2.refs_0_, bf16[128,5248]{1,0:T(8,128)(2,1)} %get-tuple-element.87.refs_1_, bf16[128,5248]{1,0:T(8,128)(2,1)} %collective-permute-done.10.refs_2_, bf16[128,5248]{1,0:T(8,128)(2,1)} %collective-permute-done.11.refs_7_.refs_3_, ...), custom_call_target="tpu_custom_call" | custom-call | tf_op jit(solution)/shard_map/grad_projector/pallas_call | solution.py:36
  225.9 4.4 %second_back.1 = (f32[128,1152]{1,0:T(8,128)}, bf16[128,1152]{1,0:T(8,128)(2,1)}, f32[4,1152]{1,0:T(4,128)}, f32[4,1152]{1,0:T(4,128)}, f32[4,1152]{1,0:T(4,128)}, /*index=5*/f32[1,1152]{1,0:T(1,128)}) custom-call(f32[128,1152]{1,0:T(8,128)} %get-tuple-element.92.refs_0_, bf16[256,1152]{1,0:T(8,128)(2,1)} %collective-permute-done.16.refs_1_, ...), custom_call_target="tpu_custom_call" | custom-call | tf_op jit(solution)/shard_map/second_back/pallas_call | solution.py:36
  235.2 3.5 collective-permute-done.19.refs_1_
  244.0 11.6 %attention_back.1 = (bf16[512,896]{1,0:T(8,128)(2,1)}, f32[128,1152]{1,0:T(8,128)}, f32[128,1152]{1,0:T(8,128)}, bf16[256,1152]{1,0:T(8,128)(2,1)}, f32[2,288]{1,0:T(2,128)}, /*index=5*/bf16[512,1152]{1,0:T(8,128)(2,1)}) custom-call(bf16[128,1152]{1,0:T(8,128)(2,1)} %get-tuple-element.104.refs_0_.refs_2_, bf16[128,1152]{1,0:T(8,128)(2,1)} %copy-done.38, ...), custom_call_target="tpu_custom_call" | custom-call | tf_op jit(solution)/shard_map/attention_back/pallas_call | solution.py:36
  261.2 5.0 %grad_heads.1 = (bf16[4,144,1184]{2,1,0:T(8,128)(2,1)}, bf16[4,144,1184]{2,1,0:T(8,128)(2,1)}) custom-call(s32[4]{0:T(128)} %pad_add_fusion.2.refs_0_, bf16[512,1152]{1,0:T(8,128)(2,1)} %get-tuple-element.89.refs_1_, bf16[512,896]{1,0:T(8,128)(2,1)} %get-tuple-element.108.refs_2_, bf16[512,1152]{1,0:T(8,128)(2,1)} %get-tuple-element.109.refs_3_, ...), custom_call_target="tpu_custom_call" | custom-call | tf_op jit(solution)/shard_map/grad_heads/pallas_call | solution.py:36
  268.2 3.8 first_back.1
  274.4 6.7 %collective-permute-done.30.refs_2_ = bf16[4,352,768]{2,1,0:T(8,128)(2,1)} collective-permute-done((bf16[4,352,768]{2,1,0:T(8,128)(2,1)}, bf16[4,352,768]{2,1,0:T(8,128)(2,1)}, u32[]{:S(2)}, u32[]{:S(2)}) %collective-permute-start.30) | collective-permute-done | bytes 2162720 | tf_op jit(solution)/shard_map/ppermute | solution.py:412
  283.6 2.0 convert_add_fusion
  296.0 4.4 %all-to-all-start.3 = ((bf16[8,4,864]{2,1,0:T(4,128)(2,1)}), bf16[8,4,864]{2,1,0:T(4,128)(2,1)S(1)}, u32[]{:S(2)}, u32[]{:S(2)}) async-start(bf16[8,4,864]{2,1,0:T(4,128)(2,1)} %bitcast.178), calls=%async_computation.3 | async-start | bytes 114688 | tf_op jit(solution)/shard_map/all_to_all | solution.py:421
  300.4 1.6 slice_add_fusion.2
  302.9 2.0 collective-permute-start.40
  305.7 7.1 %collective-permute-done.22.refs_0_ = bf16[4,144,1184]{2,1,0:T(8,128)(2,1)S(1)} collective-permute-done((bf16[4,144,1184]{2,1,0:T(8,128)(2,1)}, bf16[4,144,1184]{2,1,0:T(8,128)(2,1)S(1)}, u32[]{:S(2)}, u32[]{:S(2)}) %collective-permute-start.22) | collective-permute-done | bytes 1364000 | tf_op jit(solution)/shard_map/ppermute | solution.py:412
  312.7 8.7 %all-to-all-done.3.refs_2_.refs_0_ = bf16[8,4,864]{2,1,0:T(4,128)(2,1)S(1)} async-done(((bf16[8,4,864]{2,1,0:T(4,128)(2,1)}), bf16[8,4,864]{2,1,0:T(4,128)(2,1)S(1)}, u32[]{:S(2)}, u32[]{:S(2)}) %all-to-all-start.3) | async-done | bytes 55328 | tf_op jit(solution)/shard_map/all_to_all | solution.py:421
  325.8 1.9 fusion.14
  327.8 2.0 fusion.15
  335.5 8.1 %collective-permute-done.37 = bf16[2,144,1184]{2,1,0:T(8,128)(2,1)S(1)} collective-permute-done((bf16[2,144,1184]{2,1,0:T(8,128)(2,1)S(1)}, bf16[2,144,1184]{2,1,0:T(8,128)(2,1)S(1)}, u32[]{:S(2)}, u32[]{:S(2)}) %collective-permute-start.37) | collective-permute-done | bytes 682016 | tf_op jit(solution)/shard_map/ppermute | solution.py:412
  344.6 2.2 collective-permute-start.38
  351.8 3.6 fusion.26
  356.8 4.2 all-to-all-start.4
  361.7 18.9 %collective-permute-done.39 = bf16[1,144,1184]{2,1,0:T(8,128)(2,1)} collective-permute-done((bf16[1,144,1184]{2,1,0:T(8,128)(2,1)S(1)}, bf16[1,144,1184]{2,1,0:T(8,128)(2,1)}, u32[]{:S(2)}, u32[]{:S(2)}) %collective-permute-start.39) | collective-permute-done | bytes 341024 | tf_op jit(solution)/shard_map/ppermute | solution.py:412
  381.9 10.3 %collective-permute-done.38 = bf16[1,352,768]{2,1,0:T(8,128)(2,1)} collective-permute-done((bf16[1,352,768]{2,1,0:T(8,128)(2,1)S(1)}, bf16[1,352,768]{2,1,0:T(8,128)(2,1)}, u32[]{:S(2)}, u32[]{:S(2)}) %collective-permute-start.38) | collective-permute-done | bytes 540704 | tf_op jit(solution)/shard_map/ppermute | solution.py:412
  396.4 2.0 all-to-all-done.4
  400.2 7.8 %collective-permute-done.43 = bf16[352,768]{1,0:T(8,128)(2,1)} collective-permute-done((bf16[352,768]{1,0:T(8,128)(2,1)S(1)}, bf16[352,768]{1,0:T(8,128)(2,1)}, u32[]{:S(2)}, u32[]{:S(2)}) %collective-permute-start.43) | collective-permute-done | bytes 540704 | tf_op jit(solution)/shard_map/ppermute | solution.py:415
  (380 shorter events, 117.3 us)
Async XLA Ops:
  7.2 134.0 %all-gather.3.cloned.1.call-start = ((), (), s32[]{:S(2)}) async-start(), calls=%async_computation.5 | async-start | bytes 17842176 | tf_op jit(solution)/shard_map/all_gather | solution.py:443
  14.1 13.6 %all-to-all-start = ((s32[8,1,16]{2,1,0:T(1,128)}), s32[8,1,16]{2,1,0:T(1,128)S(1)}, u32[]{:S(2)}, u32[]{:S(2)}) async-start(s32[8,1,16]{2,1,0:T(1,128)} %broadcast_in_dim.17), calls=%async_computation | async-start | bytes 8192 | tf_op jit(solution)/shard_map/all_to_all | solution.py:421
  29.8 14.8 %all-to-all-start.1 = ((bf16[8,154,64]{1,2,0:T(8,128)(2,1)}), bf16[8,154,64]{1,2,0:T(8,128)(2,1)S(1)}, u32[]{:S(2)}, u32[]{:S(2)}) async-start(bf16[8,154,64]{1,2,0:T(8,128)(2,1)} %broadcast_in_dim.18), calls=%async_computation.1 | async-start | bytes 524288 | tf_op jit(solution)/shard_map/all_to_all | solution.py:421
  33.2 20.5 %collective-permute-start.4 = (bf16[288,1152]{1,0:T(8,128)(2,1)S(1)}, bf16[288,1152]{1,0:T(8,128)(2,1)}, u32[]{:S(2)}, u32[]{:S(2)}) collective-permute-start(bf16[288,1152]{1,0:T(8,128)(2,1)S(1)} %copy-done.17), channel_id=1, source_target_pairs={{0,2},{2,0},{1,3},{3,1},{4,6},{6,4},{5,7},{7,5},{8,10},{10,8},{9,1... | collective-permute-start | bytes 1990664 | tf_op jit(solution)/shard_map/ppermute | solution.py:415
  34.8 45.7 %collective-permute-start.3 = (bf16[288,1152]{1,0:T(8,128)(2,1)S(1)}, bf16[288,1152]{1,0:T(8,128)(2,1)}, u32[]{:S(2)}, u32[]{:S(2)}) collective-permute-start(bf16[288,1152]{1,0:T(8,128)(2,1)S(1)} %copy-done.17), channel_id=1, source_target_pairs={{0,1},{1,0},{2,3},{3,2},{4,5},{5,4},{6,7},{7,6},{8,9},{9,8},{10,11... | collective-permute-start | bytes 1990664 | tf_op jit(solution)/shard_map/ppermute | solution.py:418
  46.4 18.7 %all-to-all-start.2 = ((f32[8,8,864]{2,1,0:T(8,128)}), f32[8,8,864]{2,1,0:T(8,128)S(1)}, u32[]{:S(2)}, u32[]{:S(2)}) async-start(f32[8,8,864]{2,1,0:T(8,128)} %fusion.6), calls=%async_computation.2 | async-start | bytes 458752 | tf_op jit(solution)/shard_map/all_to_all | solution.py:421
  53.7 37.4 %collective-permute-start.5 = (bf16[288,1152]{1,0:T(8,128)(2,1)}, bf16[288,1152]{1,0:T(8,128)(2,1)}, u32[]{:S(2)}, u32[]{:S(2)}) collective-permute-start(bf16[288,1152]{1,0:T(8,128)(2,1)} %collective-permute-done.4.refs_10_), channel_id=1, source_target_pairs={{0,1},{1,0},{2,3},{3,2},{4,5},{5,4},{6,7},{7,6},{8,9},{9,8},{10,11... | collective-permute-start | bytes 1990664 | tf_op jit(solution)/shard_map/ppermute | solution.py:418
  77.0 7.8 %collective-permute-start.1 = (bf16[256,288]{1,0:T(8,128)(2,1)S(1)}, bf16[256,288]{1,0:T(8,128)(2,1)S(1)}, u32[]{:S(2)}, u32[]{:S(2)}) collective-permute-start(bf16[256,288]{1,0:T(8,128)(2,1)S(1)} %get-tuple-element.273.refs_4_), channel_id=1, source_target_pairs={{0,2},{2,0},{1,3},{3,1},{4,6},{6,4},{5,7},{7,5},{8,10},{10,8},{9,1... | collective-permute-start | bytes 442376 | tf_op jit(solution)/shard_map/ppermute | solution.py:415
  78.5 12.6 %collective-permute-start.2 = (bf16[256,288]{1,0:T(8,128)(2,1)S(1)}, bf16[256,288]{1,0:T(8,128)(2,1)S(1)}, u32[]{:S(2)}, u32[]{:S(2)}) collective-permute-start(bf16[256,288]{1,0:T(8,128)(2,1)S(1)} %collective-permute-done.refs_5_), channel_id=1, source_target_pairs={{0,2},{2,0},{1,3},{3,1},{4,6},{6,4},{5,7},{7,5},{8,10},{10,8},{9,1... | collective-permute-start | bytes 442376 | tf_op jit(solution)/shard_map/ppermute | solution.py:415
  97.6 2.2 collective-permute-start.6
  108.6 8.5 %collective-permute-start.7 = (bf16[256,1152]{1,0:T(8,128)(2,1)}, bf16[256,1152]{1,0:T(8,128)(2,1)S(1)}, u32[]{:S(2)}, u32[]{:S(2)}) collective-permute-start(bf16[256,1152]{1,0:T(8,128)(2,1)} %get-tuple-element.84), channel_id=1, source_target_pairs={{0,1},{1,0},{2,3},{3,2},{4,5},{5,4},{6,7},{7,6},{8,9},{9,8},{10,11... | collective-permute-start | bytes 1769480 | tf_op jit(solution)/shard_map/ppermute | solution.py:418
  117.2 10.0 %collective-permute-start.8 = (bf16[128,1152]{1,0:T(8,128)(2,1)S(1)}, bf16[128,1152]{1,0:T(8,128)(2,1)S(1)}, u32[]{:S(2)}, u32[]{:S(2)}) collective-permute-start(bf16[128,1152]{1,0:T(8,128)(2,1)S(1)} %add_convert_fusion.2), channel_id=1, source_target_pairs={{0,2},{2,0},{1,3},{3,1},{4,6},{6,4},{5,7},{7,5},{8,10},{10,8},{9,1... | collective-permute-start | bytes 884744 | tf_op jit(solution)/shard_map/ppermute | solution.py:415
  156.9 9.5 %collective-permute-start.9 = (bf16[128,1152]{1,0:T(8,128)(2,1)}, bf16[128,1152]{1,0:T(8,128)(2,1)S(1)}, u32[]{:S(2)}, u32[]{:S(2)}) collective-permute-start(bf16[128,1152]{1,0:T(8,128)(2,1)} %get-tuple-element.88.refs_0_), channel_id=1, source_target_pairs={{0,2},{2,0},{1,3},{3,1},{4,6},{6,4},{5,7},{7,5},{8,10},{10,8},{9,1... | collective-permute-start | bytes 884744 | tf_op jit(solution)/shard_map/ppermute | solution.py:415
  157.0 15.8 %collective-permute-start.11 = (bf16[128,5248]{1,0:T(8,128)(2,1)}, bf16[128,5248]{1,0:T(8,128)(2,1)}, u32[]{:S(2)}, u32[]{:S(2)}) collective-permute-start(bf16[128,5248]{1,0:T(8,128)(2,1)} %get-tuple-element.87.refs_1_), channel_id=1, source_target_pairs={{0,1},{1,0},{2,3},{3,2},{4,5},{5,4},{6,7},{7,6},{8,9},{9,8},{10,11... | collective-permute-start | bytes 4030472 | tf_op jit(solution)/shard_map/ppermute | solution.py:418
  167.1 31.0 %collective-permute-start.10 = (bf16[128,5248]{1,0:T(8,128)(2,1)S(1)}, bf16[128,5248]{1,0:T(8,128)(2,1)}, u32[]{:S(2)}, u32[]{:S(2)}) collective-permute-start(bf16[128,5248]{1,0:T(8,128)(2,1)S(1)} %hold.8), channel_id=1, source_target_pairs={{0,2},{2,0},{1,3},{3,1},{4,6},{6,4},{5,7},{7,5},{8,10},{10,8},{9,1... | collective-permute-start | bytes 4030472 | tf_op jit(solution)/shard_map/ppermute | solution.py:415
  167.4 3.6 collective-permute-start.13
  167.4 5.4 %collective-permute-start.15 = (bf16[128,2560]{1,0:T(8,128)(2,1)}, bf16[128,2560]{1,0:T(8,128)(2,1)}, u32[]{:S(2)}, u32[]{:S(2)}) collective-permute-start(bf16[128,2560]{1,0:T(8,128)(2,1)} %get-tuple-element.91), channel_id=1, source_target_pairs={{0,1},{1,0},{2,3},{3,2},{4,5},{5,4},{6,7},{7,6},{8,9},{9,8},{10,11... | collective-permute-start | bytes 1966088 | tf_op jit(solution)/shard_map/ppermute | solution.py:418
  182.5 18.3 %collective-permute-start.16 = (bf16[256,1152]{1,0:T(8,128)(2,1)}, bf16[256,1152]{1,0:T(8,128)(2,1)}, u32[]{:S(2)}, u32[]{:S(2)}) collective-permute-start(bf16[256,1152]{1,0:T(8,128)(2,1)} %get-tuple-element.93), channel_id=1, source_target_pairs={{0,1},{1,0},{2,3},{3,2},{4,5},{5,4},{6,7},{7,6},{8,9},{9,8},{10,11... | collective-permute-start | bytes 1769480 | tf_op jit(solution)/shard_map/ppermute | solution.py:418
  189.7 42.7 %collective-permute-start.26 = (bf16[4,144,1152]{2,1,0:T(8,128)(2,1)}, bf16[4,144,1152]{2,1,0:T(8,128)(2,1)S(1)}, u32[]{:S(2)}, u32[]{:S(2)}) collective-permute-start(bf16[4,144,1152]{2,1,0:T(8,128)(2,1)} %get-tuple-element.129), channel_id=1, source_target_pairs={{0,8},{4,12},{8,0},{12,4},{16,24},{20,28},{24,16},{28,20},{1,9},{5... | collective-permute-start | bytes 3981320 | tf_op jit(solution)/shard_map/ppermute | solution.py:412
  191.0 41.4 %collective-permute-start.27 = (bf16[4,144,1152]{2,1,0:T(8,128)(2,1)}, bf16[4,144,1152]{2,1,0:T(8,128)(2,1)S(1)}, u32[]{:S(2)}, u32[]{:S(2)}) collective-permute-start(bf16[4,144,1152]{2,1,0:T(8,128)(2,1)} %get-tuple-element.102.refs_8_), channel_id=1, source_target_pairs={{0,4},{4,0},{8,12},{12,8},{16,20},{20,16},{24,28},{28,24},{1,5},{5... | collective-permute-start | bytes 3981320 | tf_op jit(solution)/shard_map/ppermute | solution.py:412
  198.1 19.7 %collective-permute-start.12 = (bf16[128,5248]{1,0:T(8,128)(2,1)}, bf16[128,5248]{1,0:T(8,128)(2,1)S(1)}, u32[]{:S(2)}, u32[]{:S(2)}) collective-permute-start(bf16[128,5248]{1,0:T(8,128)(2,1)} %collective-permute-done.10.refs_2_), channel_id=1, source_target_pairs={{0,1},{1,0},{2,3},{3,2},{4,5},{5,4},{6,7},{7,6},{8,9},{9,8},{10,11... | collective-permute-start | bytes 4030472 | tf_op jit(solution)/shard_map/ppermute | solution.py:418
  200.1 17.7 %collective-permute-start.18 = (bf16[2,128,1280]{2,1,0:T(8,128)(2,1)S(1)}, bf16[2,128,1280]{2,1,0:T(8,128)(2,1)}, u32[]{:S(2)}, u32[]{:S(2)}) collective-permute-start(bf16[2,128,1280]{2,1,0:T(8,128)(2,1)S(1)} %pad_maximum_fusion.5), channel_id=1, source_target_pairs={{0,2},{2,0},{1,3},{3,1},{4,6},{6,4},{5,7},{7,5},{8,10},{10,8},{9,1... | collective-permute-start | bytes 1966088 | tf_op jit(solution)/shard_map/ppermute | solution.py:415
  202.5 23.4 %collective-permute-start.17 = (bf16[128,1152]{1,0:T(8,128)(2,1)}, bf16[128,1152]{1,0:T(8,128)(2,1)}, u32[]{:S(2)}, u32[]{:S(2)}) collective-permute-start(bf16[128,1152]{1,0:T(8,128)(2,1)} %add_convert_fusion.1), channel_id=1, source_target_pairs={{0,2},{2,0},{1,3},{3,1},{4,6},{6,4},{5,7},{7,5},{8,10},{10,8},{9,1... | collective-permute-start | bytes 884744 | tf_op jit(solution)/shard_map/ppermute | solution.py:415
  230.3 8.5 %collective-permute-start.19 = (bf16[128,1152]{1,0:T(8,128)(2,1)}, bf16[128,1152]{1,0:T(8,128)(2,1)S(1)}, u32[]{:S(2)}, u32[]{:S(2)}) collective-permute-start(bf16[128,1152]{1,0:T(8,128)(2,1)} %get-tuple-element.104.refs_0_.refs_2_), channel_id=1, source_target_pairs={{0,2},{2,0},{1,3},{3,1},{4,6},{6,4},{5,7},{7,5},{8,10},{10,8},{9,1... | collective-permute-start | bytes 884744 | tf_op jit(solution)/shard_map/ppermute | solution.py:415
  230.9 11.7 %collective-permute-start.20 = (bf16[128,1152]{1,0:T(8,128)(2,1)}, bf16[128,1152]{1,0:T(8,128)(2,1)S(1)}, u32[]{:S(2)}, u32[]{:S(2)}) collective-permute-start(bf16[128,1152]{1,0:T(8,128)(2,1)} %get-tuple-element.104.refs_0_.refs_2_), channel_id=1, source_target_pairs={{0,1},{1,0},{2,3},{3,2},{4,5},{5,4},{6,7},{7,6},{8,9},{9,8},{10,11... | collective-permute-start | bytes 884744 | tf_op jit(solution)/shard_map/ppermute | solution.py:418
  230.9 50.1 %collective-permute-start.30 = (bf16[4,352,768]{2,1,0:T(8,128)(2,1)}, bf16[4,352,768]{2,1,0:T(8,128)(2,1)}, u32[]{:S(2)}, u32[]{:S(2)}) collective-permute-start(bf16[4,352,768]{2,1,0:T(8,128)(2,1)} %get-tuple-element.103.refs_8_), channel_id=1, source_target_pairs={{0,4},{4,0},{8,12},{12,8},{16,20},{20,16},{24,28},{28,24},{1,5},{5... | collective-permute-start | bytes 6488072 | tf_op jit(solution)/shard_map/ppermute | solution.py:412
  234.6 39.2 %collective-permute-start.29 = (bf16[2,144,1152]{2,1,0:T(8,128)(2,1)}, bf16[2,144,1152]{2,1,0:T(8,128)(2,1)}, u32[]{:S(2)}, u32[]{:S(2)}) collective-permute-start(bf16[2,144,1152]{2,1,0:T(8,128)(2,1)} %slice.458), channel_id=1, source_target_pairs={{0,8},{4,12},{8,0},{12,4},{16,24},{20,28},{24,16},{28,20},{1,9},{5... | collective-permute-start | bytes 1990664 | tf_op jit(solution)/shard_map/ppermute | solution.py:412
  238.8 3.8 collective-permute-start.21
  242.0 32.4 %collective-permute-start.28 = (bf16[2,144,1152]{2,1,0:T(8,128)(2,1)}, bf16[2,144,1152]{2,1,0:T(8,128)(2,1)}, u32[]{:S(2)}, u32[]{:S(2)}) collective-permute-start(bf16[2,144,1152]{2,1,0:T(8,128)(2,1)} %slice.459), channel_id=1, source_target_pairs={{0,16},{4,20},{8,24},{12,28},{16,0},{20,4},{24,8},{28,12},{1,17},{... | collective-permute-start | bytes 1990664 | tf_op jit(solution)/shard_map/ppermute | solution.py:412
  255.7 2.3 collective-permute-start.23
  255.8 5.3 %collective-permute-start.25 = (f32[1,7168]{1,0:T(1,128)S(1)}, f32[1,7168]{1,0:T(1,128)S(1)}, u32[]{:S(2)}, u32[]{:S(2)}) collective-permute-start(f32[1,7168]{1,0:T(1,128)S(1)} %constant_dynamic-update-slice_fusion.6), channel_id=1, source_target_pairs={{0,1},{1,0},{2,3},{3,2},{4,5},{5,4},{6,7},{7,6},{8,9},{9,8},{10,11... | collective-permute-start | bytes 86024 | tf_op jit(solution)/shard_map/ppermute | solution.py:418
  258.9 9.4 %collective-permute-start.24 = (bf16[128,1152]{1,0:T(8,128)(2,1)}, bf16[128,1152]{1,0:T(8,128)(2,1)}, u32[]{:S(2)}, u32[]{:S(2)}) collective-permute-start(bf16[128,1152]{1,0:T(8,128)(2,1)} %add_convert_fusion), channel_id=1, source_target_pairs={{0,2},{2,0},{1,3},{3,1},{4,6},{6,4},{5,7},{7,5},{8,10},{10,8},{9,1... | collective-permute-start | bytes 884744 | tf_op jit(solution)/shard_map/ppermute | solution.py:415
  266.2 46.5 %collective-permute-start.22 = (bf16[4,144,1184]{2,1,0:T(8,128)(2,1)}, bf16[4,144,1184]{2,1,0:T(8,128)(2,1)S(1)}, u32[]{:S(2)}, u32[]{:S(2)}) collective-permute-start(bf16[4,144,1184]{2,1,0:T(8,128)(2,1)} %get-tuple-element.110.refs_8_), channel_id=1, source_target_pairs={{0,4},{4,0},{8,12},{12,8},{16,20},{20,16},{24,28},{28,24},{1,5},{5... | collective-permute-start | bytes 4091912 | tf_op jit(solution)/shard_map/ppermute | solution.py:412
  286.8 47.0 %collective-permute-start.35 = (bf16[2,352,768]{2,1,0:T(8,128)(2,1)}, bf16[2,352,768]{2,1,0:T(8,128)(2,1)}, u32[]{:S(2)}, u32[]{:S(2)}) collective-permute-start(bf16[2,352,768]{2,1,0:T(8,128)(2,1)} %slice.456.refs_1_), channel_id=1, source_target_pairs={{0,8},{4,12},{8,0},{12,4},{16,24},{20,28},{24,16},{28,20},{1,9},{5... | collective-permute-start | bytes 3244040 | tf_op jit(solution)/shard_map/ppermute | solution.py:412
  287.6 5.1 %collective-permute-start.31 = (f32[1,34816]{1,0:T(1,128)S(1)}, f32[1,34816]{1,0:T(1,128)S(1)}, u32[]{:S(2)}, u32[]{:S(2)}) collective-permute-start(f32[1,34816]{1,0:T(1,128)S(1)} %hold.11), channel_id=1, source_target_pairs={{0,2},{2,0},{1,3},{3,1},{4,6},{6,4},{5,7},{7,5},{8,10},{10,8},{9,1... | collective-permute-start | bytes 417800 | tf_op jit(solution)/shard_map/ppermute | solution.py:415
  291.4 33.2 %collective-permute-start.41 = (bf16[1,144,1152]{2,1,0:T(8,128)(2,1)}, bf16[1,144,1152]{2,1,0:T(8,128)(2,1)}, u32[]{:S(2)}, u32[]{:S(2)}) collective-permute-start(bf16[1,144,1152]{2,1,0:T(8,128)(2,1)} %slice.462), channel_id=1, source_target_pairs={{0,16},{4,20},{8,24},{12,28},{16,0},{20,4},{24,8},{28,12},{1,17},{... | collective-permute-start | bytes 995336 | tf_op jit(solution)/shard_map/ppermute | solution.py:412
  296.0 25.4 %all-to-all-start.3 = ((bf16[8,4,864]{2,1,0:T(4,128)(2,1)}), bf16[8,4,864]{2,1,0:T(4,128)(2,1)S(1)}, u32[]{:S(2)}, u32[]{:S(2)}) async-start(bf16[8,4,864]{2,1,0:T(4,128)(2,1)} %bitcast.178), calls=%async_computation.3 | async-start | bytes 114688 | tf_op jit(solution)/shard_map/all_to_all | solution.py:421
  302.9 22.1 %collective-permute-start.40 = (bf16[1,144,1152]{2,1,0:T(8,128)(2,1)}, bf16[1,144,1152]{2,1,0:T(8,128)(2,1)}, u32[]{:S(2)}, u32[]{:S(2)}) collective-permute-start(bf16[1,144,1152]{2,1,0:T(8,128)(2,1)} %slice.463), channel_id=1, source_target_pairs={{0,4},{4,0},{8,12},{12,8},{16,20},{20,16},{24,28},{28,24},{1,5},{5... | collective-permute-start | bytes 995336 | tf_op jit(solution)/shard_map/ppermute | solution.py:412
  323.0 7.2 %collective-permute-start.32 = (bf16[128,1152]{1,0:T(8,128)(2,1)}, bf16[128,1152]{1,0:T(8,128)(2,1)S(1)}, u32[]{:S(2)}, u32[]{:S(2)}) collective-permute-start(bf16[128,1152]{1,0:T(8,128)(2,1)} %copy-done.3), channel_id=1, source_target_pairs={{0,2},{2,0},{1,3},{3,1},{4,6},{6,4},{5,7},{7,5},{8,10},{10,8},{9,1... | collective-permute-start | bytes 884744 | tf_op jit(solution)/shard_map/ppermute | solution.py:415
  324.2 6.2 %collective-permute-start.33 = (bf16[128,1152]{1,0:T(8,128)(2,1)}, bf16[128,1152]{1,0:T(8,128)(2,1)S(1)}, u32[]{:S(2)}, u32[]{:S(2)}) collective-permute-start(bf16[128,1152]{1,0:T(8,128)(2,1)} %copy-done.3), channel_id=1, source_target_pairs={{0,1},{1,0},{2,3},{3,2},{4,5},{5,4},{6,7},{7,6},{8,9},{9,8},{10,11... | collective-permute-start | bytes 884744 | tf_op jit(solution)/shard_map/ppermute | solution.py:418
  324.6 19.0 %collective-permute-start.37 = (bf16[2,144,1184]{2,1,0:T(8,128)(2,1)S(1)}, bf16[2,144,1184]{2,1,0:T(8,128)(2,1)S(1)}, u32[]{:S(2)}, u32[]{:S(2)}) collective-permute-start(bf16[2,144,1184]{2,1,0:T(8,128)(2,1)S(1)} %slice.457.refs_1_), channel_id=1, source_target_pairs={{0,8},{4,12},{8,0},{12,4},{16,24},{20,28},{24,16},{28,20},{1,9},{5... | collective-permute-start | bytes 2045960 | tf_op jit(solution)/shard_map/ppermute | solution.py:412
  335.3 11.5 %collective-permute-start.36 = (bf16[8,4,864]{2,1,0:T(4,128)(2,1)S(1)}, bf16[8,4,864]{2,1,0:T(4,128)(2,1)S(1)}, u32[]{:S(2)}, u32[]{:S(2)}) collective-permute-start(bf16[8,4,864]{2,1,0:T(4,128)(2,1)S(1)} %hold.13), channel_id=1, source_target_pairs={{0,1},{1,0},{2,3},{3,2},{4,5},{5,4},{6,7},{7,6},{8,9},{9,8},{10,11... | collective-permute-start | bytes 165896 | tf_op jit(solution)/shard_map/ppermute | solution.py:418
  343.8 36.9 %collective-permute-start.39 = (bf16[1,144,1184]{2,1,0:T(8,128)(2,1)S(1)}, bf16[1,144,1184]{2,1,0:T(8,128)(2,1)}, u32[]{:S(2)}, u32[]{:S(2)}) collective-permute-start(bf16[1,144,1184]{2,1,0:T(8,128)(2,1)S(1)} %slice.461.refs_1_), channel_id=1, source_target_pairs={{0,16},{4,20},{8,24},{12,28},{16,0},{20,4},{24,8},{28,12},{1,17},{... | collective-permute-start | bytes 1022984 | tf_op jit(solution)/shard_map/ppermute | solution.py:412
  344.6 47.6 %collective-permute-start.38 = (bf16[1,352,768]{2,1,0:T(8,128)(2,1)S(1)}, bf16[1,352,768]{2,1,0:T(8,128)(2,1)}, u32[]{:S(2)}, u32[]{:S(2)}) collective-permute-start(bf16[1,352,768]{2,1,0:T(8,128)(2,1)S(1)} %slice.460.refs_2_), channel_id=1, source_target_pairs={{0,16},{4,20},{8,24},{12,28},{16,0},{20,4},{24,8},{28,12},{1,17},{... | collective-permute-start | bytes 1622024 | tf_op jit(solution)/shard_map/ppermute | solution.py:412
  356.8 41.6 %all-to-all-start.4 = ((f32[8,1,18112]{2,1,0:T(1,128)}), f32[8,1,18112]{2,1,0:T(1,128)}, u32[]{:S(2)}, u32[]{:S(2)}) async-start(f32[8,1,18112]{2,1,0:T(1,128)} %copy.131), calls=%async_computation.4 | async-start | bytes 1163264 | tf_op jit(solution)/shard_map/all_to_all | solution.py:421
  393.7 14.3 %collective-permute-start.43 = (bf16[352,768]{1,0:T(8,128)(2,1)S(1)}, bf16[352,768]{1,0:T(8,128)(2,1)}, u32[]{:S(2)}, u32[]{:S(2)}) collective-permute-start(bf16[352,768]{1,0:T(8,128)(2,1)S(1)} %fusion.20.refs_2_), channel_id=1, source_target_pairs={{0,2},{2,0},{1,3},{3,1},{4,6},{6,4},{5,7},{7,5},{8,10},{10,8},{9,1... | collective-permute-start | bytes 1622024 | tf_op jit(solution)/shard_map/ppermute | solution.py:415
  396.4 15.7 %collective-permute-start.42 = (bf16[352,768]{1,0:T(8,128)(2,1)S(1)}, bf16[352,768]{1,0:T(8,128)(2,1)}, u32[]{:S(2)}, u32[]{:S(2)}) collective-permute-start(bf16[352,768]{1,0:T(8,128)(2,1)S(1)} %fusion.20.refs_2_), channel_id=1, source_target_pairs={{0,1},{1,0},{2,3},{3,2},{4,5},{5,4},{6,7},{7,6},{8,9},{9,8},{10,11... | collective-permute-start | bytes 1622024 | tf_op jit(solution)/shard_map/ppermute | solution.py:418
  408.0 5.2 %collective-permute-start.44 = (bf16[352,768]{1,0:T(8,128)(2,1)}, bf16[352,768]{1,0:T(8,128)(2,1)S(1)}, u32[]{:S(2)}, u32[]{:S(2)}) collective-permute-start(bf16[352,768]{1,0:T(8,128)(2,1)} %collective-permute-done.43), channel_id=1, source_target_pairs={{0,1},{1,0},{2,3},{3,2},{4,5},{5,4},{6,7},{7,6},{8,9},{9,8},{10,11... | collective-permute-start | bytes 1622024 | tf_op jit(solution)/shard_map/ppermute | solution.py:418
  (77 other events, 504.1 us)
Sparse Core Ops, SparseCore 0:
  11.5 129.6 all-gather.2

commit v4 on v3

--- a/solution.py
+++ b/solution.py
@@ -322,15 +322,18 @@
             out[:, yr * wide + 2 * n : (yr + 1) * wide] = gz_ref[:, low]
 
 
-def proj_grad_kernel(hidden, place, n_outs, meta, f0, f1, f2, f3, keep, got, other, *refs):
+def proj_grad_kernel(hidden, place, n_outs, meta, f0, f1, f2, f3, keep, got, *refs):
     outs = refs[:n_outs]
     a, b, r2, r3, r1, in_sem, out_sem = refs[n_outs:]
     half = f0.shape[0]
     wide = b.shape[1]
     n = r2.shape[1]
+    f_wide = a.shape[1]
     for at, piece in enumerate((f0, f1, f2, f3)):
-        pltpu.make_async_copy(piece, a.at[at * half : (at + 1) * half, :], in_sem.at[0]).start()
-    for at, piece in enumerate((keep.at[:, 0:wide], other.at[0], got.at[:, 0:wide], other.at[1])):
+        pltpu.make_async_copy(piece.at[:, 0:f_wide], a.at[at * half : (at + 1) * half, :], in_sem.at[0]).start()
+    for at, piece in enumerate(
+        (keep.at[:, 0:wide], f1.at[:, f_wide : f_wide + wide], got.at[:, 0:wide], f1.at[:, f_wide + wide : f_wide + 2 * wide])
+    ):
         pltpu.make_async_copy(piece, b.at[at * half : (at + 1) * half, :], in_sem.at[1]).start()
     pltpu.make_async_copy(b, b, in_sem.at[1]).wait()
     pltpu.make_async_copy(a, a, in_sem.at[0]).wait()
@@ -523,8 +526,8 @@
 
     def settle_quarter(part_y, send):
         got = swap_core(send)
-        passed = swap_y((part_y + got[half:].astype(F32)).astype(BF16))
-        return got, passed
+        sent = (part_y + got[half:].astype(F32)).astype(BF16)
+        return got, swap_y(sent), sent
 
     def spread_quarter(g):
         gy = swap_y(g)
@@ -537,7 +540,7 @@
         flops=4 * T * width * ff,
         name="mlp",
     )
-    rq, ry = settle_quarter(part_y, send)
+    rq, ry, y_sent = settle_quarter(part_y, send)
 
     def k_of(w):
         return w.shape[0]
@@ -630,13 +633,12 @@
     )
     g_mlp_y, g_mlp_c = swap_y(g_mlp), swap_core(g_mlp)
     g_mlp_yc = swap_core(g_mlp_y)
-    (f_sent,) = hold([f_own], [g_mlp_y])
-    f_y = swap_y(f_sent)
     q_got = swap_core(q_send)
     f_c = swap_core(f_own)
-    f_yc = swap_core(f_y)
-    q_other = swap_y(jnp.stack([q_keep[:, q_wide:], q_got[:, q_wide:]]))
-    low_own, low_y, low_c, low_yc = (a[:, 2 * hidden :] for a in (f_own, f_y, f_c, f_yc))
+    (f_sent,) = hold([f_own], [g_mlp_y])
+    f_wide = 2 * hidden + width
+    f_sent = jnp.concatenate([f_sent, q_keep[:, q_wide:], q_got[:, q_wide:]], axis=1)
+    f_y = swap_y(f_sent)
 
     def wgrad(place, jobs, ins, outs, name, after=()):
         shapes = [(ins[a].shape[1], ins[b].shape[1]) for a, b, _ in jobs]
@@ -711,7 +713,7 @@
     f1 = k1 * block // (block + room)
 
     def proj_grads(after=()):
-        ins = [meta, f_own, f_y, f_c, f_yc, q_keep, q_got, q_other]
+        ins = [meta, f_own, f_y, f_c, f_yc, q_keep, q_got]
         whole_rows = aligned and f1 % 32 == 0
 
         def place(job, g, outs, meta_):
@@ -740,7 +742,7 @@
             functools.partial(proj_grad_kernel, hidden, place, len(shapes)),
             shapes,
             ins,
-            in_specs=[SMEM] + [ANY] * 7,
+            in_specs=[SMEM] + [ANY] * 6,
             out_specs=[ANY] * len(shapes),
             scratch=[
                 pltpu.VMEM((T, 2 * hidden + width), BF16),
@@ -782,14 +784,17 @@
         [g_mlp, g_mlp_y, g_mlp_c, g_mlp_yc, pre, fc1_w, fc2_w],
         flops=4 * T * width * ff,
         name="mlp_back",
-        after=[f_c, q_got],
-    )
-    rq, ry = settle_quarter(part_y, send)
+        after=[f_c, f_sent],
+    )
+    rq, ry, y_sent = settle_quarter(part_y, send)
     fc2_parts, fc1_parts = wgrad_dp(
         [([(0, 1, 384)], x_last), ([(2, 3, 384)], x_first)], [g_mlp_full, act, m_full, gpre], "grad_fc"
     )
     fc2_got = flip_dp(fc2_parts[1], x_last[0])
     fc1_got = flip_dp(fc1_parts[1], 1)
+    (f_y,) = hold([f_y], [fc1_parts[1], y_sent])
+    f_yc = swap_core(f_y)
+    low_own, low_y, low_c, low_yc = (a[:, 2 * hidden : f_wide] for a in (f_own, f_y, f_c, f_yc))
     pg_first, pg_second = proj_grads(after=[fc1_parts[1]])
     pg_got = flip_dp(pg_second, 1)
     g_one, g_attn, gate_one, shift_two, scale_two, g_out_b = call(
@@ -813,7 +818,7 @@
         flops=8 * T * width * wide + 10 * T * seq * wide,
         name="attention_back",
     )
-    rq, ry = settle_quarter(part_y, send)
+    rq, ry, y_sent = settle_quarter(part_y, send)
     ((heads_first, heads_second),) = wgrad_dp(
         [([(0, 1, 384), (2, 3, 384)], x_first)], [m_one, gqkv, g_attn_full, mixed], "grad_heads", after=[]
     )
@@ -846,28 +851,28 @@
     line = line + swap_y(line)
     g_mod, early = line[:, : slots * 6 * width].reshape(slots, -1).astype(BF16), line[:, slots * 6 * width :]
     g_mod = exchange_dp(g_mod.reshape(slots, n_dp, -1).transpose(1, 0, 2))
-    heads_got, g_in = hold([heads_got, g_in], [g_mod])
+    pg_v = halves(pg_v[0] + pg_got.astype(F32))
+    pg_sent = pg_v[1].astype(BF16)
+    pg_got = flip_dp(pg_sent, 4)
+    heads_got, g_in = hold([heads_got, g_in], [pg_sent])
     heads_v = halves(heads_first.astype(F32) + heads_got.astype(F32))
     heads_sent = heads_v[1].astype(BF16)
     heads_got = flip_dp(heads_sent, 2)
-    pg_v = halves(pg_v[0] + pg_got.astype(F32))
-    pg_sent = pg_v[1].astype(BF16)
-    pg_got = flip_dp(pg_sent, 4)
+    (g_mod,) = hold([g_mod], [heads_sent])
     fc2_last, fc1_last = hold([fc2_last, fc1_last], [g_mod])
-    (g_mod,) = hold([g_mod], [heads_sent, pg_sent])
     g_mod = pair([g_mod, swap_core(g_mod)], c, 1).reshape(n_dp * images, -1)
     g_ada_w = lax.dot_general(g_mod, cond_act, (((0,), (1,)), ((), ())), preferred_element_type=F32)
     g_ada_b = jnp.sum(g_mod.astype(F32), axis=0)
     g_cond = lax.dot_general(ada_w, g_mod, (((0,), (1,)), ((), ())), preferred_element_type=F32)
     own = jnp.concatenate([early, g_fc1_b, g_qv_b.reshape(1, 2 * wide)], axis=1)
     sent = jnp.concatenate([g_cond.reshape(n_dp, feats * n_images), jnp.broadcast_to(own, (n_dp, own.shape[1]))], axis=1)
-    sums = exchange_dp(sent)
     heads_v = halves(heads_v[0] + heads_got.astype(F32))
     heads_sent = heads_v[1].astype(BF16)
     heads_got = flip_dp(heads_sent, 4)
     mine = halve_all(pg_v[0] + pg_got.astype(F32), x_first[3:]).astype(BF16)
     found = quarters(mine)
-    (sums,) = hold([sums], [heads_sent, mine])
+    (sent,) = hold([sent], [heads_sent, mine])
+    sums = exchange_dp(sent)
     sums = jnp.sum(sums, axis=0)
     g_fc2_t = halve_all(fc2_v[0] + fc2_last.astype(F32), x_last[3:])
     g_fc1 = halve_all(fc1_v[0] + fc1_last.astype(F32), x_first[3:])

time: 430 us -> 414 us (0.963)
  waiting for transfers between devices: 163 us -> 149 us
  starting transfers between devices: 53.1 us -> 48.2 us
  other arithmetic: 38.4 us -> 42.7 us
    all_to_all x5, waiting for transfers between devices: 37.9 us -> 27.3 us  [exchange_dp(): return lax.all_to_all(x, 'dp', 0, 0, tiled=True)]
    ppermute x13 -> x12, waiting for transfers between devices: 54 us -> 49.7 us  [swap_y(): return lax.ppermute(x, 'tensor', [(0, 2), (2, 0), (1, 3), (3, 1)])]
    unnamed x162 -> x177, local copies, waits for them, and re-layouts: 22.5 us -> 21.7 us
    ppermute x13 -> x12, starting transfers between devices: 13.7 us -> 12.9 us  [swap_y(): return lax.ppermute(x, 'tensor', [(0, 2), (2, 0), (1, 3), (3, 1)])]
  transfers between devices with their start and end apart: 51 -> 50, of which waited for: 27 -> 23; matrix products, arithmetic and copies ran while one was open for 19% -> 20% of each run, Pallas kernels for 17% -> 17%
where the time goes in v4:
time: 414 us; the launch traced here: 409 us
  waiting for transfers between devices  149 us (36%)
  Pallas kernels  87.3 us (21%)
  local copies, waits for them, and re-layouts  57.8 us (14%)
  starting transfers between devices  48.2 us (12%)
  other arithmetic  42.7 us (10%)
  between operations  15.4 us (4%)
  matrix products  8.58 us (2%)
    pallas_call x11, Pallas kernels, call(): pl.pallas_call(kernel, out_shape=tuple(outs), in_specs=list(in_specs or [...  87.3 us
    ppermute x12, waiting for transfers between devices, flip_dp(): return lax.ppermute(x, 'dp', [(k, k ^ mask) for k in range(n_dp)])  54.5 us
    ppermute x12, waiting for transfers between devices, swap_y(): return lax.ppermute(x, 'tensor', [(0, 2), (2, 0), (1, 3), (3, 1)])  49.7 us
    all_to_all x5, waiting for transfers between devices, exchange_dp(): return lax.all_to_all(x, 'dp', 0, 0, tiled=True)  27.3 us
    all_to_all x5, starting transfers between devices, exchange_dp(): return lax.all_to_all(x, 'dp', 0, 0, tiled=True)  22.5 us
    unnamed x177, local copies, waits for them, and re-layouts  21.7 us
    all_gather x1, waiting for transfers between devices, body(): gathered = lax.all_gather(packed, ('dp', 'tensor'), axis=0)  14 us
    ppermute x12, starting transfers between devices, swap_y(): return lax.ppermute(x, 'tensor', [(0, 2), (2, 0), (1, 3), (3, 1)])  12.9 us
  transfers between devices with their start and end apart: 50, of which 23 were waited for; matrix products, arithmetic and copies ran while one was open for 20% of the time, Pallas kernels for 17%

profile of v4, /device:TPU:0, one launch (start us, length us, event | category | flops | bytes accessed | tf_op | source)
XLA Modules:
  0.0 409.2 jit_solution(14717720227284985081)
XLA Ops:
  14.1 7.3 %all-to-all-start = ((s32[8,1,16]{2,1,0:T(1,128)}), s32[8,1,16]{2,1,0:T(1,128)S(1)}, u32[]{:S(2)}, u32[]{:S(2)}) async-start(s32[8,1,16]{2,1,0:T(1,128)} %broadcast_in_dim.17), calls=%async_computation | async-start | bytes 8192 | tf_op jit(solution)/shard_map/all_to_all | solution.py:424
  21.6 6.1 %all-to-all-done = s32[8,1,16]{2,1,0:T(1,128)S(1)} async-done(((s32[8,1,16]{2,1,0:T(1,128)}), s32[8,1,16]{2,1,0:T(1,128)S(1)}, u32[]{:S(2)}, u32[]{:S(2)}) %all-to-all-start) | async-done | bytes 544 | tf_op jit(solution)/shard_map/all_to_all | solution.py:424
  29.8 3.4 all-to-all-start.1
  33.2 1.6 collective-permute-start.4
  34.8 9.7 %all-to-all-done.1 = bf16[8,154,64]{1,2,0:T(8,128)(2,1)S(1)} async-done(((bf16[8,154,64]{1,2,0:T(8,128)(2,1)}), bf16[8,154,64]{1,2,0:T(8,128)(2,1)S(1)}, u32[]{:S(2)}, u32[]{:S(2)}) %all-to-all-start.1) | async-done | bytes 157728 | tf_op jit(solution)/shard_map/all_to_all | solution.py:424
  46.4 3.9 all-to-all-start.2
  53.7 11.4 %all-to-all-done.2 = f32[8,8,864]{2,1,0:T(8,128)S(1)} async-done(((f32[8,8,864]{2,1,0:T(8,128)}), f32[8,8,864]{2,1,0:T(8,128)S(1)}, u32[]{:S(2)}, u32[]{:S(2)}) %all-to-all-start.2) | async-done | bytes 221216 | tf_op jit(solution)/shard_map/all_to_all | solution.py:424
  66.0 9.8 %attention.1 = (bf16[512,1152]{1,0:T(8,128)(2,1)}, bf16[512,288]{1,0:T(8,128)(2,1)}, bf16[512,288]{1,0:T(8,128)(2,1)}, bf16[512,288]{1,0:T(8,128)(2,1)}, bf16[512,288]{1,0:T(8,128)(2,1)}) custom-call(s32[4]{0:T(128)} %pad_add_fusion.3.refs_0_, bf16[4,128,1152]{2,1,0:T(8,128)(2,1)} %bitcast.150, f32[4,6912]{1,0:T(4,128)} %get-tuple-element.275.refs_2_.refs_5_.refs_6_, ...), custom_call_target="tpu_custom_call" | custom-call | tf_op jit(solution)/shard_map/attention/pallas_call | solution.py:36
  77.0 1.5 collective-permute-start.1
  80.5 4.2 %collective-permute-done.1.refs_6_ = bf16[256,288]{1,0:T(8,128)(2,1)S(1)} collective-permute-done((bf16[256,288]{1,0:T(8,128)(2,1)S(1)}, bf16[256,288]{1,0:T(8,128)(2,1)S(1)}, u32[]{:S(2)}, u32[]{:S(2)}) %collective-permute-start.1) | collective-permute-done | bytes 147488 | tf_op jit(solution)/shard_map/ppermute | solution.py:418
  84.8 6.4 %collective-permute-done.2.refs_7_ = bf16[256,288]{1,0:T(8,128)(2,1)S(1)} collective-permute-done((bf16[256,288]{1,0:T(8,128)(2,1)S(1)}, bf16[256,288]{1,0:T(8,128)(2,1)S(1)}, u32[]{:S(2)}, u32[]{:S(2)}) %collective-permute-start.2) | collective-permute-done | bytes 147488 | tf_op jit(solution)/shard_map/ppermute | solution.py:418
  91.8 5.8 %middle.1 = (f32[128,1152]{1,0:T(8,128)}, f32[128,1152]{1,0:T(8,128)}, bf16[256,1152]{1,0:T(8,128)(2,1)}) custom-call(s32[4]{0:T(128)} %pad_add_fusion.3.refs_0_, bf16[4,128,1152]{2,1,0:T(8,128)(2,1)} %bitcast.151, f32[4,6912]{1,0:T(4,128)} %get-tuple-element.275.refs_2_.refs_5_.refs_6_, s32[512,1]{1,0:T(8,128)} %copy.121.refs_4_.refs_3_.refs_8_, ...), custom_call_target="tpu_custom_call" | custom-call | tf_op jit(solution)/shard_map/middle/pallas_call | solution.py:36
  98.2 1.6 collective-permute-done.6.refs_1_
  100.6 7.9 %mlp.1 = (bf16[512,1152]{1,0:T(8,128)(2,1)}, f32[512,1152]{1,0:T(8,128)}, bf16[512,1152]{1,0:T(8,128)(2,1)}, f32[128,1152]{1,0:T(8,128)}, f32[128,1152]{1,0:T(8,128)}, /*index=5*/bf16[256,1152]{1,0:T(8,128)(2,1)}) custom-call(bf16[256,1152]{1,0:T(8,128)(2,1)} %get-tuple-element.82.refs_0_, bf16[256,1152]{1,0:T(8,128)(2,1)} %copy-done.40, ...), custom_call_target="tpu_custom_call" | custom-call | tf_op jit(solution)/shard_map/mlp/pallas_call | solution.py:36
  113.5 1.7 dynamic-slice_bitcast_fusion.refs_8_
  117.2 2.5 collective-permute-start.8
  121.6 5.6 %collective-permute-done.8.refs_3_ = bf16[128,1152]{1,0:T(8,128)(2,1)S(1)} collective-permute-done((bf16[128,1152]{1,0:T(8,128)(2,1)S(1)}, bf16[128,1152]{1,0:T(8,128)(2,1)S(1)}, u32[]{:S(2)}, u32[]{:S(2)}) %collective-permute-start.8) | collective-permute-done | bytes 294944 | tf_op jit(solution)/shard_map/ppermute | solution.py:418
  127.2 14.0 %all-gather.3.cloned.1.call-done = bf16[16896,512]{1,0:T(8,128)(2,1)} async-done(((bf16[528,512]{1,0:T(8,128)(2,1)}), bf16[16896,512]{1,0:T(8,128)(2,1)}) %all-gather.3.cloned.1.call-update) | async-done | bytes 17301520 | tf_op jit(solution)/shard_map/all_gather | solution.py:446
  141.2 15.7 %projector.1 = (bf16[128,5248]{1,0:T(8,128)(2,1)}, bf16[128,2560]{1,0:T(8,128)(2,1)}, bf16[128,2560]{1,0:T(8,128)(2,1)}, f32[128,1152]{1,0:T(8,128)}, bf16[128,1...) custom-call(s32[4]{0:T(128)} %pad_add_fusion.2.refs_0_, ...), custom_call_target="tpu_custom_call" | custom-call | tf_op jit(solution)/shard_map/projector/pallas_call | solution.py:36
  159.3 7.4 %collective-permute-done.9.refs_1_ = bf16[128,1152]{1,0:T(8,128)(2,1)S(1)} collective-permute-done((bf16[128,1152]{1,0:T(8,128)(2,1)}, bf16[128,1152]{1,0:T(8,128)(2,1)S(1)}, u32[]{:S(2)}, u32[]{:S(2)}) %collective-permute-start.9) | collective-permute-done | bytes 294944 | tf_op jit(solution)/shard_map/ppermute | solution.py:418
  171.7 9.0 %mlp_back.1 = (bf16[512,1152]{1,0:T(8,128)(2,1)}, bf16[512,1152]{1,0:T(8,128)(2,1)}, f32[128,1152]{1,0:T(8,128)}, f32[128,1152]{1,0:T(8,128)}, bf16[256,1152]{1,0:T(8,128)(2,1)}, /*index=5*/f32[1,1152]{1,0:T(1,128)}) custom-call(bf16[128,1152]{1,0:T(8,128)(2,1)} %get-tuple-element.88.refs_0_, bf16[128,1152]{1,0:T(8,128)(2,1)} %copy-done.4, ...), custom_call_target="tpu_custom_call" | custom-call | tf_op jit(solution)/shard_map/mlp_back/pallas_call | solution.py:36
  180.9 7.2 %grad_fc.1 = (bf16[4,144,1152]{2,1,0:T(8,128)(2,1)}, bf16[4,144,1152]{2,1,0:T(8,128)(2,1)}, bf16[4,144,1152]{2,1,0:T(8,128)(2,1)}, bf16[4,144,1152]{2,1,0:T(8,128)(2,1)}) custom-call(s32[4]{0:T(128)} %pad_add_fusion.2.refs_0_, bf16[512,1152]{1,0:T(8,128)(2,1)} %get-tuple-element.92.refs_1_, bf16[512,1152]{1,0:T(8,128)(2,1)} %get-tuple-element.93.refs_2_, ...), custom_call_target="tpu_custom_call" | custom-call | tf_op jit(solution)/shard_map/grad_fc/pallas_call | solution.py:36
  188.1 24.6 %collective-permute-done.11.refs_0_ = bf16[128,7808]{1,0:T(8,128)(2,1)} collective-permute-done((bf16[128,7808]{1,0:T(8,128)(2,1)S(1)}, bf16[128,7808]{1,0:T(8,128)(2,1)}, u32[]{:S(2)}, u32[]{:S(2)}) %collective-permute-start.11) | collective-permute-done | bytes 1998880 | tf_op jit(solution)/shard_map/ppermute | solution.py:418
  215.4 1.5 collective-permute-start.25
  220.0 7.0 %grad_projector.1 = (bf16[4,352,768]{2,1,0:T(8,128)(2,1)}, bf16[4,352,768]{2,1,0:T(8,128)(2,1)}) custom-call(s32[4]{0:T(128)} %pad_add_fusion.2.refs_0_, bf16[128,5248]{1,0:T(8,128)(2,1)} %get-tuple-element.87.refs_1_, bf16[128,7808]{1,0:T(8,128)(2,1)} %hold.10.refs_2_, bf16[128,5248]{1,0:T(8,128)(2,1)} %copy-done.16, ...), custom_call_target="tpu_custom_call" | custom-call | tf_op jit(solution)/shard_map/grad_projector/pallas_call | solution.py:36
  227.8 4.4 %second_back.1 = (f32[128,1152]{1,0:T(8,128)}, bf16[128,1152]{1,0:T(8,128)(2,1)}, f32[4,1152]{1,0:T(4,128)}, f32[4,1152]{1,0:T(4,128)}, f32[4,1152]{1,0:T(4,128)}, /*index=5*/f32[1,1152]{1,0:T(1,128)}) custom-call(f32[128,1152]{1,0:T(8,128)} %get-tuple-element.100.refs_0_, bf16[256,1152]{1,0:T(8,128)(2,1)} %copy-done.30, bf16[128,1152]{1,0:T(8,128)(2,1)} %copy-done.48, ...), custom_call_target="tpu_custom_call" | custom-call | tf_op jit(solution)/shard_map/second_back/pallas_call | solution.py:36
  234.1 11.9 %collective-permute-done.24.refs_0_ = bf16[4,144,1152]{2,1,0:T(8,128)(2,1)} collective-permute-done((bf16[4,144,1152]{2,1,0:T(8,128)(2,1)}, bf16[4,144,1152]{2,1,0:T(8,128)(2,1)}, u32[]{:S(2)}, u32[]{:S(2)}) %collective-permute-start.24) | collective-permute-done | bytes 1327136 | tf_op jit(solution)/shard_map/ppermute | solution.py:415
  246.1 1.5 collective-permute-done.25.refs_1_
  248.5 1.7 convert_add_fusion.2
  252.5 1.6 convert_add_fusion.3
  257.2 11.7 %attention_back.1 = (bf16[512,896]{1,0:T(8,128)(2,1)}, f32[128,1152]{1,0:T(8,128)}, f32[128,1152]{1,0:T(8,128)}, bf16[256,1152]{1,0:T(8,128)(2,1)}, f32[2,288]{1,0:T(2,128)}, /*index=5*/bf16[512,1152]{1,0:T(8,128)(2,1)}) custom-call(bf16[128,1152]{1,0:T(8,128)(2,1)} %get-tuple-element.104.refs_0_.refs_2_, bf16[128,1152]{1,0:T(8,128)(2,1)} %copy-done.45, ...), custom_call_target="tpu_custom_call" | custom-call | tf_op jit(solution)/shard_map/attention_back/pallas_call | solution.py:36
  274.4 5.0 %grad_heads.1 = (bf16[4,144,1184]{2,1,0:T(8,128)(2,1)}, bf16[4,144,1184]{2,1,0:T(8,128)(2,1)}) custom-call(s32[4]{0:T(128)} %pad_add_fusion.2.refs_0_, bf16[512,1152]{1,0:T(8,128)(2,1)} %get-tuple-element.99.refs_1_, bf16[512,896]{1,0:T(8,128)(2,1)} %get-tuple-element.108.refs_2_, bf16[512,1152]{1,0:T(8,128)(2,1)} %get-tuple-element.109.refs_3_, ...), custom_call_target="tpu_custom_call" | custom-call | tf_op jit(solution)/shard_map/grad_heads/pallas_call | solution.py:36
  279.4 1.6 collective-permute-start.21
  281.4 3.8 first_back.1
  288.1 5.8 %collective-permute-done.28.refs_2_ = bf16[4,352,768]{2,1,0:T(8,128)(2,1)} collective-permute-done((bf16[4,352,768]{2,1,0:T(8,128)(2,1)}, bf16[4,352,768]{2,1,0:T(8,128)(2,1)}, u32[]{:S(2)}, u32[]{:S(2)}) %collective-permute-start.28) | collective-permute-done | bytes 2162720 | tf_op jit(solution)/shard_map/ppermute | solution.py:415
  293.9 1.6 copy-done.24
  295.5 2.2 convert_add_fusion
  311.5 3.5 all-to-all-start.3
  316.5 13.9 %collective-permute-done.29 = bf16[2,352,768]{2,1,0:T(8,128)(2,1)} collective-permute-done((bf16[2,352,768]{2,1,0:T(8,128)(2,1)}, bf16[2,352,768]{2,1,0:T(8,128)(2,1)}, u32[]{:S(2)}, u32[]{:S(2)}) %collective-permute-start.29) | collective-permute-done | bytes 1081376 | tf_op jit(solution)/shard_map/ppermute | solution.py:415
  330.4 2.1 slice_add_fusion
  338.7 1.9 fusion.14
  340.6 1.9 fusion.15
  347.6 3.6 fusion.26
  353.0 3.6 collective-permute-done.37
  364.1 1.6 convert.48
  367.1 4.4 %all-to-all-start.4 = ((f32[8,1,18112]{2,1,0:T(1,128)}), f32[8,1,18112]{2,1,0:T(1,128)}, u32[]{:S(2)}, u32[]{:S(2)}) async-start(f32[8,1,18112]{2,1,0:T(1,128)} %copy.132), calls=%async_computation.4 | async-start | bytes 1163264 | tf_op jit(solution)/shard_map/all_to_all | solution.py:424
  371.5 15.1 %collective-permute-done.38 = bf16[1,144,1184]{2,1,0:T(8,128)(2,1)S(1)} collective-permute-done((bf16[1,144,1184]{2,1,0:T(8,128)(2,1)S(1)}, bf16[1,144,1184]{2,1,0:T(8,128)(2,1)S(1)}, u32[]{:S(2)}, u32[]{:S(2)}) %collective-permute-start.38) | collective-permute-done | bytes 341024 | tf_op jit(solution)/shard_map/ppermute | solution.py:415
  394.4 1.6 maximum_convert_fusion
  (392 shorter events, 111.0 us)
Async XLA Ops:
  7.2 134.0 %all-gather.3.cloned.1.call-start = ((), (), s32[]{:S(2)}) async-start(), calls=%async_computation.5 | async-start | bytes 17842176 | tf_op jit(solution)/shard_map/all_gather | solution.py:446
  14.1 13.6 %all-to-all-start = ((s32[8,1,16]{2,1,0:T(1,128)}), s32[8,1,16]{2,1,0:T(1,128)S(1)}, u32[]{:S(2)}, u32[]{:S(2)}) async-start(s32[8,1,16]{2,1,0:T(1,128)} %broadcast_in_dim.17), calls=%async_computation | async-start | bytes 8192 | tf_op jit(solution)/shard_map/all_to_all | solution.py:424
  29.8 14.8 %all-to-all-start.1 = ((bf16[8,154,64]{1,2,0:T(8,128)(2,1)}), bf16[8,154,64]{1,2,0:T(8,128)(2,1)S(1)}, u32[]{:S(2)}, u32[]{:S(2)}) async-start(bf16[8,154,64]{1,2,0:T(8,128)(2,1)} %broadcast_in_dim.18), calls=%async_computation.1 | async-start | bytes 524288 | tf_op jit(solution)/shard_map/all_to_all | solution.py:424
  33.2 20.4 %collective-permute-start.4 = (bf16[288,1152]{1,0:T(8,128)(2,1)S(1)}, bf16[288,1152]{1,0:T(8,128)(2,1)}, u32[]{:S(2)}, u32[]{:S(2)}) collective-permute-start(bf16[288,1152]{1,0:T(8,128)(2,1)S(1)} %copy-done.23), channel_id=1, source_target_pairs={{0,2},{2,0},{1,3},{3,1},{4,6},{6,4},{5,7},{7,5},{8,10},{10,8},{9,1... | collective-permute-start | bytes 1990664 | tf_op jit(solution)/shard_map/ppermute | solution.py:418
  34.8 45.7 %collective-permute-start.3 = (bf16[288,1152]{1,0:T(8,128)(2,1)S(1)}, bf16[288,1152]{1,0:T(8,128)(2,1)}, u32[]{:S(2)}, u32[]{:S(2)}) collective-permute-start(bf16[288,1152]{1,0:T(8,128)(2,1)S(1)} %copy-done.23), channel_id=1, source_target_pairs={{0,1},{1,0},{2,3},{3,2},{4,5},{5,4},{6,7},{7,6},{8,9},{9,8},{10,11... | collective-permute-start | bytes 1990664 | tf_op jit(solution)/shard_map/ppermute | solution.py:421
  46.4 18.7 %all-to-all-start.2 = ((f32[8,8,864]{2,1,0:T(8,128)}), f32[8,8,864]{2,1,0:T(8,128)S(1)}, u32[]{:S(2)}, u32[]{:S(2)}) async-start(f32[8,8,864]{2,1,0:T(8,128)} %fusion.6), calls=%async_computation.2 | async-start | bytes 458752 | tf_op jit(solution)/shard_map/all_to_all | solution.py:424
  53.7 37.5 %collective-permute-start.5 = (bf16[288,1152]{1,0:T(8,128)(2,1)}, bf16[288,1152]{1,0:T(8,128)(2,1)}, u32[]{:S(2)}, u32[]{:S(2)}) collective-permute-start(bf16[288,1152]{1,0:T(8,128)(2,1)} %collective-permute-done.4.refs_10_), channel_id=1, source_target_pairs={{0,1},{1,0},{2,3},{3,2},{4,5},{5,4},{6,7},{7,6},{8,9},{9,8},{10,11... | collective-permute-start | bytes 1990664 | tf_op jit(solution)/shard_map/ppermute | solution.py:421
  77.0 7.8 %collective-permute-start.1 = (bf16[256,288]{1,0:T(8,128)(2,1)S(1)}, bf16[256,288]{1,0:T(8,128)(2,1)S(1)}, u32[]{:S(2)}, u32[]{:S(2)}) collective-permute-start(bf16[256,288]{1,0:T(8,128)(2,1)S(1)} %get-tuple-element.273.refs_4_), channel_id=1, source_target_pairs={{0,2},{2,0},{1,3},{3,1},{4,6},{6,4},{5,7},{7,5},{8,10},{10,8},{9,1... | collective-permute-start | bytes 442376 | tf_op jit(solution)/shard_map/ppermute | solution.py:418
  78.5 12.6 %collective-permute-start.2 = (bf16[256,288]{1,0:T(8,128)(2,1)S(1)}, bf16[256,288]{1,0:T(8,128)(2,1)S(1)}, u32[]{:S(2)}, u32[]{:S(2)}) collective-permute-start(bf16[256,288]{1,0:T(8,128)(2,1)S(1)} %collective-permute-done.refs_5_), channel_id=1, source_target_pairs={{0,2},{2,0},{1,3},{3,1},{4,6},{6,4},{5,7},{7,5},{8,10},{10,8},{9,1... | collective-permute-start | bytes 442376 | tf_op jit(solution)/shard_map/ppermute | solution.py:418
  97.6 2.2 collective-permute-start.6
  108.6 8.5 %collective-permute-start.7 = (bf16[256,1152]{1,0:T(8,128)(2,1)}, bf16[256,1152]{1,0:T(8,128)(2,1)S(1)}, u32[]{:S(2)}, u32[]{:S(2)}) collective-permute-start(bf16[256,1152]{1,0:T(8,128)(2,1)} %get-tuple-element.84), channel_id=1, source_target_pairs={{0,1},{1,0},{2,3},{3,2},{4,5},{5,4},{6,7},{7,6},{8,9},{9,8},{10,11... | collective-permute-start | bytes 1769480 | tf_op jit(solution)/shard_map/ppermute | solution.py:421
  117.2 10.0 %collective-permute-start.8 = (bf16[128,1152]{1,0:T(8,128)(2,1)S(1)}, bf16[128,1152]{1,0:T(8,128)(2,1)S(1)}, u32[]{:S(2)}, u32[]{:S(2)}) collective-permute-start(bf16[128,1152]{1,0:T(8,128)(2,1)S(1)} %add_convert_fusion.2), channel_id=1, source_target_pairs={{0,2},{2,0},{1,3},{3,1},{4,6},{6,4},{5,7},{7,5},{8,10},{10,8},{9,1... | collective-permute-start | bytes 884744 | tf_op jit(solution)/shard_map/ppermute | solution.py:418
  157.0 9.7 %collective-permute-start.10 = (bf16[128,2560]{1,0:T(8,128)(2,1)}, bf16[128,2560]{1,0:T(8,128)(2,1)S(1)}, u32[]{:S(2)}, u32[]{:S(2)}) collective-permute-start(bf16[128,2560]{1,0:T(8,128)(2,1)} %get-tuple-element.90), channel_id=1, source_target_pairs={{0,1},{1,0},{2,3},{3,2},{4,5},{5,4},{6,7},{7,6},{8,9},{9,8},{10,11... | collective-permute-start | bytes 1966088 | tf_op jit(solution)/shard_map/ppermute | solution.py:421
  157.3 9.4 %collective-permute-start.9 = (bf16[128,1152]{1,0:T(8,128)(2,1)}, bf16[128,1152]{1,0:T(8,128)(2,1)S(1)}, u32[]{:S(2)}, u32[]{:S(2)}) collective-permute-start(bf16[128,1152]{1,0:T(8,128)(2,1)} %get-tuple-element.88.refs_0_), channel_id=1, source_target_pairs={{0,2},{2,0},{1,3},{3,1},{4,6},{6,4},{5,7},{7,5},{8,10},{10,8},{9,1... | collective-permute-start | bytes 884744 | tf_op jit(solution)/shard_map/ppermute | solution.py:418
  159.0 11.5 %collective-permute-start.14 = (bf16[128,5248]{1,0:T(8,128)(2,1)S(1)}, bf16[128,5248]{1,0:T(8,128)(2,1)S(1)}, u32[]{:S(2)}, u32[]{:S(2)}) collective-permute-start(bf16[128,5248]{1,0:T(8,128)(2,1)S(1)} %copy-done.17), channel_id=1, source_target_pairs={{0,1},{1,0},{2,3},{3,2},{4,5},{5,4},{6,7},{7,6},{8,9},{9,8},{10,11... | collective-permute-start | bytes 4030472 | tf_op jit(solution)/shard_map/ppermute | solution.py:421
  167.7 45.0 %collective-permute-start.11 = (bf16[128,7808]{1,0:T(8,128)(2,1)S(1)}, bf16[128,7808]{1,0:T(8,128)(2,1)}, u32[]{:S(2)}, u32[]{:S(2)}) collective-permute-start(bf16[128,7808]{1,0:T(8,128)(2,1)S(1)} %pad_maximum_fusion.refs_8_), channel_id=1, source_target_pairs={{0,2},{2,0},{1,3},{3,1},{4,6},{6,4},{5,7},{7,5},{8,10},{10,8},{9,1... | collective-permute-start | bytes 5996552 | tf_op jit(solution)/shard_map/ppermute | solution.py:418
  168.5 2.0 collective-permute-start.13
  180.7 7.3 %collective-permute-start.15 = (bf16[256,1152]{1,0:T(8,128)(2,1)}, bf16[256,1152]{1,0:T(8,128)(2,1)S(1)}, u32[]{:S(2)}, u32[]{:S(2)}) collective-permute-start(bf16[256,1152]{1,0:T(8,128)(2,1)} %get-tuple-element.98), channel_id=1, source_target_pairs={{0,1},{1,0},{2,3},{3,2},{4,5},{5,4},{6,7},{7,6},{8,9},{9,8},{10,11... | collective-permute-start | bytes 1769480 | tf_op jit(solution)/shard_map/ppermute | solution.py:421
  214.1 5.9 %collective-permute-start.16 = (bf16[128,7808]{1,0:T(8,128)(2,1)}, bf16[128,7808]{1,0:T(8,128)(2,1)}, u32[]{:S(2)}, u32[]{:S(2)}) collective-permute-start(bf16[128,7808]{1,0:T(8,128)(2,1)} %hold.10.refs_2_), channel_id=1, source_target_pairs={{0,1},{1,0},{2,3},{3,2},{4,5},{5,4},{6,7},{7,6},{8,9},{9,8},{10,11... | collective-permute-start | bytes 5996552 | tf_op jit(solution)/shard_map/ppermute | solution.py:421
  214.2 31.9 %collective-permute-start.24 = (bf16[4,144,1152]{2,1,0:T(8,128)(2,1)}, bf16[4,144,1152]{2,1,0:T(8,128)(2,1)}, u32[]{:S(2)}, u32[]{:S(2)}) collective-permute-start(bf16[4,144,1152]{2,1,0:T(8,128)(2,1)} %get-tuple-element.118), channel_id=1, source_target_pairs={{0,8},{4,12},{8,0},{12,4},{16,24},{20,28},{24,16},{28,20},{1,9},{5... | collective-permute-start | bytes 3981320 | tf_op jit(solution)/shard_map/ppermute | solution.py:415
  215.4 32.2 %collective-permute-start.25 = (bf16[4,144,1152]{2,1,0:T(8,128)(2,1)S(1)}, bf16[4,144,1152]{2,1,0:T(8,128)(2,1)}, u32[]{:S(2)}, u32[]{:S(2)}) collective-permute-start(bf16[4,144,1152]{2,1,0:T(8,128)(2,1)S(1)} %copy-done.2), channel_id=1, source_target_pairs={{0,4},{4,0},{8,12},{12,8},{16,20},{20,16},{24,28},{28,24},{1,5},{5... | collective-permute-start | bytes 3981320 | tf_op jit(solution)/shard_map/ppermute | solution.py:415
  218.2 8.8 %collective-permute-start.17 = (bf16[128,1152]{1,0:T(8,128)(2,1)}, bf16[128,1152]{1,0:T(8,128)(2,1)S(1)}, u32[]{:S(2)}, u32[]{:S(2)}) collective-permute-start(bf16[128,1152]{1,0:T(8,128)(2,1)} %copy-done.5), channel_id=1, source_target_pairs={{0,2},{2,0},{1,3},{3,1},{4,6},{6,4},{5,7},{7,5},{8,10},{10,8},{9,1... | collective-permute-start | bytes 884744 | tf_op jit(solution)/shard_map/ppermute | solution.py:418
  232.2 19.8 %collective-permute-start.18 = (bf16[128,1152]{1,0:T(8,128)(2,1)}, bf16[128,1152]{1,0:T(8,128)(2,1)S(1)}, u32[]{:S(2)}, u32[]{:S(2)}) collective-permute-start(bf16[128,1152]{1,0:T(8,128)(2,1)} %get-tuple-element.104.refs_0_.refs_2_), channel_id=1, source_target_pairs={{0,2},{2,0},{1,3},{3,1},{4,6},{6,4},{5,7},{7,5},{8,10},{10,8},{9,1... | collective-permute-start | bytes 884744 | tf_op jit(solution)/shard_map/ppermute | solution.py:418
  233.6 22.8 %collective-permute-start.19 = (bf16[128,1152]{1,0:T(8,128)(2,1)}, bf16[128,1152]{1,0:T(8,128)(2,1)S(1)}, u32[]{:S(2)}, u32[]{:S(2)}) collective-permute-start(bf16[128,1152]{1,0:T(8,128)(2,1)} %get-tuple-element.104.refs_0_.refs_2_), channel_id=1, source_target_pairs={{0,1},{1,0},{2,3},{3,2},{4,5},{5,4},{6,7},{7,6},{8,9},{9,8},{10,11... | collective-permute-start | bytes 884744 | tf_op jit(solution)/shard_map/ppermute | solution.py:421
  233.6 60.3 %collective-permute-start.28 = (bf16[4,352,768]{2,1,0:T(8,128)(2,1)}, bf16[4,352,768]{2,1,0:T(8,128)(2,1)}, u32[]{:S(2)}, u32[]{:S(2)}) collective-permute-start(bf16[4,352,768]{2,1,0:T(8,128)(2,1)} %get-tuple-element.103.refs_8_), channel_id=1, source_target_pairs={{0,4},{4,0},{8,12},{12,8},{16,20},{20,16},{24,28},{28,24},{1,5},{5... | collective-permute-start | bytes 6488072 | tf_op jit(solution)/shard_map/ppermute | solution.py:415
  251.1 35.8 %collective-permute-start.27 = (bf16[2,144,1152]{2,1,0:T(8,128)(2,1)}, bf16[2,144,1152]{2,1,0:T(8,128)(2,1)}, u32[]{:S(2)}, u32[]{:S(2)}) collective-permute-start(bf16[2,144,1152]{2,1,0:T(8,128)(2,1)} %slice.456), channel_id=1, source_target_pairs={{0,8},{4,12},{8,0},{12,4},{16,24},{20,28},{24,16},{28,20},{1,9},{5... | collective-permute-start | bytes 1990664 | tf_op jit(solution)/shard_map/ppermute | solution.py:415
  251.9 4.5 %collective-permute-start.20 = (bf16[128,1152]{1,0:T(8,128)(2,1)S(1)}, bf16[128,1152]{1,0:T(8,128)(2,1)S(1)}, u32[]{:S(2)}, u32[]{:S(2)}) collective-permute-start(bf16[128,1152]{1,0:T(8,128)(2,1)S(1)} %collective-permute-done.18.refs_1_), channel_id=1, source_target_pairs={{0,1},{1,0},{2,3},{3,2},{4,5},{5,4},{6,7},{7,6},{8,9},{9,8},{10,11... | collective-permute-start | bytes 884744 | tf_op jit(solution)/shard_map/ppermute | solution.py:421
  255.9 32.2 %collective-permute-start.26 = (bf16[2,144,1152]{2,1,0:T(8,128)(2,1)}, bf16[2,144,1152]{2,1,0:T(8,128)(2,1)}, u32[]{:S(2)}, u32[]{:S(2)}) collective-permute-start(bf16[2,144,1152]{2,1,0:T(8,128)(2,1)} %slice.457), channel_id=1, source_target_pairs={{0,16},{4,20},{8,24},{12,28},{16,0},{20,4},{24,8},{28,12},{1,17},{... | collective-permute-start | bytes 1990664 | tf_op jit(solution)/shard_map/ppermute | solution.py:415
  268.9 2.3 collective-permute-start.22
  269.0 5.3 %collective-permute-start.33 = (f32[1,7168]{1,0:T(1,128)S(1)}, f32[1,7168]{1,0:T(1,128)S(1)}, u32[]{:S(2)}, u32[]{:S(2)}) collective-permute-start(f32[1,7168]{1,0:T(1,128)S(1)} %constant_dynamic-update-slice_fusion.6), channel_id=1, source_target_pairs={{0,1},{1,0},{2,3},{3,2},{4,5},{5,4},{6,7},{7,6},{8,9},{9,8},{10,11... | collective-permute-start | bytes 86024 | tf_op jit(solution)/shard_map/ppermute | solution.py:421
  272.0 9.4 %collective-permute-start.23 = (bf16[128,1152]{1,0:T(8,128)(2,1)}, bf16[128,1152]{1,0:T(8,128)(2,1)}, u32[]{:S(2)}, u32[]{:S(2)}) collective-permute-start(bf16[128,1152]{1,0:T(8,128)(2,1)} %add_convert_fusion), channel_id=1, source_target_pairs={{0,2},{2,0},{1,3},{3,1},{4,6},{6,4},{5,7},{7,5},{8,10},{10,8},{9,1... | collective-permute-start | bytes 884744 | tf_op jit(solution)/shard_map/ppermute | solution.py:418
  279.4 54.0 %collective-permute-start.21 = (bf16[4,144,1184]{2,1,0:T(8,128)(2,1)}, bf16[4,144,1184]{2,1,0:T(8,128)(2,1)S(1)}, u32[]{:S(2)}, u32[]{:S(2)}) collective-permute-start(bf16[4,144,1184]{2,1,0:T(8,128)(2,1)} %get-tuple-element.110.refs_8_), channel_id=1, source_target_pairs={{0,4},{4,0},{8,12},{12,8},{16,20},{20,16},{24,28},{28,24},{1,5},{5... | collective-permute-start | bytes 4091912 | tf_op jit(solution)/shard_map/ppermute | solution.py:415
  298.9 31.4 %collective-permute-start.29 = (bf16[2,352,768]{2,1,0:T(8,128)(2,1)}, bf16[2,352,768]{2,1,0:T(8,128)(2,1)}, u32[]{:S(2)}, u32[]{:S(2)}) collective-permute-start(bf16[2,352,768]{2,1,0:T(8,128)(2,1)} %slice.454.refs_1_), channel_id=1, source_target_pairs={{0,8},{4,12},{8,0},{12,4},{16,24},{20,28},{24,16},{28,20},{1,9},{5... | collective-permute-start | bytes 3244040 | tf_op jit(solution)/shard_map/ppermute | solution.py:415
  302.3 35.1 %collective-permute-start.39 = (bf16[1,144,1152]{2,1,0:T(8,128)(2,1)}, bf16[1,144,1152]{2,1,0:T(8,128)(2,1)}, u32[]{:S(2)}, u32[]{:S(2)}) collective-permute-start(bf16[1,144,1152]{2,1,0:T(8,128)(2,1)} %slice.461), channel_id=1, source_target_pairs={{0,4},{4,0},{8,12},{12,8},{16,20},{20,16},{24,28},{28,24},{1,5},{5... | collective-permute-start | bytes 995336 | tf_op jit(solution)/shard_map/ppermute | solution.py:415
  303.8 5.1 %collective-permute-start.34 = (f32[1,34816]{1,0:T(1,128)S(1)}, f32[1,34816]{1,0:T(1,128)S(1)}, u32[]{:S(2)}, u32[]{:S(2)}) collective-permute-start(f32[1,34816]{1,0:T(1,128)S(1)} %hold.14), channel_id=1, source_target_pairs={{0,2},{2,0},{1,3},{3,1},{4,6},{6,4},{5,7},{7,5},{8,10},{10,8},{9,1... | collective-permute-start | bytes 417800 | tf_op jit(solution)/shard_map/ppermute | solution.py:418
  306.5 31.1 %collective-permute-start.40 = (bf16[1,144,1152]{2,1,0:T(8,128)(2,1)}, bf16[1,144,1152]{2,1,0:T(8,128)(2,1)}, u32[]{:S(2)}, u32[]{:S(2)}) collective-permute-start(bf16[1,144,1152]{2,1,0:T(8,128)(2,1)} %slice.460), channel_id=1, source_target_pairs={{0,16},{4,20},{8,24},{12,28},{16,0},{20,4},{24,8},{28,12},{1,17},{... | collective-permute-start | bytes 995336 | tf_op jit(solution)/shard_map/ppermute | solution.py:415
  311.5 25.9 %all-to-all-start.3 = ((bf16[8,4,864]{2,1,0:T(4,128)(2,1)}), bf16[8,4,864]{2,1,0:T(4,128)(2,1)S(1)}, u32[]{:S(2)}, u32[]{:S(2)}) async-start(bf16[8,4,864]{2,1,0:T(4,128)(2,1)} %bitcast.168), calls=%async_computation.3 | async-start | bytes 114688 | tf_op jit(solution)/shard_map/all_to_all | solution.py:424
  333.4 23.3 %collective-permute-start.37 = (bf16[1,352,768]{2,1,0:T(8,128)(2,1)}, bf16[1,352,768]{2,1,0:T(8,128)(2,1)}, u32[]{:S(2)}, u32[]{:S(2)}) collective-permute-start(bf16[1,352,768]{2,1,0:T(8,128)(2,1)} %slice.458.refs_2_), channel_id=1, source_target_pairs={{0,16},{4,20},{8,24},{12,28},{16,0},{20,4},{24,8},{28,12},{1,17},{... | collective-permute-start | bytes 1622024 | tf_op jit(solution)/shard_map/ppermute | solution.py:415
  335.2 26.5 %collective-permute-start.36 = (bf16[2,144,1184]{2,1,0:T(8,128)(2,1)S(1)}, bf16[2,144,1184]{2,1,0:T(8,128)(2,1)}, u32[]{:S(2)}, u32[]{:S(2)}) collective-permute-start(bf16[2,144,1184]{2,1,0:T(8,128)(2,1)S(1)} %slice.455.refs_1_), channel_id=1, source_target_pairs={{0,8},{4,12},{8,0},{12,4},{16,24},{20,28},{24,16},{28,20},{1,9},{5... | collective-permute-start | bytes 2045960 | tf_op jit(solution)/shard_map/ppermute | solution.py:415
  336.7 15.2 %collective-permute-start.30 = (bf16[128,1152]{1,0:T(8,128)(2,1)}, bf16[128,1152]{1,0:T(8,128)(2,1)}, u32[]{:S(2)}, u32[]{:S(2)}) collective-permute-start(bf16[128,1152]{1,0:T(8,128)(2,1)} %get-tuple-element.123), channel_id=1, source_target_pairs={{0,2},{2,0},{1,3},{3,1},{4,6},{6,4},{5,7},{7,5},{8,10},{10,8},{9,1... | collective-permute-start | bytes 884744 | tf_op jit(solution)/shard_map/ppermute | solution.py:418
  337.4 21.7 %collective-permute-start.31 = (bf16[128,1152]{1,0:T(8,128)(2,1)}, bf16[128,1152]{1,0:T(8,128)(2,1)}, u32[]{:S(2)}, u32[]{:S(2)}) collective-permute-start(bf16[128,1152]{1,0:T(8,128)(2,1)} %get-tuple-element.123), channel_id=1, source_target_pairs={{0,1},{1,0},{2,3},{3,2},{4,5},{5,4},{6,7},{7,6},{8,9},{9,8},{10,11... | collective-permute-start | bytes 884744 | tf_op jit(solution)/shard_map/ppermute | solution.py:421
  337.5 5.0 %collective-permute-start.35 = (bf16[8,4,864]{2,1,0:T(4,128)(2,1)S(1)}, bf16[8,4,864]{2,1,0:T(4,128)(2,1)S(1)}, u32[]{:S(2)}, u32[]{:S(2)}) collective-permute-start(bf16[8,4,864]{2,1,0:T(4,128)(2,1)S(1)} %hold.15.refs_2_), channel_id=1, source_target_pairs={{0,1},{1,0},{2,3},{3,2},{4,5},{5,4},{6,7},{7,6},{8,9},{9,8},{10,11... | collective-permute-start | bytes 165896 | tf_op jit(solution)/shard_map/ppermute | solution.py:421
  351.9 7.2 %collective-permute-start.32 = (bf16[128,1152]{1,0:T(8,128)(2,1)}, bf16[128,1152]{1,0:T(8,128)(2,1)S(1)}, u32[]{:S(2)}, u32[]{:S(2)}) collective-permute-start(bf16[128,1152]{1,0:T(8,128)(2,1)} %collective-permute-done.30), channel_id=1, source_target_pairs={{0,1},{1,0},{2,3},{3,2},{4,5},{5,4},{6,7},{7,6},{8,9},{9,8},{10,11... | collective-permute-start | bytes 884744 | tf_op jit(solution)/shard_map/ppermute | solution.py:421
  357.9 31.6 %collective-permute-start.41 = (bf16[352,768]{1,0:T(8,128)(2,1)S(1)}, bf16[352,768]{1,0:T(8,128)(2,1)}, u32[]{:S(2)}, u32[]{:S(2)}) collective-permute-start(bf16[352,768]{1,0:T(8,128)(2,1)S(1)} %fusion.20.refs_2_), channel_id=1, source_target_pairs={{0,1},{1,0},{2,3},{3,2},{4,5},{5,4},{6,7},{7,6},{8,9},{9,8},{10,11... | collective-permute-start | bytes 1622024 | tf_op jit(solution)/shard_map/ppermute | solution.py:421
  357.9 29.8 %collective-permute-start.42 = (bf16[352,768]{1,0:T(8,128)(2,1)S(1)}, bf16[352,768]{1,0:T(8,128)(2,1)}, u32[]{:S(2)}, u32[]{:S(2)}) collective-permute-start(bf16[352,768]{1,0:T(8,128)(2,1)S(1)} %fusion.20.refs_2_), channel_id=1, source_target_pairs={{0,2},{2,0},{1,3},{3,1},{4,6},{6,4},{5,7},{7,5},{8,10},{10,8},{9,1... | collective-permute-start | bytes 1622024 | tf_op jit(solution)/shard_map/ppermute | solution.py:418
  363.0 23.6 %collective-permute-start.38 = (bf16[1,144,1184]{2,1,0:T(8,128)(2,1)S(1)}, bf16[1,144,1184]{2,1,0:T(8,128)(2,1)S(1)}, u32[]{:S(2)}, u32[]{:S(2)}) collective-permute-start(bf16[1,144,1184]{2,1,0:T(8,128)(2,1)S(1)} %slice.459.refs_1_), channel_id=1, source_target_pairs={{0,16},{4,20},{8,24},{12,28},{16,0},{20,4},{24,8},{28,12},{1,17},{... | collective-permute-start | bytes 1022984 | tf_op jit(solution)/shard_map/ppermute | solution.py:415
  367.1 28.9 %all-to-all-start.4 = ((f32[8,1,18112]{2,1,0:T(1,128)}), f32[8,1,18112]{2,1,0:T(1,128)}, u32[]{:S(2)}, u32[]{:S(2)}) async-start(f32[8,1,18112]{2,1,0:T(1,128)} %copy.132), calls=%async_computation.4 | async-start | bytes 1163264 | tf_op jit(solution)/shard_map/all_to_all | solution.py:424
  387.7 2.9 collective-permute-start.43
  (83 other events, 523.3 us)
Sparse Core Ops, SparseCore 0:
  11.5 129.6 all-gather.2

commit v5 on v4

--- a/solution.py
+++ b/solution.py
@@ -832,10 +832,11 @@
     )
     heads_got = flip_dp(heads_second, 1)
 
-    fc2_next, fc1_next, pg_got = hold([fc2_next, fc1_next, pg_got], [g_in])
+    (pg_got,) = hold([pg_got], [g_in])
     pg_v = halves(pg_first.astype(F32) + pg_got.astype(F32))
     pg_sent = pg_v[1].astype(BF16)
     pg_got = flip_dp(pg_sent, 2)
+    fc2_next, fc1_next = hold([fc2_next, fc1_next], [pg_sent])
     fc2_v = fc2_v[0] + fc2_next.astype(F32)
     fc1_v = halves(fc1_v[0] + fc1_next.astype(F32))
     fc2_v = halves(fc2_v)

time: 414 us -> 414 us (level)
  waiting for transfers between devices: 149 us -> 138 us
  starting transfers between devices: 48.2 us -> 56.3 us
    all_gather x1, waiting for transfers between devices: 14 us -> 7.24 us  [body(): gathered = lax.all_gather(packed, ('dp', 'tensor'), axis=0)]
    ppermute x12, starting transfers between devices: 12.9 us -> 18.1 us  [swap_y(): return lax.ppermute(x, 'tensor', [(0, 2), (2, 0), (1, 3), (3, 1)])]
    unnamed x177 -> x165, local copies, waits for them, and re-layouts: 21.7 us -> 23.8 us
  transfers between devices with their start and end apart: 50 -> 50, of which waited for: 23 -> 20; matrix products, arithmetic and copies ran while one was open for 20% -> 20% of each run, Pallas kernels for 17% -> 17%
where the time goes in v5:
time: 414 us; the launch traced here: 409 us
  waiting for transfers between devices  138 us (33%)
  Pallas kernels  87.3 us (21%)
  local copies, waits for them, and re-layouts  60 us (14%)
  starting transfers between devices  56.3 us (14%)
  other arithmetic  44.8 us (11%)
  between operations  15.5 us (4%)
  matrix products  7.59 us (2%)
    pallas_call x11, Pallas kernels, call(): pl.pallas_call(kernel, out_shape=tuple(outs), in_specs=list(in_specs or [...  87.3 us
    ppermute x12, waiting for transfers between devices, flip_dp(): return lax.ppermute(x, 'dp', [(k, k ^ mask) for k in range(n_dp)])  51.5 us
    ppermute x12, waiting for transfers between devices, swap_y(): return lax.ppermute(x, 'tensor', [(0, 2), (2, 0), (1, 3), (3, 1)])  48.3 us
    all_to_all x5, waiting for transfers between devices, exchange_dp(): return lax.all_to_all(x, 'dp', 0, 0, tiled=True)  27.2 us
    unnamed x165, local copies, waits for them, and re-layouts  23.8 us
    all_to_all x5, starting transfers between devices, exchange_dp(): return lax.all_to_all(x, 'dp', 0, 0, tiled=True)  22.6 us
    ppermute x12, starting transfers between devices, swap_y(): return lax.ppermute(x, 'tensor', [(0, 2), (2, 0), (1, 3), (3, 1)])  18.1 us
    ppermute x12, starting transfers between devices, flip_dp(): return lax.ppermute(x, 'dp', [(k, k ^ mask) for k in range(n_dp)])  12.5 us
  transfers between devices with their start and end apart: 50, of which 20 were waited for; matrix products, arithmetic and copies ran while one was open for 20% of the time, Pallas kernels for 17%

profile of v5, /device:TPU:0, one launch (start us, length us, event | category | flops | bytes accessed | tf_op | source)
XLA Modules:
  0.0 409.4 jit_solution(9306344238775687413)
XLA Ops:
  14.1 7.3 %all-to-all-start = ((s32[8,1,16]{2,1,0:T(1,128)}), s32[8,1,16]{2,1,0:T(1,128)S(1)}, u32[]{:S(2)}, u32[]{:S(2)}) async-start(s32[8,1,16]{2,1,0:T(1,128)} %broadcast_in_dim.17), calls=%async_computation | async-start | bytes 8192 | tf_op jit(solution)/shard_map/all_to_all | solution.py:424
  21.6 6.1 %all-to-all-done = s32[8,1,16]{2,1,0:T(1,128)S(1)} async-done(((s32[8,1,16]{2,1,0:T(1,128)}), s32[8,1,16]{2,1,0:T(1,128)S(1)}, u32[]{:S(2)}, u32[]{:S(2)}) %all-to-all-start) | async-done | bytes 544 | tf_op jit(solution)/shard_map/all_to_all | solution.py:424
  29.8 3.4 all-to-all-start.1
  33.2 1.6 collective-permute-start.4
  34.8 9.7 %all-to-all-done.1 = bf16[8,154,64]{1,2,0:T(8,128)(2,1)S(1)} async-done(((bf16[8,154,64]{1,2,0:T(8,128)(2,1)}), bf16[8,154,64]{1,2,0:T(8,128)(2,1)S(1)}, u32[]{:S(2)}, u32[]{:S(2)}) %all-to-all-start.1) | async-done | bytes 157728 | tf_op jit(solution)/shard_map/all_to_all | solution.py:424
  46.4 3.9 all-to-all-start.2
  53.8 11.3 %all-to-all-done.2 = f32[8,8,864]{2,1,0:T(8,128)S(1)} async-done(((f32[8,8,864]{2,1,0:T(8,128)}), f32[8,8,864]{2,1,0:T(8,128)S(1)}, u32[]{:S(2)}, u32[]{:S(2)}) %all-to-all-start.2) | async-done | bytes 221216 | tf_op jit(solution)/shard_map/all_to_all | solution.py:424
  67.7 9.8 %attention.1 = (bf16[512,1152]{1,0:T(8,128)(2,1)}, bf16[512,288]{1,0:T(8,128)(2,1)}, bf16[512,288]{1,0:T(8,128)(2,1)}, bf16[512,288]{1,0:T(8,128)(2,1)}, bf16[512,288]{1,0:T(8,128)(2,1)}) custom-call(s32[4]{0:T(128)} %pad_add_fusion.3.refs_0_, bf16[4,128,1152]{2,1,0:T(8,128)(2,1)} %bitcast.150, f32[4,6912]{1,0:T(4,128)} %get-tuple-element.273.refs_2_.refs_5_.refs_6_, ...), custom_call_target="tpu_custom_call" | custom-call | tf_op jit(solution)/shard_map/attention/pallas_call | solution.py:36
  82.2 4.3 %collective-permute-done.1.refs_6_ = bf16[256,288]{1,0:T(8,128)(2,1)S(1)} collective-permute-done((bf16[256,288]{1,0:T(8,128)(2,1)S(1)}, bf16[256,288]{1,0:T(8,128)(2,1)S(1)}, u32[]{:S(2)}, u32[]{:S(2)}) %collective-permute-start.1) | collective-permute-done | bytes 147488 | tf_op jit(solution)/shard_map/ppermute | solution.py:418
  86.4 8.0 %collective-permute-done.2.refs_7_ = bf16[256,288]{1,0:T(8,128)(2,1)S(1)} collective-permute-done((bf16[256,288]{1,0:T(8,128)(2,1)S(1)}, bf16[256,288]{1,0:T(8,128)(2,1)S(1)}, u32[]{:S(2)}, u32[]{:S(2)}) %collective-permute-start.2) | collective-permute-done | bytes 147488 | tf_op jit(solution)/shard_map/ppermute | solution.py:418
  95.1 5.7 %middle.1 = (f32[128,1152]{1,0:T(8,128)}, f32[128,1152]{1,0:T(8,128)}, bf16[256,1152]{1,0:T(8,128)(2,1)}) custom-call(s32[4]{0:T(128)} %pad_add_fusion.3.refs_0_, bf16[4,128,1152]{2,1,0:T(8,128)(2,1)} %bitcast.151, f32[4,6912]{1,0:T(4,128)} %get-tuple-element.273.refs_2_.refs_5_.refs_6_, s32[512,1]{1,0:T(8,128)} %copy.121.refs_4_.refs_3_.refs_8_, ...), custom_call_target="tpu_custom_call" | custom-call | tf_op jit(solution)/shard_map/middle/pallas_call | solution.py:36
  101.4 1.6 collective-permute-done.6.refs_1_
  103.8 7.9 %mlp.1 = (bf16[512,1152]{1,0:T(8,128)(2,1)}, f32[512,1152]{1,0:T(8,128)}, bf16[512,1152]{1,0:T(8,128)(2,1)}, f32[128,1152]{1,0:T(8,128)}, f32[128,1152]{1,0:T(8,128)}, /*index=5*/bf16[256,1152]{1,0:T(8,128)(2,1)}) custom-call(bf16[256,1152]{1,0:T(8,128)(2,1)} %get-tuple-element.81.refs_0_, bf16[256,1152]{1,0:T(8,128)(2,1)} %copy-done.36, ...), custom_call_target="tpu_custom_call" | custom-call | tf_op jit(solution)/shard_map/mlp/pallas_call | solution.py:36
  118.3 1.7 dynamic-slice_bitcast_fusion.refs_8_
  121.7 2.8 collective-permute-start.8
  126.4 5.6 %collective-permute-done.8.refs_3_ = bf16[128,1152]{1,0:T(8,128)(2,1)S(1)} collective-permute-done((bf16[128,1152]{1,0:T(8,128)(2,1)S(1)}, bf16[128,1152]{1,0:T(8,128)(2,1)S(1)}, u32[]{:S(2)}, u32[]{:S(2)}) %collective-permute-start.8) | collective-permute-done | bytes 294944 | tf_op jit(solution)/shard_map/ppermute | solution.py:418
  132.0 7.2 %all-gather.3.cloned.1.call-done = bf16[16896,512]{1,0:T(8,128)(2,1)} async-done(((bf16[528,512]{1,0:T(8,128)(2,1)}), bf16[16896,512]{1,0:T(8,128)(2,1)}) %all-gather.3.cloned.1.call-update) | async-done | bytes 17301520 | tf_op jit(solution)/shard_map/all_gather | solution.py:446
  139.3 15.8 %projector.1 = (bf16[128,5248]{1,0:T(8,128)(2,1)}, bf16[128,2560]{1,0:T(8,128)(2,1)}, bf16[128,2560]{1,0:T(8,128)(2,1)}, f32[128,1152]{1,0:T(8,128)}, bf16[128,1...) custom-call(s32[4]{0:T(128)} %pad_add_fusion.2.refs_0_, ...), custom_call_target="tpu_custom_call" | custom-call | tf_op jit(solution)/shard_map/projector/pallas_call | solution.py:36
  158.8 5.9 %collective-permute-done.9.refs_1_ = bf16[128,1152]{1,0:T(8,128)(2,1)S(1)} collective-permute-done((bf16[128,1152]{1,0:T(8,128)(2,1)}, bf16[128,1152]{1,0:T(8,128)(2,1)S(1)}, u32[]{:S(2)}, u32[]{:S(2)}) %collective-permute-start.9) | collective-permute-done | bytes 294944 | tf_op jit(solution)/shard_map/ppermute | solution.py:418
  170.6 9.0 %mlp_back.1 = (bf16[512,1152]{1,0:T(8,128)(2,1)}, bf16[512,1152]{1,0:T(8,128)(2,1)}, f32[128,1152]{1,0:T(8,128)}, f32[128,1152]{1,0:T(8,128)}, bf16[256,1152]{1,0:T(8,128)(2,1)}, /*index=5*/f32[1,1152]{1,0:T(1,128)}) custom-call(bf16[128,1152]{1,0:T(8,128)(2,1)} %get-tuple-element.87.refs_0_, bf16[128,1152]{1,0:T(8,128)(2,1)} %copy-done.4, ...), custom_call_target="tpu_custom_call" | custom-call | tf_op jit(solution)/shard_map/mlp_back/pallas_call | solution.py:36
  179.7 7.2 %grad_fc.1 = (bf16[4,144,1152]{2,1,0:T(8,128)(2,1)}, bf16[4,144,1152]{2,1,0:T(8,128)(2,1)}, bf16[4,144,1152]{2,1,0:T(8,128)(2,1)}, bf16[4,144,1152]{2,1,0:T(8,128)(2,1)}) custom-call(s32[4]{0:T(128)} %pad_add_fusion.2.refs_0_, bf16[512,1152]{1,0:T(8,128)(2,1)} %get-tuple-element.91.refs_1_, bf16[512,1152]{1,0:T(8,128)(2,1)} %get-tuple-element.92.refs_2_, ...), custom_call_target="tpu_custom_call" | custom-call | tf_op jit(solution)/shard_map/grad_fc/pallas_call | solution.py:36
  187.0 23.8 %collective-permute-done.11.refs_0_ = bf16[128,7808]{1,0:T(8,128)(2,1)} collective-permute-done((bf16[128,7808]{1,0:T(8,128)(2,1)S(1)}, bf16[128,7808]{1,0:T(8,128)(2,1)}, u32[]{:S(2)}, u32[]{:S(2)}) %collective-permute-start.11) | collective-permute-done | bytes 1998880 | tf_op jit(solution)/shard_map/ppermute | solution.py:418
  212.3 3.6 collective-permute-start.35
  218.5 1.6 collective-permute-start.17
  221.3 7.0 %grad_projector.1 = (bf16[4,352,768]{2,1,0:T(8,128)(2,1)}, bf16[4,352,768]{2,1,0:T(8,128)(2,1)}) custom-call(s32[4]{0:T(128)} %pad_add_fusion.2.refs_0_, bf16[128,5248]{1,0:T(8,128)(2,1)} %get-tuple-element.86.refs_1_, bf16[128,7808]{1,0:T(8,128)(2,1)} %hold.11.refs_2_, bf16[128,5248]{1,0:T(8,128)(2,1)} %copy-done.16, ...), custom_call_target="tpu_custom_call" | custom-call | tf_op jit(solution)/shard_map/grad_projector/pallas_call | solution.py:36
  229.0 4.4 %second_back.1 = (f32[128,1152]{1,0:T(8,128)}, bf16[128,1152]{1,0:T(8,128)(2,1)}, f32[4,1152]{1,0:T(4,128)}, f32[4,1152]{1,0:T(4,128)}, f32[4,1152]{1,0:T(4,128)}, /*index=5*/f32[1,1152]{1,0:T(1,128)}) custom-call(f32[128,1152]{1,0:T(8,128)} %get-tuple-element.99.refs_0_, bf16[256,1152]{1,0:T(8,128)(2,1)} %copy-done.28, bf16[128,1152]{1,0:T(8,128)(2,1)} %copy-done.43, ...), custom_call_target="tpu_custom_call" | custom-call | tf_op jit(solution)/shard_map/second_back/pallas_call | solution.py:36
  234.9 11.0 %collective-permute-done.35.refs_0_ = bf16[4,144,1152]{2,1,0:T(8,128)(2,1)} collective-permute-done((bf16[4,144,1152]{2,1,0:T(8,128)(2,1)}, bf16[4,144,1152]{2,1,0:T(8,128)(2,1)}, u32[]{:S(2)}, u32[]{:S(2)}) %collective-permute-start.35) | collective-permute-done | bytes 1327136 | tf_op jit(solution)/shard_map/ppermute | solution.py:415
  245.9 2.0 collective-permute-done.36.refs_1_
  248.9 1.7 convert_add_fusion.2
  252.9 1.6 convert_add_fusion.3
  258.2 11.6 %attention_back.1 = (bf16[512,896]{1,0:T(8,128)(2,1)}, f32[128,1152]{1,0:T(8,128)}, f32[128,1152]{1,0:T(8,128)}, bf16[256,1152]{1,0:T(8,128)(2,1)}, f32[2,288]{1,0:T(2,128)}, /*index=5*/bf16[512,1152]{1,0:T(8,128)(2,1)}) custom-call(bf16[128,1152]{1,0:T(8,128)(2,1)} %get-tuple-element.103.refs_0_.refs_2_, bf16[128,1152]{1,0:T(8,128)(2,1)} %copy-done.40, ...), custom_call_target="tpu_custom_call" | custom-call | tf_op jit(solution)/shard_map/attention_back/pallas_call | solution.py:36
  275.9 5.0 %grad_heads.1 = (bf16[4,144,1184]{2,1,0:T(8,128)(2,1)}, bf16[4,144,1184]{2,1,0:T(8,128)(2,1)}) custom-call(s32[4]{0:T(128)} %pad_add_fusion.2.refs_0_, bf16[512,1152]{1,0:T(8,128)(2,1)} %get-tuple-element.98.refs_1_, bf16[512,896]{1,0:T(8,128)(2,1)} %get-tuple-element.107.refs_2_, bf16[512,1152]{1,0:T(8,128)(2,1)} %get-tuple-element.108.refs_3_, ...), custom_call_target="tpu_custom_call" | custom-call | tf_op jit(solution)/shard_map/grad_heads/pallas_call | solution.py:36
  282.5 3.8 first_back.1
  288.1 6.2 %collective-permute-done.24.refs_0_ = bf16[4,352,768]{2,1,0:T(8,128)(2,1)} collective-permute-done((bf16[4,352,768]{2,1,0:T(8,128)(2,1)}, bf16[4,352,768]{2,1,0:T(8,128)(2,1)}, u32[]{:S(2)}, u32[]{:S(2)}) %collective-permute-start.24) | collective-permute-done | bytes 2162720 | tf_op jit(solution)/shard_map/ppermute | solution.py:415
  294.3 1.6 copy-done.24
  295.9 2.0 convert_add_fusion
  311.2 3.7 all-to-all-start.3
  315.6 14.8 %collective-permute-done.25 = bf16[2,352,768]{2,1,0:T(8,128)(2,1)} collective-permute-done((bf16[2,352,768]{2,1,0:T(8,128)(2,1)S(1)}, bf16[2,352,768]{2,1,0:T(8,128)(2,1)}, u32[]{:S(2)}, u32[]{:S(2)}) %collective-permute-start.25) | collective-permute-done | bytes 1081376 | tf_op jit(solution)/shard_map/ppermute | solution.py:415
  330.4 2.1 slice_add_fusion
  334.7 1.7 convert_add_fusion.1
  340.8 1.9 fusion.14
  342.7 1.9 fusion.15
  346.4 2.0 copy.131
  348.4 1.9 reshape.359
  351.4 2.7 fusion.26
  359.7 4.2 %collective-permute-done.32 = bf16[2,144,1184]{2,1,0:T(8,128)(2,1)} collective-permute-done((bf16[2,144,1184]{2,1,0:T(8,128)(2,1)S(1)}, bf16[2,144,1184]{2,1,0:T(8,128)(2,1)}, u32[]{:S(2)}, u32[]{:S(2)}) %collective-permute-start.32) | collective-permute-done | bytes 682016 | tf_op jit(solution)/shard_map/ppermute | solution.py:415
  369.3 4.3 %all-to-all-start.4 = ((f32[8,1,18112]{2,1,0:T(1,128)}), f32[8,1,18112]{2,1,0:T(1,128)}, u32[]{:S(2)}, u32[]{:S(2)}) async-start(f32[8,1,18112]{2,1,0:T(1,128)} %copy.132), calls=%async_computation.4 | async-start | bytes 1163264 | tf_op jit(solution)/shard_map/all_to_all | solution.py:424
  373.6 13.2 %collective-permute-done.34 = bf16[1,144,1184]{2,1,0:T(8,128)(2,1)S(1)} collective-permute-done((bf16[1,144,1184]{2,1,0:T(8,128)(2,1)S(1)}, bf16[1,144,1184]{2,1,0:T(8,128)(2,1)S(1)}, u32[]{:S(2)}, u32[]{:S(2)}) %collective-permute-start.34) | collective-permute-done | bytes 341024 | tf_op jit(solution)/shard_map/ppermute | solution.py:415
  (381 shorter events, 116.8 us)
Async XLA Ops:
  7.2 132.0 %all-gather.3.cloned.1.call-start = ((), (), s32[]{:S(2)}) async-start(), calls=%async_computation.5 | async-start | bytes 17842176 | tf_op jit(solution)/shard_map/all_gather | solution.py:446
  14.1 13.6 %all-to-all-start = ((s32[8,1,16]{2,1,0:T(1,128)}), s32[8,1,16]{2,1,0:T(1,128)S(1)}, u32[]{:S(2)}, u32[]{:S(2)}) async-start(s32[8,1,16]{2,1,0:T(1,128)} %broadcast_in_dim.17), calls=%async_computation | async-start | bytes 8192 | tf_op jit(solution)/shard_map/all_to_all | solution.py:424
  29.8 14.8 %all-to-all-start.1 = ((bf16[8,154,64]{1,2,0:T(8,128)(2,1)}), bf16[8,154,64]{1,2,0:T(8,128)(2,1)S(1)}, u32[]{:S(2)}, u32[]{:S(2)}) async-start(bf16[8,154,64]{1,2,0:T(8,128)(2,1)} %broadcast_in_dim.18), calls=%async_computation.1 | async-start | bytes 524288 | tf_op jit(solution)/shard_map/all_to_all | solution.py:424
  33.2 20.5 %collective-permute-start.4 = (bf16[288,1152]{1,0:T(8,128)(2,1)S(1)}, bf16[288,1152]{1,0:T(8,128)(2,1)}, u32[]{:S(2)}, u32[]{:S(2)}) collective-permute-start(bf16[288,1152]{1,0:T(8,128)(2,1)S(1)} %copy-done.23), channel_id=1, source_target_pairs={{0,2},{2,0},{1,3},{3,1},{4,6},{6,4},{5,7},{7,5},{8,10},{10,8},{9,1... | collective-permute-start | bytes 1990664 | tf_op jit(solution)/shard_map/ppermute | solution.py:418
  34.8 47.4 %collective-permute-start.3 = (bf16[288,1152]{1,0:T(8,128)(2,1)S(1)}, bf16[288,1152]{1,0:T(8,128)(2,1)}, u32[]{:S(2)}, u32[]{:S(2)}) collective-permute-start(bf16[288,1152]{1,0:T(8,128)(2,1)S(1)} %copy-done.23), channel_id=1, source_target_pairs={{0,1},{1,0},{2,3},{3,2},{4,5},{5,4},{6,7},{7,6},{8,9},{9,8},{10,11... | collective-permute-start | bytes 1990664 | tf_op jit(solution)/shard_map/ppermute | solution.py:421
  46.4 18.7 %all-to-all-start.2 = ((f32[8,8,864]{2,1,0:T(8,128)}), f32[8,8,864]{2,1,0:T(8,128)S(1)}, u32[]{:S(2)}, u32[]{:S(2)}) async-start(f32[8,8,864]{2,1,0:T(8,128)} %fusion.6), calls=%async_computation.2 | async-start | bytes 458752 | tf_op jit(solution)/shard_map/all_to_all | solution.py:424
  53.7 40.7 %collective-permute-start.5 = (bf16[288,1152]{1,0:T(8,128)(2,1)}, bf16[288,1152]{1,0:T(8,128)(2,1)}, u32[]{:S(2)}, u32[]{:S(2)}) collective-permute-start(bf16[288,1152]{1,0:T(8,128)(2,1)} %collective-permute-done.4.refs_10_), channel_id=1, source_target_pairs={{0,1},{1,0},{2,3},{3,2},{4,5},{5,4},{6,7},{7,6},{8,9},{9,8},{10,11... | collective-permute-start | bytes 1990664 | tf_op jit(solution)/shard_map/ppermute | solution.py:421
  78.6 7.8 %collective-permute-start.1 = (bf16[256,288]{1,0:T(8,128)(2,1)S(1)}, bf16[256,288]{1,0:T(8,128)(2,1)S(1)}, u32[]{:S(2)}, u32[]{:S(2)}) collective-permute-start(bf16[256,288]{1,0:T(8,128)(2,1)S(1)} %get-tuple-element.271.refs_4_), channel_id=1, source_target_pairs={{0,2},{2,0},{1,3},{3,1},{4,6},{6,4},{5,7},{7,5},{8,10},{10,8},{9,1... | collective-permute-start | bytes 442376 | tf_op jit(solution)/shard_map/ppermute | solution.py:418
  80.2 14.2 %collective-permute-start.2 = (bf16[256,288]{1,0:T(8,128)(2,1)S(1)}, bf16[256,288]{1,0:T(8,128)(2,1)S(1)}, u32[]{:S(2)}, u32[]{:S(2)}) collective-permute-start(bf16[256,288]{1,0:T(8,128)(2,1)S(1)} %collective-permute-done.refs_5_), channel_id=1, source_target_pairs={{0,2},{2,0},{1,3},{3,1},{4,6},{6,4},{5,7},{7,5},{8,10},{10,8},{9,1... | collective-permute-start | bytes 442376 | tf_op jit(solution)/shard_map/ppermute | solution.py:418
  100.8 2.2 collective-permute-start.6
  111.8 8.6 %collective-permute-start.7 = (bf16[256,1152]{1,0:T(8,128)(2,1)}, bf16[256,1152]{1,0:T(8,128)(2,1)S(1)}, u32[]{:S(2)}, u32[]{:S(2)}) collective-permute-start(bf16[256,1152]{1,0:T(8,128)(2,1)} %get-tuple-element.83), channel_id=1, source_target_pairs={{0,1},{1,0},{2,3},{3,2},{4,5},{5,4},{6,7},{7,6},{8,9},{9,8},{10,11... | collective-permute-start | bytes 1769480 | tf_op jit(solution)/shard_map/ppermute | solution.py:421
  121.7 10.3 %collective-permute-start.8 = (bf16[128,1152]{1,0:T(8,128)(2,1)S(1)}, bf16[128,1152]{1,0:T(8,128)(2,1)S(1)}, u32[]{:S(2)}, u32[]{:S(2)}) collective-permute-start(bf16[128,1152]{1,0:T(8,128)(2,1)S(1)} %add_convert_fusion.2), channel_id=1, source_target_pairs={{0,2},{2,0},{1,3},{3,1},{4,6},{6,4},{5,7},{7,5},{8,10},{10,8},{9,1... | collective-permute-start | bytes 884744 | tf_op jit(solution)/shard_map/ppermute | solution.py:418
  155.0 9.7 %collective-permute-start.10 = (bf16[128,2560]{1,0:T(8,128)(2,1)}, bf16[128,2560]{1,0:T(8,128)(2,1)S(1)}, u32[]{:S(2)}, u32[]{:S(2)}) collective-permute-start(bf16[128,2560]{1,0:T(8,128)(2,1)} %get-tuple-element.89), channel_id=1, source_target_pairs={{0,1},{1,0},{2,3},{3,2},{4,5},{5,4},{6,7},{7,6},{8,9},{9,8},{10,11... | collective-permute-start | bytes 1966088 | tf_op jit(solution)/shard_map/ppermute | solution.py:421
  155.4 9.4 %collective-permute-start.9 = (bf16[128,1152]{1,0:T(8,128)(2,1)}, bf16[128,1152]{1,0:T(8,128)(2,1)S(1)}, u32[]{:S(2)}, u32[]{:S(2)}) collective-permute-start(bf16[128,1152]{1,0:T(8,128)(2,1)} %get-tuple-element.87.refs_0_), channel_id=1, source_target_pairs={{0,2},{2,0},{1,3},{3,1},{4,6},{6,4},{5,7},{7,5},{8,10},{10,8},{9,1... | collective-permute-start | bytes 884744 | tf_op jit(solution)/shard_map/ppermute | solution.py:418
  158.6 10.8 %collective-permute-start.14 = (bf16[128,5248]{1,0:T(8,128)(2,1)S(1)}, bf16[128,5248]{1,0:T(8,128)(2,1)S(1)}, u32[]{:S(2)}, u32[]{:S(2)}) collective-permute-start(bf16[128,5248]{1,0:T(8,128)(2,1)S(1)} %copy-done.17), channel_id=1, source_target_pairs={{0,1},{1,0},{2,3},{3,2},{4,5},{5,4},{6,7},{7,6},{8,9},{9,8},{10,11... | collective-permute-start | bytes 4030472 | tf_op jit(solution)/shard_map/ppermute | solution.py:421
  165.8 45.0 %collective-permute-start.11 = (bf16[128,7808]{1,0:T(8,128)(2,1)S(1)}, bf16[128,7808]{1,0:T(8,128)(2,1)}, u32[]{:S(2)}, u32[]{:S(2)}) collective-permute-start(bf16[128,7808]{1,0:T(8,128)(2,1)S(1)} %pad_maximum_fusion.refs_8_), channel_id=1, source_target_pairs={{0,2},{2,0},{1,3},{3,1},{4,6},{6,4},{5,7},{7,5},{8,10},{10,8},{9,1... | collective-permute-start | bytes 5996552 | tf_op jit(solution)/shard_map/ppermute | solution.py:418
  167.4 2.0 collective-permute-start.13
  179.6 7.3 %collective-permute-start.15 = (bf16[256,1152]{1,0:T(8,128)(2,1)}, bf16[256,1152]{1,0:T(8,128)(2,1)S(1)}, u32[]{:S(2)}, u32[]{:S(2)}) collective-permute-start(bf16[256,1152]{1,0:T(8,128)(2,1)} %get-tuple-element.97), channel_id=1, source_target_pairs={{0,1},{1,0},{2,3},{3,2},{4,5},{5,4},{6,7},{7,6},{8,9},{9,8},{10,11... | collective-permute-start | bytes 1769480 | tf_op jit(solution)/shard_map/ppermute | solution.py:421
  212.2 9.1 %collective-permute-start.16 = (bf16[128,7808]{1,0:T(8,128)(2,1)}, bf16[128,7808]{1,0:T(8,128)(2,1)}, u32[]{:S(2)}, u32[]{:S(2)}) collective-permute-start(bf16[128,7808]{1,0:T(8,128)(2,1)} %hold.11.refs_2_), channel_id=1, source_target_pairs={{0,1},{1,0},{2,3},{3,2},{4,5},{5,4},{6,7},{7,6},{8,9},{9,8},{10,11... | collective-permute-start | bytes 5996552 | tf_op jit(solution)/shard_map/ppermute | solution.py:421
  212.3 33.6 %collective-permute-start.35 = (bf16[4,144,1152]{2,1,0:T(8,128)(2,1)}, bf16[4,144,1152]{2,1,0:T(8,128)(2,1)}, u32[]{:S(2)}, u32[]{:S(2)}) collective-permute-start(bf16[4,144,1152]{2,1,0:T(8,128)(2,1)} %get-tuple-element.133), channel_id=1, source_target_pairs={{0,8},{4,12},{8,0},{12,4},{16,24},{20,28},{24,16},{28,20},{1,9},{5... | collective-permute-start | bytes 3981320 | tf_op jit(solution)/shard_map/ppermute | solution.py:415
  215.8 32.1 %collective-permute-start.36 = (bf16[4,144,1152]{2,1,0:T(8,128)(2,1)S(1)}, bf16[4,144,1152]{2,1,0:T(8,128)(2,1)}, u32[]{:S(2)}, u32[]{:S(2)}) collective-permute-start(bf16[4,144,1152]{2,1,0:T(8,128)(2,1)S(1)} %copy-done.2), channel_id=1, source_target_pairs={{0,4},{4,0},{8,12},{12,8},{16,20},{20,16},{24,28},{28,24},{1,5},{5... | collective-permute-start | bytes 3981320 | tf_op jit(solution)/shard_map/ppermute | solution.py:415
  218.5 9.7 %collective-permute-start.17 = (bf16[128,1152]{1,0:T(8,128)(2,1)}, bf16[128,1152]{1,0:T(8,128)(2,1)S(1)}, u32[]{:S(2)}, u32[]{:S(2)}) collective-permute-start(bf16[128,1152]{1,0:T(8,128)(2,1)} %copy-done.5), channel_id=1, source_target_pairs={{0,2},{2,0},{1,3},{3,1},{4,6},{6,4},{5,7},{7,5},{8,10},{10,8},{9,1... | collective-permute-start | bytes 884744 | tf_op jit(solution)/shard_map/ppermute | solution.py:418
  233.4 18.8 %collective-permute-start.18 = (bf16[128,1152]{1,0:T(8,128)(2,1)}, bf16[128,1152]{1,0:T(8,128)(2,1)S(1)}, u32[]{:S(2)}, u32[]{:S(2)}) collective-permute-start(bf16[128,1152]{1,0:T(8,128)(2,1)} %get-tuple-element.103.refs_0_.refs_2_), channel_id=1, source_target_pairs={{0,2},{2,0},{1,3},{3,1},{4,6},{6,4},{5,7},{7,5},{8,10},{10,8},{9,1... | collective-permute-start | bytes 884744 | tf_op jit(solution)/shard_map/ppermute | solution.py:418
  234.3 23.1 %collective-permute-start.19 = (bf16[128,1152]{1,0:T(8,128)(2,1)}, bf16[128,1152]{1,0:T(8,128)(2,1)S(1)}, u32[]{:S(2)}, u32[]{:S(2)}) collective-permute-start(bf16[128,1152]{1,0:T(8,128)(2,1)} %get-tuple-element.103.refs_0_.refs_2_), channel_id=1, source_target_pairs={{0,1},{1,0},{2,3},{3,2},{4,5},{5,4},{6,7},{7,6},{8,9},{9,8},{10,11... | collective-permute-start | bytes 884744 | tf_op jit(solution)/shard_map/ppermute | solution.py:421
  234.3 60.0 %collective-permute-start.24 = (bf16[4,352,768]{2,1,0:T(8,128)(2,1)}, bf16[4,352,768]{2,1,0:T(8,128)(2,1)}, u32[]{:S(2)}, u32[]{:S(2)}) collective-permute-start(bf16[4,352,768]{2,1,0:T(8,128)(2,1)} %get-tuple-element.102.refs_8_), channel_id=1, source_target_pairs={{0,4},{4,0},{8,12},{12,8},{16,20},{20,16},{24,28},{28,24},{1,5},{5... | collective-permute-start | bytes 6488072 | tf_op jit(solution)/shard_map/ppermute | solution.py:415
  251.5 47.9 %collective-permute-start.37 = (bf16[2,144,1152]{2,1,0:T(8,128)(2,1)}, bf16[2,144,1152]{2,1,0:T(8,128)(2,1)}, u32[]{:S(2)}, u32[]{:S(2)}) collective-permute-start(bf16[2,144,1152]{2,1,0:T(8,128)(2,1)} %slice.457), channel_id=1, source_target_pairs={{0,16},{4,20},{8,24},{12,28},{16,0},{20,4},{24,8},{28,12},{1,17},{... | collective-permute-start | bytes 1990664 | tf_op jit(solution)/shard_map/ppermute | solution.py:415
  252.2 5.2 %collective-permute-start.20 = (bf16[128,1152]{1,0:T(8,128)(2,1)S(1)}, bf16[128,1152]{1,0:T(8,128)(2,1)S(1)}, u32[]{:S(2)}, u32[]{:S(2)}) collective-permute-start(bf16[128,1152]{1,0:T(8,128)(2,1)S(1)} %collective-permute-done.18.refs_1_), channel_id=1, source_target_pairs={{0,1},{1,0},{2,3},{3,2},{4,5},{5,4},{6,7},{7,6},{8,9},{9,8},{10,11... | collective-permute-start | bytes 884744 | tf_op jit(solution)/shard_map/ppermute | solution.py:421
  256.2 43.2 %collective-permute-start.38 = (bf16[2,144,1152]{2,1,0:T(8,128)(2,1)}, bf16[2,144,1152]{2,1,0:T(8,128)(2,1)}, u32[]{:S(2)}, u32[]{:S(2)}) collective-permute-start(bf16[2,144,1152]{2,1,0:T(8,128)(2,1)} %slice.456), channel_id=1, source_target_pairs={{0,8},{4,12},{8,0},{12,4},{16,24},{20,28},{24,16},{28,20},{1,9},{5... | collective-permute-start | bytes 1990664 | tf_op jit(solution)/shard_map/ppermute | solution.py:415
  269.9 2.3 collective-permute-start.22
  270.0 5.8 %collective-permute-start.29 = (f32[1,7168]{1,0:T(1,128)S(1)}, f32[1,7168]{1,0:T(1,128)S(1)}, u32[]{:S(2)}, u32[]{:S(2)}) collective-permute-start(f32[1,7168]{1,0:T(1,128)S(1)} %constant_dynamic-update-slice_fusion.6), channel_id=1, source_target_pairs={{0,1},{1,0},{2,3},{3,2},{4,5},{5,4},{6,7},{7,6},{8,9},{9,8},{10,11... | collective-permute-start | bytes 86024 | tf_op jit(solution)/shard_map/ppermute | solution.py:421
  273.0 9.5 %collective-permute-start.23 = (bf16[128,1152]{1,0:T(8,128)(2,1)}, bf16[128,1152]{1,0:T(8,128)(2,1)}, u32[]{:S(2)}, u32[]{:S(2)}) collective-permute-start(bf16[128,1152]{1,0:T(8,128)(2,1)} %add_convert_fusion), channel_id=1, source_target_pairs={{0,2},{2,0},{1,3},{3,1},{4,6},{6,4},{5,7},{7,5},{8,10},{10,8},{9,1... | collective-permute-start | bytes 884744 | tf_op jit(solution)/shard_map/ppermute | solution.py:418
  280.9 51.8 %collective-permute-start.21 = (bf16[4,144,1184]{2,1,0:T(8,128)(2,1)}, bf16[4,144,1184]{2,1,0:T(8,128)(2,1)}, u32[]{:S(2)}, u32[]{:S(2)}) collective-permute-start(bf16[4,144,1184]{2,1,0:T(8,128)(2,1)} %get-tuple-element.109.refs_8_), channel_id=1, source_target_pairs={{0,4},{4,0},{8,12},{12,8},{16,20},{20,16},{24,28},{28,24},{1,5},{5... | collective-permute-start | bytes 4091912 | tf_op jit(solution)/shard_map/ppermute | solution.py:415
  298.0 32.4 %collective-permute-start.25 = (bf16[2,352,768]{2,1,0:T(8,128)(2,1)S(1)}, bf16[2,352,768]{2,1,0:T(8,128)(2,1)}, u32[]{:S(2)}, u32[]{:S(2)}) collective-permute-start(bf16[2,352,768]{2,1,0:T(8,128)(2,1)S(1)} %slice.454.refs_1_.refs_2_), channel_id=1, source_target_pairs={{0,8},{4,12},{8,0},{12,4},{16,24},{20,28},{24,16},{28,20},{1,9},{5... | collective-permute-start | bytes 3244040 | tf_op jit(solution)/shard_map/ppermute | solution.py:415
  303.5 36.0 %collective-permute-start.39 = (bf16[1,144,1152]{2,1,0:T(8,128)(2,1)}, bf16[1,144,1152]{2,1,0:T(8,128)(2,1)}, u32[]{:S(2)}, u32[]{:S(2)}) collective-permute-start(bf16[1,144,1152]{2,1,0:T(8,128)(2,1)} %slice.461), channel_id=1, source_target_pairs={{0,4},{4,0},{8,12},{12,8},{16,20},{20,16},{24,28},{28,24},{1,5},{5... | collective-permute-start | bytes 995336 | tf_op jit(solution)/shard_map/ppermute | solution.py:415
  304.9 5.1 %collective-permute-start.30 = (f32[1,34816]{1,0:T(1,128)S(1)}, f32[1,34816]{1,0:T(1,128)S(1)}, u32[]{:S(2)}, u32[]{:S(2)}) collective-permute-start(f32[1,34816]{1,0:T(1,128)S(1)} %hold.14), channel_id=1, source_target_pairs={{0,2},{2,0},{1,3},{3,1},{4,6},{6,4},{5,7},{7,5},{8,10},{10,8},{9,1... | collective-permute-start | bytes 417800 | tf_op jit(solution)/shard_map/ppermute | solution.py:418
  308.5 31.0 %collective-permute-start.40 = (bf16[1,144,1152]{2,1,0:T(8,128)(2,1)}, bf16[1,144,1152]{2,1,0:T(8,128)(2,1)}, u32[]{:S(2)}, u32[]{:S(2)}) collective-permute-start(bf16[1,144,1152]{2,1,0:T(8,128)(2,1)} %slice.460), channel_id=1, source_target_pairs={{0,16},{4,20},{8,24},{12,28},{16,0},{20,4},{24,8},{28,12},{1,17},{... | collective-permute-start | bytes 995336 | tf_op jit(solution)/shard_map/ppermute | solution.py:415
  311.2 28.3 %all-to-all-start.3 = ((bf16[8,4,864]{2,1,0:T(4,128)(2,1)}), bf16[8,4,864]{2,1,0:T(4,128)(2,1)S(1)}, u32[]{:S(2)}, u32[]{:S(2)}) async-start(bf16[8,4,864]{2,1,0:T(4,128)(2,1)} %bitcast.140), calls=%async_computation.3 | async-start | bytes 114688 | tf_op jit(solution)/shard_map/all_to_all | solution.py:424
  332.6 23.3 %collective-permute-start.33 = (bf16[1,352,768]{2,1,0:T(8,128)(2,1)S(1)}, bf16[1,352,768]{2,1,0:T(8,128)(2,1)}, u32[]{:S(2)}, u32[]{:S(2)}) collective-permute-start(bf16[1,352,768]{2,1,0:T(8,128)(2,1)S(1)} %slice.458.refs_2_), channel_id=1, source_target_pairs={{0,16},{4,20},{8,24},{12,28},{16,0},{20,4},{24,8},{28,12},{1,17},{... | collective-permute-start | bytes 1622024 | tf_op jit(solution)/shard_map/ppermute | solution.py:415
  336.4 27.4 %collective-permute-start.32 = (bf16[2,144,1184]{2,1,0:T(8,128)(2,1)S(1)}, bf16[2,144,1184]{2,1,0:T(8,128)(2,1)}, u32[]{:S(2)}, u32[]{:S(2)}) collective-permute-start(bf16[2,144,1184]{2,1,0:T(8,128)(2,1)S(1)} %slice.455.refs_1_), channel_id=1, source_target_pairs={{0,8},{4,12},{8,0},{12,4},{16,24},{20,28},{24,16},{28,20},{1,9},{5... | collective-permute-start | bytes 2045960 | tf_op jit(solution)/shard_map/ppermute | solution.py:415
  338.0 16.8 %collective-permute-start.26 = (bf16[128,1152]{1,0:T(8,128)(2,1)}, bf16[128,1152]{1,0:T(8,128)(2,1)}, u32[]{:S(2)}, u32[]{:S(2)}) collective-permute-start(bf16[128,1152]{1,0:T(8,128)(2,1)} %get-tuple-element.116), channel_id=1, source_target_pairs={{0,2},{2,0},{1,3},{3,1},{4,6},{6,4},{5,7},{7,5},{8,10},{10,8},{9,1... | collective-permute-start | bytes 884744 | tf_op jit(solution)/shard_map/ppermute | solution.py:418
  339.5 19.1 %collective-permute-start.27 = (bf16[128,1152]{1,0:T(8,128)(2,1)}, bf16[128,1152]{1,0:T(8,128)(2,1)}, u32[]{:S(2)}, u32[]{:S(2)}) collective-permute-start(bf16[128,1152]{1,0:T(8,128)(2,1)} %get-tuple-element.116), channel_id=1, source_target_pairs={{0,1},{1,0},{2,3},{3,2},{4,5},{5,4},{6,7},{7,6},{8,9},{9,8},{10,11... | collective-permute-start | bytes 884744 | tf_op jit(solution)/shard_map/ppermute | solution.py:421
  339.6 5.0 %collective-permute-start.31 = (bf16[8,4,864]{2,1,0:T(4,128)(2,1)S(1)}, bf16[8,4,864]{2,1,0:T(4,128)(2,1)S(1)}, u32[]{:S(2)}, u32[]{:S(2)}) collective-permute-start(bf16[8,4,864]{2,1,0:T(4,128)(2,1)S(1)} %hold.15.refs_2_), channel_id=1, source_target_pairs={{0,1},{1,0},{2,3},{3,2},{4,5},{5,4},{6,7},{7,6},{8,9},{9,8},{10,11... | collective-permute-start | bytes 165896 | tf_op jit(solution)/shard_map/ppermute | solution.py:421
  354.7 3.9 collective-permute-start.28
  357.2 32.5 %collective-permute-start.41 = (bf16[352,768]{1,0:T(8,128)(2,1)S(1)}, bf16[352,768]{1,0:T(8,128)(2,1)}, u32[]{:S(2)}, u32[]{:S(2)}) collective-permute-start(bf16[352,768]{1,0:T(8,128)(2,1)S(1)} %fusion.20.refs_2_), channel_id=1, source_target_pairs={{0,1},{1,0},{2,3},{3,2},{4,5},{5,4},{6,7},{7,6},{8,9},{9,8},{10,11... | collective-permute-start | bytes 1622024 | tf_op jit(solution)/shard_map/ppermute | solution.py:421
  357.8 30.2 %collective-permute-start.42 = (bf16[352,768]{1,0:T(8,128)(2,1)S(1)}, bf16[352,768]{1,0:T(8,128)(2,1)}, u32[]{:S(2)}, u32[]{:S(2)}) collective-permute-start(bf16[352,768]{1,0:T(8,128)(2,1)S(1)} %fusion.20.refs_2_), channel_id=1, source_target_pairs={{0,2},{2,0},{1,3},{3,1},{4,6},{6,4},{5,7},{7,5},{8,10},{10,8},{9,1... | collective-permute-start | bytes 1622024 | tf_op jit(solution)/shard_map/ppermute | solution.py:418
  365.2 21.6 %collective-permute-start.34 = (bf16[1,144,1184]{2,1,0:T(8,128)(2,1)S(1)}, bf16[1,144,1184]{2,1,0:T(8,128)(2,1)S(1)}, u32[]{:S(2)}, u32[]{:S(2)}) collective-permute-start(bf16[1,144,1184]{2,1,0:T(8,128)(2,1)S(1)} %slice.459.refs_1_), channel_id=1, source_target_pairs={{0,16},{4,20},{8,24},{12,28},{16,0},{20,4},{24,8},{28,12},{1,17},{... | collective-permute-start | bytes 1022984 | tf_op jit(solution)/shard_map/ppermute | solution.py:415
  369.3 26.9 %all-to-all-start.4 = ((f32[8,1,18112]{2,1,0:T(1,128)}), f32[8,1,18112]{2,1,0:T(1,128)}, u32[]{:S(2)}, u32[]{:S(2)}) async-start(f32[8,1,18112]{2,1,0:T(1,128)} %copy.132), calls=%async_computation.4 | async-start | bytes 1163264 | tf_op jit(solution)/shard_map/all_to_all | solution.py:424
  388.0 2.9 collective-permute-start.43
  (77 other events, 513.9 us)
Sparse Core Ops, SparseCore 0:
  11.5 127.6 all-gather.2
